TPU v7x, 128 devices: a whole 4x4x4 slice. The times are simulated.
128 devices in a mesh: layer: 4 (over x), node: 32 (over z, y, core).
Axes of the slice: x: 4, y: 4, z: 4, core: 2. Of those that a mesh axis runs over, the one named last changes fastest.
Arguments:
- features: bfloat16 [4, 16384, 512], P(None, 'node'), may hold values from -6 to 6
- weights: bfloat16 [4, 512, 512], P('layer'), may hold values from -0.25 to 0.25
- boundary: int32 [4, 32, 128], P(None, 'node'), may hold values from 0 to 511
- pick_index: int32 [4, 32, 32, 64], P(None, 'node'), may hold values from 0 to 127
- counts: int32 [4, 32, 4], P(None, 'node'), may hold values from 1 to 12, 20 in all within a row
- tile_cols: int32 [4, 32, 20], P(None, 'node'), may hold values from 0 to 23
- tile_vals: bfloat16 [4, 32, 20, 128, 128], P(None, 'node'), may hold values from -0.25 to 0.25
Outputs:
- jumping: bfloat16 [4, 16384, 2048], P(None, 'node', 'layer')
Inputs may be any that keep to these rules, and one draw needn't show every extreme that they name: boundary[c, n, k] is a row index within device n's own 512 rows of span c. pick_index[c, p, q, b] names which of device p's offered rows is device q's b-th boundary row from p; every list has exactly 64 entries. For each span and device the counts sum to 20, and the largest is exactly 12. `tile_cols`: column tiles 0 .. 3 are the device's own rows, the next 4 its rows of the earlier span, the rest its boundary rows.
All inputs are finite; a program needn't handle non-finite values.
Results may differ from a plain program's by a relative error of at most 0.02.
Values may be sent and summed in bfloat16 or wider, within the bound.
No kernel may reach another device: no remote copies, remote signals or barrier semaphores. Data moves between devices by JAX's collectives and lax.ppermute only.
A program may use at most 128 MiB of HBM per device.

v0:
```python
import functools

import jax
import jax.numpy as jnp
from jax import lax
from jax.experimental import pallas as pl
from jax.experimental.pallas import tpu as pltpu
from jax.sharding import PartitionSpec as P

TILE = 128
ANY = pl.BlockSpec(memory_space=pl.ANY)
SMEM = pl.BlockSpec(memory_space=pltpu.SMEM)
VMEM = pl.BlockSpec(memory_space=pltpu.VMEM)


def offer(rows, export_sel, chooser, sent_ref):
    exported = jnp.dot(export_sel, rows, preferred_element_type=jnp.float32).astype(jnp.bfloat16)
    sent = jnp.dot(chooser, exported, preferred_element_type=jnp.float32)
    sent_ref[...] = sent.astype(jnp.bfloat16)


def first_kernel(span_ref, features_ref, export_ref, chooser_ref, sent_ref, rows, sem):
    copy = pltpu.make_async_copy(features_ref.at[span_ref[0]], rows, sem)
    copy.start()
    copy.wait()
    offer(rows[...], export_ref[...], chooser_ref[...], sent_ref)


def layer_kernel(
    layer_id, first, last,
    span_ref, counts_ref, cols_ref, current_ref, previous_ref, received_ref, vals_ref, weights_ref,
    export_ref, chooser_ref, *rest,
):
    if last:
        out_ref, space, tiles, weight, total, sems = rest
    else:
        out_ref, sent_ref, space, tiles, weight, total, sems = rest
    span = span_ref[0]
    row_count = total.shape[0]
    if first:
        current_src = current_ref.at[span]
        previous_src = previous_ref.at[jnp.maximum(span - 1, 0)]
    else:
        current_src, previous_src = current_ref, previous_ref
    own = space.at[pl.ds(0, row_count)]
    earlier = space.at[pl.ds(row_count, row_count)]
    others = space.at[pl.ds(2 * row_count, received_ref.shape[0])]
    copies = [
        pltpu.make_async_copy(vals_ref.at[span, 0], tiles, sems.at[0]),
        pltpu.make_async_copy(current_src, own, sems.at[1]),
        pltpu.make_async_copy(previous_src, earlier, sems.at[2]),
        pltpu.make_async_copy(received_ref, others, sems.at[3]),
        pltpu.make_async_copy(weights_ref.at[layer_id], weight, sems.at[4]),
    ]
    for copy in copies:
        copy.start()
    total[...] = jnp.zeros_like(total)
    for copy in copies:
        copy.wait()

    @pl.when(span == 0)
    def _():
        earlier[...] = jnp.zeros_like(earlier)

    ends = []
    reached = 0
    for r in range(counts_ref.shape[1] - 1):
        reached = reached + counts_ref[span, r]
        ends.append(reached)
    for f in range(cols_ref.shape[1]):
        owner = sum((f >= end).astype(jnp.int32) for end in ends)
        row_at = pl.ds(pl.multiple_of(owner * TILE, TILE), TILE)
        col_at = pl.ds(pl.multiple_of(cols_ref[span, f] * TILE, TILE), TILE)
        total[row_at, :] += jnp.dot(tiles[f], space[col_at, :], preferred_element_type=jnp.float32)
    aggregate = total[...].astype(jnp.bfloat16)
    linear = jnp.dot(aggregate, weight[...], preferred_element_type=jnp.float32)
    fresh = jnp.maximum(linear, 0.0).astype(jnp.bfloat16)
    out_ref[...] = fresh
    if not last:
        offer(fresh, export_ref[...], chooser_ref[...], sent_ref)


def on_device(features, weights, boundary, pick_index, counts, tile_cols, tile_vals):
    spans, row_count, width = features.shape
    layers = lax.axis_size("layer")
    nodes = lax.axis_size("node")
    picks, offered = pick_index.shape[3], boundary.shape[2]
    span = lax.axis_index("layer")
    span_arr = span.astype(jnp.int32)[None]
    all_weights = lax.all_gather(weights[0], "layer")
    listed = lax.dynamic_index_in_dim(boundary, span, 0, keepdims=False)[0]
    export_sel = (listed[:, None] == jnp.arange(row_count, dtype=jnp.int32)).astype(jnp.bfloat16)
    lists = lax.dynamic_index_in_dim(pick_index, span, 0, keepdims=False)[0].reshape(-1)
    chooser = (lists[:, None] == jnp.arange(offered, dtype=jnp.int32)).astype(jnp.bfloat16)
    counts, tile_cols = counts[:, 0], tile_cols[:, 0]
    sent_shape = jax.ShapeDtypeStruct((nodes * picks, width), jnp.bfloat16)
    out_shape = jax.ShapeDtypeStruct((row_count, width), jnp.bfloat16)
    params = pltpu.CompilerParams(vmem_limit_bytes=40 << 20)
    sent = pl.pallas_call(
        first_kernel,
        out_shape=sent_shape,
        in_specs=[SMEM, ANY, VMEM, VMEM],
        out_specs=VMEM,
        scratch_shapes=[pltpu.VMEM((row_count, width), jnp.bfloat16), pltpu.SemaphoreType.DMA],
        compiler_params=params,
    )(span_arr, features, export_sel, chooser)
    current = previous = features
    outputs = []
    ring = [(i, (i + 1) % layers) for i in range(layers)]
    for layer_id in range(layers):
        first, last = layer_id == 0, layer_id == layers - 1
        received = lax.all_to_all(
            sent.reshape(nodes, picks, width), "node", split_axis=0, concat_axis=0, tiled=True
        ).reshape(nodes * picks, width)
        results = pl.pallas_call(
            functools.partial(layer_kernel, layer_id, first, last),
            out_shape=[out_shape] if last else [out_shape, sent_shape],
            in_specs=[SMEM, SMEM, SMEM, ANY, ANY, ANY, ANY, ANY, VMEM, VMEM],
            out_specs=[VMEM] if last else [VMEM, VMEM],
            scratch_shapes=[
                pltpu.VMEM((2 * row_count + nodes * picks, width), jnp.bfloat16),
                pltpu.VMEM(tile_vals.shape[2:], jnp.bfloat16),
                pltpu.VMEM((width, width), jnp.bfloat16),
                pltpu.VMEM((row_count, width), jnp.float32),
                pltpu.SemaphoreType.DMA((5,)),
            ],
            compiler_params=params,
        )(span_arr, counts, tile_cols, current, previous, received, tile_vals, all_weights, export_sel, chooser)
        outputs.append(results[0])
        if not last:
            current, sent = results
            previous = lax.ppermute(current, "layer", ring)
    return lax.all_to_all(jnp.stack(outputs), "layer", split_axis=0, concat_axis=0, tiled=True)


def solution(mesh):
    return jax.shard_map(
        on_device,
        mesh=mesh,
        in_specs=(
            P(None, "node", None),
            P("layer", None, None),
            P(None, "node", None),
            P(None, "node", None, None),
            P(None, "node", None),
            P(None, "node", None),
            P(None, "node", None, None, None),
        ),
        out_specs=P(None, "node", "layer"),
        check_vma=False,
    )
```

profile of v0, /device:TPU:6, one launch (start us, length us, event | category | flops | bytes accessed | tf_op | source)
XLA Modules:
  0.0 226.4 jit_solution(10851508412678979283)
XLA Ops:
  6.5 0.0 copy-start
  6.5 0.0 all-gather.2.cloned.1.call-start
  6.5 0.7 all-gather.2.cloned.1.call-update
  7.3 0.1 copy-done
  7.4 0.1 eq.34
  7.5 0.7 dynamic-slice_bitcast_fusion
  8.1 0.1 fusion.1.export_ref
  8.2 0.3 fusion.chooser_ref
  8.5 0.0 copy-start.6
  8.6 1.6 copy-done.6
  10.1 1.0 shard_map.73
  11.1 0.0 copy-start.1
  11.1 0.0 copy-start.26
  11.1 0.0 copy-start.27
  11.1 36.9 %all_to_all.25 = bf16[32,64,512]{2,1,0:T(8,128)(2,1)} all-to-all(bf16[32,64,512]{2,1,0:T(8,128)(2,1)S(1)} %bitcast.19), channel_id=1, replica_groups=mesh['layer'=4,'node'=32] {'node'}, dimensions={0} | all-to-all | bytes 4194304 | tf_op jit(solution)/shard_map/all_to_all | solution.py:112
  48.1 0.0 copy-done.1
  48.1 0.0 copy-done.26
  48.1 0.0 copy-done.27
  48.1 0.0 copy-start.2
  48.1 1.6 copy-done.2
  49.7 1.6 copy-done.7
  51.3 1.6 copy-done.8
  52.9 3.3 %shard_map.74 = (bf16[512,512]{1,0:T(8,128)(2,1)S(1)}, bf16[2048,512]{1,0:T(8,128)(2,1)S(1)}) custom-call(s32[1]{0:T(128)} %bitcast.span_ref, s32[4,4]{1,0:T(4,128)S(1)} %bitcast.28, s32[4,20]{1,0:T(4,128)S(1)} %bitcast.32, bf16[4,512,512]{2,1,0:T(8,128)(2,1)S(1)} %copy-done.7, bf16[4,512,512]{2,1,0:T(8,128)(2,1)S(1)} %copy-done.7, ...), custom_call_target="tpu_custom_call" | custom-call | tf_op jit(solution)/shard_map/pallas_call | solution.py:115
  56.2 0.0 copy-start.11
  56.2 1.3 copy-done.11
  57.5 0.8 copy-done.14
  58.3 4.8 %all-to-all-start.1 = ((bf16[32,64,512]{2,1,0:T(8,128)(2,1)}), bf16[32,64,512]{2,1,0:T(8,128)(2,1)}, u32[]{:S(2)}, u32[]{:S(2)}) async-start(bf16[32,64,512]{2,1,0:T(8,128)(2,1)} %bitcast.23), calls=%async_computation.1 | async-start | bytes 4194304 | tf_op jit(solution)/shard_map/all_to_all | solution.py:112
  63.1 0.6 collective-permute-start
  63.6 13.6 %collective-permute-done.previous_ref = bf16[512,512]{1,0:T(8,128)(2,1)S(1)} collective-permute-done((bf16[512,512]{1,0:T(8,128)(2,1)}, bf16[512,512]{1,0:T(8,128)(2,1)S(1)}, u32[]{:S(2)}, u32[]{:S(2)}) %collective-permute-start) | collective-permute-done | bytes 524320 | tf_op jit(solution)/shard_map/ppermute | solution.py:132
  77.3 0.8 copy-done.22
  78.1 14.9 %all-to-all-done.1 = bf16[32,64,512]{2,1,0:T(8,128)(2,1)} async-done(((bf16[32,64,512]{2,1,0:T(8,128)(2,1)}), bf16[32,64,512]{2,1,0:T(8,128)(2,1)}, u32[]{:S(2)}, u32[]{:S(2)}) %all-to-all-start.1) | async-done | bytes 2097184 | tf_op jit(solution)/shard_map/all_to_all | solution.py:112
  93.0 1.6 copy-done.3
  94.6 1.0 copy-done.15
  95.7 1.0 copy-done.23
  96.7 4.6 %shard_map.75 = (bf16[512,512]{1,0:T(8,128)(2,1)S(1)}, bf16[2048,512]{1,0:T(8,128)(2,1)S(1)}) custom-call(s32[1]{0:T(128)} %bitcast.span_ref, s32[4,4]{1,0:T(4,128)S(1)} %bitcast.29, s32[4,20]{1,0:T(4,128)S(1)} %bitcast.33, bf16[512,512]{1,0:T(8,128)(2,1)S(1)} %copy-done.15, bf16[512,512]{1,0:T(8,128)(2,1)S(1)} %copy-done.23, ...), custom_call_target="tpu_custom_call" | custom-call | tf_op jit(solution)/shard_map/pallas_call | solution.py:115
  101.3 0.0 copy-start.9
  101.3 1.3 copy-done.9
  102.6 0.8 copy-done.17
  103.5 4.8 %all-to-all-start.2 = ((bf16[32,64,512]{2,1,0:T(8,128)(2,1)}), bf16[32,64,512]{2,1,0:T(8,128)(2,1)}, u32[]{:S(2)}, u32[]{:S(2)}) async-start(bf16[32,64,512]{2,1,0:T(8,128)(2,1)} %bitcast.21), calls=%async_computation.2 | async-start | bytes 4194304 | tf_op jit(solution)/shard_map/all_to_all | solution.py:112
  108.3 0.6 collective-permute-start.1
  108.9 13.6 %collective-permute-done.1.previous_ref = bf16[512,512]{1,0:T(8,128)(2,1)S(1)} collective-permute-done((bf16[512,512]{1,0:T(8,128)(2,1)}, bf16[512,512]{1,0:T(8,128)(2,1)S(1)}, u32[]{:S(2)}, u32[]{:S(2)}) %collective-permute-start.1) | collective-permute-done | bytes 524320 | tf_op jit(solution)/shard_map/ppermute | solution.py:132
  122.5 0.8 copy-done.24
  123.3 15.0 %all-to-all-done.2 = bf16[32,64,512]{2,1,0:T(8,128)(2,1)} async-done(((bf16[32,64,512]{2,1,0:T(8,128)(2,1)}), bf16[32,64,512]{2,1,0:T(8,128)(2,1)}, u32[]{:S(2)}, u32[]{:S(2)}) %all-to-all-start.2) | async-done | bytes 2097184 | tf_op jit(solution)/shard_map/all_to_all | solution.py:112
  138.2 1.6 copy-done.4
  139.8 1.0 copy-done.18
  140.9 1.0 copy-done.25
  141.9 4.6 %shard_map.76 = (bf16[512,512]{1,0:T(8,128)(2,1)S(1)}, bf16[2048,512]{1,0:T(8,128)(2,1)S(1)}) custom-call(s32[1]{0:T(128)} %bitcast.span_ref, s32[4,4]{1,0:T(4,128)S(1)} %bitcast.30, s32[4,20]{1,0:T(4,128)S(1)} %bitcast.34, bf16[512,512]{1,0:T(8,128)(2,1)S(1)} %copy-done.18, bf16[512,512]{1,0:T(8,128)(2,1)S(1)} %copy-done.25, ...), custom_call_target="tpu_custom_call" | custom-call | tf_op jit(solution)/shard_map/pallas_call | solution.py:115
  146.5 0.0 copy-start.10
  146.5 1.3 copy-done.10
  147.8 0.8 copy-done.12
  148.6 4.8 %all-to-all-start.3 = ((bf16[32,64,512]{2,1,0:T(8,128)(2,1)}), bf16[32,64,512]{2,1,0:T(8,128)(2,1)}, u32[]{:S(2)}, u32[]{:S(2)}) async-start(bf16[32,64,512]{2,1,0:T(8,128)(2,1)} %bitcast.22), calls=%async_computation.3 | async-start | bytes 4194304 | tf_op jit(solution)/shard_map/all_to_all | solution.py:112
  153.4 0.6 collective-permute-start.2
  154.0 13.6 %collective-permute-done.2.previous_ref = bf16[512,512]{1,0:T(8,128)(2,1)S(1)} collective-permute-done((bf16[512,512]{1,0:T(8,128)(2,1)}, bf16[512,512]{1,0:T(8,128)(2,1)S(1)}, u32[]{:S(2)}, u32[]{:S(2)}) %collective-permute-start.2) | collective-permute-done | bytes 524320 | tf_op jit(solution)/shard_map/ppermute | solution.py:132
  167.6 0.8 copy-done.20
  168.4 14.9 %all-to-all-done.3 = bf16[32,64,512]{2,1,0:T(8,128)(2,1)} async-done(((bf16[32,64,512]{2,1,0:T(8,128)(2,1)}), bf16[32,64,512]{2,1,0:T(8,128)(2,1)}, u32[]{:S(2)}, u32[]{:S(2)}) %all-to-all-start.3) | async-done | bytes 2097184 | tf_op jit(solution)/shard_map/all_to_all | solution.py:112
  183.4 1.6 copy-done.5
  185.0 1.0 copy-done.13
  186.0 1.0 copy-done.21
  187.0 3.8 %shard_map.77 = bf16[512,512]{1,0:T(8,128)(2,1)S(1)} custom-call(s32[1]{0:T(128)} %bitcast.span_ref, s32[4,4]{1,0:T(4,128)S(1)} %bitcast.31, s32[4,20]{1,0:T(4,128)S(1)} %bitcast.35, bf16[512,512]{1,0:T(8,128)(2,1)S(1)} %copy-done.13, bf16[512,512]{1,0:T(8,128)(2,1)S(1)} %copy-done.21, bf16[2048,512]{1,0:T(8,128)(2,1)} %bitcast.14.received_ref, ...), custom_call_target="tpu_custom_call" | custom-call | tf_op jit(solution)/shard_map/pallas_call | solution.py:115
  190.8 0.0 copy-done.16
  190.8 0.0 copy-done.19
  190.8 0.3 pad_maximum_fusion
  191.1 27.1 %all_to_all.26 = bf16[4,512,512]{2,1,0:T(8,128)(2,1)S(1)} all-to-all(bf16[4,512,512]{2,1,0:T(8,128)(2,1)S(1)} %pad_maximum_fusion), channel_id=1, replica_groups=mesh['layer'=4,'node'=32] {'layer'}, dimensions={0} | all-to-all | bytes 4194304 | tf_op jit(solution)/shard_map/all_to_all | solution.py:133
  218.2 1.3 copy.9
  (21 shorter events, 0.0 us)
Async XLA Ops:
  6.5 0.8 copy-start
  6.5 41.6 %all-gather.2.cloned.1.call-start = ((), (), s32[]{:S(2)}) async-start(), calls=%async_computation.5 | async-start | bytes 2621440 | tf_op jit(solution)/shard_map/all_gather | solution.py:90
  8.5 1.6 copy-start.6
  11.1 37.0 %copy-start.1 = (bf16[4,1,20,128,128]{4,3,2,1,0:T(8,128)(2,1)S(1)}, bf16[4,1,20,128,128]{4,3,2,1,0:T(8,128)(2,1)}, u32[]{:S(2)}) copy-start(bf16[4,1,20,128,128]{4,3,2,1,0:T(8,128)(2,1)} %vals_ref.7) | copy-start | bytes 7864324
  11.1 37.0 %copy-start.26 = (s32[4,1,4]{2,1,0:T(1,128)S(1)}, s32[4,1,4]{2,1,0:T(1,128)}, u32[]{:S(2)}) copy-start(s32[4,1,4]{2,1,0:T(1,128)} %param.11) | copy-start | bytes 196
  11.1 37.0 %copy-start.27 = (s32[4,1,20]{2,1,0:T(1,128)S(1)}, s32[4,1,20]{2,1,0:T(1,128)}, u32[]{:S(2)}) copy-start(s32[4,1,20]{2,1,0:T(1,128)} %param.12) | copy-start | bytes 964
  48.1 1.6 copy-start.2
  49.7 1.6 copy-start.7
  51.3 1.6 copy-start.8
  56.2 1.3 copy-start.11
  57.5 0.8 copy-start.14
  58.3 34.7 %all-to-all-start.1 = ((bf16[32,64,512]{2,1,0:T(8,128)(2,1)}), bf16[32,64,512]{2,1,0:T(8,128)(2,1)}, u32[]{:S(2)}, u32[]{:S(2)}) async-start(bf16[32,64,512]{2,1,0:T(8,128)(2,1)} %bitcast.23), calls=%async_computation.1 | async-start | bytes 4194304 | tf_op jit(solution)/shard_map/all_to_all | solution.py:112
  63.1 14.2 %collective-permute-start = (bf16[512,512]{1,0:T(8,128)(2,1)}, bf16[512,512]{1,0:T(8,128)(2,1)S(1)}, u32[]{:S(2)}, u32[]{:S(2)}) collective-permute-start(bf16[512,512]{1,0:T(8,128)(2,1)} %copy-done.14), channel_id=1, source_target_pairs={{0,32},{32,64},{64,96},{96,0},{1,33},{33,65},{65,97},{97,1},{2,34}... | collective-permute-start | bytes 1572872 | tf_op jit(solution)/shard_map/ppermute | solution.py:132
  77.3 0.8 copy-start.22
  93.0 1.6 copy-start.3
  94.6 1.0 copy-start.15
  95.7 1.0 copy-start.23
  101.3 1.3 copy-start.9
  102.6 0.8 copy-start.17
  103.5 34.7 %all-to-all-start.2 = ((bf16[32,64,512]{2,1,0:T(8,128)(2,1)}), bf16[32,64,512]{2,1,0:T(8,128)(2,1)}, u32[]{:S(2)}, u32[]{:S(2)}) async-start(bf16[32,64,512]{2,1,0:T(8,128)(2,1)} %bitcast.21), calls=%async_computation.2 | async-start | bytes 4194304 | tf_op jit(solution)/shard_map/all_to_all | solution.py:112
  108.3 14.2 %collective-permute-start.1 = (bf16[512,512]{1,0:T(8,128)(2,1)}, bf16[512,512]{1,0:T(8,128)(2,1)S(1)}, u32[]{:S(2)}, u32[]{:S(2)}) collective-permute-start(bf16[512,512]{1,0:T(8,128)(2,1)} %copy-done.17), channel_id=1, source_target_pairs={{0,32},{32,64},{64,96},{96,0},{1,33},{33,65},{65,97},{97,1},{2,34}... | collective-permute-start | bytes 1572872 | tf_op jit(solution)/shard_map/ppermute | solution.py:132
  122.5 0.8 copy-start.24
  138.2 1.6 copy-start.4
  139.8 1.0 copy-start.18
  140.9 1.0 copy-start.25
  146.5 1.3 copy-start.10
  147.8 0.8 copy-start.12
  148.6 34.7 %all-to-all-start.3 = ((bf16[32,64,512]{2,1,0:T(8,128)(2,1)}), bf16[32,64,512]{2,1,0:T(8,128)(2,1)}, u32[]{:S(2)}, u32[]{:S(2)}) async-start(bf16[32,64,512]{2,1,0:T(8,128)(2,1)} %bitcast.22), calls=%async_computation.3 | async-start | bytes 4194304 | tf_op jit(solution)/shard_map/all_to_all | solution.py:112
  153.4 14.2 %collective-permute-start.2 = (bf16[512,512]{1,0:T(8,128)(2,1)}, bf16[512,512]{1,0:T(8,128)(2,1)S(1)}, u32[]{:S(2)}, u32[]{:S(2)}) collective-permute-start(bf16[512,512]{1,0:T(8,128)(2,1)} %copy-done.12), channel_id=1, source_target_pairs={{0,32},{32,64},{64,96},{96,0},{1,33},{33,65},{65,97},{97,1},{2,34}... | collective-permute-start | bytes 1572872 | tf_op jit(solution)/shard_map/ppermute | solution.py:132
  167.6 0.8 copy-start.20
  183.4 1.6 copy-start.5
  185.0 1.0 copy-start.13
  186.0 1.0 copy-start.21
  187.0 3.8 %copy-start.16 = (bf16[512,512]{1,0:T(8,128)(2,1)S(1)}, bf16[512,512]{1,0:T(8,128)(2,1)}, u32[]{:S(2)}) copy-start(bf16[512,512]{1,0:T(8,128)(2,1)} %copy-done.14) | copy-start | bytes 1572868
  187.0 3.8 %copy-start.19 = (bf16[512,512]{1,0:T(8,128)(2,1)S(1)}, bf16[512,512]{1,0:T(8,128)(2,1)}, u32[]{:S(2)}) copy-start(bf16[512,512]{1,0:T(8,128)(2,1)} %copy-done.17) | copy-start | bytes 1572868
Sparse Core Ops, SparseCore 0:
  9.0 31.2 all-gather.1
where the time goes:
time: 229 us; the launch traced here: 226 us
  waiting for transfers between devices  86.3 us (38%)
  blocking collectives  64 us (28%)
  local copies, waits for them, and re-layouts  28.4 us (12%)
  Pallas kernels  17.2 us (8%)
  starting transfers between devices  16.1 us (7%)
  between operations  13.6 us (6%)
    all_to_all x3, waiting for transfers between devices, on_device(): lax.all_to_all(sent.reshape(nodes, picks, width), 'node', split_axis=0, c...  44.8 us
    ppermute x3, waiting for transfers between devices, on_device(): previous = lax.ppermute(current, 'layer', ring)  40.8 us
    all_to_all x1, blocking collectives, on_device(): lax.all_to_all(sent.reshape(nodes, picks, width), 'node', split_axis=0, c...  36.9 us
    unnamed x57, local copies, waits for them, and re-layouts  27.6 us
    all_to_all x1, blocking collectives, on_device(): lax.all_to_all(jnp.stack(outputs), 'layer', split_axis=0, concat_axis=0,...  27.1 us
    pallas_call x4, Pallas kernels, on_device(): pl.pallas_call(functools.partial(layer_kernel, layer_id, first, last), ou...  16.2 us
    all_to_all x3, starting transfers between devices, on_device(): lax.all_to_all(sent.reshape(nodes, picks, width), 'node', split_axis=0, c...  14.4 us
  transfers between devices with their start and end apart: 7, of which 6 were waited for; matrix products, arithmetic and copies ran while one was open for 1% of the time, Pallas kernels for 0%

commit v1 on v0

--- a/solution.py
+++ b/solution.py
@@ -28,9 +28,9 @@
 
 def layer_kernel(
     layer_id, first, last,
-    span_ref, counts_ref, cols_ref, current_ref, previous_ref, received_ref, vals_ref, weights_ref,
-    export_ref, chooser_ref, *rest,
+    span_ref, counts_ref, cols_ref, current_ref, previous_ref, received_ref, vals_ref, export_ref, chooser_ref, *rest,
 ):
+    weight_refs, rest = rest[:4], rest[4:]
     if last:
         out_ref, space, tiles, weight, total, sems = rest
     else:
@@ -45,18 +45,23 @@
     own = space.at[pl.ds(0, row_count)]
     earlier = space.at[pl.ds(row_count, row_count)]
     others = space.at[pl.ds(2 * row_count, received_ref.shape[0])]
+    for distance, source in enumerate(weight_refs):
+        @pl.when((span + len(weight_refs) - distance) % len(weight_refs) == layer_id)
+        def _():
+            pltpu.make_async_copy(source, weight, sems.at[4]).start()
+
     copies = [
         pltpu.make_async_copy(vals_ref.at[span, 0], tiles, sems.at[0]),
         pltpu.make_async_copy(current_src, own, sems.at[1]),
         pltpu.make_async_copy(previous_src, earlier, sems.at[2]),
         pltpu.make_async_copy(received_ref, others, sems.at[3]),
-        pltpu.make_async_copy(weights_ref.at[layer_id], weight, sems.at[4]),
     ]
     for copy in copies:
         copy.start()
     total[...] = jnp.zeros_like(total)
     for copy in copies:
         copy.wait()
+    pltpu.make_async_copy(weight_refs[0], weight, sems.at[4]).wait()
 
     @pl.when(span == 0)
     def _():
@@ -80,6 +85,33 @@
         offer(fresh, export_ref[...], chooser_ref[...], sent_ref)
 
 
+def place_kernel(span_ref, *refs):
+    spans = refs[-2].shape[0]
+    out_ref, sems = refs[-2], refs[-1]
+    layers = (len(refs) - 2) // spans
+    span = span_ref[0]
+    for layer_id in range(layers):
+        @pl.when(span == layer_id)
+        def _():
+            copies = []
+            for distance in range(spans):
+                source = refs[layer_id * spans + distance]
+                target = out_ref.at[(layer_id - distance) % spans]
+                copies.append(pltpu.make_async_copy(source, target, sems.at[distance]))
+            for copy in copies:
+                copy.start()
+            for copy in copies:
+                copy.wait()
+
+
+def shifted(block, distance, only=None):
+    planes = lax.axis_size("layer")
+    route = [(i, (i + distance) % planes) for i in range(planes)]
+    if only is not None:
+        route = [pair for pair in route if pair[1] == only]
+    return lax.ppermute(block, "layer", route)
+
+
 def on_device(features, weights, boundary, pick_index, counts, tile_cols, tile_vals):
     spans, row_count, width = features.shape
     layers = lax.axis_size("layer")
@@ -87,7 +119,6 @@
     picks, offered = pick_index.shape[3], boundary.shape[2]
     span = lax.axis_index("layer")
     span_arr = span.astype(jnp.int32)[None]
-    all_weights = lax.all_gather(weights[0], "layer")
     listed = lax.dynamic_index_in_dim(boundary, span, 0, keepdims=False)[0]
     export_sel = (listed[:, None] == jnp.arange(row_count, dtype=jnp.int32)).astype(jnp.bfloat16)
     lists = lax.dynamic_index_in_dim(pick_index, span, 0, keepdims=False)[0].reshape(-1)
@@ -95,7 +126,7 @@
     counts, tile_cols = counts[:, 0], tile_cols[:, 0]
     sent_shape = jax.ShapeDtypeStruct((nodes * picks, width), jnp.bfloat16)
     out_shape = jax.ShapeDtypeStruct((row_count, width), jnp.bfloat16)
-    params = pltpu.CompilerParams(vmem_limit_bytes=40 << 20)
+    params = pltpu.CompilerParams(vmem_limit_bytes=56 << 20)
     sent = pl.pallas_call(
         first_kernel,
         out_shape=sent_shape,
@@ -105,17 +136,20 @@
         compiler_params=params,
     )(span_arr, features, export_sel, chooser)
     current = previous = features
-    outputs = []
-    ring = [(i, (i + 1) % layers) for i in range(layers)]
+    mine = weights[0]
+    known = None
+    placed = []
     for layer_id in range(layers):
         first, last = layer_id == 0, layer_id == layers - 1
         received = lax.all_to_all(
             sent.reshape(nodes, picks, width), "node", split_axis=0, concat_axis=0, tiled=True
         ).reshape(nodes * picks, width)
+        if first:
+            known = [mine] + [shifted(mine, distance) for distance in range(1, layers)]
         results = pl.pallas_call(
             functools.partial(layer_kernel, layer_id, first, last),
             out_shape=[out_shape] if last else [out_shape, sent_shape],
-            in_specs=[SMEM, SMEM, SMEM, ANY, ANY, ANY, ANY, ANY, VMEM, VMEM],
+            in_specs=[SMEM, SMEM, SMEM, ANY, ANY, ANY, ANY, VMEM, VMEM] + [ANY] * layers,
             out_specs=[VMEM] if last else [VMEM, VMEM],
             scratch_shapes=[
                 pltpu.VMEM((2 * row_count + nodes * picks, width), jnp.bfloat16),
@@ -125,12 +159,20 @@
                 pltpu.SemaphoreType.DMA((5,)),
             ],
             compiler_params=params,
-        )(span_arr, counts, tile_cols, current, previous, received, tile_vals, all_weights, export_sel, chooser)
-        outputs.append(results[0])
+        )(span_arr, counts, tile_cols, current, previous, received, tile_vals, export_sel, chooser, *known)
+        current = results[0]
         if not last:
-            current, sent = results
-            previous = lax.ppermute(current, "layer", ring)
-    return lax.all_to_all(jnp.stack(outputs), "layer", split_axis=0, concat_axis=0, tiled=True)
+            sent = results[1]
+        previous = shifted(current, 1, layer_id if last else None)
+        placed += [current, previous, shifted(current, 2, layer_id), shifted(current, 3, layer_id)]
+    return pl.pallas_call(
+        place_kernel,
+        out_shape=jax.ShapeDtypeStruct(features.shape, features.dtype),
+        in_specs=[SMEM] + [ANY] * len(placed),
+        out_specs=ANY,
+        scratch_shapes=[pltpu.SemaphoreType.DMA((spans,))],
+        compiler_params=params,
+    )(span_arr, *placed)
 
 
 def solution(mesh):

time: 229 us -> 278 us (1.21)
  Pallas kernels: 17.2 us -> 95.4 us
  blocking collectives: 64 us -> 0 us
  waiting for transfers between devices: 86.3 us -> 123 us
  starting transfers between devices: 16.1 us -> 48.2 us
  local copies, waits for them, and re-layouts: 28.4 us -> 8.47 us
  between operations: 13.6 us -> 0.26 us
    pallas_call x0 -> x1, Pallas kernels: none -> 64.7 us  [on_device(): pl.pallas_call(place_kernel, out_shape=jax.ShapeDtypeStruct(features.shap...]
    all_to_all x2 -> x0, blocking collectives: 64 us -> none  [the longest x1 36.9 us: on_device(): lax.all_to_all(sent.reshape(nodes, picks, width), 'node', split_axis=0, c...]
    ppermute x3 -> x15, waiting for transfers between devices: 40.8 us -> 84.6 us  [shifted(): return lax.ppermute(block, 'layer', route)]
    ppermute x3 -> x15, starting transfers between devices: 1.78 us -> 26.8 us  [shifted(): return lax.ppermute(block, 'layer', route)]
    unnamed x57 -> x38, local copies, waits for them, and re-layouts: 27.6 us -> 7.74 us
    pallas_call x4, Pallas kernels: 16.2 us -> 26.3 us  [on_device(): pl.pallas_call(functools.partial(layer_kernel, layer_id, first, last), ou...]
    all_to_all x3 -> x4, starting transfers between devices: 14.4 us -> 21.4 us  [on_device(): lax.all_to_all(sent.reshape(nodes, picks, width), 'node', split_axis=0, c...]
    all_to_all x3 -> x4, waiting for transfers between devices: 44.8 us -> 38.4 us  [on_device(): lax.all_to_all(sent.reshape(nodes, picks, width), 'node', split_axis=0, c...]
  transfers between devices with their start and end apart: 7 -> 19, of which waited for: 6 -> 14; matrix products, arithmetic and copies ran while one was open for 1% -> 0% of each run, Pallas kernels for 0% -> 2%
where the time goes in v1:
time: 278 us; the launch traced here: 277 us
  waiting for transfers between devices  123 us (44%)
  Pallas kernels  95.4 us (34%)
  starting transfers between devices  48.2 us (17%)
  local copies, waits for them, and re-layouts  8.47 us (3%)
    ppermute x15, waiting for transfers between devices, shifted(): return lax.ppermute(block, 'layer', route)  84.6 us
    pallas_call x1, Pallas kernels, on_device(): pl.pallas_call(place_kernel, out_shape=jax.ShapeDtypeStruct(features.shap...  64.7 us
    all_to_all x4, waiting for transfers between devices, on_device(): lax.all_to_all(sent.reshape(nodes, picks, width), 'node', split_axis=0, c...  38.4 us
    ppermute x15, starting transfers between devices, shifted(): return lax.ppermute(block, 'layer', route)  26.8 us
    pallas_call x4, Pallas kernels, on_device(): pl.pallas_call(functools.partial(layer_kernel, layer_id, first, last), ou...  26.3 us
    all_to_all x4, starting transfers between devices, on_device(): lax.all_to_all(sent.reshape(nodes, picks, width), 'node', split_axis=0, c...  21.4 us
    unnamed x38, local copies, waits for them, and re-layouts  7.74 us
  transfers between devices with their start and end apart: 19, of which 14 were waited for; matrix products, arithmetic and copies ran while one was open for 0% of the time, Pallas kernels for 2%

profile of v1, /device:TPU:6, one launch (start us, length us, event | category | flops | bytes accessed | tf_op | source)
XLA Modules:
  0.0 277.1 jit_solution(17482088001425663244)
XLA Ops:
  0.0 0.0 copy-start
  0.0 0.8 copy-done
  0.8 0.1 eq.34
  0.9 1.1 fusion.chooser_ref
  2.1 0.7 dynamic-slice_bitcast_fusion
  2.7 0.7 fusion.1.export_ref
  3.5 4.4 %shard_map.73 = bf16[2048,512]{1,0:T(8,128)(2,1)} custom-call(s32[1]{0:T(128)} %bitcast.span_ref, bf16[4,512,512]{2,1,0:T(8,128)(2,1)} %previous_ref.1, bf16[128,512]{1,0:T(8,128)(2,1)} %fusion.1.export_ref, bf16[2048,128]{1,0:T(8,128)(2,1)} %fusion.chooser_ref), custom_call_target="tpu_custom_call" | custom-call | tf_op jit(solution)/shard_map/pallas_call | solution.py:130
  7.9 0.0 copy-start.5
  7.9 8.5 %all-to-all-start = ((bf16[32,64,512]{2,1,0:T(8,128)(2,1)}), bf16[32,64,512]{2,1,0:T(8,128)(2,1)S(1)}, u32[]{:S(2)}, u32[]{:S(2)}) async-start(bf16[32,64,512]{2,1,0:T(8,128)(2,1)} %bitcast.16), calls=%async_computation | async-start | bytes 4194304 | tf_op jit(solution)/shard_map/all_to_all | solution.py:144
  16.4 0.0 copy-done.5
  16.4 0.5 collective-permute-start
  16.9 2.4 collective-permute-start.1
  19.3 0.0 collective-permute-start.2
  19.3 11.9 %collective-permute-done.rest_1_ = bf16[512,512]{1,0:T(8,128)(2,1)S(1)} collective-permute-done((bf16[512,512]{1,0:T(8,128)(2,1)S(1)}, bf16[512,512]{1,0:T(8,128)(2,1)S(1)}, u32[]{:S(2)}, u32[]{:S(2)}) %collective-permute-start) | collective-permute-done | bytes 524320 | tf_op jit(solution)/shard_map/ppermute | solution.py:112
  31.2 2.1 collective-permute-done.1.rest_2_
  33.3 0.8 copy-done.7
  34.0 9.5 %collective-permute-done.2.rest_3_ = bf16[512,512]{1,0:T(8,128)(2,1)} collective-permute-done((bf16[512,512]{1,0:T(8,128)(2,1)S(1)}, bf16[512,512]{1,0:T(8,128)(2,1)}, u32[]{:S(2)}, u32[]{:S(2)}) %collective-permute-start.2) | collective-permute-done | bytes 524320 | tf_op jit(solution)/shard_map/ppermute | solution.py:112
  43.6 2.8 all-to-all-done
  46.3 0.0 copy-done.6
  46.3 1.3 copy-done.2
  47.7 6.9 %shard_map.74 = (bf16[512,512]{1,0:T(8,128)(2,1)}, bf16[2048,512]{1,0:T(8,128)(2,1)}) custom-call(s32[1]{0:T(128)} %bitcast.span_ref, s32[4,4]{1,0:T(4,128)} %bitcast.31, s32[4,20]{1,0:T(4,128)} %bitcast.35, bf16[4,512,512]{2,1,0:T(8,128)(2,1)} %previous_ref.1, bf16[4,512,512]{2,1,0:T(8,128)(2,1)} %previous_ref.1, bf16[2048,512]{1,0:T(8,128)(2,1)} %bitcast.18, ...), custom_call_target="tpu_custom_call" | custom-call | tf_op jit(solution)/shard_map/pallas_call | solution.py:149
  54.6 0.0 copy-start.11
  54.6 4.6 %all-to-all-start.1 = ((bf16[32,64,512]{2,1,0:T(8,128)(2,1)}), bf16[32,64,512]{2,1,0:T(8,128)(2,1)S(1)}, u32[]{:S(2)}, u32[]{:S(2)}) async-start(bf16[32,64,512]{2,1,0:T(8,128)(2,1)} %bitcast.29), calls=%async_computation.1 | async-start | bytes 4194304 | tf_op jit(solution)/shard_map/all_to_all | solution.py:144
  59.2 0.0 copy-done.11
  59.3 1.8 collective-permute-start.3
  61.0 12.4 %collective-permute-done.3.previous_ref.refs_1_ = bf16[512,512]{1,0:T(8,128)(2,1)S(1)} collective-permute-done((bf16[512,512]{1,0:T(8,128)(2,1)S(1)}, bf16[512,512]{1,0:T(8,128)(2,1)S(1)}, u32[]{:S(2)}, u32[]{:S(2)}) %collective-permute-start.3) | collective-permute-done | bytes 524320 | tf_op jit(solution)/shard_map/ppermute | solution.py:112
  73.4 15.8 %all-to-all-done.1 = bf16[32,64,512]{2,1,0:T(8,128)(2,1)S(1)} async-done(((bf16[32,64,512]{2,1,0:T(8,128)(2,1)}), bf16[32,64,512]{2,1,0:T(8,128)(2,1)S(1)}, u32[]{:S(2)}, u32[]{:S(2)}) %all-to-all-start.1) | async-done | bytes 2097184 | tf_op jit(solution)/shard_map/all_to_all | solution.py:144
  89.2 0.0 copy-done.12
  89.2 1.3 copy-done.3
  90.6 6.9 %shard_map.75 = (bf16[512,512]{1,0:T(8,128)(2,1)}, bf16[2048,512]{1,0:T(8,128)(2,1)}) custom-call(s32[1]{0:T(128)} %bitcast.span_ref, s32[4,4]{1,0:T(4,128)} %bitcast.32, s32[4,20]{1,0:T(4,128)} %bitcast.36, bf16[512,512]{1,0:T(8,128)(2,1)} %get-tuple-element.11.current_ref.refs_0_, bf16[512,512]{1,0:T(8,128)(2,1)} %copy-done.12, ...), custom_call_target="tpu_custom_call" | custom-call | tf_op jit(solution)/shard_map/pallas_call | solution.py:149
  97.5 4.2 %all-to-all-start.2 = ((bf16[32,64,512]{2,1,0:T(8,128)(2,1)}), bf16[32,64,512]{2,1,0:T(8,128)(2,1)S(1)}, u32[]{:S(2)}, u32[]{:S(2)}) async-start(bf16[32,64,512]{2,1,0:T(8,128)(2,1)} %bitcast.30), calls=%async_computation.2 | async-start | bytes 4194304 | tf_op jit(solution)/shard_map/all_to_all | solution.py:144
  101.7 1.8 collective-permute-start.6
  103.5 12.3 %collective-permute-done.6.previous_ref.refs_5_ = bf16[512,512]{1,0:T(8,128)(2,1)S(1)} collective-permute-done((bf16[512,512]{1,0:T(8,128)(2,1)S(1)}, bf16[512,512]{1,0:T(8,128)(2,1)S(1)}, u32[]{:S(2)}, u32[]{:S(2)}) %collective-permute-start.6) | collective-permute-done | bytes 524320 | tf_op jit(solution)/shard_map/ppermute | solution.py:112
  115.7 15.9 %all-to-all-done.2 = bf16[32,64,512]{2,1,0:T(8,128)(2,1)S(1)} async-done(((bf16[32,64,512]{2,1,0:T(8,128)(2,1)}), bf16[32,64,512]{2,1,0:T(8,128)(2,1)S(1)}, u32[]{:S(2)}, u32[]{:S(2)}) %all-to-all-start.2) | async-done | bytes 2097184 | tf_op jit(solution)/shard_map/all_to_all | solution.py:144
  131.6 1.3 copy-done.4
  133.0 6.9 %shard_map.76 = (bf16[512,512]{1,0:T(8,128)(2,1)}, bf16[2048,512]{1,0:T(8,128)(2,1)}) custom-call(s32[1]{0:T(128)} %bitcast.span_ref, s32[4,4]{1,0:T(4,128)} %bitcast.33, s32[4,20]{1,0:T(4,128)} %bitcast.37, bf16[512,512]{1,0:T(8,128)(2,1)} %get-tuple-element.13.current_ref.refs_4_, bf16[512,512]{1,0:T(8,128)(2,1)} %copy-done.14, ...), custom_call_target="tpu_custom_call" | custom-call | tf_op jit(solution)/shard_map/pallas_call | solution.py:149
  139.9 0.0 copy-start.8
  139.9 4.2 %all-to-all-start.3 = ((bf16[32,64,512]{2,1,0:T(8,128)(2,1)}), bf16[32,64,512]{2,1,0:T(8,128)(2,1)S(1)}, u32[]{:S(2)}, u32[]{:S(2)}) async-start(bf16[32,64,512]{2,1,0:T(8,128)(2,1)} %bitcast.28), calls=%async_computation.3 | async-start | bytes 4194304 | tf_op jit(solution)/shard_map/all_to_all | solution.py:144
  144.0 0.0 copy-done.8
  144.1 1.8 collective-permute-start.9
  145.9 1.4 collective-permute-start.4
  147.3 1.5 collective-permute-start.5
  148.8 5.8 %collective-permute-start.7 = (bf16[512,512]{1,0:T(8,128)(2,1)}, bf16[512,512]{1,0:T(8,128)(2,1)}, u32[]{:S(2)}, u32[]{:S(2)}) collective-permute-start(bf16[512,512]{1,0:T(8,128)(2,1)} %get-tuple-element.13.current_ref.refs_4_), channel_id=1, source_target_pairs={{96,32},{97,33},{98,34},{99,35},{100,36},{101,37},{102,38},{103,39... | collective-permute-start | bytes 1572872 | tf_op jit(solution)/shard_map/ppermute | solution.py:112
  154.6 1.5 collective-permute-start.8
  156.1 12.6 %collective-permute-done.9.previous_ref.refs_9_ = bf16[512,512]{1,0:T(8,128)(2,1)S(1)} collective-permute-done((bf16[512,512]{1,0:T(8,128)(2,1)S(1)}, bf16[512,512]{1,0:T(8,128)(2,1)S(1)}, u32[]{:S(2)}, u32[]{:S(2)}) %collective-permute-start.9) | collective-permute-done | bytes 524320 | tf_op jit(solution)/shard_map/ppermute | solution.py:112
  168.7 1.5 collective-permute-start.10
  170.1 3.9 %all-to-all-done.3 = bf16[32,64,512]{2,1,0:T(8,128)(2,1)S(1)} async-done(((bf16[32,64,512]{2,1,0:T(8,128)(2,1)}), bf16[32,64,512]{2,1,0:T(8,128)(2,1)S(1)}, u32[]{:S(2)}, u32[]{:S(2)}) %all-to-all-start.3) | async-done | bytes 2097184 | tf_op jit(solution)/shard_map/all_to_all | solution.py:144
  174.0 1.3 copy-done.1
  175.3 5.5 %shard_map.77.refs_12_ = bf16[512,512]{1,0:T(8,128)(2,1)} custom-call(s32[1]{0:T(128)} %bitcast.span_ref, s32[4,4]{1,0:T(4,128)} %bitcast.34, s32[4,20]{1,0:T(4,128)} %bitcast.38, bf16[512,512]{1,0:T(8,128)(2,1)} %get-tuple-element.15.current_ref.refs_8_, bf16[512,512]{1,0:T(8,128)(2,1)} %copy-done.10, bf16[2048,512]{1,0:T(8,128)(2,1)} %bitcast.17, ...), custom_call_target="tpu_custom_call" | custom-call | tf_op jit(solution)/shard_map/pallas_call | solution.py:149
  180.9 0.0 collective-permute-done.4.refs_2_
  180.9 2.9 %collective-permute-start.11 = (bf16[512,512]{1,0:T(8,128)(2,1)S(1)}, bf16[512,512]{1,0:T(8,128)(2,1)S(1)}, u32[]{:S(2)}, u32[]{:S(2)}) collective-permute-start(bf16[512,512]{1,0:T(8,128)(2,1)S(1)} %copy-done.9), channel_id=1, source_target_pairs={{96,64},{97,65},{98,66},{99,67},{100,68},{101,69},{102,70},{103,71... | collective-permute-start | bytes 1572872 | tf_op jit(solution)/shard_map/ppermute | solution.py:112
  183.8 0.0 collective-permute-done.5.refs_3_
  183.8 1.3 collective-permute-start.12
  185.1 0.0 collective-permute-done.7.refs_6_
  185.1 1.3 collective-permute-start.13
  186.4 0.0 collective-permute-done.8.refs_7_
  186.5 1.3 collective-permute-start.14
  187.8 0.0 collective-permute-done.10.refs_10_
  187.8 5.5 %collective-permute-done.11.refs_11_ = bf16[512,512]{1,0:T(8,128)(2,1)S(1)} collective-permute-done((bf16[512,512]{1,0:T(8,128)(2,1)S(1)}, bf16[512,512]{1,0:T(8,128)(2,1)S(1)}, u32[]{:S(2)}, u32[]{:S(2)}) %collective-permute-start.11) | collective-permute-done | bytes 524320 | tf_op jit(solution)/shard_map/ppermute | solution.py:112
  193.3 4.4 %collective-permute-done.12.refs_13_ = bf16[512,512]{1,0:T(8,128)(2,1)S(1)} collective-permute-done((bf16[512,512]{1,0:T(8,128)(2,1)}, bf16[512,512]{1,0:T(8,128)(2,1)S(1)}, u32[]{:S(2)}, u32[]{:S(2)}) %collective-permute-start.12) | collective-permute-done | bytes 524320 | tf_op jit(solution)/shard_map/ppermute | solution.py:112
  197.6 2.9 %collective-permute-done.13.refs_14_ = bf16[512,512]{1,0:T(8,128)(2,1)S(1)} collective-permute-done((bf16[512,512]{1,0:T(8,128)(2,1)}, bf16[512,512]{1,0:T(8,128)(2,1)S(1)}, u32[]{:S(2)}, u32[]{:S(2)}) %collective-permute-start.13) | collective-permute-done | bytes 524320 | tf_op jit(solution)/shard_map/ppermute | solution.py:112
  200.5 11.1 %collective-permute-done.14.refs_15_ = bf16[512,512]{1,0:T(8,128)(2,1)S(1)} collective-permute-done((bf16[512,512]{1,0:T(8,128)(2,1)}, bf16[512,512]{1,0:T(8,128)(2,1)S(1)}, u32[]{:S(2)}, u32[]{:S(2)}) %collective-permute-start.14) | collective-permute-done | bytes 524320 | tf_op jit(solution)/shard_map/ppermute | solution.py:112
  211.7 0.8 copy-done.18
  212.5 64.7 %shard_map.78 = bf16[4,512,512]{2,1,0:T(8,128)(2,1)} custom-call(s32[1]{0:T(128)} %bitcast.span_ref, bf16[512,512]{1,0:T(8,128)(2,1)} %get-tuple-element.11.current_ref.refs_0_, bf16[512,512]{1,0:T(8,128)(2,1)} %copy-done.12, bf16[512,512]{1,0:T(8,128)(2,1)} %collective-permute-done.4.refs_2_, bf16[512,512]{1,0:T(8,128)(2,1)} %collective-permute-done.5.refs_3_, ...), custom_call_target="tpu_custom_call" | custom-call | tf_op jit(solution)/shard_map/pallas_call | solution.py:168
  (23 shorter events, 0.0 us)
Async XLA Ops:
  0.0 0.8 copy-start
  7.9 8.5 %copy-start.5 = (bf16[1,512,512]{2,1,0:T(8,128)(2,1)S(1)}, bf16[1,512,512]{2,1,0:T(8,128)(2,1)}, u32[]{:S(2)}) copy-start(bf16[1,512,512]{2,1,0:T(8,128)(2,1)} %param.8) | copy-start | bytes 1572868
  7.9 38.5 %all-to-all-start = ((bf16[32,64,512]{2,1,0:T(8,128)(2,1)}), bf16[32,64,512]{2,1,0:T(8,128)(2,1)S(1)}, u32[]{:S(2)}, u32[]{:S(2)}) async-start(bf16[32,64,512]{2,1,0:T(8,128)(2,1)} %bitcast.16), calls=%async_computation | async-start | bytes 4194304 | tf_op jit(solution)/shard_map/all_to_all | solution.py:144
  16.4 14.8 %collective-permute-start = (bf16[512,512]{1,0:T(8,128)(2,1)S(1)}, bf16[512,512]{1,0:T(8,128)(2,1)S(1)}, u32[]{:S(2)}, u32[]{:S(2)}) collective-permute-start(bf16[512,512]{1,0:T(8,128)(2,1)S(1)} %bitcast.25), channel_id=1, source_target_pairs={{0,32},{32,64},{64,96},{96,0},{1,33},{33,65},{65,97},{97,1},{2,34}... | collective-permute-start | bytes 1572872 | tf_op jit(solution)/shard_map/ppermute | solution.py:112
  16.9 16.3 %collective-permute-start.1 = (bf16[512,512]{1,0:T(8,128)(2,1)S(1)}, bf16[512,512]{1,0:T(8,128)(2,1)S(1)}, u32[]{:S(2)}, u32[]{:S(2)}) collective-permute-start(bf16[512,512]{1,0:T(8,128)(2,1)S(1)} %bitcast.26), channel_id=1, source_target_pairs={{0,64},{32,96},{64,0},{96,32},{1,65},{33,97},{65,1},{97,33},{2,66}... | collective-permute-start | bytes 1572872 | tf_op jit(solution)/shard_map/ppermute | solution.py:112
  19.3 24.3 %collective-permute-start.2 = (bf16[512,512]{1,0:T(8,128)(2,1)S(1)}, bf16[512,512]{1,0:T(8,128)(2,1)}, u32[]{:S(2)}, u32[]{:S(2)}) collective-permute-start(bf16[512,512]{1,0:T(8,128)(2,1)S(1)} %bitcast.27), channel_id=1, source_target_pairs={{0,96},{32,0},{64,32},{96,64},{1,97},{33,1},{65,33},{97,65},{2,98}... | collective-permute-start | bytes 1572872 | tf_op jit(solution)/shard_map/ppermute | solution.py:112
  31.2 15.2 %copy-start.6 = (bf16[512,512]{1,0:T(8,128)(2,1)}, bf16[512,512]{1,0:T(8,128)(2,1)S(1)}, u32[]{:S(2)}) copy-start(bf16[512,512]{1,0:T(8,128)(2,1)S(1)} %collective-permute-done.rest_1_) | copy-start | bytes 1572868
  33.2 0.8 copy-start.7
  46.3 1.3 copy-start.2
  54.6 4.7 %copy-start.11 = (bf16[512,512]{1,0:T(8,128)(2,1)S(1)}, bf16[512,512]{1,0:T(8,128)(2,1)}, u32[]{:S(2)}) copy-start(bf16[512,512]{1,0:T(8,128)(2,1)} %get-tuple-element.11.current_ref.refs_0_) | copy-start | bytes 1572868
  54.6 34.6 %all-to-all-start.1 = ((bf16[32,64,512]{2,1,0:T(8,128)(2,1)}), bf16[32,64,512]{2,1,0:T(8,128)(2,1)S(1)}, u32[]{:S(2)}, u32[]{:S(2)}) async-start(bf16[32,64,512]{2,1,0:T(8,128)(2,1)} %bitcast.29), calls=%async_computation.1 | async-start | bytes 4194304 | tf_op jit(solution)/shard_map/all_to_all | solution.py:144
  59.3 14.2 %collective-permute-start.3 = (bf16[512,512]{1,0:T(8,128)(2,1)S(1)}, bf16[512,512]{1,0:T(8,128)(2,1)S(1)}, u32[]{:S(2)}, u32[]{:S(2)}) collective-permute-start(bf16[512,512]{1,0:T(8,128)(2,1)S(1)} %copy-done.11), channel_id=1, source_target_pairs={{0,32},{32,64},{64,96},{96,0},{1,33},{33,65},{65,97},{97,1},{2,34}... | collective-permute-start | bytes 1572872 | tf_op jit(solution)/shard_map/ppermute | solution.py:112
  73.4 15.8 %copy-start.12 = (bf16[512,512]{1,0:T(8,128)(2,1)}, bf16[512,512]{1,0:T(8,128)(2,1)S(1)}, u32[]{:S(2)}) copy-start(bf16[512,512]{1,0:T(8,128)(2,1)S(1)} %collective-permute-done.3.previous_ref.refs_1_) | copy-start | bytes 1572868
  89.2 1.3 copy-start.3
  97.5 4.2 %copy-start.13 = (bf16[512,512]{1,0:T(8,128)(2,1)S(1)}, bf16[512,512]{1,0:T(8,128)(2,1)}, u32[]{:S(2)}) copy-start(bf16[512,512]{1,0:T(8,128)(2,1)} %get-tuple-element.13.current_ref.refs_4_) | copy-start | bytes 1572868
  97.5 34.1 %all-to-all-start.2 = ((bf16[32,64,512]{2,1,0:T(8,128)(2,1)}), bf16[32,64,512]{2,1,0:T(8,128)(2,1)S(1)}, u32[]{:S(2)}, u32[]{:S(2)}) async-start(bf16[32,64,512]{2,1,0:T(8,128)(2,1)} %bitcast.30), calls=%async_computation.2 | async-start | bytes 4194304 | tf_op jit(solution)/shard_map/all_to_all | solution.py:144
  101.7 14.1 %collective-permute-start.6 = (bf16[512,512]{1,0:T(8,128)(2,1)S(1)}, bf16[512,512]{1,0:T(8,128)(2,1)S(1)}, u32[]{:S(2)}, u32[]{:S(2)}) collective-permute-start(bf16[512,512]{1,0:T(8,128)(2,1)S(1)} %copy-done.13), channel_id=1, source_target_pairs={{0,32},{32,64},{64,96},{96,0},{1,33},{33,65},{65,97},{97,1},{2,34}... | collective-permute-start | bytes 1572872 | tf_op jit(solution)/shard_map/ppermute | solution.py:112
  115.7 15.9 %copy-start.14 = (bf16[512,512]{1,0:T(8,128)(2,1)}, bf16[512,512]{1,0:T(8,128)(2,1)S(1)}, u32[]{:S(2)}) copy-start(bf16[512,512]{1,0:T(8,128)(2,1)S(1)} %collective-permute-done.6.previous_ref.refs_5_) | copy-start | bytes 1572868
  131.6 1.3 copy-start.4
  139.9 4.2 %copy-start.8 = (bf16[512,512]{1,0:T(8,128)(2,1)S(1)}, bf16[512,512]{1,0:T(8,128)(2,1)}, u32[]{:S(2)}) copy-start(bf16[512,512]{1,0:T(8,128)(2,1)} %get-tuple-element.15.current_ref.refs_8_) | copy-start | bytes 1572868
  139.9 34.1 %all-to-all-start.3 = ((bf16[32,64,512]{2,1,0:T(8,128)(2,1)}), bf16[32,64,512]{2,1,0:T(8,128)(2,1)S(1)}, u32[]{:S(2)}, u32[]{:S(2)}) async-start(bf16[32,64,512]{2,1,0:T(8,128)(2,1)} %bitcast.28), calls=%async_computation.3 | async-start | bytes 4194304 | tf_op jit(solution)/shard_map/all_to_all | solution.py:144
  144.1 24.6 %collective-permute-start.9 = (bf16[512,512]{1,0:T(8,128)(2,1)S(1)}, bf16[512,512]{1,0:T(8,128)(2,1)S(1)}, u32[]{:S(2)}, u32[]{:S(2)}) collective-permute-start(bf16[512,512]{1,0:T(8,128)(2,1)S(1)} %copy-done.8), channel_id=1, source_target_pairs={{0,32},{32,64},{64,96},{96,0},{1,33},{33,65},{65,97},{97,1},{2,34}... | collective-permute-start | bytes 1572872 | tf_op jit(solution)/shard_map/ppermute | solution.py:112
  145.9 35.0 %collective-permute-start.4 = (bf16[512,512]{1,0:T(8,128)(2,1)}, bf16[512,512]{1,0:T(8,128)(2,1)}, u32[]{:S(2)}, u32[]{:S(2)}) collective-permute-start(bf16[512,512]{1,0:T(8,128)(2,1)} %get-tuple-element.11.current_ref.refs_0_), channel_id=1, source_target_pairs={{64,0},{65,1},{66,2},{67,3},{68,4},{69,5},{70,6},{71,7},{72,8},{73... | collective-permute-start | bytes 1572872 | tf_op jit(solution)/shard_map/ppermute | solution.py:112
  147.3 36.5 %collective-permute-start.5 = (bf16[512,512]{1,0:T(8,128)(2,1)}, bf16[512,512]{1,0:T(8,128)(2,1)}, u32[]{:S(2)}, u32[]{:S(2)}) collective-permute-start(bf16[512,512]{1,0:T(8,128)(2,1)} %get-tuple-element.11.current_ref.refs_0_), channel_id=1, source_target_pairs={{32,0},{33,1},{34,2},{35,3},{36,4},{37,5},{38,6},{39,7},{40,8},{41... | collective-permute-start | bytes 1572872 | tf_op jit(solution)/shard_map/ppermute | solution.py:112
  148.8 36.4 %collective-permute-start.7 = (bf16[512,512]{1,0:T(8,128)(2,1)}, bf16[512,512]{1,0:T(8,128)(2,1)}, u32[]{:S(2)}, u32[]{:S(2)}) collective-permute-start(bf16[512,512]{1,0:T(8,128)(2,1)} %get-tuple-element.13.current_ref.refs_4_), channel_id=1, source_target_pairs={{96,32},{97,33},{98,34},{99,35},{100,36},{101,37},{102,38},{103,39... | collective-permute-start | bytes 1572872 | tf_op jit(solution)/shard_map/ppermute | solution.py:112
  154.6 31.8 %collective-permute-start.8 = (bf16[512,512]{1,0:T(8,128)(2,1)}, bf16[512,512]{1,0:T(8,128)(2,1)}, u32[]{:S(2)}, u32[]{:S(2)}) collective-permute-start(bf16[512,512]{1,0:T(8,128)(2,1)} %get-tuple-element.13.current_ref.refs_4_), channel_id=1, source_target_pairs={{64,32},{65,33},{66,34},{67,35},{68,36},{69,37},{70,38},{71,39},{7... | collective-permute-start | bytes 1572872 | tf_op jit(solution)/shard_map/ppermute | solution.py:112
  168.7 5.4 %copy-start.10 = (bf16[512,512]{1,0:T(8,128)(2,1)}, bf16[512,512]{1,0:T(8,128)(2,1)S(1)}, u32[]{:S(2)}) copy-start(bf16[512,512]{1,0:T(8,128)(2,1)S(1)} %collective-permute-done.9.previous_ref.refs_9_) | copy-start | bytes 1572868
  168.7 19.1 %collective-permute-start.10 = (bf16[512,512]{1,0:T(8,128)(2,1)S(1)}, bf16[512,512]{1,0:T(8,128)(2,1)}, u32[]{:S(2)}, u32[]{:S(2)}) collective-permute-start(bf16[512,512]{1,0:T(8,128)(2,1)S(1)} %copy-done.8), channel_id=1, source_target_pairs={{0,64},{1,65},{2,66},{3,67},{4,68},{5,69},{6,70},{7,71},{8,72},{9,... | collective-permute-start | bytes 1572872 | tf_op jit(solution)/shard_map/ppermute | solution.py:112
  174.0 1.3 copy-start.1
  175.3 5.6 %copy-start.9 = (bf16[512,512]{1,0:T(8,128)(2,1)S(1)}, bf16[512,512]{1,0:T(8,128)(2,1)}, u32[]{:S(2)}) copy-start(bf16[512,512]{1,0:T(8,128)(2,1)} %get-tuple-element.15.current_ref.refs_8_) | copy-start | bytes 1572868
  180.9 12.3 %collective-permute-start.11 = (bf16[512,512]{1,0:T(8,128)(2,1)S(1)}, bf16[512,512]{1,0:T(8,128)(2,1)S(1)}, u32[]{:S(2)}, u32[]{:S(2)}) collective-permute-start(bf16[512,512]{1,0:T(8,128)(2,1)S(1)} %copy-done.9), channel_id=1, source_target_pairs={{96,64},{97,65},{98,66},{99,67},{100,68},{101,69},{102,70},{103,71... | collective-permute-start | bytes 1572872 | tf_op jit(solution)/shard_map/ppermute | solution.py:112
  183.8 13.8 %collective-permute-start.12 = (bf16[512,512]{1,0:T(8,128)(2,1)}, bf16[512,512]{1,0:T(8,128)(2,1)S(1)}, u32[]{:S(2)}, u32[]{:S(2)}) collective-permute-start(bf16[512,512]{1,0:T(8,128)(2,1)} %shard_map.77.refs_12_), channel_id=1, source_target_pairs={{64,96},{65,97},{66,98},{67,99},{68,100},{69,101},{70,102},{71,103... | collective-permute-start | bytes 1572872 | tf_op jit(solution)/shard_map/ppermute | solution.py:112
  185.1 15.4 %collective-permute-start.13 = (bf16[512,512]{1,0:T(8,128)(2,1)}, bf16[512,512]{1,0:T(8,128)(2,1)S(1)}, u32[]{:S(2)}, u32[]{:S(2)}) collective-permute-start(bf16[512,512]{1,0:T(8,128)(2,1)} %shard_map.77.refs_12_), channel_id=1, source_target_pairs={{32,96},{33,97},{34,98},{35,99},{36,100},{37,101},{38,102},{39,103... | collective-permute-start | bytes 1572872 | tf_op jit(solution)/shard_map/ppermute | solution.py:112
  186.5 25.2 %collective-permute-start.14 = (bf16[512,512]{1,0:T(8,128)(2,1)}, bf16[512,512]{1,0:T(8,128)(2,1)S(1)}, u32[]{:S(2)}, u32[]{:S(2)}) collective-permute-start(bf16[512,512]{1,0:T(8,128)(2,1)} %shard_map.77.refs_12_), channel_id=1, source_target_pairs={{0,96},{1,97},{2,98},{3,99},{4,100},{5,101},{6,102},{7,103},{8,104... | collective-permute-start | bytes 1572872 | tf_op jit(solution)/shard_map/ppermute | solution.py:112
  193.3 18.4 %copy-start.15 = (bf16[512,512]{1,0:T(8,128)(2,1)}, bf16[512,512]{1,0:T(8,128)(2,1)S(1)}, u32[]{:S(2)}) copy-start(bf16[512,512]{1,0:T(8,128)(2,1)S(1)} %collective-permute-done.11.refs_11_) | copy-start | bytes 1572868
  197.6 14.1 %copy-start.16 = (bf16[512,512]{1,0:T(8,128)(2,1)}, bf16[512,512]{1,0:T(8,128)(2,1)S(1)}, u32[]{:S(2)}) copy-start(bf16[512,512]{1,0:T(8,128)(2,1)S(1)} %collective-permute-done.12.refs_13_) | copy-start | bytes 1572868
  200.5 11.1 %copy-start.17 = (bf16[512,512]{1,0:T(8,128)(2,1)}, bf16[512,512]{1,0:T(8,128)(2,1)S(1)}, u32[]{:S(2)}) copy-start(bf16[512,512]{1,0:T(8,128)(2,1)S(1)} %collective-permute-done.13.refs_14_) | copy-start | bytes 1572868
  211.7 0.8 copy-start.18

commit v2 on v0

v2 whole, which is shorter than its diff:
```python
import functools

import jax
import jax.numpy as jnp
from jax import lax
from jax.experimental import pallas as pl
from jax.experimental.pallas import tpu as pltpu
from jax.sharding import PartitionSpec as P

TILE = 128
SIDE = 4
CORES = 2
EXTRA = 16
ANY = pl.BlockSpec(memory_space=pl.ANY)
SMEM = pl.BlockSpec(memory_space=pltpu.SMEM)
VMEM = pl.BlockSpec(memory_space=pltpu.VMEM)
PLACES = [(z, y, core) for z in range(SIDE) for y in range(SIDE) for core in range(CORES)]


def node_of(z, y, core):
    return ((z % SIDE) * SIDE + y % SIDE) * CORES + core


def along(block, distance, phase):
    route = []
    for z, y, core in PLACES:
        if core == phase:
            target = node_of(z, y + distance, core)
        else:
            target = node_of(z + distance, y, core)
        route.append((node_of(z, y, core), target))
    return lax.ppermute(block, "node", route)


def other_core(block):
    route = [(node_of(z, y, core), node_of(z, y, 1 - core)) for z, y, core in PLACES]
    return lax.ppermute(block, "node", route)


def to_plane(block, pairs):
    return lax.ppermute(block, "layer", pairs)


def offered_rows(listed, rows):
    row_ids = lax.broadcasted_iota(jnp.int32, (rows.shape[0], listed.shape[1]), 0)
    selector = (row_ids == listed).astype(jnp.bfloat16)
    picked = lax.dot_general(
        selector, rows, (((0,), (0,)), ((), ())), preferred_element_type=jnp.float32
    )
    return picked.astype(jnp.bfloat16)


def first_kernel(place_ref, features_ref, boundary_ref, lists_ref, block_ref, rows, sem):
    span, node = place_ref[0], place_ref[1]
    copy = pltpu.make_async_copy(features_ref.at[span], rows, sem)
    copy.start()
    offered = boundary_ref.shape[2]
    nodes, picks = lists_ref.shape[2:]
    block_ref[pl.ds(offered, EXTRA), :] = jnp.zeros((EXTRA, block_ref.shape[1]), jnp.bfloat16)
    lists = lists_ref[span, 0].astype(jnp.float32).astype(jnp.bfloat16)
    for core in range(CORES):
        @pl.when(node % CORES == core)
        def _():
            for part in range(nodes // EXTRA):
                lanes = pl.ds(part * CORES * picks + core * picks, picks)
                block_ref[pl.ds(offered, EXTRA), lanes] = lists[part * EXTRA:(part + 1) * EXTRA]
    copy.wait()
    block_ref[pl.ds(0, offered), :] = offered_rows(boundary_ref[span], rows[...])


def layer_kernel(
    layer_id, first, last,
    place_ref, counts_ref, cols_ref, boundary_ref, current_ref, previous_ref, tiles_ref, *rest,
):
    weight_refs, rest = rest[:SIDE], rest[SIDE:]
    mine_refs, rest = rest[:SIDE], rest[SIDE:]
    theirs_refs, rest = rest[:SIDE], rest[SIDE:]
    outs = 1 if last else 3 if first else 2
    out_ref = rest[0]
    block_ref = None if last else rest[1]
    space, tiles, weight, total, sems = rest[outs:outs + 5]
    if first:
        wide_ref = rest[2]
        raw_lists, lists = rest[outs + 5:]
    span, node = place_ref[0], place_ref[1]
    row_count = total.shape[0]
    offered = boundary_ref.shape[2]
    z, y, core = node // (SIDE * CORES), (node // CORES) % SIDE, node % CORES
    copies = []

    def fetch(source, target):
        copy = pltpu.make_async_copy(source, target, sems.at[len(copies)])
        copies.append(copy)
        copy.start()

    each = mine_refs[0].shape[0] // SIDE
    for refs, kind in ((mine_refs, core), (theirs_refs, 1 - core)):
        for j in range(SIDE):
            for k in range(SIDE):
                dz = jnp.where(kind == 0, j, k)
                dy = jnp.where(kind == 0, k, j)
                chip = ((z + SIDE - dz) % SIDE) * SIDE + (y + SIDE - dy) % SIDE
                start = pl.multiple_of(2 * row_count + (chip * CORES + kind) * offered, offered)
                fetch(refs[j].at[pl.ds(k * each, offered)], space.at[pl.ds(start, offered)])
                if first:
                    source = refs[j].at[pl.ds(k * each + offered, EXTRA)]
                    fetch(source, raw_lists.at[chip * CORES + kind])
    if first:
        fetch(current_ref.at[span], space.at[pl.ds(0, row_count)])
        fetch(previous_ref.at[jnp.maximum(span - 1, 0)], space.at[pl.ds(row_count, row_count)])
        fetch(tiles_ref.at[span, 0], tiles)
    else:
        fetch(current_ref, space.at[pl.ds(0, row_count)])
        fetch(previous_ref, space.at[pl.ds(row_count, row_count)])
        fetch(tiles_ref, tiles)
    weight_sem = sems.at[len(copies)]
    for distance, source in enumerate(weight_refs):
        @pl.when((span + SIDE - distance) % SIDE == layer_id)
        def _():
            pltpu.make_async_copy(source, weight, weight_sem).start()
    total[...] = jnp.zeros_like(total)
    for copy in copies:
        copy.wait()
    pltpu.make_async_copy(weight_refs[0], weight, weight_sem).wait()

    @pl.when(span == 0)
    def _():
        space[pl.ds(row_count, row_count), :] = jnp.zeros((row_count, space.shape[1]), space.dtype)

    if first:
        lane_block = pl.ds(pl.multiple_of((node // EXTRA) * TILE, TILE), TILE)
        wanted = lax.broadcasted_iota(jnp.int32, (EXTRA, TILE), 0) == node % EXTRA
        lanes = lax.broadcasted_iota(jnp.int32, (1, TILE), 1)
        half = jnp.where(lanes >= TILE // CORES, offered, 0)
        for chip in range(SIDE * SIDE):
            both = raw_lists[chip * CORES, :, lane_block] + raw_lists[chip * CORES + 1, :, lane_block]
            row = jnp.sum(jnp.where(wanted, both.astype(jnp.float32), 0.0), axis=0, keepdims=True)
            lists[pl.ds(chip, 1), :] = row.astype(jnp.int32) + half
        slot_rows = lax.broadcasted_iota(jnp.int32, (CORES * offered, TILE), 0)

    ends = []
    reached = 0
    for r in range(counts_ref.shape[1] - 1):
        reached = reached + counts_ref[span, r]
        ends.append(reached)
    own_tiles = 2 * row_count // TILE
    for f in range(cols_ref.shape[1]):
        owner = sum((f >= end).astype(jnp.int32) for end in ends)
        col = cols_ref[span, f]
        if first:
            plain = lanes + TILE * (col % CORES)
            listed = lists[pl.ds(jnp.maximum(col - own_tiles, 0), 1), :]
            target = jnp.where(col < own_tiles, plain, listed)
            selector = (slot_rows == target).astype(jnp.bfloat16)
            wide = lax.dot_general(
                tiles[f], selector, (((1,), (1,)), ((), ())), preferred_element_type=jnp.float32
            ).astype(jnp.bfloat16)
            wide_ref[f] = wide
        else:
            wide = tiles[f]
        slot = jnp.where(col < own_tiles, col // CORES, col - own_tiles // CORES)
        row_at = pl.ds(pl.multiple_of(owner * TILE, TILE), TILE)
        slot_at = pl.ds(pl.multiple_of(slot * CORES * offered, CORES * offered), CORES * offered)
        total[row_at, :] += jnp.dot(wide, space[slot_at, :], preferred_element_type=jnp.float32)
    aggregate = total[...].astype(jnp.bfloat16)
    linear = jnp.dot(aggregate, weight[...], preferred_element_type=jnp.float32)
    fresh = jnp.maximum(linear, 0.0).astype(jnp.bfloat16)
    out_ref[...] = fresh
    if not last:
        block_ref[...] = offered_rows(boundary_ref[span], fresh)


def place_kernel(place_ref, *refs):
    out_ref, held, in_sems, out_sems = refs[-4:]
    spans = out_ref.shape[0]
    span = place_ref[0]
    parts = []
    for distance in range(spans):
        pieces = 2 if distance == 2 else 1
        rows = held.shape[1] // pieces
        parts += [(distance, rows * i, rows) for i in range(pieces)]
    for layer_id in range(spans):
        @pl.when(span == layer_id)
        def _():
            ins, outs = [], []
            for i, (distance, start, rows) in enumerate(parts):
                staged = held.at[distance, pl.ds(start, rows)]
                target = out_ref.at[(layer_id - distance) % spans, pl.ds(start, rows)]
                source = refs[layer_id * len(parts) + i]
                ins.append(pltpu.make_async_copy(source, staged, in_sems.at[i]))
                outs.append(pltpu.make_async_copy(staged, target, out_sems.at[i]))
            for copy in ins:
                copy.start()
            for i in range(len(parts)):
                ins[i].wait()
                outs[i].start()
            for copy in outs:
                copy.wait()


def on_device(features, weights, boundary, pick_index, counts, tile_cols, tile_vals):
    spans, row_count, width = features.shape
    layers = lax.axis_size("layer")
    nodes = lax.axis_size("node")
    picks, offered = pick_index.shape[3], boundary.shape[2]
    tile_total = tile_vals.shape[2]
    place = jnp.stack([lax.axis_index("layer"), lax.axis_index("node")]).astype(jnp.int32)
    counts, tile_cols = counts[:, 0], tile_cols[:, 0]
    rows_shape = jax.ShapeDtypeStruct((row_count, width), jnp.bfloat16)
    wide_shape = jax.ShapeDtypeStruct((tile_total, TILE, CORES * offered), jnp.bfloat16)
    block_shape = jax.ShapeDtypeStruct((offered, width), jnp.bfloat16)
    params = pltpu.CompilerParams(vmem_limit_bytes=56 << 20)
    block = pl.pallas_call(
        first_kernel,
        out_shape=jax.ShapeDtypeStruct((offered + EXTRA, width), jnp.bfloat16),
        in_specs=[SMEM, ANY, VMEM, VMEM],
        out_specs=VMEM,
        scratch_shapes=[pltpu.VMEM((row_count, width), jnp.bfloat16), pltpu.SemaphoreType.DMA],
        compiler_params=params,
    )(place, features, boundary, pick_index)
    current = previous = features
    tiles = tile_vals
    known = None
    placed = []
    for layer_id in range(layers):
        first, last = layer_id == 0, layer_id == layers - 1
        row = jnp.concatenate([block] + [along(block, k, 0) for k in range(1, SIDE)], 0)
        mine = [row] + [along(row, j, 1) for j in range(1, SIDE)]
        theirs = [other_core(part) for part in mine]
        if first:
            known = [weights[0]]
            for distance in range(1, layers):
                known.append(to_plane(weights[0], [(i, (i + distance) % layers) for i in range(layers)]))
        scratch = [
            pltpu.VMEM((2 * row_count + nodes * offered, width), jnp.bfloat16),
            pltpu.VMEM(tile_vals.shape[2:] if first else wide_shape.shape, jnp.bfloat16),
            pltpu.VMEM((width, width), jnp.bfloat16),
            pltpu.VMEM((row_count, width), jnp.float32),
            pltpu.SemaphoreType.DMA((2 * nodes + 4,)),
        ]
        if first:
            scratch += [
                pltpu.VMEM((nodes, EXTRA, width), jnp.bfloat16),
                pltpu.VMEM((SIDE * SIDE, TILE), jnp.int32),
            ]
        outs = [rows_shape] if last else [rows_shape, block_shape]
        if first:
            outs.append(wide_shape)
        results = pl.pallas_call(
            functools.partial(layer_kernel, layer_id, first, last),
            out_shape=outs,
            in_specs=[SMEM, SMEM, SMEM, VMEM] + [ANY] * (3 + 3 * SIDE),
            out_specs=[VMEM] * len(outs),
            scratch_shapes=scratch,
            compiler_params=params,
        )(place, counts, tile_cols, boundary, current, previous, tiles, *known, *mine, *theirs)
        current = results[0]
        if not last:
            block = results[1]
        if first:
            tiles = results[2]
        before, after, across = [(layer_id + step) % layers for step in (3, 1, 2)]
        half = row_count // 2
        if last:
            previous = to_plane(current, [(before, layer_id)])
        else:
            previous = to_plane(current, [(i, (i + 1) % layers) for i in range(layers)])
        relayed = to_plane(current[:half], [(across, before)])
        placed += [
            current,
            previous,
            to_plane(relayed, [(before, layer_id)]),
            to_plane(current[half:], [(across, layer_id)]),
            to_plane(current, [(after, layer_id)]),
        ]
    return pl.pallas_call(
        place_kernel,
        out_shape=jax.ShapeDtypeStruct(features.shape, features.dtype),
        in_specs=[SMEM] + [ANY] * len(placed),
        out_specs=ANY,
        scratch_shapes=[
            pltpu.VMEM(features.shape, features.dtype),
            pltpu.SemaphoreType.DMA((5,)),
            pltpu.SemaphoreType.DMA((5,)),
        ],
        compiler_params=params,
    )(place, *placed)


def solution(mesh):
    return jax.shard_map(
        on_device,
        mesh=mesh,
        in_specs=(
            P(None, "node", None),
            P("layer", None, None),
            P(None, "node", None),
            P(None, "node", None, None),
            P(None, "node", None),
            P(None, "node", None),
            P(None, "node", None, None, None),
        ),
        out_specs=P(None, "node", "layer"),
        check_vma=False,
    )
```

time: 229 us -> 227 us (level)
  starting transfers between devices: 16.1 us -> 85.4 us
  blocking collectives: 64 us -> 0 us
  local copies, waits for them, and re-layouts: 28.4 us -> 9.17 us
  Pallas kernels: 17.2 us -> 36 us
  between operations: 13.6 us -> 1.06 us
  waiting for transfers between devices: 86.3 us -> 93.3 us
    ppermute x3 -> x63, starting transfers between devices: 1.78 us -> 85.4 us  [the longest x24 39.6 us: along(): return lax.ppermute(block, 'node', route)]
    all_to_all x2 -> x0, blocking collectives: 64 us -> none  [the longest x1 36.9 us: on_device(): lax.all_to_all(sent.reshape(nodes, picks, width), 'node', split_axis=0, c...]
    ppermute x3 -> x63, waiting for transfers between devices: 40.8 us -> 93.3 us  [the longest x23 55.3 us: to_plane(): return lax.ppermute(block, 'layer', pairs)]
    all_to_all x3 -> x0, waiting for transfers between devices: 44.8 us -> none  [on_device(): lax.all_to_all(sent.reshape(nodes, picks, width), 'node', split_axis=0, c...]
    unnamed x57 -> x113, local copies, waits for them, and re-layouts: 27.6 us -> 7.97 us
    all_to_all x3 -> x0, starting transfers between devices: 14.4 us -> none  [on_device(): lax.all_to_all(sent.reshape(nodes, picks, width), 'node', split_axis=0, c...]
    pallas_call x4, Pallas kernels: 16.2 us -> 30 us  [on_device(): pl.pallas_call(functools.partial(layer_kernel, layer_id, first, last), ou...]
    pallas_call x1 -> x2, Pallas kernels: 0.96 us -> 6.04 us  [the longest x1 3.15 us: on_device(): pl.pallas_call(place_kernel, out_shape=jax.ShapeDtypeStruct(features.shap...]
  transfers between devices with their start and end apart: 7 -> 63, of which waited for: 6 -> 26; matrix products, arithmetic and copies ran while one was open for 1% -> 2% of each run, Pallas kernels for 0% -> 6%
where the time goes in v2:
time: 227 us
  waiting for transfers between devices  93.3 us (41%)
  starting transfers between devices  85.4 us (38%)
  Pallas kernels  36 us (16%)
  local copies, waits for them, and re-layouts  9.17 us (4%)
    ppermute x23, waiting for transfers between devices, to_plane(): return lax.ppermute(block, 'layer', pairs)  55.3 us
    ppermute x24, starting transfers between devices, along(): return lax.ppermute(block, 'node', route)  39.6 us
    ppermute x23, starting transfers between devices, to_plane(): return lax.ppermute(block, 'layer', pairs)  39.4 us
    ppermute x24, waiting for transfers between devices, along(): return lax.ppermute(block, 'node', route)  35.9 us
    pallas_call x4, Pallas kernels, on_device(): pl.pallas_call(functools.partial(layer_kernel, layer_id, first, last), ou...  30 us
    unnamed x113, local copies, waits for them, and re-layouts  7.97 us
    ppermute x16, starting transfers between devices, other_core(): return lax.ppermute(block, 'node', route)  6.38 us
  transfers between devices with their start and end apart: 63, of which 26 were waited for; matrix products, arithmetic and copies ran while one was open for 2% of the time, Pallas kernels for 6%

profile of v2, /device:TPU:6, one launch (start us, length us, event | category | flops | bytes accessed | tf_op | source)
XLA Modules:
  0.0 226.5 jit_solution(3834828510419948197)
XLA Ops:
  0.6 2.9 %shard_map.73 = bf16[144,512]{1,0:T(8,128)(2,1)} custom-call(s32[2]{0:T(128)} %pad_add_fusion.place_ref, bf16[4,512,512]{2,1,0:T(8,128)(2,1)} %previous_ref.1, s32[4,1,128]{2,1,0:T(1,128)} %boundary_ref.9, s32[4,1,32,64]{3,2,1,0:T(8,128)} %lists_ref.1), custom_call_target="tpu_custom_call" | custom-call | tf_op jit(solution)/shard_map/pallas_call | solution.py:213
  3.5 1.6 collective-permute-start.3
  5.1 2.9 %collective-permute-start.4 = (bf16[144,512]{1,0:T(8,128)(2,1)}, bf16[144,512]{1,0:T(8,128)(2,1)S(1)}, u32[]{:S(2)}, u32[]{:S(2)}) collective-permute-start(bf16[144,512]{1,0:T(8,128)(2,1)} %shard_map.73), channel_id=1, source_target_pairs={{0,4},{1,17},{2,6},{3,19},{4,0},{5,21},{6,2},{7,23},{8,12},{9,25},... | collective-permute-start | bytes 442376 | tf_op jit(solution)/shard_map/ppermute | solution.py:32
  8.0 1.3 collective-permute-start.5
  10.1 2.8 %collective-permute-done.4 = bf16[144,512]{1,0:T(8,128)(2,1)S(1)} collective-permute-done((bf16[144,512]{1,0:T(8,128)(2,1)}, bf16[144,512]{1,0:T(8,128)(2,1)S(1)}, u32[]{:S(2)}, u32[]{:S(2)}) %collective-permute-start.4) | collective-permute-done | bytes 147488 | tf_op jit(solution)/shard_map/ppermute | solution.py:32
  13.4 0.9 pad_maximum_fusion.rest_4_
  14.4 2.0 collective-permute-start.6
  16.3 3.6 %collective-permute-start.7 = (bf16[576,512]{1,0:T(8,128)(2,1)S(1)}, bf16[576,512]{1,0:T(8,128)(2,1)S(1)}, u32[]{:S(2)}, u32[]{:S(2)}) collective-permute-start(bf16[576,512]{1,0:T(8,128)(2,1)S(1)} %pad_maximum_fusion.rest_4_), channel_id=1, source_target_pairs={{0,16},{1,5},{2,18},{3,7},{4,20},{5,1},{6,22},{7,3},{8,24},{9,13},... | collective-permute-start | bytes 1769480 | tf_op jit(solution)/shard_map/ppermute | solution.py:32
  19.9 1.0 collective-permute-start.8
  21.4 2.4 %collective-permute-start.1 = (bf16[512,512]{1,0:T(8,128)(2,1)S(1)}, bf16[512,512]{1,0:T(8,128)(2,1)S(1)}, u32[]{:S(2)}, u32[]{:S(2)}) collective-permute-start(bf16[512,512]{1,0:T(8,128)(2,1)S(1)} %bitcast.10), channel_id=1, source_target_pairs={{0,64},{32,96},{64,0},{96,32},{1,65},{33,97},{65,1},{97,33},{2,66}... | collective-permute-start | bytes 1572872 | tf_op jit(solution)/shard_map/ppermute | solution.py:41
  23.8 12.0 %collective-permute-done.rest_1_ = bf16[512,512]{1,0:T(8,128)(2,1)S(1)} collective-permute-done((bf16[512,512]{1,0:T(8,128)(2,1)S(1)}, bf16[512,512]{1,0:T(8,128)(2,1)S(1)}, u32[]{:S(2)}, u32[]{:S(2)}) %collective-permute-start) | collective-permute-done | bytes 524320 | tf_op jit(solution)/shard_map/ppermute | solution.py:41
  36.9 7.8 %collective-permute-start.2 = (bf16[512,512]{1,0:T(8,128)(2,1)S(1)}, bf16[512,512]{1,0:T(8,128)(2,1)S(1)}, u32[]{:S(2)}, u32[]{:S(2)}) collective-permute-start(bf16[512,512]{1,0:T(8,128)(2,1)S(1)} %bitcast.11), channel_id=1, source_target_pairs={{0,96},{32,0},{64,32},{96,64},{1,97},{33,1},{65,33},{97,65},{2,98}... | collective-permute-start | bytes 1572872 | tf_op jit(solution)/shard_map/ppermute | solution.py:41
  44.6 10.8 %collective-permute-done.2.rest_3_ = bf16[512,512]{1,0:T(8,128)(2,1)S(1)} collective-permute-done((bf16[512,512]{1,0:T(8,128)(2,1)S(1)}, bf16[512,512]{1,0:T(8,128)(2,1)S(1)}, u32[]{:S(2)}, u32[]{:S(2)}) %collective-permute-start.2) | collective-permute-done | bytes 524320 | tf_op jit(solution)/shard_map/ppermute | solution.py:41
  57.0 9.8 %shard_map.74 = (bf16[512,512]{1,0:T(8,128)(2,1)}, bf16[128,512]{1,0:T(8,128)(2,1)}, bf16[20,128,256]{2,1,0:T(8,128)(2,1)}) custom-call(s32[2]{0:T(128)} %pad_add_fusion.place_ref, s32[4,4]{1,0:T(4,128)} %bitcast.12, s32[4,20]{1,0:T(4,128)} %bitcast.16, s32[4,1,128]{2,1,0:T(1,128)} %boundary_ref.9, bf16[4,512,512]{2,1,0:T(8,128)(2,1)} %previous_ref.1, ...), custom_call_target="tpu_custom_call" | custom-call | tf_op jit(solution)/shard_map/pallas_call | solution.py:249
  67.5 0.9 constant_dynamic-update-slice_fusion.3
  68.4 2.8 %collective-permute-start.20 = (bf16[128,512]{1,0:T(8,128)(2,1)}, bf16[128,512]{1,0:T(8,128)(2,1)S(1)}, u32[]{:S(2)}, u32[]{:S(2)}) collective-permute-start(bf16[128,512]{1,0:T(8,128)(2,1)} %get-tuple-element.14), channel_id=1, source_target_pairs={{0,6},{1,25},{2,0},{3,27},{4,2},{5,29},{6,4},{7,31},{8,14},{9,1},{... | collective-permute-start | bytes 393224 | tf_op jit(solution)/shard_map/ppermute | solution.py:32
  71.2 3.5 %collective-permute-done.18 = bf16[128,512]{1,0:T(8,128)(2,1)S(1)} collective-permute-done((bf16[128,512]{1,0:T(8,128)(2,1)}, bf16[128,512]{1,0:T(8,128)(2,1)S(1)}, u32[]{:S(2)}, u32[]{:S(2)}) %collective-permute-start.18) | collective-permute-done | bytes 131104 | tf_op jit(solution)/shard_map/ppermute | solution.py:32
  75.6 2.0 collective-permute-start.21
  77.6 4.1 %collective-permute-start.22 = (bf16[512,512]{1,0:T(8,128)(2,1)S(1)}, bf16[512,512]{1,0:T(8,128)(2,1)S(1)}, u32[]{:S(2)}, u32[]{:S(2)}) collective-permute-start(bf16[512,512]{1,0:T(8,128)(2,1)S(1)} %constant_dynamic-update-slice_fusion.rest_4_), channel_id=1, source_target_pairs={{0,16},{1,5},{2,18},{3,7},{4,20},{5,1},{6,22},{7,3},{8,24},{9,13},... | collective-permute-start | bytes 1572872 | tf_op jit(solution)/shard_map/ppermute | solution.py:32
  81.6 1.1 collective-permute-start.23
  82.7 1.8 collective-permute-start.13
  84.5 2.9 %collective-permute-done.21.rest_5_ = bf16[512,512]{1,0:T(8,128)(2,1)S(1)} collective-permute-done((bf16[512,512]{1,0:T(8,128)(2,1)S(1)}, bf16[512,512]{1,0:T(8,128)(2,1)S(1)}, u32[]{:S(2)}, u32[]{:S(2)}) %collective-permute-start.21) | collective-permute-done | bytes 524320 | tf_op jit(solution)/shard_map/ppermute | solution.py:32
  87.3 3.8 %collective-permute-start.25 = (bf16[512,512]{1,0:T(8,128)(2,1)S(1)}, bf16[512,512]{1,0:T(8,128)(2,1)S(1)}, u32[]{:S(2)}, u32[]{:S(2)}) collective-permute-start(bf16[512,512]{1,0:T(8,128)(2,1)S(1)} %collective-permute-done.21.rest_5_), channel_id=1, source_target_pairs={{0,1},{1,0},{2,3},{3,2},{4,5},{5,4},{6,7},{7,6},{8,9},{9,8},{10,11... | collective-permute-start | bytes 1572872 | tf_op jit(solution)/shard_map/ppermute | solution.py:37
  91.2 3.2 %collective-permute-done.22.rest_6_ = bf16[512,512]{1,0:T(8,128)(2,1)S(1)} collective-permute-done((bf16[512,512]{1,0:T(8,128)(2,1)S(1)}, bf16[512,512]{1,0:T(8,128)(2,1)S(1)}, u32[]{:S(2)}, u32[]{:S(2)}) %collective-permute-start.22) | collective-permute-done | bytes 524320 | tf_op jit(solution)/shard_map/ppermute | solution.py:32
  95.0 1.4 collective-permute-done.26.rest_10_
  97.9 6.8 %shard_map.75 = (bf16[512,512]{1,0:T(8,128)(2,1)}, bf16[128,512]{1,0:T(8,128)(2,1)}) custom-call(s32[2]{0:T(128)} %pad_add_fusion.place_ref, s32[4,4]{1,0:T(4,128)} %bitcast.13, s32[4,20]{1,0:T(4,128)} %bitcast.17, s32[4,1,128]{2,1,0:T(1,128)} %boundary_ref.9, bf16[512,512]{1,0:T(8,128)(2,1)} %get-tuple-element.12.current_ref.refs_0_, ...), custom_call_target="tpu_custom_call" | custom-call | tf_op jit(solution)/shard_map/pallas_call | solution.py:249
  104.7 1.7 collective-permute-start.33
  106.4 2.5 %collective-permute-start.34 = (bf16[128,512]{1,0:T(8,128)(2,1)}, bf16[128,512]{1,0:T(8,128)(2,1)S(1)}, u32[]{:S(2)}, u32[]{:S(2)}) collective-permute-start(bf16[128,512]{1,0:T(8,128)(2,1)} %get-tuple-element.16), channel_id=1, source_target_pairs={{0,4},{1,17},{2,6},{3,19},{4,0},{5,21},{6,2},{7,23},{8,12},{9,25},... | collective-permute-start | bytes 393224 | tf_op jit(solution)/shard_map/ppermute | solution.py:32
  108.9 0.9 constant_dynamic-update-slice_fusion.7
  110.2 1.0 collective-permute-done.33
  111.2 2.3 %collective-permute-done.34 = bf16[128,512]{1,0:T(8,128)(2,1)S(1)} collective-permute-done((bf16[128,512]{1,0:T(8,128)(2,1)}, bf16[128,512]{1,0:T(8,128)(2,1)S(1)}, u32[]{:S(2)}, u32[]{:S(2)}) %collective-permute-start.34) | collective-permute-done | bytes 131104 | tf_op jit(solution)/shard_map/ppermute | solution.py:32
  113.5 1.6 collective-permute-done.35
  115.1 0.8 collective-permute-start.36
  116.0 2.1 collective-permute-start.37
  118.1 1.6 collective-permute-start.38
  119.6 2.0 collective-permute-start.28
  121.6 9.6 %collective-permute-done.36.rest_5_ = bf16[512,512]{1,0:T(8,128)(2,1)S(1)} collective-permute-done((bf16[512,512]{1,0:T(8,128)(2,1)S(1)}, bf16[512,512]{1,0:T(8,128)(2,1)S(1)}, u32[]{:S(2)}, u32[]{:S(2)}) %collective-permute-start.36) | collective-permute-done | bytes 524320 | tf_op jit(solution)/shard_map/ppermute | solution.py:32
  132.2 1.4 collective-permute-done.28.previous_ref.refs_6_
  133.5 1.3 collective-permute-start.14
  136.9 6.7 %shard_map.76 = (bf16[512,512]{1,0:T(8,128)(2,1)}, bf16[128,512]{1,0:T(8,128)(2,1)}) custom-call(s32[2]{0:T(128)} %pad_add_fusion.place_ref, s32[4,4]{1,0:T(4,128)} %bitcast.14, s32[4,20]{1,0:T(4,128)} %bitcast.18, s32[4,1,128]{2,1,0:T(1,128)} %boundary_ref.9, bf16[512,512]{1,0:T(8,128)(2,1)} %get-tuple-element.15.current_ref.refs_5_, ...), custom_call_target="tpu_custom_call" | custom-call | tf_op jit(solution)/shard_map/pallas_call | solution.py:249
  144.5 1.4 collective-permute-start.16
  145.9 3.3 %collective-permute-start.15 = (bf16[256,512]{1,0:T(8,128)(2,1)S(1)}, bf16[256,512]{1,0:T(8,128)(2,1)S(1)}, u32[]{:S(2)}, u32[]{:S(2)}) collective-permute-start(bf16[256,512]{1,0:T(8,128)(2,1)S(1)} %collective-permute-done.14), channel_id=1, source_target_pairs={{96,0},{97,1},{98,2},{99,3},{100,4},{101,5},{102,6},{103,7},{104,8... | collective-permute-start | bytes 786440 | tf_op jit(solution)/shard_map/ppermute | solution.py:41
  149.2 2.7 %collective-permute-start.49 = (bf16[128,512]{1,0:T(8,128)(2,1)}, bf16[128,512]{1,0:T(8,128)(2,1)S(1)}, u32[]{:S(2)}, u32[]{:S(2)}) collective-permute-start(bf16[128,512]{1,0:T(8,128)(2,1)} %get-tuple-element.18), channel_id=1, source_target_pairs={{0,4},{1,17},{2,6},{3,19},{4,0},{5,21},{6,2},{7,23},{8,12},{9,25},... | collective-permute-start | bytes 393224 | tf_op jit(solution)/shard_map/ppermute | solution.py:32
  151.9 0.9 constant_dynamic-update-slice_fusion.11
  153.7 2.3 %collective-permute-done.49 = bf16[128,512]{1,0:T(8,128)(2,1)S(1)} collective-permute-done((bf16[128,512]{1,0:T(8,128)(2,1)}, bf16[128,512]{1,0:T(8,128)(2,1)S(1)}, u32[]{:S(2)}, u32[]{:S(2)}) %collective-permute-start.49) | collective-permute-done | bytes 131104 | tf_op jit(solution)/shard_map/ppermute | solution.py:32
  156.0 2.1 collective-permute-done.50
  158.8 2.9 %collective-permute-start.52 = (bf16[512,512]{1,0:T(8,128)(2,1)S(1)}, bf16[512,512]{1,0:T(8,128)(2,1)S(1)}, u32[]{:S(2)}, u32[]{:S(2)}) collective-permute-start(bf16[512,512]{1,0:T(8,128)(2,1)S(1)} %constant_dynamic-update-slice_fusion.8.rest_4_), channel_id=1, source_target_pairs={{0,16},{1,5},{2,18},{3,7},{4,20},{5,1},{6,22},{7,3},{8,24},{9,13},... | collective-permute-start | bytes 1572872 | tf_op jit(solution)/shard_map/ppermute | solution.py:32
  162.2 4.3 %collective-permute-start.29 = (bf16[256,512]{1,0:T(8,128)(2,1)S(1)}, bf16[256,512]{1,0:T(8,128)(2,1)}, u32[]{:S(2)}, u32[]{:S(2)}) collective-permute-start(bf16[256,512]{1,0:T(8,128)(2,1)S(1)} %get-tuple-element.24), channel_id=1, source_target_pairs={{96,0},{97,1},{98,2},{99,3},{100,4},{101,5},{102,6},{103,7},{104,8... | collective-permute-start | bytes 786440 | tf_op jit(solution)/shard_map/ppermute | solution.py:41
  166.5 5.9 %collective-permute-done.29 = bf16[256,512]{1,0:T(8,128)(2,1)} collective-permute-done((bf16[256,512]{1,0:T(8,128)(2,1)S(1)}, bf16[256,512]{1,0:T(8,128)(2,1)}, u32[]{:S(2)}, u32[]{:S(2)}) %collective-permute-start.29) | collective-permute-done | bytes 262176 | tf_op jit(solution)/shard_map/ppermute | solution.py:41
  172.9 1.6 collective-permute-done.52.rest_6_
  175.1 7.6 %collective-permute-done.43.previous_ref.refs_11_ = bf16[512,512]{1,0:T(8,128)(2,1)S(1)} collective-permute-done((bf16[512,512]{1,0:T(8,128)(2,1)S(1)}, bf16[512,512]{1,0:T(8,128)(2,1)S(1)}, u32[]{:S(2)}, u32[]{:S(2)}) %collective-permute-start.43) | collective-permute-done | bytes 524320 | tf_op jit(solution)/shard_map/ppermute | solution.py:41
  183.5 2.0 collective-permute-start.31
  185.5 1.4 collective-permute-start.30
  186.9 1.3 collective-permute-start.47
  188.2 1.4 collective-permute-start.44
  189.7 6.7 %shard_map.77.refs_15_ = bf16[512,512]{1,0:T(8,128)(2,1)} custom-call(s32[2]{0:T(128)} %pad_add_fusion.place_ref, s32[4,4]{1,0:T(4,128)} %bitcast.15, s32[4,20]{1,0:T(4,128)} %bitcast.19, s32[4,1,128]{2,1,0:T(1,128)} %boundary_ref.9, bf16[512,512]{1,0:T(8,128)(2,1)} %get-tuple-element.17.current_ref.refs_10_, bf16[512,512]{1,0:T(8,128)(2,1)} %copy-done.10, ...), custom_call_target="tpu_custom_call" | custom-call | tf_op jit(solution)/shard_map/pallas_call | solution.py:249
  196.4 1.1 fusion
  198.2 1.3 collective-permute-start.58
  199.5 1.3 collective-permute-start.62
  202.2 1.3 collective-permute-start.61
  203.5 1.3 collective-permute-start.60
  204.9 14.4 %collective-permute-done.61.refs_18_ = bf16[256,512]{1,0:T(8,128)(2,1)S(1)} collective-permute-done((bf16[256,512]{1,0:T(8,128)(2,1)S(1)}, bf16[256,512]{1,0:T(8,128)(2,1)S(1)}, u32[]{:S(2)}, u32[]{:S(2)}) %collective-permute-start.61) | collective-permute-done | bytes 262176 | tf_op jit(solution)/shard_map/ppermute | solution.py:41
  219.2 2.4 %collective-permute-done.62.refs_19_ = bf16[512,512]{1,0:T(8,128)(2,1)S(1)} collective-permute-done((bf16[512,512]{1,0:T(8,128)(2,1)}, bf16[512,512]{1,0:T(8,128)(2,1)S(1)}, u32[]{:S(2)}, u32[]{:S(2)}) %collective-permute-start.62) | collective-permute-done | bytes 524320 | tf_op jit(solution)/shard_map/ppermute | solution.py:41
  223.2 3.1 %shard_map.78 = bf16[4,512,512]{2,1,0:T(8,128)(2,1)} custom-call(s32[2]{0:T(128)} %pad_add_fusion.place_ref, bf16[512,512]{1,0:T(8,128)(2,1)} %get-tuple-element.12.current_ref.refs_0_, bf16[512,512]{1,0:T(8,128)(2,1)} %copy-done.8, bf16[256,512]{1,0:T(8,128)(2,1)} %copy-done.47, bf16[256,512]{1,0:T(8,128)(2,1)} %collective-permute-done.16.refs_3_, ...), custom_call_target="tpu_custom_call" | custom-call | tf_op jit(solution)/shard_map/pallas_call | solution.py:276
  (190 shorter events, 19.8 us)
Async XLA Ops:
  3.5 6.6 %collective-permute-start.3 = (bf16[144,512]{1,0:T(8,128)(2,1)}, bf16[144,512]{1,0:T(8,128)(2,1)S(1)}, u32[]{:S(2)}, u32[]{:S(2)}) collective-permute-start(bf16[144,512]{1,0:T(8,128)(2,1)} %shard_map.73), channel_id=1, source_target_pairs={{0,2},{1,9},{2,4},{3,11},{4,6},{5,13},{6,0},{7,15},{8,10},{9,17},{... | collective-permute-start | bytes 442376 | tf_op jit(solution)/shard_map/ppermute | solution.py:32
  5.1 7.8 %collective-permute-start.4 = (bf16[144,512]{1,0:T(8,128)(2,1)}, bf16[144,512]{1,0:T(8,128)(2,1)S(1)}, u32[]{:S(2)}, u32[]{:S(2)}) collective-permute-start(bf16[144,512]{1,0:T(8,128)(2,1)} %shard_map.73), channel_id=1, source_target_pairs={{0,4},{1,17},{2,6},{3,19},{4,0},{5,21},{6,2},{7,23},{8,12},{9,25},... | collective-permute-start | bytes 442376 | tf_op jit(solution)/shard_map/ppermute | solution.py:32
  8.0 5.4 %collective-permute-start.5 = (bf16[144,512]{1,0:T(8,128)(2,1)}, bf16[144,512]{1,0:T(8,128)(2,1)S(1)}, u32[]{:S(2)}, u32[]{:S(2)}) collective-permute-start(bf16[144,512]{1,0:T(8,128)(2,1)} %shard_map.73), channel_id=1, source_target_pairs={{0,6},{1,25},{2,0},{3,27},{4,2},{5,29},{6,4},{7,31},{8,14},{9,1},{... | collective-permute-start | bytes 442376 | tf_op jit(solution)/shard_map/ppermute | solution.py:32
  14.3 41.2 %copy-start.7 = (bf16[576,512]{1,0:T(8,128)(2,1)}, bf16[576,512]{1,0:T(8,128)(2,1)S(1)}, u32[]{:S(2)}) copy-start(bf16[576,512]{1,0:T(8,128)(2,1)S(1)} %pad_maximum_fusion.rest_4_) | copy-start | bytes 1769476
  14.4 21.5 %collective-permute-start.6 = (bf16[576,512]{1,0:T(8,128)(2,1)S(1)}, bf16[576,512]{1,0:T(8,128)(2,1)S(1)}, u32[]{:S(2)}, u32[]{:S(2)}) collective-permute-start(bf16[576,512]{1,0:T(8,128)(2,1)S(1)} %pad_maximum_fusion.rest_4_), channel_id=1, source_target_pairs={{0,8},{1,3},{2,10},{3,5},{4,12},{5,7},{6,14},{7,1},{8,16},{9,11},{... | collective-permute-start | bytes 1769480 | tf_op jit(solution)/shard_map/ppermute | solution.py:32
  16.3 20.0 %collective-permute-start.7 = (bf16[576,512]{1,0:T(8,128)(2,1)S(1)}, bf16[576,512]{1,0:T(8,128)(2,1)S(1)}, u32[]{:S(2)}, u32[]{:S(2)}) collective-permute-start(bf16[576,512]{1,0:T(8,128)(2,1)S(1)} %pad_maximum_fusion.rest_4_), channel_id=1, source_target_pairs={{0,16},{1,5},{2,18},{3,7},{4,20},{5,1},{6,22},{7,3},{8,24},{9,13},... | collective-permute-start | bytes 1769480 | tf_op jit(solution)/shard_map/ppermute | solution.py:32
  19.9 16.5 %collective-permute-start.8 = (bf16[576,512]{1,0:T(8,128)(2,1)S(1)}, bf16[576,512]{1,0:T(8,128)(2,1)S(1)}, u32[]{:S(2)}, u32[]{:S(2)}) collective-permute-start(bf16[576,512]{1,0:T(8,128)(2,1)S(1)} %pad_maximum_fusion.rest_4_), channel_id=1, source_target_pairs={{0,24},{1,7},{2,26},{3,1},{4,28},{5,3},{6,30},{7,5},{8,0},{9,15},{... | collective-permute-start | bytes 1769480 | tf_op jit(solution)/shard_map/ppermute | solution.py:32
  20.9 14.9 %collective-permute-start = (bf16[512,512]{1,0:T(8,128)(2,1)S(1)}, bf16[512,512]{1,0:T(8,128)(2,1)S(1)}, u32[]{:S(2)}, u32[]{:S(2)}) collective-permute-start(bf16[512,512]{1,0:T(8,128)(2,1)S(1)} %bitcast.9), channel_id=1, source_target_pairs={{0,32},{32,64},{64,96},{96,0},{1,33},{33,65},{65,97},{97,1},{2,34}... | collective-permute-start | bytes 1572872 | tf_op jit(solution)/shard_map/ppermute | solution.py:41
  21.4 15.4 %collective-permute-start.1 = (bf16[512,512]{1,0:T(8,128)(2,1)S(1)}, bf16[512,512]{1,0:T(8,128)(2,1)S(1)}, u32[]{:S(2)}, u32[]{:S(2)}) collective-permute-start(bf16[512,512]{1,0:T(8,128)(2,1)S(1)} %bitcast.10), channel_id=1, source_target_pairs={{0,64},{32,96},{64,0},{96,32},{1,65},{33,97},{65,1},{97,33},{2,66}... | collective-permute-start | bytes 1572872 | tf_op jit(solution)/shard_map/ppermute | solution.py:41
  35.8 19.7 %collective-permute-start.9 = (bf16[576,512]{1,0:T(8,128)(2,1)S(1)}, bf16[576,512]{1,0:T(8,128)(2,1)S(1)}, u32[]{:S(2)}, u32[]{:S(2)}) collective-permute-start(bf16[576,512]{1,0:T(8,128)(2,1)S(1)} %pad_maximum_fusion.rest_4_), channel_id=1, source_target_pairs={{0,1},{1,0},{2,3},{3,2},{4,5},{5,4},{6,7},{7,6},{8,9},{9,8},{10,11... | collective-permute-start | bytes 1769480 | tf_op jit(solution)/shard_map/ppermute | solution.py:37
  35.8 19.6 %collective-permute-start.10 = (bf16[576,512]{1,0:T(8,128)(2,1)S(1)}, bf16[576,512]{1,0:T(8,128)(2,1)S(1)}, u32[]{:S(2)}, u32[]{:S(2)}) collective-permute-start(bf16[576,512]{1,0:T(8,128)(2,1)S(1)} %collective-permute-done.6.rest_5_), channel_id=1, source_target_pairs={{0,1},{1,0},{2,3},{3,2},{4,5},{5,4},{6,7},{7,6},{8,9},{9,8},{10,11... | collective-permute-start | bytes 1769480 | tf_op jit(solution)/shard_map/ppermute | solution.py:37
  36.3 19.2 %collective-permute-start.11 = (bf16[576,512]{1,0:T(8,128)(2,1)S(1)}, bf16[576,512]{1,0:T(8,128)(2,1)S(1)}, u32[]{:S(2)}, u32[]{:S(2)}) collective-permute-start(bf16[576,512]{1,0:T(8,128)(2,1)S(1)} %collective-permute-done.7.rest_6_), channel_id=1, source_target_pairs={{0,1},{1,0},{2,3},{3,2},{4,5},{5,4},{6,7},{7,6},{8,9},{9,8},{10,11... | collective-permute-start | bytes 1769480 | tf_op jit(solution)/shard_map/ppermute | solution.py:37
  36.4 19.1 %collective-permute-start.12 = (bf16[576,512]{1,0:T(8,128)(2,1)S(1)}, bf16[576,512]{1,0:T(8,128)(2,1)S(1)}, u32[]{:S(2)}, u32[]{:S(2)}) collective-permute-start(bf16[576,512]{1,0:T(8,128)(2,1)S(1)} %collective-permute-done.8.rest_7_), channel_id=1, source_target_pairs={{0,1},{1,0},{2,3},{3,2},{4,5},{5,4},{6,7},{7,6},{8,9},{9,8},{10,11... | collective-permute-start | bytes 1769480 | tf_op jit(solution)/shard_map/ppermute | solution.py:37
  36.9 18.6 %collective-permute-start.2 = (bf16[512,512]{1,0:T(8,128)(2,1)S(1)}, bf16[512,512]{1,0:T(8,128)(2,1)S(1)}, u32[]{:S(2)}, u32[]{:S(2)}) collective-permute-start(bf16[512,512]{1,0:T(8,128)(2,1)S(1)} %bitcast.11), channel_id=1, source_target_pairs={{0,96},{32,0},{64,32},{96,64},{1,97},{33,1},{65,33},{97,65},{2,98}... | collective-permute-start | bytes 1572872 | tf_op jit(solution)/shard_map/ppermute | solution.py:41
  66.8 7.9 %collective-permute-start.18 = (bf16[128,512]{1,0:T(8,128)(2,1)}, bf16[128,512]{1,0:T(8,128)(2,1)S(1)}, u32[]{:S(2)}, u32[]{:S(2)}) collective-permute-start(bf16[128,512]{1,0:T(8,128)(2,1)} %get-tuple-element.14), channel_id=1, source_target_pairs={{0,2},{1,9},{2,4},{3,11},{4,6},{5,13},{6,0},{7,15},{8,10},{9,17},{... | collective-permute-start | bytes 393224 | tf_op jit(solution)/shard_map/ppermute | solution.py:32
  67.3 7.4 %collective-permute-start.19 = (bf16[128,512]{1,0:T(8,128)(2,1)}, bf16[128,512]{1,0:T(8,128)(2,1)S(1)}, u32[]{:S(2)}, u32[]{:S(2)}) collective-permute-start(bf16[128,512]{1,0:T(8,128)(2,1)} %get-tuple-element.14), channel_id=1, source_target_pairs={{0,4},{1,17},{2,6},{3,19},{4,0},{5,21},{6,2},{7,23},{8,12},{9,25},... | collective-permute-start | bytes 393224 | tf_op jit(solution)/shard_map/ppermute | solution.py:32
  68.4 7.1 %collective-permute-start.20 = (bf16[128,512]{1,0:T(8,128)(2,1)}, bf16[128,512]{1,0:T(8,128)(2,1)S(1)}, u32[]{:S(2)}, u32[]{:S(2)}) collective-permute-start(bf16[128,512]{1,0:T(8,128)(2,1)} %get-tuple-element.14), channel_id=1, source_target_pairs={{0,6},{1,25},{2,0},{3,27},{4,2},{5,29},{6,4},{7,31},{8,14},{9,1},{... | collective-permute-start | bytes 393224 | tf_op jit(solution)/shard_map/ppermute | solution.py:32
  75.6 11.8 %collective-permute-start.21 = (bf16[512,512]{1,0:T(8,128)(2,1)S(1)}, bf16[512,512]{1,0:T(8,128)(2,1)S(1)}, u32[]{:S(2)}, u32[]{:S(2)}) collective-permute-start(bf16[512,512]{1,0:T(8,128)(2,1)S(1)} %constant_dynamic-update-slice_fusion.rest_4_), channel_id=1, source_target_pairs={{0,8},{1,3},{2,10},{3,5},{4,12},{5,7},{6,14},{7,1},{8,16},{9,11},{... | collective-permute-start | bytes 1572872 | tf_op jit(solution)/shard_map/ppermute | solution.py:32
  77.6 16.9 %collective-permute-start.22 = (bf16[512,512]{1,0:T(8,128)(2,1)S(1)}, bf16[512,512]{1,0:T(8,128)(2,1)S(1)}, u32[]{:S(2)}, u32[]{:S(2)}) collective-permute-start(bf16[512,512]{1,0:T(8,128)(2,1)S(1)} %constant_dynamic-update-slice_fusion.rest_4_), channel_id=1, source_target_pairs={{0,16},{1,5},{2,18},{3,7},{4,20},{5,1},{6,22},{7,3},{8,24},{9,13},... | collective-permute-start | bytes 1572872 | tf_op jit(solution)/shard_map/ppermute | solution.py:32
  81.6 12.8 %collective-permute-start.23 = (bf16[512,512]{1,0:T(8,128)(2,1)S(1)}, bf16[512,512]{1,0:T(8,128)(2,1)S(1)}, u32[]{:S(2)}, u32[]{:S(2)}) collective-permute-start(bf16[512,512]{1,0:T(8,128)(2,1)S(1)} %constant_dynamic-update-slice_fusion.rest_4_), channel_id=1, source_target_pairs={{0,24},{1,7},{2,26},{3,1},{4,28},{5,3},{6,30},{7,5},{8,0},{9,15},{... | collective-permute-start | bytes 1572872 | tf_op jit(solution)/shard_map/ppermute | solution.py:32
  82.7 12.2 %collective-permute-start.13 = (bf16[512,512]{1,0:T(8,128)(2,1)}, bf16[512,512]{1,0:T(8,128)(2,1)S(1)}, u32[]{:S(2)}, u32[]{:S(2)}) collective-permute-start(bf16[512,512]{1,0:T(8,128)(2,1)} %get-tuple-element.12.current_ref.refs_0_), channel_id=1, source_target_pairs={{0,32},{32,64},{64,96},{96,0},{1,33},{33,65},{65,97},{97,1},{2,34}... | collective-permute-start | bytes 1572872 | tf_op jit(solution)/shard_map/ppermute | solution.py:41
  84.5 10.5 %collective-permute-start.24 = (bf16[512,512]{1,0:T(8,128)(2,1)S(1)}, bf16[512,512]{1,0:T(8,128)(2,1)S(1)}, u32[]{:S(2)}, u32[]{:S(2)}) collective-permute-start(bf16[512,512]{1,0:T(8,128)(2,1)S(1)} %constant_dynamic-update-slice_fusion.rest_4_), channel_id=1, source_target_pairs={{0,1},{1,0},{2,3},{3,2},{4,5},{5,4},{6,7},{7,6},{8,9},{9,8},{10,11... | collective-permute-start | bytes 1572872 | tf_op jit(solution)/shard_map/ppermute | solution.py:37
  87.3 7.6 %collective-permute-start.25 = (bf16[512,512]{1,0:T(8,128)(2,1)S(1)}, bf16[512,512]{1,0:T(8,128)(2,1)S(1)}, u32[]{:S(2)}, u32[]{:S(2)}) collective-permute-start(bf16[512,512]{1,0:T(8,128)(2,1)S(1)} %collective-permute-done.21.rest_5_), channel_id=1, source_target_pairs={{0,1},{1,0},{2,3},{3,2},{4,5},{5,4},{6,7},{7,6},{8,9},{9,8},{10,11... | collective-permute-start | bytes 1572872 | tf_op jit(solution)/shard_map/ppermute | solution.py:37
  94.4 1.9 collective-permute-start.26
  94.4 2.6 %collective-permute-start.27 = (bf16[512,512]{1,0:T(8,128)(2,1)S(1)}, bf16[512,512]{1,0:T(8,128)(2,1)S(1)}, u32[]{:S(2)}, u32[]{:S(2)}) collective-permute-start(bf16[512,512]{1,0:T(8,128)(2,1)S(1)} %collective-permute-done.23.rest_7_), channel_id=1, source_target_pairs={{0,1},{1,0},{2,3},{3,2},{4,5},{5,4},{6,7},{7,6},{8,9},{9,8},{10,11... | collective-permute-start | bytes 1572872 | tf_op jit(solution)/shard_map/ppermute | solution.py:37
  104.7 6.5 %collective-permute-start.33 = (bf16[128,512]{1,0:T(8,128)(2,1)}, bf16[128,512]{1,0:T(8,128)(2,1)S(1)}, u32[]{:S(2)}, u32[]{:S(2)}) collective-permute-start(bf16[128,512]{1,0:T(8,128)(2,1)} %get-tuple-element.16), channel_id=1, source_target_pairs={{0,2},{1,9},{2,4},{3,11},{4,6},{5,13},{6,0},{7,15},{8,10},{9,17},{... | collective-permute-start | bytes 393224 | tf_op jit(solution)/shard_map/ppermute | solution.py:32
  106.4 7.0 %collective-permute-start.34 = (bf16[128,512]{1,0:T(8,128)(2,1)}, bf16[128,512]{1,0:T(8,128)(2,1)S(1)}, u32[]{:S(2)}, u32[]{:S(2)}) collective-permute-start(bf16[128,512]{1,0:T(8,128)(2,1)} %get-tuple-element.16), channel_id=1, source_target_pairs={{0,4},{1,17},{2,6},{3,19},{4,0},{5,21},{6,2},{7,23},{8,12},{9,25},... | collective-permute-start | bytes 393224 | tf_op jit(solution)/shard_map/ppermute | solution.py:32
  109.9 5.2 %collective-permute-start.35 = (bf16[128,512]{1,0:T(8,128)(2,1)}, bf16[128,512]{1,0:T(8,128)(2,1)S(1)}, u32[]{:S(2)}, u32[]{:S(2)}) collective-permute-start(bf16[128,512]{1,0:T(8,128)(2,1)} %get-tuple-element.16), channel_id=1, source_target_pairs={{0,6},{1,25},{2,0},{3,27},{4,2},{5,29},{6,4},{7,31},{8,14},{9,1},{... | collective-permute-start | bytes 393224 | tf_op jit(solution)/shard_map/ppermute | solution.py:32
  115.1 16.1 %collective-permute-start.36 = (bf16[512,512]{1,0:T(8,128)(2,1)S(1)}, bf16[512,512]{1,0:T(8,128)(2,1)S(1)}, u32[]{:S(2)}, u32[]{:S(2)}) collective-permute-start(bf16[512,512]{1,0:T(8,128)(2,1)S(1)} %constant_dynamic-update-slice_fusion.4.rest_4_), channel_id=1, source_target_pairs={{0,8},{1,3},{2,10},{3,5},{4,12},{5,7},{6,14},{7,1},{8,16},{9,11},{... | collective-permute-start | bytes 1572872 | tf_op jit(solution)/shard_map/ppermute | solution.py:32
  116.0 15.2 %collective-permute-start.37 = (bf16[512,512]{1,0:T(8,128)(2,1)S(1)}, bf16[512,512]{1,0:T(8,128)(2,1)S(1)}, u32[]{:S(2)}, u32[]{:S(2)}) collective-permute-start(bf16[512,512]{1,0:T(8,128)(2,1)S(1)} %constant_dynamic-update-slice_fusion.4.rest_4_), channel_id=1, source_target_pairs={{0,16},{1,5},{2,18},{3,7},{4,20},{5,1},{6,22},{7,3},{8,24},{9,13},... | collective-permute-start | bytes 1572872 | tf_op jit(solution)/shard_map/ppermute | solution.py:32
  118.1 14.0 %collective-permute-start.38 = (bf16[512,512]{1,0:T(8,128)(2,1)S(1)}, bf16[512,512]{1,0:T(8,128)(2,1)S(1)}, u32[]{:S(2)}, u32[]{:S(2)}) collective-permute-start(bf16[512,512]{1,0:T(8,128)(2,1)S(1)} %constant_dynamic-update-slice_fusion.4.rest_4_), channel_id=1, source_target_pairs={{0,24},{1,7},{2,26},{3,1},{4,28},{5,3},{6,30},{7,5},{8,0},{9,15},{... | collective-permute-start | bytes 1572872 | tf_op jit(solution)/shard_map/ppermute | solution.py:32
  119.6 13.9 %collective-permute-start.28 = (bf16[512,512]{1,0:T(8,128)(2,1)}, bf16[512,512]{1,0:T(8,128)(2,1)S(1)}, u32[]{:S(2)}, u32[]{:S(2)}) collective-permute-start(bf16[512,512]{1,0:T(8,128)(2,1)} %get-tuple-element.15.current_ref.refs_5_), channel_id=1, source_target_pairs={{0,32},{32,64},{64,96},{96,0},{1,33},{33,65},{65,97},{97,1},{2,34}... | collective-permute-start | bytes 1572872 | tf_op jit(solution)/shard_map/ppermute | solution.py:41
  121.6 13.2 %collective-permute-start.39 = (bf16[512,512]{1,0:T(8,128)(2,1)S(1)}, bf16[512,512]{1,0:T(8,128)(2,1)S(1)}, u32[]{:S(2)}, u32[]{:S(2)}) collective-permute-start(bf16[512,512]{1,0:T(8,128)(2,1)S(1)} %constant_dynamic-update-slice_fusion.4.rest_4_), channel_id=1, source_target_pairs={{0,1},{1,0},{2,3},{3,2},{4,5},{5,4},{6,7},{7,6},{8,9},{9,8},{10,11... | collective-permute-start | bytes 1572872 | tf_op jit(solution)/shard_map/ppermute | solution.py:37
  131.2 3.6 %collective-permute-start.40 = (bf16[512,512]{1,0:T(8,128)(2,1)S(1)}, bf16[512,512]{1,0:T(8,128)(2,1)S(1)}, u32[]{:S(2)}, u32[]{:S(2)}) collective-permute-start(bf16[512,512]{1,0:T(8,128)(2,1)S(1)} %collective-permute-done.36.rest_5_), channel_id=1, source_target_pairs={{0,1},{1,0},{2,3},{3,2},{4,5},{5,4},{6,7},{7,6},{8,9},{9,8},{10,11... | collective-permute-start | bytes 1572872 | tf_op jit(solution)/shard_map/ppermute | solution.py:37
  131.2 3.6 %collective-permute-start.41 = (bf16[512,512]{1,0:T(8,128)(2,1)S(1)}, bf16[512,512]{1,0:T(8,128)(2,1)S(1)}, u32[]{:S(2)}, u32[]{:S(2)}) collective-permute-start(bf16[512,512]{1,0:T(8,128)(2,1)S(1)} %collective-permute-done.37.rest_6_), channel_id=1, source_target_pairs={{0,1},{1,0},{2,3},{3,2},{4,5},{5,4},{6,7},{7,6},{8,9},{9,8},{10,11... | collective-permute-start | bytes 1572872 | tf_op jit(solution)/shard_map/ppermute | solution.py:37
  132.1 2.8 %collective-permute-start.42 = (bf16[512,512]{1,0:T(8,128)(2,1)S(1)}, bf16[512,512]{1,0:T(8,128)(2,1)S(1)}, u32[]{:S(2)}, u32[]{:S(2)}) collective-permute-start(bf16[512,512]{1,0:T(8,128)(2,1)S(1)} %collective-permute-done.38.rest_7_), channel_id=1, source_target_pairs={{0,1},{1,0},{2,3},{3,2},{4,5},{5,4},{6,7},{7,6},{8,9},{9,8},{10,11... | collective-permute-start | bytes 1572872 | tf_op jit(solution)/shard_map/ppermute | solution.py:37
  133.5 12.4 %collective-permute-start.14 = (bf16[256,512]{1,0:T(8,128)(2,1)S(1)}, bf16[256,512]{1,0:T(8,128)(2,1)S(1)}, u32[]{:S(2)}, u32[]{:S(2)}) collective-permute-start(bf16[256,512]{1,0:T(8,128)(2,1)S(1)} %get-tuple-element.26), channel_id=1, source_target_pairs={{64,96},{65,97},{66,98},{67,99},{68,100},{69,101},{70,102},{71,103... | collective-permute-start | bytes 786440 | tf_op jit(solution)/shard_map/ppermute | solution.py:41
  143.6 9.2 %collective-permute-start.48 = (bf16[128,512]{1,0:T(8,128)(2,1)}, bf16[128,512]{1,0:T(8,128)(2,1)S(1)}, u32[]{:S(2)}, u32[]{:S(2)}) collective-permute-start(bf16[128,512]{1,0:T(8,128)(2,1)} %get-tuple-element.18), channel_id=1, source_target_pairs={{0,2},{1,9},{2,4},{3,11},{4,6},{5,13},{6,0},{7,15},{8,10},{9,17},{... | collective-permute-start | bytes 393224 | tf_op jit(solution)/shard_map/ppermute | solution.py:32
  143.7 22.7 %collective-permute-start.17 = (bf16[512,512]{1,0:T(8,128)(2,1)S(1)}, bf16[512,512]{1,0:T(8,128)(2,1)S(1)}, u32[]{:S(2)}, u32[]{:S(2)}) collective-permute-start(bf16[512,512]{1,0:T(8,128)(2,1)S(1)} %copy-done.4), channel_id=1, source_target_pairs={{32,0},{33,1},{34,2},{35,3},{36,4},{37,5},{38,6},{39,7},{40,8},{41... | collective-permute-start | bytes 1572872 | tf_op jit(solution)/shard_map/ppermute | solution.py:41
  144.5 17.2 %collective-permute-start.16 = (bf16[256,512]{1,0:T(8,128)(2,1)S(1)}, bf16[256,512]{1,0:T(8,128)(2,1)}, u32[]{:S(2)}, u32[]{:S(2)}) collective-permute-start(bf16[256,512]{1,0:T(8,128)(2,1)S(1)} %get-tuple-element.25), channel_id=1, source_target_pairs={{64,0},{65,1},{66,2},{67,3},{68,4},{69,5},{70,6},{71,7},{72,8},{73... | collective-permute-start | bytes 786440 | tf_op jit(solution)/shard_map/ppermute | solution.py:41
  145.9 16.2 %collective-permute-start.15 = (bf16[256,512]{1,0:T(8,128)(2,1)S(1)}, bf16[256,512]{1,0:T(8,128)(2,1)S(1)}, u32[]{:S(2)}, u32[]{:S(2)}) collective-permute-start(bf16[256,512]{1,0:T(8,128)(2,1)S(1)} %collective-permute-done.14), channel_id=1, source_target_pairs={{96,0},{97,1},{98,2},{99,3},{100,4},{101,5},{102,6},{103,7},{104,8... | collective-permute-start | bytes 786440 | tf_op jit(solution)/shard_map/ppermute | solution.py:41
  149.2 6.8 %collective-permute-start.49 = (bf16[128,512]{1,0:T(8,128)(2,1)}, bf16[128,512]{1,0:T(8,128)(2,1)S(1)}, u32[]{:S(2)}, u32[]{:S(2)}) collective-permute-start(bf16[128,512]{1,0:T(8,128)(2,1)} %get-tuple-element.18), channel_id=1, source_target_pairs={{0,4},{1,17},{2,6},{3,19},{4,0},{5,21},{6,2},{7,23},{8,12},{9,25},... | collective-permute-start | bytes 393224 | tf_op jit(solution)/shard_map/ppermute | solution.py:32
  152.9 5.2 %collective-permute-start.50 = (bf16[128,512]{1,0:T(8,128)(2,1)}, bf16[128,512]{1,0:T(8,128)(2,1)S(1)}, u32[]{:S(2)}, u32[]{:S(2)}) collective-permute-start(bf16[128,512]{1,0:T(8,128)(2,1)} %get-tuple-element.18), channel_id=1, source_target_pairs={{0,6},{1,25},{2,0},{3,27},{4,2},{5,29},{6,4},{7,31},{8,14},{9,1},{... | collective-permute-start | bytes 393224 | tf_op jit(solution)/shard_map/ppermute | solution.py:32
  158.1 14.3 %collective-permute-start.51 = (bf16[512,512]{1,0:T(8,128)(2,1)S(1)}, bf16[512,512]{1,0:T(8,128)(2,1)S(1)}, u32[]{:S(2)}, u32[]{:S(2)}) collective-permute-start(bf16[512,512]{1,0:T(8,128)(2,1)S(1)} %constant_dynamic-update-slice_fusion.8.rest_4_), channel_id=1, source_target_pairs={{0,8},{1,3},{2,10},{3,5},{4,12},{5,7},{6,14},{7,1},{8,16},{9,11},{... | collective-permute-start | bytes 1572872 | tf_op jit(solution)/shard_map/ppermute | solution.py:32
  158.8 15.7 %collective-permute-start.52 = (bf16[512,512]{1,0:T(8,128)(2,1)S(1)}, bf16[512,512]{1,0:T(8,128)(2,1)S(1)}, u32[]{:S(2)}, u32[]{:S(2)}) collective-permute-start(bf16[512,512]{1,0:T(8,128)(2,1)S(1)} %constant_dynamic-update-slice_fusion.8.rest_4_), channel_id=1, source_target_pairs={{0,16},{1,5},{2,18},{3,7},{4,20},{5,1},{6,22},{7,3},{8,24},{9,13},... | collective-permute-start | bytes 1572872 | tf_op jit(solution)/shard_map/ppermute | solution.py:32
  161.7 13.4 %collective-permute-start.53 = (bf16[512,512]{1,0:T(8,128)(2,1)S(1)}, bf16[512,512]{1,0:T(8,128)(2,1)S(1)}, u32[]{:S(2)}, u32[]{:S(2)}) collective-permute-start(bf16[512,512]{1,0:T(8,128)(2,1)S(1)} %constant_dynamic-update-slice_fusion.8.rest_4_), channel_id=1, source_target_pairs={{0,24},{1,7},{2,26},{3,1},{4,28},{5,3},{6,30},{7,5},{8,0},{9,15},{... | collective-permute-start | bytes 1572872 | tf_op jit(solution)/shard_map/ppermute | solution.py:32
  162.2 10.2 %collective-permute-start.29 = (bf16[256,512]{1,0:T(8,128)(2,1)S(1)}, bf16[256,512]{1,0:T(8,128)(2,1)}, u32[]{:S(2)}, u32[]{:S(2)}) collective-permute-start(bf16[256,512]{1,0:T(8,128)(2,1)S(1)} %get-tuple-element.24), channel_id=1, source_target_pairs={{96,0},{97,1},{98,2},{99,3},{100,4},{101,5},{102,6},{103,7},{104,8... | collective-permute-start | bytes 786440 | tf_op jit(solution)/shard_map/ppermute | solution.py:41
  166.5 16.3 %collective-permute-start.43 = (bf16[512,512]{1,0:T(8,128)(2,1)S(1)}, bf16[512,512]{1,0:T(8,128)(2,1)S(1)}, u32[]{:S(2)}, u32[]{:S(2)}) collective-permute-start(bf16[512,512]{1,0:T(8,128)(2,1)S(1)} %copy-done.6), channel_id=1, source_target_pairs={{0,32},{32,64},{64,96},{96,0},{1,33},{33,65},{65,97},{97,1},{2,34}... | collective-permute-start | bytes 1572872 | tf_op jit(solution)/shard_map/ppermute | solution.py:41
  172.4 11.1 %collective-permute-start.54 = (bf16[512,512]{1,0:T(8,128)(2,1)S(1)}, bf16[512,512]{1,0:T(8,128)(2,1)S(1)}, u32[]{:S(2)}, u32[]{:S(2)}) collective-permute-start(bf16[512,512]{1,0:T(8,128)(2,1)S(1)} %constant_dynamic-update-slice_fusion.8.rest_4_), channel_id=1, source_target_pairs={{0,1},{1,0},{2,3},{3,2},{4,5},{5,4},{6,7},{7,6},{8,9},{9,8},{10,11... | collective-permute-start | bytes 1572872 | tf_op jit(solution)/shard_map/ppermute | solution.py:37
  172.4 13.1 %collective-permute-start.55 = (bf16[512,512]{1,0:T(8,128)(2,1)S(1)}, bf16[512,512]{1,0:T(8,128)(2,1)S(1)}, u32[]{:S(2)}, u32[]{:S(2)}) collective-permute-start(bf16[512,512]{1,0:T(8,128)(2,1)S(1)} %collective-permute-done.51.rest_5_), channel_id=1, source_target_pairs={{0,1},{1,0},{2,3},{3,2},{4,5},{5,4},{6,7},{7,6},{8,9},{9,8},{10,11... | collective-permute-start | bytes 1572872 | tf_op jit(solution)/shard_map/ppermute | solution.py:37
  174.5 12.4 %collective-permute-start.56 = (bf16[512,512]{1,0:T(8,128)(2,1)S(1)}, bf16[512,512]{1,0:T(8,128)(2,1)S(1)}, u32[]{:S(2)}, u32[]{:S(2)}) collective-permute-start(bf16[512,512]{1,0:T(8,128)(2,1)S(1)} %collective-permute-done.52.rest_6_), channel_id=1, source_target_pairs={{0,1},{1,0},{2,3},{3,2},{4,5},{5,4},{6,7},{7,6},{8,9},{9,8},{10,11... | collective-permute-start | bytes 1572872 | tf_op jit(solution)/shard_map/ppermute | solution.py:37
  175.1 13.1 %collective-permute-start.57 = (bf16[512,512]{1,0:T(8,128)(2,1)S(1)}, bf16[512,512]{1,0:T(8,128)(2,1)S(1)}, u32[]{:S(2)}, u32[]{:S(2)}) collective-permute-start(bf16[512,512]{1,0:T(8,128)(2,1)S(1)} %collective-permute-done.53.rest_7_), channel_id=1, source_target_pairs={{0,1},{1,0},{2,3},{3,2},{4,5},{5,4},{6,7},{7,6},{8,9},{9,8},{10,11... | collective-permute-start | bytes 1572872 | tf_op jit(solution)/shard_map/ppermute | solution.py:37
  182.8 16.7 %collective-permute-start.32 = (bf16[512,512]{1,0:T(8,128)(2,1)S(1)}, bf16[512,512]{1,0:T(8,128)(2,1)S(1)}, u32[]{:S(2)}, u32[]{:S(2)}) collective-permute-start(bf16[512,512]{1,0:T(8,128)(2,1)S(1)} %copy-done.5), channel_id=1, source_target_pairs={{64,32},{65,33},{66,34},{67,35},{68,36},{69,37},{70,38},{71,39},{7... | collective-permute-start | bytes 1572872 | tf_op jit(solution)/shard_map/ppermute | solution.py:41
  183.5 14.0 %collective-permute-start.31 = (bf16[256,512]{1,0:T(8,128)(2,1)S(1)}, bf16[256,512]{1,0:T(8,128)(2,1)}, u32[]{:S(2)}, u32[]{:S(2)}) collective-permute-start(bf16[256,512]{1,0:T(8,128)(2,1)S(1)} %get-tuple-element.23), channel_id=1, source_target_pairs={{96,32},{97,33},{98,34},{99,35},{100,36},{101,37},{102,38},{103,39... | collective-permute-start | bytes 786440 | tf_op jit(solution)/shard_map/ppermute | solution.py:41
  185.5 12.7 %collective-permute-start.30 = (bf16[256,512]{1,0:T(8,128)(2,1)}, bf16[256,512]{1,0:T(8,128)(2,1)}, u32[]{:S(2)}, u32[]{:S(2)}) collective-permute-start(bf16[256,512]{1,0:T(8,128)(2,1)} %collective-permute-done.29), channel_id=1, source_target_pairs={{0,32},{1,33},{2,34},{3,35},{4,36},{5,37},{6,38},{7,39},{8,40},{9,... | collective-permute-start | bytes 786440 | tf_op jit(solution)/shard_map/ppermute | solution.py:41
  186.9 15.3 %collective-permute-start.47 = (bf16[512,512]{1,0:T(8,128)(2,1)S(1)}, bf16[512,512]{1,0:T(8,128)(2,1)S(1)}, u32[]{:S(2)}, u32[]{:S(2)}) collective-permute-start(bf16[512,512]{1,0:T(8,128)(2,1)S(1)} %copy-done.6), channel_id=1, source_target_pairs={{96,64},{97,65},{98,66},{99,67},{100,68},{101,69},{102,70},{103,71... | collective-permute-start | bytes 1572872 | tf_op jit(solution)/shard_map/ppermute | solution.py:41
  188.2 12.6 %collective-permute-start.44 = (bf16[256,512]{1,0:T(8,128)(2,1)S(1)}, bf16[256,512]{1,0:T(8,128)(2,1)}, u32[]{:S(2)}, u32[]{:S(2)}) collective-permute-start(bf16[256,512]{1,0:T(8,128)(2,1)S(1)} %get-tuple-element.22), channel_id=1, source_target_pairs={{0,32},{1,33},{2,34},{3,35},{4,36},{5,37},{6,38},{7,39},{8,40},{9,... | collective-permute-start | bytes 786440 | tf_op jit(solution)/shard_map/ppermute | solution.py:41
  197.5 4.0 %collective-permute-start.46 = (bf16[256,512]{1,0:T(8,128)(2,1)S(1)}, bf16[256,512]{1,0:T(8,128)(2,1)S(1)}, u32[]{:S(2)}, u32[]{:S(2)}) collective-permute-start(bf16[256,512]{1,0:T(8,128)(2,1)S(1)} %get-tuple-element.21), channel_id=1, source_target_pairs={{0,64},{1,65},{2,66},{3,67},{4,68},{5,69},{6,70},{7,71},{8,72},{9,... | collective-permute-start | bytes 786440 | tf_op jit(solution)/shard_map/ppermute | solution.py:41
  198.2 21.1 %collective-permute-start.58 = (bf16[512,512]{1,0:T(8,128)(2,1)}, bf16[512,512]{1,0:T(8,128)(2,1)S(1)}, u32[]{:S(2)}, u32[]{:S(2)}) collective-permute-start(bf16[512,512]{1,0:T(8,128)(2,1)} %shard_map.77.refs_15_), channel_id=1, source_target_pairs={{64,96},{65,97},{66,98},{67,99},{68,100},{69,101},{70,102},{71,103... | collective-permute-start | bytes 1572872 | tf_op jit(solution)/shard_map/ppermute | solution.py:41
  199.5 22.2 %collective-permute-start.62 = (bf16[512,512]{1,0:T(8,128)(2,1)}, bf16[512,512]{1,0:T(8,128)(2,1)S(1)}, u32[]{:S(2)}, u32[]{:S(2)}) collective-permute-start(bf16[512,512]{1,0:T(8,128)(2,1)} %shard_map.77.refs_15_), channel_id=1, source_target_pairs={{0,96},{1,97},{2,98},{3,99},{4,100},{5,101},{6,102},{7,103},{8,104... | collective-permute-start | bytes 1572872 | tf_op jit(solution)/shard_map/ppermute | solution.py:41
  200.8 2.7 %collective-permute-start.59 = (bf16[256,512]{1,0:T(8,128)(2,1)S(1)}, bf16[256,512]{1,0:T(8,128)(2,1)S(1)}, u32[]{:S(2)}, u32[]{:S(2)}) collective-permute-start(bf16[256,512]{1,0:T(8,128)(2,1)S(1)} %get-tuple-element.20), channel_id=1, source_target_pairs={{32,64},{33,65},{34,66},{35,67},{36,68},{37,69},{38,70},{39,71},{4... | collective-permute-start | bytes 786440 | tf_op jit(solution)/shard_map/ppermute | solution.py:41
  201.5 3.3 %collective-permute-start.45 = (bf16[256,512]{1,0:T(8,128)(2,1)}, bf16[256,512]{1,0:T(8,128)(2,1)S(1)}, u32[]{:S(2)}, u32[]{:S(2)}) collective-permute-start(bf16[256,512]{1,0:T(8,128)(2,1)} %collective-permute-done.44), channel_id=1, source_target_pairs={{32,64},{33,65},{34,66},{35,67},{36,68},{37,69},{38,70},{39,71},{4... | collective-permute-start | bytes 786440 | tf_op jit(solution)/shard_map/ppermute | solution.py:41
  202.2 17.0 %collective-permute-start.61 = (bf16[256,512]{1,0:T(8,128)(2,1)S(1)}, bf16[256,512]{1,0:T(8,128)(2,1)S(1)}, u32[]{:S(2)}, u32[]{:S(2)}) collective-permute-start(bf16[256,512]{1,0:T(8,128)(2,1)S(1)} %get-tuple-element.19), channel_id=1, source_target_pairs={{32,96},{33,97},{34,98},{35,99},{36,100},{37,101},{38,102},{39,103... | collective-permute-start | bytes 786440 | tf_op jit(solution)/shard_map/ppermute | solution.py:41
  203.5 18.9 %collective-permute-start.60 = (bf16[256,512]{1,0:T(8,128)(2,1)S(1)}, bf16[256,512]{1,0:T(8,128)(2,1)S(1)}, u32[]{:S(2)}, u32[]{:S(2)}) collective-permute-start(bf16[256,512]{1,0:T(8,128)(2,1)S(1)} %collective-permute-done.59), channel_id=1, source_target_pairs={{64,96},{65,97},{66,98},{67,99},{68,100},{69,101},{70,102},{71,103... | collective-permute-start | bytes 786440 | tf_op jit(solution)/shard_map/ppermute | solution.py:41
  (51 other events, 503.4 us)

commit v3 on v2

v3 whole, which is shorter than its diff:
```python
import functools

import jax
import jax.numpy as jnp
from jax import lax
from jax.experimental import pallas as pl
from jax.experimental.pallas import tpu as pltpu
from jax.sharding import PartitionSpec as P

TILE = 128
SIDE = 4
CORES = 2
EXTRA = 16
ANY = pl.BlockSpec(memory_space=pl.ANY)
SMEM = pl.BlockSpec(memory_space=pltpu.SMEM)
VMEM = pl.BlockSpec(memory_space=pltpu.VMEM)
PLACES = [(z, y, core) for z in range(SIDE) for y in range(SIDE) for core in range(CORES)]


def node_of(z, y, core):
    return ((z % SIDE) * SIDE + y % SIDE) * CORES + core


def along(block, distance, phase):
    route = []
    for z, y, core in PLACES:
        if core == phase:
            target = node_of(z, y + distance, core)
        else:
            target = node_of(z + distance, y, core)
        route.append((node_of(z, y, core), target))
    return lax.ppermute(block, "node", route)


def other_core(block):
    route = [(node_of(z, y, core), node_of(z, y, 1 - core)) for z, y, core in PLACES]
    return lax.ppermute(block, "node", route)


def to_plane(block, pairs):
    return lax.ppermute(block, "layer", pairs)


def offered_rows(listed, rows):
    row_ids = lax.broadcasted_iota(jnp.int32, (rows.shape[0], listed.shape[1]), 0)
    selector = (row_ids == listed).astype(jnp.bfloat16)
    picked = lax.dot_general(
        selector, rows, (((0,), (0,)), ((), ())), preferred_element_type=jnp.float32
    )
    return picked.astype(jnp.bfloat16)


def first_kernel(place_ref, rows_ref, listed_ref, lists_ref, block_ref):
    node = place_ref[1]
    offered = listed_ref.shape[1]
    nodes, picks = lists_ref.shape
    block_ref[pl.ds(offered, EXTRA), :] = jnp.zeros((EXTRA, block_ref.shape[1]), jnp.bfloat16)
    lists = lists_ref[...].astype(jnp.float32).astype(jnp.bfloat16)
    for core in range(CORES):
        @pl.when(node % CORES == core)
        def _():
            for part in range(nodes // EXTRA):
                lanes = pl.ds(part * CORES * picks + core * picks, picks)
                block_ref[pl.ds(offered, EXTRA), lanes] = lists[part * EXTRA:(part + 1) * EXTRA]
    block_ref[pl.ds(0, offered), :] = offered_rows(listed_ref[...], rows_ref[...])


def layer_kernel(
    layer_id, first, last,
    place_ref, counts_ref, cols_ref, listed_ref, current_ref, previous_ref, tiles_ref, halves_ref, others_ref,
    *rest,
):
    mine_refs, theirs_refs, rest = rest[:SIDE], rest[SIDE:2 * SIDE], rest[2 * SIDE:]
    outs = 1 if last else 3 if first else 2
    out_ref = rest[0]
    space, total = rest[outs:outs + 2]
    span, node = place_ref[0], place_ref[1]
    row_count = total.shape[0]
    offered = listed_ref.shape[1]
    z, y, core = node // (SIDE * CORES), (node // CORES) % SIDE, node % CORES
    each = mine_refs[0].shape[0] // SIDE
    if first:
        lists = rest[outs + 2]
        lists[...] = jnp.zeros_like(lists)
        lane_block = pl.ds(pl.multiple_of((node // EXTRA) * TILE, TILE), TILE)
        wanted = lax.broadcasted_iota(jnp.int32, (EXTRA, TILE), 0) == node % EXTRA
    for refs, kind in ((mine_refs, core), (theirs_refs, 1 - core)):
        for j in range(SIDE):
            for k in range(SIDE):
                dz = jnp.where(kind == 0, j, k)
                dy = jnp.where(kind == 0, k, j)
                chip = ((z + SIDE - dz) % SIDE) * SIDE + (y + SIDE - dy) % SIDE
                start = pl.multiple_of(2 * row_count + (chip * CORES + kind) * offered, offered)
                space[pl.ds(start, offered), :] = refs[j][pl.ds(k * each, offered), :]
                if first:
                    raw = refs[j][pl.ds(k * each + offered, EXTRA), lane_block].astype(jnp.float32)
                    row = jnp.sum(jnp.where(wanted, raw, 0.0), axis=0, keepdims=True)
                    lists[pl.ds(chip, 1), :] += row
    space[pl.ds(0, row_count), :] = current_ref[...]

    @pl.when(span == 0)
    def _():
        space[pl.ds(row_count, row_count), :] = jnp.zeros((row_count, space.shape[1]), space.dtype)

    @pl.when(span > 0)
    def _():
        space[pl.ds(row_count, row_count), :] = previous_ref[...]

    total[...] = jnp.zeros_like(total)
    if first:
        wide_ref = rest[2]
        lanes = lax.broadcasted_iota(jnp.int32, (1, TILE), 1)
        shift = jnp.where(lanes >= TILE // CORES, offered, 0)
        slot_rows = lax.broadcasted_iota(jnp.int32, (CORES * offered, TILE), 0)

    ends = []
    reached = 0
    for r in range(counts_ref.shape[1] - 1):
        reached = reached + counts_ref[span, r]
        ends.append(reached)
    own_tiles = 2 * row_count // TILE
    for f in range(cols_ref.shape[1]):
        owner = sum((f >= end).astype(jnp.int32) for end in ends)
        col = cols_ref[span, f]
        if first:
            plain = lanes + TILE * (col % CORES)
            listed = lists[pl.ds(jnp.maximum(col - own_tiles, 0), 1), :].astype(jnp.int32) + shift
            target = jnp.where(col < own_tiles, plain, listed)
            selector = (slot_rows == target).astype(jnp.bfloat16)
            wide = lax.dot_general(
                tiles_ref[f], selector, (((1,), (1,)), ((), ())), preferred_element_type=jnp.float32
            ).astype(jnp.bfloat16)
            wide_ref[f] = wide
        else:
            wide = tiles_ref[f]
        slot = jnp.where(col < own_tiles, col // CORES, col - own_tiles // CORES)
        row_at = pl.ds(pl.multiple_of(owner * TILE, TILE), TILE)
        slot_at = pl.ds(pl.multiple_of(slot * CORES * offered, CORES * offered), CORES * offered)
        total[row_at, :] += jnp.dot(wide, space[slot_at, :], preferred_element_type=jnp.float32)
    half = halves_ref.shape[0] // SIDE
    distance = (span + SIDE - layer_id) % SIDE
    held = pl.ds(pl.multiple_of(distance * half, half), half)
    linear = 0.0
    for ref, kind in ((halves_ref, core), (others_ref, 1 - core)):
        columns = pl.ds(pl.multiple_of(kind * half, half), half)
        aggregate = total[:, columns].astype(jnp.bfloat16)
        linear = linear + jnp.dot(aggregate, ref[held, :], preferred_element_type=jnp.float32)
    fresh = jnp.maximum(linear, 0.0).astype(jnp.bfloat16)
    out_ref[...] = fresh
    if not last:
        rest[1][...] = offered_rows(listed_ref[...], fresh)


def place_kernel(place_ref, *refs):
    out_ref, held, in_sems, out_sems = refs[-4:]
    spans = out_ref.shape[0]
    span = place_ref[0]
    first_ref = 0
    for layer_id in range(spans):
        halved = 2 if layer_id == spans - 1 else 1
        parts = []
        for distance in range(spans):
            pieces = halved if distance == 2 else 1
            rows = held.shape[1] // pieces
            parts += [(distance, rows * i, rows) for i in range(pieces)]
        sources = refs[first_ref:first_ref + len(parts)]
        first_ref += len(parts)

        @pl.when(span == layer_id)
        def _():
            ins, outs = [], []
            for i, (distance, start, rows) in enumerate(parts):
                staged = held.at[distance, pl.ds(start, rows)]
                target = out_ref.at[(layer_id - distance) % spans, pl.ds(start, rows)]
                ins.append(pltpu.make_async_copy(sources[i], staged, in_sems.at[i]))
                outs.append(pltpu.make_async_copy(staged, target, out_sems.at[i]))
            for copy in ins:
                copy.start()
            for i in range(len(parts)):
                ins[i].wait()
                outs[i].start()
            for copy in outs:
                copy.wait()


def on_device(features, weights, boundary, pick_index, counts, tile_cols, tile_vals):
    spans, row_count, width = features.shape
    layers = lax.axis_size("layer")
    nodes = lax.axis_size("node")
    offered = boundary.shape[2]
    tile_total = tile_vals.shape[2]
    node = lax.axis_index("node")
    span = lax.axis_index("layer")
    place = jnp.stack([span, node]).astype(jnp.int32)
    current = lax.dynamic_index_in_dim(features, span, 0, keepdims=False)
    listed = lax.dynamic_index_in_dim(boundary, span, 0, keepdims=False)
    lists = lax.dynamic_index_in_dim(pick_index, span, 0, keepdims=False)[0]
    counts, tile_cols = counts[:, 0], tile_cols[:, 0]
    rows_shape = jax.ShapeDtypeStruct((row_count, width), jnp.bfloat16)
    wide_shape = jax.ShapeDtypeStruct((tile_total, TILE, CORES * offered), jnp.bfloat16)
    block_shape = jax.ShapeDtypeStruct((offered, width), jnp.bfloat16)
    params = pltpu.CompilerParams(vmem_limit_bytes=16 << 20)
    block = pl.pallas_call(
        first_kernel,
        out_shape=jax.ShapeDtypeStruct((offered + EXTRA, width), jnp.bfloat16),
        in_specs=[SMEM, VMEM, VMEM, VMEM],
        out_specs=VMEM,
        compiler_params=params,
    )(place, current, listed, lists)
    previous = lax.dynamic_index_in_dim(features, jnp.maximum(span - 1, 0), 0, keepdims=False)
    tiles = lax.dynamic_index_in_dim(tile_vals, span, 0, keepdims=False)[0]
    known = moving = None
    placed = []
    for layer_id in range(layers):
        first, last = layer_id == 0, layer_id == layers - 1
        row = jnp.concatenate([block] + [along(block, k, 0) for k in range(1, SIDE)], 0)
        if first:
            half = lax.dynamic_slice_in_dim(weights[0], (node % CORES) * (width // CORES), width // CORES, 0)
            half, row = lax.optimization_barrier((half, row))
            halves = [half]
            for distance in range(1, layers):
                halves.append(to_plane(half, [(i, (i + distance) % layers) for i in range(layers)]))
            halves = jnp.concatenate(halves, 0)
            known = [halves, other_core(halves)]
        mine = [row] + [along(row, j, 1) for j in range(1, SIDE)]
        theirs = [other_core(part) for part in mine]
        if moving is not None:
            mine, theirs, moving = lax.optimization_barrier((mine, theirs, moving))
            previous = moving[0]
            placed += [current] + moving
        scratch = [
            pltpu.VMEM((2 * row_count + nodes * offered, width), jnp.bfloat16),
            pltpu.VMEM((row_count, width), jnp.float32),
        ]
        if first:
            scratch.append(pltpu.VMEM((SIDE * SIDE, TILE), jnp.float32))
        outs = [rows_shape] if last else [rows_shape, block_shape]
        if first:
            outs.append(wide_shape)
        results = pl.pallas_call(
            functools.partial(layer_kernel, layer_id, first, last),
            out_shape=outs,
            in_specs=[SMEM, SMEM, SMEM] + [VMEM] * (6 + 2 * SIDE),
            out_specs=[VMEM] * len(outs),
            scratch_shapes=scratch,
            compiler_params=params,
        )(place, counts, tile_cols, listed, current, previous, tiles, *known, *mine, *theirs)
        current = results[0]
        if not last:
            block = results[1]
        if first:
            tiles = results[2]
        before, after, across = [(layer_id + step) % layers for step in (3, 1, 2)]
        if not last:
            moving = [
                to_plane(current, [(i, (i + 1) % layers) for i in range(layers)]),
                to_plane(current, [(across, layer_id)]),
                to_plane(current, [(after, layer_id)]),
            ]
        else:
            half = row_count // 2
            relayed = to_plane(current[:half], [(across, before)])
            placed += [
                current,
                to_plane(current, [(before, layer_id)]),
                to_plane(relayed, [(before, layer_id)]),
                to_plane(current[half:], [(across, layer_id)]),
                to_plane(current, [(after, layer_id)]),
            ]
    return pl.pallas_call(
        place_kernel,
        out_shape=jax.ShapeDtypeStruct(features.shape, features.dtype),
        in_specs=[SMEM] + [ANY] * len(placed),
        out_specs=ANY,
        scratch_shapes=[
            pltpu.VMEM(features.shape, features.dtype),
            pltpu.SemaphoreType.DMA((5,)),
            pltpu.SemaphoreType.DMA((5,)),
        ],
        compiler_params=params,
    )(place, *placed)


def solution(mesh):
    return jax.shard_map(
        on_device,
        mesh=mesh,
        in_specs=(
            P(None, "node", None),
            P("layer", None, None),
            P(None, "node", None),
            P(None, "node", None, None),
            P(None, "node", None),
            P(None, "node", None),
            P(None, "node", None, None, None),
        ),
        out_specs=P(None, "node", "layer"),
        check_vma=False,
    )
```

time: 227 us -> 186 us (0.82)
  Pallas kernels: 36 us -> 15.7 us
  waiting for transfers between devices: 93.3 us -> 84.8 us
  starting transfers between devices: 85.4 us -> 78.9 us
  local copies, waits for them, and re-layouts: 9.17 us -> 4.86 us
    pallas_call x4, Pallas kernels: 30 us -> 12.8 us  [on_device(): pl.pallas_call(functools.partial(layer_kernel, layer_id, first, last), ou...]
    ppermute x24, waiting for transfers between devices: 35.9 us -> 20.6 us  [along(): return lax.ppermute(block, 'node', route)]
    unnamed x113 -> x20, local copies, waits for them, and re-layouts: 7.97 us -> 0.17 us
    ppermute x16 -> x17, waiting for transfers between devices: 2.14 us -> 7.89 us  [other_core(): return lax.ppermute(block, 'node', route)]
    squeeze x0 -> x4, local copies, waits for them, and re-layouts: none -> 3.64 us  [the longest x1 2.06 us: on_device(): lax.dynamic_index_in_dim(features, jnp.maximum(span - 1, 0), 0, keepdims=...]
    ppermute x16 -> x17, starting transfers between devices: 6.38 us -> 3.38 us  [other_core(): return lax.ppermute(block, 'node', route)]
    ppermute x23 -> x17, starting transfers between devices: 39.4 us -> 37.6 us  [to_plane(): return lax.ppermute(block, 'layer', pairs)]
    ppermute x23 -> x17, waiting for transfers between devices: 55.3 us -> 56.3 us  [to_plane(): return lax.ppermute(block, 'layer', pairs)]
  transfers between devices with their start and end apart: 63 -> 58, of which waited for: 26 -> 30; matrix products, arithmetic and copies ran while one was open for 2% -> 1% of each run, Pallas kernels for 6% -> 0%
where the time goes in v3:
time: 186 us
  waiting for transfers between devices  84.8 us (46%)
  starting transfers between devices  78.9 us (42%)
  Pallas kernels  15.7 us (8%)
  local copies, waits for them, and re-layouts  4.86 us (3%)
    ppermute x17, waiting for transfers between devices, to_plane(): return lax.ppermute(block, 'layer', pairs)  56.3 us
    ppermute x24, starting transfers between devices, along(): return lax.ppermute(block, 'node', route)  37.9 us
    ppermute x17, starting transfers between devices, to_plane(): return lax.ppermute(block, 'layer', pairs)  37.6 us
    ppermute x24, waiting for transfers between devices, along(): return lax.ppermute(block, 'node', route)  20.6 us
    pallas_call x4, Pallas kernels, on_device(): pl.pallas_call(functools.partial(layer_kernel, layer_id, first, last), ou...  12.8 us
    ppermute x17, waiting for transfers between devices, other_core(): return lax.ppermute(block, 'node', route)  7.89 us
  transfers between devices with their start and end apart: 58, of which 30 were waited for; matrix products, arithmetic and copies ran while one was open for 1% of the time, Pallas kernels for 0%

profile of v3, /device:TPU:6, one launch (start us, length us, event | category | flops | bytes accessed | tf_op | source)
XLA Modules:
  0.0 185.9 jit_solution(16320295286795267876)
XLA Ops:
  0.0 0.8 fusion.listed_ref
  0.8 0.7 dynamic-slice_bitcast_fusion.4.lists_ref
  1.6 2.1 %dynamic-slice_bitcast_fusion.1 = (bf16[512,512]{1,0:T(8,128)(2,1)}, bf16[512,512]{1,0:T(8,128)(2,1)S(1)}) fusion(bf16[4,512,512]{2,1,0:T(8,128)(2,1)} %param.7, s32[]{:T(128)S(6)} %max.3, s32[]{:T(128)S(6)} %select_n.21), kind=kLoop, calls=%fused_computation.2 | loop fusion | bytes 2097160 | tf_op jit(solution)/shard_map/jit(dynamic_index_in_dim)/squeeze | solution.py:210
  3.7 0.8 shard_map.73
  4.5 3.1 %collective-permute-start.2 = (bf16[144,512]{1,0:T(8,128)(2,1)S(1)}, bf16[144,512]{1,0:T(8,128)(2,1)S(1)}, u32[]{:S(2)}, u32[]{:S(2)}) collective-permute-start(bf16[144,512]{1,0:T(8,128)(2,1)S(1)} %shard_map.73), channel_id=1, source_target_pairs={{0,6},{1,25},{2,0},{3,27},{4,2},{5,29},{6,4},{7,31},{8,14},{9,1},{... | collective-permute-start | bytes 442376 | tf_op jit(solution)/shard_map/ppermute | solution.py:32
  8.2 1.0 collective-permute-start
  9.2 1.0 dynamic-slice_bitcast_fusion.3
  10.1 1.7 collective-permute-done.2
  11.8 2.6 %collective-permute-done.1 = bf16[144,512]{1,0:T(8,128)(2,1)} collective-permute-done((bf16[144,512]{1,0:T(8,128)(2,1)S(1)}, bf16[144,512]{1,0:T(8,128)(2,1)}, u32[]{:S(2)}, u32[]{:S(2)}) %collective-permute-start.1) | collective-permute-done | bytes 147488 | tf_op jit(solution)/shard_map/ppermute | solution.py:32
  14.4 1.5 collective-permute-done
  15.9 1.0 pad_maximum_fusion.rest_0_
  17.6 2.3 %collective-permute-start.4 = (bf16[256,512]{1,0:T(8,128)(2,1)S(1)}, bf16[256,512]{1,0:T(8,128)(2,1)S(1)}, u32[]{:S(2)}, u32[]{:S(2)}) collective-permute-start(bf16[256,512]{1,0:T(8,128)(2,1)S(1)} %dynamic-slice_bitcast_fusion.3), channel_id=1, source_target_pairs={{0,64},{32,96},{64,0},{96,32},{1,65},{33,97},{65,1},{97,33},{2,66}... | collective-permute-start | bytes 786440 | tf_op jit(solution)/shard_map/ppermute | solution.py:41
  19.9 2.0 %collective-permute-start.7 = (bf16[576,512]{1,0:T(8,128)(2,1)S(1)}, bf16[576,512]{1,0:T(8,128)(2,1)S(1)}, u32[]{:S(2)}, u32[]{:S(2)}) collective-permute-start(bf16[576,512]{1,0:T(8,128)(2,1)S(1)} %pad_maximum_fusion.rest_0_), channel_id=1, source_target_pairs={{0,8},{1,3},{2,10},{3,5},{4,12},{5,7},{6,14},{7,1},{8,16},{9,11},{... | collective-permute-start | bytes 1769480 | tf_op jit(solution)/shard_map/ppermute | solution.py:32
  21.9 3.6 %collective-permute-start.8 = (bf16[576,512]{1,0:T(8,128)(2,1)S(1)}, bf16[576,512]{1,0:T(8,128)(2,1)S(1)}, u32[]{:S(2)}, u32[]{:S(2)}) collective-permute-start(bf16[576,512]{1,0:T(8,128)(2,1)S(1)} %pad_maximum_fusion.rest_0_), channel_id=1, source_target_pairs={{0,16},{1,5},{2,18},{3,7},{4,20},{5,1},{6,22},{7,3},{8,24},{9,13},... | collective-permute-start | bytes 1769480 | tf_op jit(solution)/shard_map/ppermute | solution.py:32
  25.5 0.8 collective-permute-done.3
  26.2 1.9 %collective-permute-start.9 = (bf16[576,512]{1,0:T(8,128)(2,1)S(1)}, bf16[576,512]{1,0:T(8,128)(2,1)S(1)}, u32[]{:S(2)}, u32[]{:S(2)}) collective-permute-start(bf16[576,512]{1,0:T(8,128)(2,1)S(1)} %pad_maximum_fusion.rest_0_), channel_id=1, source_target_pairs={{0,24},{1,7},{2,26},{3,1},{4,28},{5,3},{6,30},{7,5},{8,0},{9,15},{... | collective-permute-start | bytes 1769480 | tf_op jit(solution)/shard_map/ppermute | solution.py:32
  28.4 3.7 %collective-permute-done.5 = bf16[256,512]{1,0:T(8,128)(2,1)S(1)} collective-permute-done((bf16[256,512]{1,0:T(8,128)(2,1)S(1)}, bf16[256,512]{1,0:T(8,128)(2,1)S(1)}, u32[]{:S(2)}, u32[]{:S(2)}) %collective-permute-start.5) | collective-permute-done | bytes 262176 | tf_op jit(solution)/shard_map/ppermute | solution.py:41
  32.8 6.8 %collective-permute-done.8.rest_2_ = bf16[576,512]{1,0:T(8,128)(2,1)S(1)} collective-permute-done((bf16[576,512]{1,0:T(8,128)(2,1)S(1)}, bf16[576,512]{1,0:T(8,128)(2,1)S(1)}, u32[]{:S(2)}, u32[]{:S(2)}) %collective-permute-start.8) | collective-permute-done | bytes 589856 | tf_op jit(solution)/shard_map/ppermute | solution.py:32
  40.3 1.4 collective-permute-done.12.rest_6_
  41.7 0.8 collective-permute-done.13.rest_7_
  42.5 5.2 %shard_map.74 = (bf16[512,512]{1,0:T(8,128)(2,1)S(1)}, bf16[128,512]{1,0:T(8,128)(2,1)S(1)}, bf16[20,128,256]{2,1,0:T(8,128)(2,1)S(1)}) custom-call(s32[2]{0:T(128)S(1)} %pad_add_fusion.place_ref, s32[4,4]{1,0:T(4,128)S(1)} %bitcast.16, s32[4,20]{1,0:T(4,128)S(1)} %bitcast.20, s32[1,128]{1,0:T(1,128)S(1)} %fusion.listed_ref, ...), custom_call_target="tpu_custom_call" | custom-call | tf_op jit(solution)/shard_map/pallas_call | solution.py:240
  47.9 2.0 %collective-permute-start.15 = (bf16[128,512]{1,0:T(8,128)(2,1)S(1)}, bf16[128,512]{1,0:T(8,128)(2,1)S(1)}, u32[]{:S(2)}, u32[]{:S(2)}) collective-permute-start(bf16[128,512]{1,0:T(8,128)(2,1)S(1)} %get-tuple-element.50), channel_id=1, source_target_pairs={{0,4},{1,17},{2,6},{3,19},{4,0},{5,21},{6,2},{7,23},{8,12},{9,25},... | collective-permute-start | bytes 393224 | tf_op jit(solution)/shard_map/ppermute | solution.py:32
  49.9 1.3 collective-permute-start.16
  51.2 3.2 %collective-permute-start.24 = (bf16[512,512]{1,0:T(8,128)(2,1)S(1)}, bf16[512,512]{1,0:T(8,128)(2,1)S(1)}, u32[]{:S(2)}, u32[]{:S(2)}) collective-permute-start(bf16[512,512]{1,0:T(8,128)(2,1)S(1)} %get-tuple-element.49.current_ref.refs_0_), channel_id=1, source_target_pairs={{0,32},{32,64},{64,96},{96,0},{1,33},{33,65},{65,97},{97,1},{2,34}... | collective-permute-start | bytes 1572872 | tf_op jit(solution)/shard_map/ppermute | solution.py:41
  55.5 0.9 collective-permute-done.16
  56.3 1.1 collective-permute-start.17
  57.4 1.8 collective-permute-start.18
  59.2 1.5 collective-permute-start.19
  60.7 16.6 %collective-permute-done.24.previous_ref.refs_1_ = bf16[512,512]{1,0:T(8,128)(2,1)S(1)} collective-permute-done((bf16[512,512]{1,0:T(8,128)(2,1)S(1)}, bf16[512,512]{1,0:T(8,128)(2,1)S(1)}, u32[]{:S(2)}, u32[]{:S(2)}) %collective-permute-start.24) | collective-permute-done | bytes 524320 | tf_op jit(solution)/shard_map/ppermute | solution.py:41
  79.2 0.9 collective-permute-done.20.rest_4_
  80.0 0.7 collective-permute-done.21.rest_5_
  80.8 0.7 collective-permute-done.22.rest_6_
  81.5 0.7 collective-permute-done.23.rest_7_
  82.3 2.6 %shard_map.75 = (bf16[512,512]{1,0:T(8,128)(2,1)S(1)}, bf16[128,512]{1,0:T(8,128)(2,1)S(1)}) custom-call(s32[2]{0:T(128)S(1)} %pad_add_fusion.place_ref, s32[4,4]{1,0:T(4,128)S(1)} %bitcast.17, s32[4,20]{1,0:T(4,128)S(1)} %bitcast.21, s32[1,128]{1,0:T(1,128)S(1)} %fusion.listed_ref, bf16[512,512]{1,0:T(8,128)(2,1)S(1)} %get-tuple-element.49.current_ref.refs_0_, ...), custom_call_target="tpu_custom_call" | custom-call | tf_op jit(solution)/shard_map/pallas_call | solution.py:240
  84.9 2.0 %collective-permute-start.28 = (bf16[128,512]{1,0:T(8,128)(2,1)S(1)}, bf16[128,512]{1,0:T(8,128)(2,1)S(1)}, u32[]{:S(2)}, u32[]{:S(2)}) collective-permute-start(bf16[128,512]{1,0:T(8,128)(2,1)S(1)} %get-tuple-element.64), channel_id=1, source_target_pairs={{0,4},{1,17},{2,6},{3,19},{4,0},{5,21},{6,2},{7,23},{8,12},{9,25},... | collective-permute-start | bytes 393224 | tf_op jit(solution)/shard_map/ppermute | solution.py:32
  86.9 1.3 collective-permute-start.29
  88.2 14.0 %collective-permute-start.37 = (bf16[512,512]{1,0:T(8,128)(2,1)S(1)}, bf16[512,512]{1,0:T(8,128)(2,1)S(1)}, u32[]{:S(2)}, u32[]{:S(2)}) collective-permute-start(bf16[512,512]{1,0:T(8,128)(2,1)S(1)} %get-tuple-element.63.current_ref.refs_4_), channel_id=1, source_target_pairs={{0,32},{32,64},{64,96},{96,0},{1,33},{33,65},{65,97},{97,1},{2,34}... | collective-permute-start | bytes 1572872 | tf_op jit(solution)/shard_map/ppermute | solution.py:41
  102.3 1.3 collective-permute-start.38
  103.8 2.2 %collective-permute-start.31 = (bf16[512,512]{1,0:T(8,128)(2,1)S(1)}, bf16[512,512]{1,0:T(8,128)(2,1)S(1)}, u32[]{:S(2)}, u32[]{:S(2)}) collective-permute-start(bf16[512,512]{1,0:T(8,128)(2,1)S(1)} %constant_dynamic-update-slice_fusion.8.rest_0_), channel_id=1, source_target_pairs={{0,16},{1,5},{2,18},{3,7},{4,20},{5,1},{6,22},{7,3},{8,24},{9,13},... | collective-permute-start | bytes 1572872 | tf_op jit(solution)/shard_map/ppermute | solution.py:32
  105.9 2.5 %collective-permute-start.32 = (bf16[512,512]{1,0:T(8,128)(2,1)S(1)}, bf16[512,512]{1,0:T(8,128)(2,1)S(1)}, u32[]{:S(2)}, u32[]{:S(2)}) collective-permute-start(bf16[512,512]{1,0:T(8,128)(2,1)S(1)} %constant_dynamic-update-slice_fusion.8.rest_0_), channel_id=1, source_target_pairs={{0,24},{1,7},{2,26},{3,1},{4,28},{5,3},{6,30},{7,5},{8,0},{9,15},{... | collective-permute-start | bytes 1572872 | tf_op jit(solution)/shard_map/ppermute | solution.py:32
  108.5 4.7 %collective-permute-done.37.previous_ref.refs_5_ = bf16[512,512]{1,0:T(8,128)(2,1)S(1)} collective-permute-done((bf16[512,512]{1,0:T(8,128)(2,1)S(1)}, bf16[512,512]{1,0:T(8,128)(2,1)S(1)}, u32[]{:S(2)}, u32[]{:S(2)}) %collective-permute-start.37) | collective-permute-done | bytes 524320 | tf_op jit(solution)/shard_map/ppermute | solution.py:41
  114.4 5.4 %collective-permute-done.30.rest_1_ = bf16[512,512]{1,0:T(8,128)(2,1)S(1)} collective-permute-done((bf16[512,512]{1,0:T(8,128)(2,1)S(1)}, bf16[512,512]{1,0:T(8,128)(2,1)S(1)}, u32[]{:S(2)}, u32[]{:S(2)}) %collective-permute-start.30) | collective-permute-done | bytes 524320 | tf_op jit(solution)/shard_map/ppermute | solution.py:32
  120.7 1.0 collective-permute-done.34.rest_5_
  121.7 0.7 collective-permute-done.35.rest_6_
  122.4 0.7 collective-permute-done.36.rest_7_
  123.2 2.6 %shard_map.76 = (bf16[512,512]{1,0:T(8,128)(2,1)S(1)}, bf16[128,512]{1,0:T(8,128)(2,1)S(1)}) custom-call(s32[2]{0:T(128)S(1)} %pad_add_fusion.place_ref, s32[4,4]{1,0:T(4,128)S(1)} %bitcast.18, s32[4,20]{1,0:T(4,128)S(1)} %bitcast.22, s32[1,128]{1,0:T(1,128)S(1)} %fusion.listed_ref, bf16[512,512]{1,0:T(8,128)(2,1)S(1)} %get-tuple-element.63.current_ref.refs_4_, ...), custom_call_target="tpu_custom_call" | custom-call | tf_op jit(solution)/shard_map/pallas_call | solution.py:240
  125.7 1.0 collective-permute-start.40
  126.7 2.1 %collective-permute-start.41 = (bf16[128,512]{1,0:T(8,128)(2,1)S(1)}, bf16[128,512]{1,0:T(8,128)(2,1)S(1)}, u32[]{:S(2)}, u32[]{:S(2)}) collective-permute-start(bf16[128,512]{1,0:T(8,128)(2,1)S(1)} %get-tuple-element.77), channel_id=1, source_target_pairs={{0,4},{1,17},{2,6},{3,19},{4,0},{5,21},{6,2},{7,23},{8,12},{9,25},... | collective-permute-start | bytes 393224 | tf_op jit(solution)/shard_map/ppermute | solution.py:32
  128.8 2.6 %collective-permute-start.42 = (bf16[128,512]{1,0:T(8,128)(2,1)S(1)}, bf16[128,512]{1,0:T(8,128)(2,1)S(1)}, u32[]{:S(2)}, u32[]{:S(2)}) collective-permute-start(bf16[128,512]{1,0:T(8,128)(2,1)S(1)} %get-tuple-element.77), channel_id=1, source_target_pairs={{0,6},{1,25},{2,0},{3,27},{4,2},{5,29},{6,4},{7,31},{8,14},{9,1},{... | collective-permute-start | bytes 393224 | tf_op jit(solution)/shard_map/ppermute | solution.py:32
  131.4 2.2 %collective-permute-start.50 = (bf16[512,512]{1,0:T(8,128)(2,1)S(1)}, bf16[512,512]{1,0:T(8,128)(2,1)S(1)}, u32[]{:S(2)}, u32[]{:S(2)}) collective-permute-start(bf16[512,512]{1,0:T(8,128)(2,1)S(1)} %get-tuple-element.76.current_ref.refs_8_), channel_id=1, source_target_pairs={{0,32},{32,64},{64,96},{96,0},{1,33},{33,65},{65,97},{97,1},{2,34}... | collective-permute-start | bytes 1572872 | tf_op jit(solution)/shard_map/ppermute | solution.py:41
  134.4 0.9 collective-permute-start.43
  135.3 2.7 %collective-permute-start.44 = (bf16[512,512]{1,0:T(8,128)(2,1)S(1)}, bf16[512,512]{1,0:T(8,128)(2,1)S(1)}, u32[]{:S(2)}, u32[]{:S(2)}) collective-permute-start(bf16[512,512]{1,0:T(8,128)(2,1)S(1)} %constant_dynamic-update-slice_fusion.12.rest_0_), channel_id=1, source_target_pairs={{0,16},{1,5},{2,18},{3,7},{4,20},{5,1},{6,22},{7,3},{8,24},{9,13},... | collective-permute-start | bytes 1572872 | tf_op jit(solution)/shard_map/ppermute | solution.py:32
  138.6 5.8 %collective-permute-done.50.previous_ref.refs_9_ = bf16[512,512]{1,0:T(8,128)(2,1)S(1)} collective-permute-done((bf16[512,512]{1,0:T(8,128)(2,1)S(1)}, bf16[512,512]{1,0:T(8,128)(2,1)S(1)}, u32[]{:S(2)}, u32[]{:S(2)}) %collective-permute-start.50) | collective-permute-done | bytes 524320 | tf_op jit(solution)/shard_map/ppermute | solution.py:41
  144.4 5.3 %collective-permute-start.52 = (bf16[512,512]{1,0:T(8,128)(2,1)S(1)}, bf16[512,512]{1,0:T(8,128)(2,1)S(1)}, u32[]{:S(2)}, u32[]{:S(2)}) collective-permute-start(bf16[512,512]{1,0:T(8,128)(2,1)S(1)} %get-tuple-element.76.current_ref.refs_8_), channel_id=1, source_target_pairs={{96,64},{97,65},{98,66},{99,67},{100,68},{101,69},{102,70},{103,71... | collective-permute-start | bytes 1572872 | tf_op jit(solution)/shard_map/ppermute | solution.py:41
  151.4 5.0 %collective-permute-done.52.refs_11_ = bf16[512,512]{1,0:T(8,128)(2,1)S(1)} collective-permute-done((bf16[512,512]{1,0:T(8,128)(2,1)S(1)}, bf16[512,512]{1,0:T(8,128)(2,1)S(1)}, u32[]{:S(2)}, u32[]{:S(2)}) %collective-permute-start.52) | collective-permute-done | bytes 524320 | tf_op jit(solution)/shard_map/ppermute | solution.py:41
  156.4 2.4 %shard_map.77.refs_12_ = bf16[512,512]{1,0:T(8,128)(2,1)S(1)} custom-call(s32[2]{0:T(128)S(1)} %pad_add_fusion.place_ref, s32[4,4]{1,0:T(4,128)S(1)} %bitcast.19, s32[4,20]{1,0:T(4,128)S(1)} %bitcast.23, s32[1,128]{1,0:T(1,128)S(1)} %fusion.listed_ref, bf16[512,512]{1,0:T(8,128)(2,1)S(1)} %get-tuple-element.76.current_ref.refs_8_, ...), custom_call_target="tpu_custom_call" | custom-call | tf_op jit(solution)/shard_map/pallas_call | solution.py:240
  158.8 1.3 collective-permute-start.53
  160.1 1.3 collective-permute-start.57
  162.1 1.3 collective-permute-start.56
  163.4 1.3 collective-permute-start.55
  164.7 13.3 %collective-permute-done.56.refs_15_ = bf16[256,512]{1,0:T(8,128)(2,1)S(1)} collective-permute-done((bf16[256,512]{1,0:T(8,128)(2,1)S(1)}, bf16[256,512]{1,0:T(8,128)(2,1)S(1)}, u32[]{:S(2)}, u32[]{:S(2)}) %collective-permute-start.56) | collective-permute-done | bytes 262176 | tf_op jit(solution)/shard_map/ppermute | solution.py:41
  178.1 4.8 %collective-permute-done.57.refs_16_ = bf16[512,512]{1,0:T(8,128)(2,1)S(1)} collective-permute-done((bf16[512,512]{1,0:T(8,128)(2,1)S(1)}, bf16[512,512]{1,0:T(8,128)(2,1)S(1)}, u32[]{:S(2)}, u32[]{:S(2)}) %collective-permute-start.57) | collective-permute-done | bytes 524320 | tf_op jit(solution)/shard_map/ppermute | solution.py:41
  182.8 0.8 collective-permute-done.55.refs_14_
  183.6 2.1 %shard_map.78 = bf16[4,512,512]{2,1,0:T(8,128)(2,1)} custom-call(s32[2]{0:T(128)S(1)} %pad_add_fusion.place_ref, bf16[512,512]{1,0:T(8,128)(2,1)S(1)} %get-tuple-element.49.current_ref.refs_0_, bf16[512,512]{1,0:T(8,128)(2,1)S(1)} %collective-permute-done.24.previous_ref.refs_1_, bf16[512,512]{1,0:T(8,128)(2,1)S(1)} %collective-permute-done.25.refs_2_, ...), custom_call_target="tpu_custom_call" | custom-call | tf_op jit(solution)/shard_map/pallas_call | solution.py:270
  (90 shorter events, 11.9 us)
Async XLA Ops:
  0.0 40.2 %copy-start = (bf16[4,1,20,128,128]{4,3,2,1,0:T(8,128)(2,1)S(1)}, bf16[4,1,20,128,128]{4,3,2,1,0:T(8,128)(2,1)}, u32[]{:S(2)}) copy-start(bf16[4,1,20,128,128]{4,3,2,1,0:T(8,128)(2,1)} %param.13) | copy-start | bytes 7864324
  4.5 7.4 %collective-permute-start.2 = (bf16[144,512]{1,0:T(8,128)(2,1)S(1)}, bf16[144,512]{1,0:T(8,128)(2,1)S(1)}, u32[]{:S(2)}, u32[]{:S(2)}) collective-permute-start(bf16[144,512]{1,0:T(8,128)(2,1)S(1)} %shard_map.73), channel_id=1, source_target_pairs={{0,6},{1,25},{2,0},{3,27},{4,2},{5,29},{6,4},{7,31},{8,14},{9,1},{... | collective-permute-start | bytes 442376 | tf_op jit(solution)/shard_map/ppermute | solution.py:32
  7.6 6.9 %collective-permute-start.1 = (bf16[144,512]{1,0:T(8,128)(2,1)S(1)}, bf16[144,512]{1,0:T(8,128)(2,1)}, u32[]{:S(2)}, u32[]{:S(2)}) collective-permute-start(bf16[144,512]{1,0:T(8,128)(2,1)S(1)} %shard_map.73), channel_id=1, source_target_pairs={{0,4},{1,17},{2,6},{3,19},{4,0},{5,21},{6,2},{7,23},{8,12},{9,25},... | collective-permute-start | bytes 442376 | tf_op jit(solution)/shard_map/ppermute | solution.py:32
  8.2 7.7 %collective-permute-start = (bf16[144,512]{1,0:T(8,128)(2,1)S(1)}, bf16[144,512]{1,0:T(8,128)(2,1)}, u32[]{:S(2)}, u32[]{:S(2)}) collective-permute-start(bf16[144,512]{1,0:T(8,128)(2,1)S(1)} %shard_map.73), channel_id=1, source_target_pairs={{0,2},{1,9},{2,4},{3,11},{4,6},{5,13},{6,0},{7,15},{8,10},{9,17},{... | collective-permute-start | bytes 442376 | tf_op jit(solution)/shard_map/ppermute | solution.py:32
  16.9 9.3 %collective-permute-start.3 = (bf16[256,512]{1,0:T(8,128)(2,1)S(1)}, bf16[256,512]{1,0:T(8,128)(2,1)S(1)}, u32[]{:S(2)}, u32[]{:S(2)}) collective-permute-start(bf16[256,512]{1,0:T(8,128)(2,1)S(1)} %dynamic-slice_bitcast_fusion.3), channel_id=1, source_target_pairs={{0,32},{32,64},{64,96},{96,0},{1,33},{33,65},{65,97},{97,1},{2,34}... | collective-permute-start | bytes 786440 | tf_op jit(solution)/shard_map/ppermute | solution.py:41
  17.6 10.8 %collective-permute-start.4 = (bf16[256,512]{1,0:T(8,128)(2,1)S(1)}, bf16[256,512]{1,0:T(8,128)(2,1)S(1)}, u32[]{:S(2)}, u32[]{:S(2)}) collective-permute-start(bf16[256,512]{1,0:T(8,128)(2,1)S(1)} %dynamic-slice_bitcast_fusion.3), channel_id=1, source_target_pairs={{0,64},{32,96},{64,0},{96,32},{1,65},{33,97},{65,1},{97,33},{2,66}... | collective-permute-start | bytes 786440 | tf_op jit(solution)/shard_map/ppermute | solution.py:41
  19.9 12.2 %collective-permute-start.5 = (bf16[256,512]{1,0:T(8,128)(2,1)S(1)}, bf16[256,512]{1,0:T(8,128)(2,1)S(1)}, u32[]{:S(2)}, u32[]{:S(2)}) collective-permute-start(bf16[256,512]{1,0:T(8,128)(2,1)S(1)} %dynamic-slice_bitcast_fusion.3), channel_id=1, source_target_pairs={{0,96},{32,0},{64,32},{96,64},{1,97},{33,1},{65,33},{97,65},{2,98}... | collective-permute-start | bytes 786440 | tf_op jit(solution)/shard_map/ppermute | solution.py:41
  19.9 12.8 %collective-permute-start.7 = (bf16[576,512]{1,0:T(8,128)(2,1)S(1)}, bf16[576,512]{1,0:T(8,128)(2,1)S(1)}, u32[]{:S(2)}, u32[]{:S(2)}) collective-permute-start(bf16[576,512]{1,0:T(8,128)(2,1)S(1)} %pad_maximum_fusion.rest_0_), channel_id=1, source_target_pairs={{0,8},{1,3},{2,10},{3,5},{4,12},{5,7},{6,14},{7,1},{8,16},{9,11},{... | collective-permute-start | bytes 1769480 | tf_op jit(solution)/shard_map/ppermute | solution.py:32
  21.9 17.8 %collective-permute-start.8 = (bf16[576,512]{1,0:T(8,128)(2,1)S(1)}, bf16[576,512]{1,0:T(8,128)(2,1)S(1)}, u32[]{:S(2)}, u32[]{:S(2)}) collective-permute-start(bf16[576,512]{1,0:T(8,128)(2,1)S(1)} %pad_maximum_fusion.rest_0_), channel_id=1, source_target_pairs={{0,16},{1,5},{2,18},{3,7},{4,20},{5,1},{6,22},{7,3},{8,24},{9,13},... | collective-permute-start | bytes 1769480 | tf_op jit(solution)/shard_map/ppermute | solution.py:32
  26.2 13.4 %collective-permute-start.9 = (bf16[576,512]{1,0:T(8,128)(2,1)S(1)}, bf16[576,512]{1,0:T(8,128)(2,1)S(1)}, u32[]{:S(2)}, u32[]{:S(2)}) collective-permute-start(bf16[576,512]{1,0:T(8,128)(2,1)S(1)} %pad_maximum_fusion.rest_0_), channel_id=1, source_target_pairs={{0,24},{1,7},{2,26},{3,1},{4,28},{5,3},{6,30},{7,5},{8,0},{9,15},{... | collective-permute-start | bytes 1769480 | tf_op jit(solution)/shard_map/ppermute | solution.py:32
  28.1 14.4 %copy-start.1 = (bf16[512,512]{1,0:T(8,128)(2,1)S(1)}, bf16[512,512]{1,0:T(8,128)(2,1)}, u32[]{:S(2)}) copy-start(bf16[512,512]{1,0:T(8,128)(2,1)} %get-tuple-element.89.previous_ref) | copy-start | bytes 1572868
  28.1 14.4 %copy-start.2 = (s32[4,1,4]{2,1,0:T(1,128)S(1)}, s32[4,1,4]{2,1,0:T(1,128)}, u32[]{:S(2)}) copy-start(s32[4,1,4]{2,1,0:T(1,128)} %param.11) | copy-start | bytes 196
  28.2 14.4 %copy-start.3 = (s32[4,1,20]{2,1,0:T(1,128)S(1)}, s32[4,1,20]{2,1,0:T(1,128)}, u32[]{:S(2)}) copy-start(s32[4,1,20]{2,1,0:T(1,128)} %param.12) | copy-start | bytes 964
  32.2 10.4 %collective-permute-start.6 = (bf16[1024,512]{1,0:T(8,128)(2,1)S(1)}, bf16[1024,512]{1,0:T(8,128)(2,1)S(1)}, u32[]{:S(2)}, u32[]{:S(2)}) collective-permute-start(bf16[1024,512]{1,0:T(8,128)(2,1)S(1)} %constant_dynamic-update-slice_fusion.halves_ref), channel_id=1, source_target_pairs={{0,1},{1,0},{2,3},{3,2},{4,5},{5,4},{6,7},{7,6},{8,9},{9,8},{10,11... | collective-permute-start | bytes 3145736 | tf_op jit(solution)/shard_map/ppermute | solution.py:37
  32.2 8.0 %collective-permute-start.10 = (bf16[576,512]{1,0:T(8,128)(2,1)S(1)}, bf16[576,512]{1,0:T(8,128)(2,1)S(1)}, u32[]{:S(2)}, u32[]{:S(2)}) collective-permute-start(bf16[576,512]{1,0:T(8,128)(2,1)S(1)} %pad_maximum_fusion.rest_0_), channel_id=1, source_target_pairs={{0,1},{1,0},{2,3},{3,2},{4,5},{5,4},{6,7},{7,6},{8,9},{9,8},{10,11... | collective-permute-start | bytes 1769480 | tf_op jit(solution)/shard_map/ppermute | solution.py:37
  32.7 7.5 %collective-permute-start.11 = (bf16[576,512]{1,0:T(8,128)(2,1)S(1)}, bf16[576,512]{1,0:T(8,128)(2,1)S(1)}, u32[]{:S(2)}, u32[]{:S(2)}) collective-permute-start(bf16[576,512]{1,0:T(8,128)(2,1)S(1)} %collective-permute-done.7.rest_1_), channel_id=1, source_target_pairs={{0,1},{1,0},{2,3},{3,2},{4,5},{5,4},{6,7},{7,6},{8,9},{9,8},{10,11... | collective-permute-start | bytes 1769480 | tf_op jit(solution)/shard_map/ppermute | solution.py:37
  39.7 2.0 %collective-permute-start.12 = (bf16[576,512]{1,0:T(8,128)(2,1)S(1)}, bf16[576,512]{1,0:T(8,128)(2,1)S(1)}, u32[]{:S(2)}, u32[]{:S(2)}) collective-permute-start(bf16[576,512]{1,0:T(8,128)(2,1)S(1)} %collective-permute-done.8.rest_2_), channel_id=1, source_target_pairs={{0,1},{1,0},{2,3},{3,2},{4,5},{5,4},{6,7},{7,6},{8,9},{9,8},{10,11... | collective-permute-start | bytes 1769480 | tf_op jit(solution)/shard_map/ppermute | solution.py:37
  39.7 2.8 %collective-permute-start.13 = (bf16[576,512]{1,0:T(8,128)(2,1)S(1)}, bf16[576,512]{1,0:T(8,128)(2,1)S(1)}, u32[]{:S(2)}, u32[]{:S(2)}) collective-permute-start(bf16[576,512]{1,0:T(8,128)(2,1)S(1)} %collective-permute-done.9.rest_3_), channel_id=1, source_target_pairs={{0,1},{1,0},{2,3},{3,2},{4,5},{5,4},{6,7},{7,6},{8,9},{9,8},{10,11... | collective-permute-start | bytes 1769480 | tf_op jit(solution)/shard_map/ppermute | solution.py:37
  47.8 7.7 %collective-permute-start.14 = (bf16[128,512]{1,0:T(8,128)(2,1)S(1)}, bf16[128,512]{1,0:T(8,128)(2,1)S(1)}, u32[]{:S(2)}, u32[]{:S(2)}) collective-permute-start(bf16[128,512]{1,0:T(8,128)(2,1)S(1)} %get-tuple-element.50), channel_id=1, source_target_pairs={{0,2},{1,9},{2,4},{3,11},{4,6},{5,13},{6,0},{7,15},{8,10},{9,17},{... | collective-permute-start | bytes 393224 | tf_op jit(solution)/shard_map/ppermute | solution.py:32
  47.9 7.6 %collective-permute-start.15 = (bf16[128,512]{1,0:T(8,128)(2,1)S(1)}, bf16[128,512]{1,0:T(8,128)(2,1)S(1)}, u32[]{:S(2)}, u32[]{:S(2)}) collective-permute-start(bf16[128,512]{1,0:T(8,128)(2,1)S(1)} %get-tuple-element.50), channel_id=1, source_target_pairs={{0,4},{1,17},{2,6},{3,19},{4,0},{5,21},{6,2},{7,23},{8,12},{9,25},... | collective-permute-start | bytes 393224 | tf_op jit(solution)/shard_map/ppermute | solution.py:32
  49.9 6.4 %collective-permute-start.16 = (bf16[128,512]{1,0:T(8,128)(2,1)S(1)}, bf16[128,512]{1,0:T(8,128)(2,1)S(1)}, u32[]{:S(2)}, u32[]{:S(2)}) collective-permute-start(bf16[128,512]{1,0:T(8,128)(2,1)S(1)} %get-tuple-element.50), channel_id=1, source_target_pairs={{0,6},{1,25},{2,0},{3,27},{4,2},{5,29},{6,4},{7,31},{8,14},{9,1},{... | collective-permute-start | bytes 393224 | tf_op jit(solution)/shard_map/ppermute | solution.py:32
  51.2 26.2 %collective-permute-start.24 = (bf16[512,512]{1,0:T(8,128)(2,1)S(1)}, bf16[512,512]{1,0:T(8,128)(2,1)S(1)}, u32[]{:S(2)}, u32[]{:S(2)}) collective-permute-start(bf16[512,512]{1,0:T(8,128)(2,1)S(1)} %get-tuple-element.49.current_ref.refs_0_), channel_id=1, source_target_pairs={{0,32},{32,64},{64,96},{96,0},{1,33},{33,65},{65,97},{97,1},{2,34}... | collective-permute-start | bytes 1572872 | tf_op jit(solution)/shard_map/ppermute | solution.py:41
  54.4 23.6 %collective-permute-start.25 = (bf16[512,512]{1,0:T(8,128)(2,1)S(1)}, bf16[512,512]{1,0:T(8,128)(2,1)S(1)}, u32[]{:S(2)}, u32[]{:S(2)}) collective-permute-start(bf16[512,512]{1,0:T(8,128)(2,1)S(1)} %get-tuple-element.49.current_ref.refs_0_), channel_id=1, source_target_pairs={{64,0},{65,1},{66,2},{67,3},{68,4},{69,5},{70,6},{71,7},{72,8},{73... | collective-permute-start | bytes 1572872 | tf_op jit(solution)/shard_map/ppermute | solution.py:41
  56.3 21.8 %collective-permute-start.17 = (bf16[512,512]{1,0:T(8,128)(2,1)S(1)}, bf16[512,512]{1,0:T(8,128)(2,1)S(1)}, u32[]{:S(2)}, u32[]{:S(2)}) collective-permute-start(bf16[512,512]{1,0:T(8,128)(2,1)S(1)} %constant_dynamic-update-slice_fusion.4.rest_0_), channel_id=1, source_target_pairs={{0,8},{1,3},{2,10},{3,5},{4,12},{5,7},{6,14},{7,1},{8,16},{9,11},{... | collective-permute-start | bytes 1572872 | tf_op jit(solution)/shard_map/ppermute | solution.py:32
  57.4 21.2 %collective-permute-start.18 = (bf16[512,512]{1,0:T(8,128)(2,1)S(1)}, bf16[512,512]{1,0:T(8,128)(2,1)S(1)}, u32[]{:S(2)}, u32[]{:S(2)}) collective-permute-start(bf16[512,512]{1,0:T(8,128)(2,1)S(1)} %constant_dynamic-update-slice_fusion.4.rest_0_), channel_id=1, source_target_pairs={{0,16},{1,5},{2,18},{3,7},{4,20},{5,1},{6,22},{7,3},{8,24},{9,13},... | collective-permute-start | bytes 1572872 | tf_op jit(solution)/shard_map/ppermute | solution.py:32
  59.2 19.5 %collective-permute-start.19 = (bf16[512,512]{1,0:T(8,128)(2,1)S(1)}, bf16[512,512]{1,0:T(8,128)(2,1)S(1)}, u32[]{:S(2)}, u32[]{:S(2)}) collective-permute-start(bf16[512,512]{1,0:T(8,128)(2,1)S(1)} %constant_dynamic-update-slice_fusion.4.rest_0_), channel_id=1, source_target_pairs={{0,24},{1,7},{2,26},{3,1},{4,28},{5,3},{6,30},{7,5},{8,0},{9,15},{... | collective-permute-start | bytes 1572872 | tf_op jit(solution)/shard_map/ppermute | solution.py:32
  77.3 1.8 collective-permute-start.26
  78.0 2.0 %collective-permute-start.20 = (bf16[512,512]{1,0:T(8,128)(2,1)S(1)}, bf16[512,512]{1,0:T(8,128)(2,1)S(1)}, u32[]{:S(2)}, u32[]{:S(2)}) collective-permute-start(bf16[512,512]{1,0:T(8,128)(2,1)S(1)} %constant_dynamic-update-slice_fusion.4.rest_0_), channel_id=1, source_target_pairs={{0,1},{1,0},{2,3},{3,2},{4,5},{5,4},{6,7},{7,6},{8,9},{9,8},{10,11... | collective-permute-start | bytes 1572872 | tf_op jit(solution)/shard_map/ppermute | solution.py:37
  78.1 2.6 %collective-permute-start.21 = (bf16[512,512]{1,0:T(8,128)(2,1)S(1)}, bf16[512,512]{1,0:T(8,128)(2,1)S(1)}, u32[]{:S(2)}, u32[]{:S(2)}) collective-permute-start(bf16[512,512]{1,0:T(8,128)(2,1)S(1)} %collective-permute-done.17.rest_1_), channel_id=1, source_target_pairs={{0,1},{1,0},{2,3},{3,2},{4,5},{5,4},{6,7},{7,6},{8,9},{9,8},{10,11... | collective-permute-start | bytes 1572872 | tf_op jit(solution)/shard_map/ppermute | solution.py:37
  78.6 2.9 %collective-permute-start.22 = (bf16[512,512]{1,0:T(8,128)(2,1)S(1)}, bf16[512,512]{1,0:T(8,128)(2,1)S(1)}, u32[]{:S(2)}, u32[]{:S(2)}) collective-permute-start(bf16[512,512]{1,0:T(8,128)(2,1)S(1)} %collective-permute-done.18.rest_2_), channel_id=1, source_target_pairs={{0,1},{1,0},{2,3},{3,2},{4,5},{5,4},{6,7},{7,6},{8,9},{9,8},{10,11... | collective-permute-start | bytes 1572872 | tf_op jit(solution)/shard_map/ppermute | solution.py:37
  78.7 3.5 %collective-permute-start.23 = (bf16[512,512]{1,0:T(8,128)(2,1)S(1)}, bf16[512,512]{1,0:T(8,128)(2,1)S(1)}, u32[]{:S(2)}, u32[]{:S(2)}) collective-permute-start(bf16[512,512]{1,0:T(8,128)(2,1)S(1)} %collective-permute-done.19.rest_3_), channel_id=1, source_target_pairs={{0,1},{1,0},{2,3},{3,2},{4,5},{5,4},{6,7},{7,6},{8,9},{9,8},{10,11... | collective-permute-start | bytes 1572872 | tf_op jit(solution)/shard_map/ppermute | solution.py:37
  84.8 18.7 %collective-permute-start.27 = (bf16[128,512]{1,0:T(8,128)(2,1)S(1)}, bf16[128,512]{1,0:T(8,128)(2,1)S(1)}, u32[]{:S(2)}, u32[]{:S(2)}) collective-permute-start(bf16[128,512]{1,0:T(8,128)(2,1)S(1)} %get-tuple-element.64), channel_id=1, source_target_pairs={{0,2},{1,9},{2,4},{3,11},{4,6},{5,13},{6,0},{7,15},{8,10},{9,17},{... | collective-permute-start | bytes 393224 | tf_op jit(solution)/shard_map/ppermute | solution.py:32
  84.9 18.7 %collective-permute-start.28 = (bf16[128,512]{1,0:T(8,128)(2,1)S(1)}, bf16[128,512]{1,0:T(8,128)(2,1)S(1)}, u32[]{:S(2)}, u32[]{:S(2)}) collective-permute-start(bf16[128,512]{1,0:T(8,128)(2,1)S(1)} %get-tuple-element.64), channel_id=1, source_target_pairs={{0,4},{1,17},{2,6},{3,19},{4,0},{5,21},{6,2},{7,23},{8,12},{9,25},... | collective-permute-start | bytes 393224 | tf_op jit(solution)/shard_map/ppermute | solution.py:32
  86.9 16.7 %collective-permute-start.29 = (bf16[128,512]{1,0:T(8,128)(2,1)S(1)}, bf16[128,512]{1,0:T(8,128)(2,1)S(1)}, u32[]{:S(2)}, u32[]{:S(2)}) collective-permute-start(bf16[128,512]{1,0:T(8,128)(2,1)S(1)} %get-tuple-element.64), channel_id=1, source_target_pairs={{0,6},{1,25},{2,0},{3,27},{4,2},{5,29},{6,4},{7,31},{8,14},{9,1},{... | collective-permute-start | bytes 393224 | tf_op jit(solution)/shard_map/ppermute | solution.py:32
  88.2 24.9 %collective-permute-start.37 = (bf16[512,512]{1,0:T(8,128)(2,1)S(1)}, bf16[512,512]{1,0:T(8,128)(2,1)S(1)}, u32[]{:S(2)}, u32[]{:S(2)}) collective-permute-start(bf16[512,512]{1,0:T(8,128)(2,1)S(1)} %get-tuple-element.63.current_ref.refs_4_), channel_id=1, source_target_pairs={{0,32},{32,64},{64,96},{96,0},{1,33},{33,65},{65,97},{97,1},{2,34}... | collective-permute-start | bytes 1572872 | tf_op jit(solution)/shard_map/ppermute | solution.py:41
  102.3 12.1 %collective-permute-start.38 = (bf16[512,512]{1,0:T(8,128)(2,1)S(1)}, bf16[512,512]{1,0:T(8,128)(2,1)S(1)}, u32[]{:S(2)}, u32[]{:S(2)}) collective-permute-start(bf16[512,512]{1,0:T(8,128)(2,1)S(1)} %get-tuple-element.63.current_ref.refs_4_), channel_id=1, source_target_pairs={{96,32},{97,33},{98,34},{99,35},{100,36},{101,37},{102,38},{103,39... | collective-permute-start | bytes 1572872 | tf_op jit(solution)/shard_map/ppermute | solution.py:41
  103.7 16.1 %collective-permute-start.30 = (bf16[512,512]{1,0:T(8,128)(2,1)S(1)}, bf16[512,512]{1,0:T(8,128)(2,1)S(1)}, u32[]{:S(2)}, u32[]{:S(2)}) collective-permute-start(bf16[512,512]{1,0:T(8,128)(2,1)S(1)} %constant_dynamic-update-slice_fusion.8.rest_0_), channel_id=1, source_target_pairs={{0,8},{1,3},{2,10},{3,5},{4,12},{5,7},{6,14},{7,1},{8,16},{9,11},{... | collective-permute-start | bytes 1572872 | tf_op jit(solution)/shard_map/ppermute | solution.py:32
  103.8 16.0 %collective-permute-start.31 = (bf16[512,512]{1,0:T(8,128)(2,1)S(1)}, bf16[512,512]{1,0:T(8,128)(2,1)S(1)}, u32[]{:S(2)}, u32[]{:S(2)}) collective-permute-start(bf16[512,512]{1,0:T(8,128)(2,1)S(1)} %constant_dynamic-update-slice_fusion.8.rest_0_), channel_id=1, source_target_pairs={{0,16},{1,5},{2,18},{3,7},{4,20},{5,1},{6,22},{7,3},{8,24},{9,13},... | collective-permute-start | bytes 1572872 | tf_op jit(solution)/shard_map/ppermute | solution.py:32
  105.9 14.7 %collective-permute-start.32 = (bf16[512,512]{1,0:T(8,128)(2,1)S(1)}, bf16[512,512]{1,0:T(8,128)(2,1)S(1)}, u32[]{:S(2)}, u32[]{:S(2)}) collective-permute-start(bf16[512,512]{1,0:T(8,128)(2,1)S(1)} %constant_dynamic-update-slice_fusion.8.rest_0_), channel_id=1, source_target_pairs={{0,24},{1,7},{2,26},{3,1},{4,28},{5,3},{6,30},{7,5},{8,0},{9,15},{... | collective-permute-start | bytes 1572872 | tf_op jit(solution)/shard_map/ppermute | solution.py:32
  113.1 7.6 %collective-permute-start.39 = (bf16[512,512]{1,0:T(8,128)(2,1)S(1)}, bf16[512,512]{1,0:T(8,128)(2,1)S(1)}, u32[]{:S(2)}, u32[]{:S(2)}) collective-permute-start(bf16[512,512]{1,0:T(8,128)(2,1)S(1)} %get-tuple-element.63.current_ref.refs_4_), channel_id=1, source_target_pairs={{64,32},{65,33},{66,34},{67,35},{68,36},{69,37},{70,38},{71,39},{7... | collective-permute-start | bytes 1572872 | tf_op jit(solution)/shard_map/ppermute | solution.py:41
  114.4 6.3 %collective-permute-start.33 = (bf16[512,512]{1,0:T(8,128)(2,1)S(1)}, bf16[512,512]{1,0:T(8,128)(2,1)S(1)}, u32[]{:S(2)}, u32[]{:S(2)}) collective-permute-start(bf16[512,512]{1,0:T(8,128)(2,1)S(1)} %constant_dynamic-update-slice_fusion.8.rest_0_), channel_id=1, source_target_pairs={{0,1},{1,0},{2,3},{3,2},{4,5},{5,4},{6,7},{7,6},{8,9},{9,8},{10,11... | collective-permute-start | bytes 1572872 | tf_op jit(solution)/shard_map/ppermute | solution.py:37
  119.8 1.9 %collective-permute-start.34 = (bf16[512,512]{1,0:T(8,128)(2,1)S(1)}, bf16[512,512]{1,0:T(8,128)(2,1)S(1)}, u32[]{:S(2)}, u32[]{:S(2)}) collective-permute-start(bf16[512,512]{1,0:T(8,128)(2,1)S(1)} %collective-permute-done.30.rest_1_), channel_id=1, source_target_pairs={{0,1},{1,0},{2,3},{3,2},{4,5},{5,4},{6,7},{7,6},{8,9},{9,8},{10,11... | collective-permute-start | bytes 1572872 | tf_op jit(solution)/shard_map/ppermute | solution.py:37
  119.8 2.7 %collective-permute-start.35 = (bf16[512,512]{1,0:T(8,128)(2,1)S(1)}, bf16[512,512]{1,0:T(8,128)(2,1)S(1)}, u32[]{:S(2)}, u32[]{:S(2)}) collective-permute-start(bf16[512,512]{1,0:T(8,128)(2,1)S(1)} %collective-permute-done.31.rest_2_), channel_id=1, source_target_pairs={{0,1},{1,0},{2,3},{3,2},{4,5},{5,4},{6,7},{7,6},{8,9},{9,8},{10,11... | collective-permute-start | bytes 1572872 | tf_op jit(solution)/shard_map/ppermute | solution.py:37
  120.7 2.5 %collective-permute-start.36 = (bf16[512,512]{1,0:T(8,128)(2,1)S(1)}, bf16[512,512]{1,0:T(8,128)(2,1)S(1)}, u32[]{:S(2)}, u32[]{:S(2)}) collective-permute-start(bf16[512,512]{1,0:T(8,128)(2,1)S(1)} %collective-permute-done.32.rest_3_), channel_id=1, source_target_pairs={{0,1},{1,0},{2,3},{3,2},{4,5},{5,4},{6,7},{7,6},{8,9},{9,8},{10,11... | collective-permute-start | bytes 1572872 | tf_op jit(solution)/shard_map/ppermute | solution.py:37
  125.7 8.6 %collective-permute-start.40 = (bf16[128,512]{1,0:T(8,128)(2,1)S(1)}, bf16[128,512]{1,0:T(8,128)(2,1)S(1)}, u32[]{:S(2)}, u32[]{:S(2)}) collective-permute-start(bf16[128,512]{1,0:T(8,128)(2,1)S(1)} %get-tuple-element.77), channel_id=1, source_target_pairs={{0,2},{1,9},{2,4},{3,11},{4,6},{5,13},{6,0},{7,15},{8,10},{9,17},{... | collective-permute-start | bytes 393224 | tf_op jit(solution)/shard_map/ppermute | solution.py:32
  126.7 7.6 %collective-permute-start.41 = (bf16[128,512]{1,0:T(8,128)(2,1)S(1)}, bf16[128,512]{1,0:T(8,128)(2,1)S(1)}, u32[]{:S(2)}, u32[]{:S(2)}) collective-permute-start(bf16[128,512]{1,0:T(8,128)(2,1)S(1)} %get-tuple-element.77), channel_id=1, source_target_pairs={{0,4},{1,17},{2,6},{3,19},{4,0},{5,21},{6,2},{7,23},{8,12},{9,25},... | collective-permute-start | bytes 393224 | tf_op jit(solution)/shard_map/ppermute | solution.py:32
  128.8 5.5 %collective-permute-start.42 = (bf16[128,512]{1,0:T(8,128)(2,1)S(1)}, bf16[128,512]{1,0:T(8,128)(2,1)S(1)}, u32[]{:S(2)}, u32[]{:S(2)}) collective-permute-start(bf16[128,512]{1,0:T(8,128)(2,1)S(1)} %get-tuple-element.77), channel_id=1, source_target_pairs={{0,6},{1,25},{2,0},{3,27},{4,2},{5,29},{6,4},{7,31},{8,14},{9,1},{... | collective-permute-start | bytes 393224 | tf_op jit(solution)/shard_map/ppermute | solution.py:32
  131.4 13.0 %collective-permute-start.50 = (bf16[512,512]{1,0:T(8,128)(2,1)S(1)}, bf16[512,512]{1,0:T(8,128)(2,1)S(1)}, u32[]{:S(2)}, u32[]{:S(2)}) collective-permute-start(bf16[512,512]{1,0:T(8,128)(2,1)S(1)} %get-tuple-element.76.current_ref.refs_8_), channel_id=1, source_target_pairs={{0,32},{32,64},{64,96},{96,0},{1,33},{33,65},{65,97},{97,1},{2,34}... | collective-permute-start | bytes 1572872 | tf_op jit(solution)/shard_map/ppermute | solution.py:41
  133.6 16.1 %collective-permute-start.51 = (bf16[512,512]{1,0:T(8,128)(2,1)S(1)}, bf16[512,512]{1,0:T(8,128)(2,1)S(1)}, u32[]{:S(2)}, u32[]{:S(2)}) collective-permute-start(bf16[512,512]{1,0:T(8,128)(2,1)S(1)} %get-tuple-element.76.current_ref.refs_8_), channel_id=1, source_target_pairs={{0,64},{1,65},{2,66},{3,67},{4,68},{5,69},{6,70},{7,71},{8,72},{9,... | collective-permute-start | bytes 1572872 | tf_op jit(solution)/shard_map/ppermute | solution.py:41
  134.4 15.4 %collective-permute-start.43 = (bf16[512,512]{1,0:T(8,128)(2,1)S(1)}, bf16[512,512]{1,0:T(8,128)(2,1)S(1)}, u32[]{:S(2)}, u32[]{:S(2)}) collective-permute-start(bf16[512,512]{1,0:T(8,128)(2,1)S(1)} %constant_dynamic-update-slice_fusion.12.rest_0_), channel_id=1, source_target_pairs={{0,8},{1,3},{2,10},{3,5},{4,12},{5,7},{6,14},{7,1},{8,16},{9,11},{... | collective-permute-start | bytes 1572872 | tf_op jit(solution)/shard_map/ppermute | solution.py:32
  135.3 15.4 %collective-permute-start.44 = (bf16[512,512]{1,0:T(8,128)(2,1)S(1)}, bf16[512,512]{1,0:T(8,128)(2,1)S(1)}, u32[]{:S(2)}, u32[]{:S(2)}) collective-permute-start(bf16[512,512]{1,0:T(8,128)(2,1)S(1)} %constant_dynamic-update-slice_fusion.12.rest_0_), channel_id=1, source_target_pairs={{0,16},{1,5},{2,18},{3,7},{4,20},{5,1},{6,22},{7,3},{8,24},{9,13},... | collective-permute-start | bytes 1572872 | tf_op jit(solution)/shard_map/ppermute | solution.py:32
  137.9 13.4 %collective-permute-start.45 = (bf16[512,512]{1,0:T(8,128)(2,1)S(1)}, bf16[512,512]{1,0:T(8,128)(2,1)S(1)}, u32[]{:S(2)}, u32[]{:S(2)}) collective-permute-start(bf16[512,512]{1,0:T(8,128)(2,1)S(1)} %constant_dynamic-update-slice_fusion.12.rest_0_), channel_id=1, source_target_pairs={{0,24},{1,7},{2,26},{3,1},{4,28},{5,3},{6,30},{7,5},{8,0},{9,15},{... | collective-permute-start | bytes 1572872 | tf_op jit(solution)/shard_map/ppermute | solution.py:32
  144.4 12.0 %collective-permute-start.52 = (bf16[512,512]{1,0:T(8,128)(2,1)S(1)}, bf16[512,512]{1,0:T(8,128)(2,1)S(1)}, u32[]{:S(2)}, u32[]{:S(2)}) collective-permute-start(bf16[512,512]{1,0:T(8,128)(2,1)S(1)} %get-tuple-element.76.current_ref.refs_8_), channel_id=1, source_target_pairs={{96,64},{97,65},{98,66},{99,67},{100,68},{101,69},{102,70},{103,71... | collective-permute-start | bytes 1572872 | tf_op jit(solution)/shard_map/ppermute | solution.py:41
  149.7 6.6 %collective-permute-start.46 = (bf16[512,512]{1,0:T(8,128)(2,1)S(1)}, bf16[512,512]{1,0:T(8,128)(2,1)S(1)}, u32[]{:S(2)}, u32[]{:S(2)}) collective-permute-start(bf16[512,512]{1,0:T(8,128)(2,1)S(1)} %constant_dynamic-update-slice_fusion.12.rest_0_), channel_id=1, source_target_pairs={{0,1},{1,0},{2,3},{3,2},{4,5},{5,4},{6,7},{7,6},{8,9},{9,8},{10,11... | collective-permute-start | bytes 1572872 | tf_op jit(solution)/shard_map/ppermute | solution.py:37
  149.8 6.5 %collective-permute-start.47 = (bf16[512,512]{1,0:T(8,128)(2,1)S(1)}, bf16[512,512]{1,0:T(8,128)(2,1)S(1)}, u32[]{:S(2)}, u32[]{:S(2)}) collective-permute-start(bf16[512,512]{1,0:T(8,128)(2,1)S(1)} %collective-permute-done.43.rest_1_), channel_id=1, source_target_pairs={{0,1},{1,0},{2,3},{3,2},{4,5},{5,4},{6,7},{7,6},{8,9},{9,8},{10,11... | collective-permute-start | bytes 1572872 | tf_op jit(solution)/shard_map/ppermute | solution.py:37
  150.7 5.6 %collective-permute-start.48 = (bf16[512,512]{1,0:T(8,128)(2,1)S(1)}, bf16[512,512]{1,0:T(8,128)(2,1)S(1)}, u32[]{:S(2)}, u32[]{:S(2)}) collective-permute-start(bf16[512,512]{1,0:T(8,128)(2,1)S(1)} %collective-permute-done.44.rest_2_), channel_id=1, source_target_pairs={{0,1},{1,0},{2,3},{3,2},{4,5},{5,4},{6,7},{7,6},{8,9},{9,8},{10,11... | collective-permute-start | bytes 1572872 | tf_op jit(solution)/shard_map/ppermute | solution.py:37
  151.4 5.0 %collective-permute-start.49 = (bf16[512,512]{1,0:T(8,128)(2,1)S(1)}, bf16[512,512]{1,0:T(8,128)(2,1)S(1)}, u32[]{:S(2)}, u32[]{:S(2)}) collective-permute-start(bf16[512,512]{1,0:T(8,128)(2,1)S(1)} %collective-permute-done.45.rest_3_), channel_id=1, source_target_pairs={{0,1},{1,0},{2,3},{3,2},{4,5},{5,4},{6,7},{7,6},{8,9},{9,8},{10,11... | collective-permute-start | bytes 1572872 | tf_op jit(solution)/shard_map/ppermute | solution.py:37
  158.8 19.3 %collective-permute-start.53 = (bf16[512,512]{1,0:T(8,128)(2,1)S(1)}, bf16[512,512]{1,0:T(8,128)(2,1)S(1)}, u32[]{:S(2)}, u32[]{:S(2)}) collective-permute-start(bf16[512,512]{1,0:T(8,128)(2,1)S(1)} %shard_map.77.refs_12_), channel_id=1, source_target_pairs={{64,96},{65,97},{66,98},{67,99},{68,100},{69,101},{70,102},{71,103... | collective-permute-start | bytes 1572872 | tf_op jit(solution)/shard_map/ppermute | solution.py:41
  160.1 22.7 %collective-permute-start.57 = (bf16[512,512]{1,0:T(8,128)(2,1)S(1)}, bf16[512,512]{1,0:T(8,128)(2,1)S(1)}, u32[]{:S(2)}, u32[]{:S(2)}) collective-permute-start(bf16[512,512]{1,0:T(8,128)(2,1)S(1)} %shard_map.77.refs_12_), channel_id=1, source_target_pairs={{0,96},{1,97},{2,98},{3,99},{4,100},{5,101},{6,102},{7,103},{8,104... | collective-permute-start | bytes 1572872 | tf_op jit(solution)/shard_map/ppermute | solution.py:41
  161.4 2.0 %collective-permute-start.54 = (bf16[256,512]{1,0:T(8,128)(2,1)S(1)}, bf16[256,512]{1,0:T(8,128)(2,1)S(1)}, u32[]{:S(2)}, u32[]{:S(2)}) collective-permute-start(bf16[256,512]{1,0:T(8,128)(2,1)S(1)} %get-tuple-element.92), channel_id=1, source_target_pairs={{32,64},{33,65},{34,66},{35,67},{36,68},{37,69},{38,70},{39,71},{4... | collective-permute-start | bytes 786440 | tf_op jit(solution)/shard_map/ppermute | solution.py:41
  162.1 15.9 %collective-permute-start.56 = (bf16[256,512]{1,0:T(8,128)(2,1)S(1)}, bf16[256,512]{1,0:T(8,128)(2,1)S(1)}, u32[]{:S(2)}, u32[]{:S(2)}) collective-permute-start(bf16[256,512]{1,0:T(8,128)(2,1)S(1)} %get-tuple-element.91), channel_id=1, source_target_pairs={{32,96},{33,97},{34,98},{35,99},{36,100},{37,101},{38,102},{39,103... | collective-permute-start | bytes 786440 | tf_op jit(solution)/shard_map/ppermute | solution.py:41
  163.4 20.2 %collective-permute-start.55 = (bf16[256,512]{1,0:T(8,128)(2,1)S(1)}, bf16[256,512]{1,0:T(8,128)(2,1)S(1)}, u32[]{:S(2)}, u32[]{:S(2)}) collective-permute-start(bf16[256,512]{1,0:T(8,128)(2,1)S(1)} %collective-permute-done.54), channel_id=1, source_target_pairs={{64,96},{65,97},{66,98},{67,99},{68,100},{69,101},{70,102},{71,103... | collective-permute-start | bytes 786440 | tf_op jit(solution)/shard_map/ppermute | solution.py:41

commit v4 on v3

--- a/solution.py
+++ b/solution.py
@@ -71,7 +71,9 @@
     *rest,
 ):
     mine_refs, theirs_refs, rest = rest[:SIDE], rest[SIDE:2 * SIDE], rest[2 * SIDE:]
-    outs = 1 if last else 3 if first else 2
+    if not first:
+        back_ref, *rest = rest
+    outs = 1 if last else 3
     out_ref = rest[0]
     space, total = rest[outs:outs + 2]
     span, node = place_ref[0], place_ref[1]
@@ -149,6 +151,16 @@
     out_ref[...] = fresh
     if not last:
         rest[1][...] = offered_rows(listed_ref[...], fresh)
+    if not first and not last:
+        moved_ref = rest[2]
+
+        @pl.when(span == layer_id)
+        def _():
+            moved_ref[...] = back_ref[...]
+
+        @pl.when(span != layer_id)
+        def _():
+            moved_ref[...] = fresh
 
 
 def place_kernel(place_ref, *refs):
@@ -209,14 +221,13 @@
     )(place, current, listed, lists)
     previous = lax.dynamic_index_in_dim(features, jnp.maximum(span - 1, 0), 0, keepdims=False)
     tiles = lax.dynamic_index_in_dim(tile_vals, span, 0, keepdims=False)[0]
-    known = moving = None
+    known = forward = back = None
     placed = []
     for layer_id in range(layers):
         first, last = layer_id == 0, layer_id == layers - 1
         row = jnp.concatenate([block] + [along(block, k, 0) for k in range(1, SIDE)], 0)
         if first:
             half = lax.dynamic_slice_in_dim(weights[0], (node % CORES) * (width // CORES), width // CORES, 0)
-            half, row = lax.optimization_barrier((half, row))
             halves = [half]
             for distance in range(1, layers):
                 halves.append(to_plane(half, [(i, (i + distance) % layers) for i in range(layers)]))
@@ -224,10 +235,9 @@
             known = [halves, other_core(halves)]
         mine = [row] + [along(row, j, 1) for j in range(1, SIDE)]
         theirs = [other_core(part) for part in mine]
-        if moving is not None:
-            mine, theirs, moving = lax.optimization_barrier((mine, theirs, moving))
-            previous = moving[0]
-            placed += [current] + moving
+        if back is not None:
+            previous = forward
+            placed.append([current, forward, None, back])
         scratch = [
             pltpu.VMEM((2 * row_count + nodes * offered, width), jnp.bfloat16),
             pltpu.VMEM((row_count, width), jnp.float32),
@@ -237,14 +247,16 @@
         outs = [rows_shape] if last else [rows_shape, block_shape]
         if first:
             outs.append(wide_shape)
+        elif not last:
+            outs.append(rows_shape)
         results = pl.pallas_call(
             functools.partial(layer_kernel, layer_id, first, last),
             out_shape=outs,
-            in_specs=[SMEM, SMEM, SMEM] + [VMEM] * (6 + 2 * SIDE),
+            in_specs=[SMEM, SMEM, SMEM] + [VMEM] * (6 + 2 * SIDE + (not first)),
             out_specs=[VMEM] * len(outs),
             scratch_shapes=scratch,
             compiler_params=params,
-        )(place, counts, tile_cols, listed, current, previous, tiles, *known, *mine, *theirs)
+        )(place, counts, tile_cols, listed, current, previous, tiles, *known, *mine, *theirs, *([] if first else [back]))
         current = results[0]
         if not last:
             block = results[1]
@@ -252,21 +264,27 @@
             tiles = results[2]
         before, after, across = [(layer_id + step) % layers for step in (3, 1, 2)]
         if not last:
-            moving = [
-                to_plane(current, [(i, (i + 1) % layers) for i in range(layers)]),
-                to_plane(current, [(across, layer_id)]),
-                to_plane(current, [(after, layer_id)]),
-            ]
+            forward = to_plane(current, [(i, (i + 1) % layers) for i in range(layers)])
+            pairs = [(after, layer_id), (across, after)]
+            moved = current
+            if not first:
+                pairs.append((layer_id, before))
+                moved = results[2]
+            back = to_plane(moved, pairs)
+            if not first:
+                placed[-1][2] = back
         else:
             half = row_count // 2
             relayed = to_plane(current[:half], [(across, before)])
-            placed += [
+            placed[-1][2] = to_plane(back, [(layer_id, before)])
+            placed.append([
                 current,
                 to_plane(current, [(before, layer_id)]),
                 to_plane(relayed, [(before, layer_id)]),
                 to_plane(current[half:], [(across, layer_id)]),
                 to_plane(current, [(after, layer_id)]),
-            ]
+            ])
+    placed = sum(placed, [])
     return pl.pallas_call(
         place_kernel,
         out_shape=jax.ShapeDtypeStruct(features.shape, features.dtype),

time: 186 us -> 163 us (0.88)
  waiting for transfers between devices: 84.8 us -> 72.9 us
  starting transfers between devices: 78.9 us -> 67.2 us
    ppermute x17 -> x15, waiting for transfers between devices: 56.3 us -> 32.8 us  [to_plane(): return lax.ppermute(block, 'layer', pairs)]
    ppermute x24, waiting for transfers between devices: 20.6 us -> 33.4 us  [along(): return lax.ppermute(block, 'node', route)]
    ppermute x17 -> x15, starting transfers between devices: 37.6 us -> 25.5 us  [to_plane(): return lax.ppermute(block, 'layer', pairs)]
  transfers between devices with their start and end apart: 58 -> 56, of which waited for: 30 -> 30; matrix products, arithmetic and copies ran while one was open for 1% -> 1% of each run, Pallas kernels for 0% -> 1%
where the time goes in v4:
time: 163 us; the launch traced here: 162 us
  waiting for transfers between devices  72.9 us (45%)
  starting transfers between devices  67.2 us (41%)
  Pallas kernels  15.7 us (10%)
  local copies, waits for them, and re-layouts  4.78 us (3%)
    ppermute x24, starting transfers between devices, along(): return lax.ppermute(block, 'node', route)  39.1 us
    ppermute x24, waiting for transfers between devices, along(): return lax.ppermute(block, 'node', route)  33.4 us
    ppermute x15, waiting for transfers between devices, to_plane(): return lax.ppermute(block, 'layer', pairs)  32.8 us
    ppermute x15, starting transfers between devices, to_plane(): return lax.ppermute(block, 'layer', pairs)  25.5 us
    pallas_call x4, Pallas kernels, on_device(): pl.pallas_call(functools.partial(layer_kernel, layer_id, first, last), ou...  12.8 us
    ppermute x17, waiting for transfers between devices, other_core(): return lax.ppermute(block, 'node', route)  6.75 us
  transfers between devices with their start and end apart: 56, of which 30 were waited for; matrix products, arithmetic and copies ran while one was open for 1% of the time, Pallas kernels for 1%

profile of v4, /device:TPU:6, one launch (start us, length us, event | category | flops | bytes accessed | tf_op | source)
XLA Modules:
  0.0 162.4 jit_solution(9152547510362937952)
XLA Ops:
  0.0 0.8 fusion.listed_ref
  0.8 0.7 dynamic-slice_bitcast_fusion.4.lists_ref
  1.5 2.1 %dynamic-slice_bitcast_fusion.1 = (bf16[512,512]{1,0:T(8,128)(2,1)}, bf16[512,512]{1,0:T(8,128)(2,1)S(1)}) fusion(bf16[4,512,512]{2,1,0:T(8,128)(2,1)} %param.7, s32[]{:T(128)S(6)} %max.3, s32[]{:T(128)S(6)} %select_n.21), kind=kLoop, calls=%fused_computation.3 | loop fusion | bytes 2097160 | tf_op jit(solution)/shard_map/jit(dynamic_index_in_dim)/squeeze | solution.py:222
  3.7 0.8 shard_map.73
  4.5 1.6 %collective-permute-start.4 = (bf16[144,512]{1,0:T(8,128)(2,1)S(1)}, bf16[144,512]{1,0:T(8,128)(2,1)S(1)}, u32[]{:S(2)}, u32[]{:S(2)}) collective-permute-start(bf16[144,512]{1,0:T(8,128)(2,1)S(1)} %shard_map.73), channel_id=1, source_target_pairs={{0,2},{1,9},{2,4},{3,11},{4,6},{5,13},{6,0},{7,15},{8,10},{9,17},{... | collective-permute-start | bytes 442376 | tf_op jit(solution)/shard_map/ppermute | solution.py:32
  6.1 2.9 %collective-permute-start.5 = (bf16[144,512]{1,0:T(8,128)(2,1)S(1)}, bf16[144,512]{1,0:T(8,128)(2,1)}, u32[]{:S(2)}, u32[]{:S(2)}) collective-permute-start(bf16[144,512]{1,0:T(8,128)(2,1)S(1)} %shard_map.73), channel_id=1, source_target_pairs={{0,4},{1,17},{2,6},{3,19},{4,0},{5,21},{6,2},{7,23},{8,12},{9,25},... | collective-permute-start | bytes 442376 | tf_op jit(solution)/shard_map/ppermute | solution.py:32
  9.0 1.3 collective-permute-start.6
  10.4 1.0 dynamic-slice_bitcast_fusion.3
  12.0 2.3 %collective-permute-start.1 = (bf16[256,512]{1,0:T(8,128)(2,1)S(1)}, bf16[256,512]{1,0:T(8,128)(2,1)S(1)}, u32[]{:S(2)}, u32[]{:S(2)}) collective-permute-start(bf16[256,512]{1,0:T(8,128)(2,1)S(1)} %dynamic-slice_bitcast_fusion.3), channel_id=1, source_target_pairs={{0,64},{32,96},{64,0},{96,32},{1,65},{33,97},{65,1},{97,33},{2,66}... | collective-permute-start | bytes 786440 | tf_op jit(solution)/shard_map/ppermute | solution.py:41
  14.4 1.0 pad_maximum_fusion.1.rest_0_
  15.4 2.0 %collective-permute-start.7 = (bf16[576,512]{1,0:T(8,128)(2,1)S(1)}, bf16[576,512]{1,0:T(8,128)(2,1)S(1)}, u32[]{:S(2)}, u32[]{:S(2)}) collective-permute-start(bf16[576,512]{1,0:T(8,128)(2,1)S(1)} %pad_maximum_fusion.1.rest_0_), channel_id=1, source_target_pairs={{0,8},{1,3},{2,10},{3,5},{4,12},{5,7},{6,14},{7,1},{8,16},{9,11},{... | collective-permute-start | bytes 1769480 | tf_op jit(solution)/shard_map/ppermute | solution.py:32
  17.4 3.6 %collective-permute-start.8 = (bf16[576,512]{1,0:T(8,128)(2,1)S(1)}, bf16[576,512]{1,0:T(8,128)(2,1)S(1)}, u32[]{:S(2)}, u32[]{:S(2)}) collective-permute-start(bf16[576,512]{1,0:T(8,128)(2,1)S(1)} %pad_maximum_fusion.1.rest_0_), channel_id=1, source_target_pairs={{0,16},{1,5},{2,18},{3,7},{4,20},{5,1},{6,22},{7,3},{8,24},{9,13},... | collective-permute-start | bytes 1769480 | tf_op jit(solution)/shard_map/ppermute | solution.py:32
  21.0 1.5 collective-permute-start.9
  22.8 4.0 %collective-permute-done.2 = bf16[256,512]{1,0:T(8,128)(2,1)S(1)} collective-permute-done((bf16[256,512]{1,0:T(8,128)(2,1)S(1)}, bf16[256,512]{1,0:T(8,128)(2,1)S(1)}, u32[]{:S(2)}, u32[]{:S(2)}) %collective-permute-start.2) | collective-permute-done | bytes 262176 | tf_op jit(solution)/shard_map/ppermute | solution.py:41
  27.6 7.5 %collective-permute-done.8.rest_2_ = bf16[576,512]{1,0:T(8,128)(2,1)S(1)} collective-permute-done((bf16[576,512]{1,0:T(8,128)(2,1)S(1)}, bf16[576,512]{1,0:T(8,128)(2,1)S(1)}, u32[]{:S(2)}, u32[]{:S(2)}) %collective-permute-start.8) | collective-permute-done | bytes 589856 | tf_op jit(solution)/shard_map/ppermute | solution.py:32
  35.7 1.4 collective-permute-done.12.rest_6_
  37.1 0.8 collective-permute-done.13.rest_7_
  38.0 5.2 %shard_map.74 = (bf16[512,512]{1,0:T(8,128)(2,1)S(1)}, bf16[128,512]{1,0:T(8,128)(2,1)S(1)}, bf16[20,128,256]{2,1,0:T(8,128)(2,1)S(1)}) custom-call(s32[2]{0:T(128)S(1)} %pad_add_fusion.place_ref, s32[4,4]{1,0:T(4,128)S(1)} %bitcast.16, s32[4,20]{1,0:T(4,128)S(1)} %bitcast.20, s32[1,128]{1,0:T(1,128)S(1)} %fusion.listed_ref, ...), custom_call_target="tpu_custom_call" | custom-call | tf_op jit(solution)/shard_map/pallas_call | solution.py:252
  43.2 1.2 collective-permute-start.15
  44.4 2.8 %collective-permute-start.16 = (bf16[128,512]{1,0:T(8,128)(2,1)S(1)}, bf16[128,512]{1,0:T(8,128)(2,1)S(1)}, u32[]{:S(2)}, u32[]{:S(2)}) collective-permute-start(bf16[128,512]{1,0:T(8,128)(2,1)S(1)} %get-tuple-element.16), channel_id=1, source_target_pairs={{0,4},{1,17},{2,6},{3,19},{4,0},{5,21},{6,2},{7,23},{8,12},{9,25},... | collective-permute-start | bytes 393224 | tf_op jit(solution)/shard_map/ppermute | solution.py:32
  47.3 1.1 collective-permute-start.17
  48.3 1.7 %collective-permute-start.14 = (bf16[512,512]{1,0:T(8,128)(2,1)S(1)}, bf16[512,512]{1,0:T(8,128)(2,1)S(1)}, u32[]{:S(2)}, u32[]{:S(2)}) collective-permute-start(bf16[512,512]{1,0:T(8,128)(2,1)S(1)} %get-tuple-element.14.current_ref.refs_0_), channel_id=1, source_target_pairs={{0,32},{32,64},{64,96},{96,0},{1,33},{33,65},{65,97},{97,1},{2,34}... | collective-permute-start | bytes 1572872 | tf_op jit(solution)/shard_map/ppermute | solution.py:41
  50.1 1.5 collective-permute-done.16
  52.3 0.7 collective-permute-start.18
  53.0 2.1 %collective-permute-start.19 = (bf16[512,512]{1,0:T(8,128)(2,1)S(1)}, bf16[512,512]{1,0:T(8,128)(2,1)S(1)}, u32[]{:S(2)}, u32[]{:S(2)}) collective-permute-start(bf16[512,512]{1,0:T(8,128)(2,1)S(1)} %constant_dynamic-update-slice_fusion.rest_0_), channel_id=1, source_target_pairs={{0,16},{1,5},{2,18},{3,7},{4,20},{5,1},{6,22},{7,3},{8,24},{9,13},... | collective-permute-start | bytes 1572872 | tf_op jit(solution)/shard_map/ppermute | solution.py:32
  55.2 1.5 collective-permute-start.20
  57.4 4.2 %collective-permute-done.14.previous_ref.refs_1_ = bf16[512,512]{1,0:T(8,128)(2,1)S(1)} collective-permute-done((bf16[512,512]{1,0:T(8,128)(2,1)S(1)}, bf16[512,512]{1,0:T(8,128)(2,1)S(1)}, u32[]{:S(2)}, u32[]{:S(2)}) %collective-permute-start.14) | collective-permute-done | bytes 524320 | tf_op jit(solution)/shard_map/ppermute | solution.py:41
  61.6 6.8 %collective-permute-done.18.rest_1_ = bf16[512,512]{1,0:T(8,128)(2,1)S(1)} collective-permute-done((bf16[512,512]{1,0:T(8,128)(2,1)S(1)}, bf16[512,512]{1,0:T(8,128)(2,1)S(1)}, u32[]{:S(2)}, u32[]{:S(2)}) %collective-permute-start.18) | collective-permute-done | bytes 524320 | tf_op jit(solution)/shard_map/ppermute | solution.py:32
  69.3 1.0 collective-permute-done.22.rest_5_
  70.3 0.7 collective-permute-done.23.rest_6_
  71.0 0.7 collective-permute-done.24.rest_7_
  71.8 2.6 %shard_map.75 = (bf16[512,512]{1,0:T(8,128)(2,1)S(1)}, bf16[128,512]{1,0:T(8,128)(2,1)S(1)}, bf16[512,512]{1,0:T(8,128)(2,1)S(1)}) custom-call(s32[2]{0:T(128)S(1)} %pad_add_fusion.place_ref, s32[4,4]{1,0:T(4,128)S(1)} %bitcast.17, s32[4,20]{1,0:T(4,128)S(1)} %bitcast.21, s32[1,128]{1,0:T(1,128)S(1)} %fusion.listed_ref, ...), custom_call_target="tpu_custom_call" | custom-call | tf_op jit(solution)/shard_map/pallas_call | solution.py:252
  74.4 1.2 collective-permute-start.28
  75.6 2.5 %collective-permute-start.29 = (bf16[128,512]{1,0:T(8,128)(2,1)S(1)}, bf16[128,512]{1,0:T(8,128)(2,1)S(1)}, u32[]{:S(2)}, u32[]{:S(2)}) collective-permute-start(bf16[128,512]{1,0:T(8,128)(2,1)S(1)} %get-tuple-element.19), channel_id=1, source_target_pairs={{0,4},{1,17},{2,6},{3,19},{4,0},{5,21},{6,2},{7,23},{8,12},{9,25},... | collective-permute-start | bytes 393224 | tf_op jit(solution)/shard_map/ppermute | solution.py:32
  78.2 0.8 collective-permute-start.30
  79.0 2.8 %collective-permute-start.26 = (bf16[512,512]{1,0:T(8,128)(2,1)S(1)}, bf16[512,512]{1,0:T(8,128)(2,1)S(1)}, u32[]{:S(2)}, u32[]{:S(2)}) collective-permute-start(bf16[512,512]{1,0:T(8,128)(2,1)S(1)} %get-tuple-element.17), channel_id=1, source_target_pairs={{64,32},{96,64},{32,0},{65,33},{97,65},{33,1},{66,34},{98,66},{34,... | collective-permute-start | bytes 1572872 | tf_op jit(solution)/shard_map/ppermute | solution.py:41
  81.7 0.8 collective-permute-done.29
  82.5 0.7 collective-permute-done.30
  83.7 3.1 %collective-permute-start.32 = (bf16[512,512]{1,0:T(8,128)(2,1)S(1)}, bf16[512,512]{1,0:T(8,128)(2,1)S(1)}, u32[]{:S(2)}, u32[]{:S(2)}) collective-permute-start(bf16[512,512]{1,0:T(8,128)(2,1)S(1)} %constant_dynamic-update-slice_fusion.4.rest_0_), channel_id=1, source_target_pairs={{0,16},{1,5},{2,18},{3,7},{4,20},{5,1},{6,22},{7,3},{8,24},{9,13},... | collective-permute-start | bytes 1572872 | tf_op jit(solution)/shard_map/ppermute | solution.py:32
  87.0 3.1 %collective-permute-start.27 = (bf16[512,512]{1,0:T(8,128)(2,1)S(1)}, bf16[512,512]{1,0:T(8,128)(2,1)S(1)}, u32[]{:S(2)}, u32[]{:S(2)}) collective-permute-start(bf16[512,512]{1,0:T(8,128)(2,1)S(1)} %get-tuple-element.18.current_ref.refs_4_), channel_id=1, source_target_pairs={{0,32},{32,64},{64,96},{96,0},{1,33},{33,65},{65,97},{97,1},{2,34}... | collective-permute-start | bytes 1572872 | tf_op jit(solution)/shard_map/ppermute | solution.py:41
  90.1 1.6 collective-permute-done.26.rest_8_.refs_2_.refs_7_
  91.7 2.0 %collective-permute-done.31.rest_1_ = bf16[512,512]{1,0:T(8,128)(2,1)S(1)} collective-permute-done((bf16[512,512]{1,0:T(8,128)(2,1)S(1)}, bf16[512,512]{1,0:T(8,128)(2,1)S(1)}, u32[]{:S(2)}, u32[]{:S(2)}) %collective-permute-start.31) | collective-permute-done | bytes 524320 | tf_op jit(solution)/shard_map/ppermute | solution.py:32
  93.7 5.9 %collective-permute-done.32.rest_2_ = bf16[512,512]{1,0:T(8,128)(2,1)S(1)} collective-permute-done((bf16[512,512]{1,0:T(8,128)(2,1)S(1)}, bf16[512,512]{1,0:T(8,128)(2,1)S(1)}, u32[]{:S(2)}, u32[]{:S(2)}) %collective-permute-start.32) | collective-permute-done | bytes 524320 | tf_op jit(solution)/shard_map/ppermute | solution.py:32
  100.2 1.2 collective-permute-done.36.rest_6_
  101.5 0.7 collective-permute-done.37.rest_7_
  102.2 2.6 %shard_map.76 = (bf16[512,512]{1,0:T(8,128)(2,1)S(1)}, bf16[128,512]{1,0:T(8,128)(2,1)S(1)}, bf16[512,512]{1,0:T(8,128)(2,1)S(1)}) custom-call(s32[2]{0:T(128)S(1)} %pad_add_fusion.place_ref, s32[4,4]{1,0:T(4,128)S(1)} %bitcast.18, s32[4,20]{1,0:T(4,128)S(1)} %bitcast.22, s32[1,128]{1,0:T(1,128)S(1)} %fusion.listed_ref, ...), custom_call_target="tpu_custom_call" | custom-call | tf_op jit(solution)/shard_map/pallas_call | solution.py:252
  104.8 0.9 collective-permute-start.41
  105.8 3.0 %collective-permute-start.42 = (bf16[128,512]{1,0:T(8,128)(2,1)S(1)}, bf16[128,512]{1,0:T(8,128)(2,1)S(1)}, u32[]{:S(2)}, u32[]{:S(2)}) collective-permute-start(bf16[128,512]{1,0:T(8,128)(2,1)S(1)} %get-tuple-element.22), channel_id=1, source_target_pairs={{0,4},{1,17},{2,6},{3,19},{4,0},{5,21},{6,2},{7,23},{8,12},{9,25},... | collective-permute-start | bytes 393224 | tf_op jit(solution)/shard_map/ppermute | solution.py:32
  109.1 3.0 %collective-permute-start.38 = (bf16[512,512]{1,0:T(8,128)(2,1)S(1)}, bf16[512,512]{1,0:T(8,128)(2,1)S(1)}, u32[]{:S(2)}, u32[]{:S(2)}) collective-permute-start(bf16[512,512]{1,0:T(8,128)(2,1)S(1)} %get-tuple-element.20), channel_id=1, source_target_pairs={{96,64},{0,96},{64,32},{97,65},{1,97},{65,33},{98,66},{2,98},{66,3... | collective-permute-start | bytes 1572872 | tf_op jit(solution)/shard_map/ppermute | solution.py:41
  112.1 1.0 collective-permute-done.42
  114.2 3.7 %collective-permute-start.45 = (bf16[512,512]{1,0:T(8,128)(2,1)S(1)}, bf16[512,512]{1,0:T(8,128)(2,1)S(1)}, u32[]{:S(2)}, u32[]{:S(2)}) collective-permute-start(bf16[512,512]{1,0:T(8,128)(2,1)S(1)} %constant_dynamic-update-slice_fusion.8.rest_0_), channel_id=1, source_target_pairs={{0,16},{1,5},{2,18},{3,7},{4,20},{5,1},{6,22},{7,3},{8,24},{9,13},... | collective-permute-start | bytes 1572872 | tf_op jit(solution)/shard_map/ppermute | solution.py:32
  117.9 2.7 %collective-permute-start.39 = (bf16[512,512]{1,0:T(8,128)(2,1)S(1)}, bf16[512,512]{1,0:T(8,128)(2,1)S(1)}, u32[]{:S(2)}, u32[]{:S(2)}) collective-permute-start(bf16[512,512]{1,0:T(8,128)(2,1)S(1)} %get-tuple-element.21.current_ref.refs_8_), channel_id=1, source_target_pairs={{0,32},{32,64},{64,96},{96,0},{1,33},{33,65},{65,97},{97,1},{2,34}... | collective-permute-start | bytes 1572872 | tf_op jit(solution)/shard_map/ppermute | solution.py:41
  120.6 4.9 %collective-permute-done.38.rest_8_.refs_6_.refs_11_ = bf16[512,512]{1,0:T(8,128)(2,1)S(1)} collective-permute-done((bf16[512,512]{1,0:T(8,128)(2,1)S(1)}, bf16[512,512]{1,0:T(8,128)(2,1)S(1)}, u32[]{:S(2)}, u32[]{:S(2)}) %collective-permute-start.38) | collective-permute-done | bytes 524320 | tf_op jit(solution)/shard_map/ppermute | solution.py:41
  126.0 4.6 %collective-permute-done.45.rest_2_ = bf16[512,512]{1,0:T(8,128)(2,1)S(1)} collective-permute-done((bf16[512,512]{1,0:T(8,128)(2,1)S(1)}, bf16[512,512]{1,0:T(8,128)(2,1)S(1)}, u32[]{:S(2)}, u32[]{:S(2)}) %collective-permute-start.45) | collective-permute-done | bytes 524320 | tf_op jit(solution)/shard_map/ppermute | solution.py:32
  131.1 2.7 %collective-permute-start.40 = (bf16[512,512]{1,0:T(8,128)(2,1)S(1)}, bf16[512,512]{1,0:T(8,128)(2,1)S(1)}, u32[]{:S(2)}, u32[]{:S(2)}) collective-permute-start(bf16[512,512]{1,0:T(8,128)(2,1)S(1)} %collective-permute-done.38.rest_8_.refs_6_.refs_11_), channel_id=1, source_target_pairs={{96,64},{97,65},{98,66},{99,67},{100,68},{101,69},{102,70},{103,71... | collective-permute-start | bytes 1572872 | tf_op jit(solution)/shard_map/ppermute | solution.py:41
  133.9 2.4 %shard_map.77.refs_12_ = bf16[512,512]{1,0:T(8,128)(2,1)S(1)} custom-call(s32[2]{0:T(128)S(1)} %pad_add_fusion.place_ref, s32[4,4]{1,0:T(4,128)S(1)} %bitcast.19, s32[4,20]{1,0:T(4,128)S(1)} %bitcast.23, s32[1,128]{1,0:T(1,128)S(1)} %fusion.listed_ref, bf16[512,512]{1,0:T(8,128)(2,1)S(1)} %get-tuple-element.21.current_ref.refs_8_, ...), custom_call_target="tpu_custom_call" | custom-call | tf_op jit(solution)/shard_map/pallas_call | solution.py:252
  136.4 1.3 collective-permute-start.51
  137.7 1.3 collective-permute-start.55
  139.7 1.3 collective-permute-start.54
  141.0 1.3 collective-permute-start.53
  142.3 3.1 %collective-permute-done.40.refs_10_ = bf16[512,512]{1,0:T(8,128)(2,1)S(1)} collective-permute-done((bf16[512,512]{1,0:T(8,128)(2,1)S(1)}, bf16[512,512]{1,0:T(8,128)(2,1)S(1)}, u32[]{:S(2)}, u32[]{:S(2)}) %collective-permute-start.40) | collective-permute-done | bytes 524320 | tf_op jit(solution)/shard_map/ppermute | solution.py:41
  145.3 6.9 %collective-permute-done.54.refs_15_ = bf16[256,512]{1,0:T(8,128)(2,1)S(1)} collective-permute-done((bf16[256,512]{1,0:T(8,128)(2,1)S(1)}, bf16[256,512]{1,0:T(8,128)(2,1)S(1)}, u32[]{:S(2)}, u32[]{:S(2)}) %collective-permute-start.54) | collective-permute-done | bytes 262176 | tf_op jit(solution)/shard_map/ppermute | solution.py:41
  152.3 7.8 %collective-permute-done.55.refs_16_ = bf16[512,512]{1,0:T(8,128)(2,1)S(1)} collective-permute-done((bf16[512,512]{1,0:T(8,128)(2,1)S(1)}, bf16[512,512]{1,0:T(8,128)(2,1)S(1)}, u32[]{:S(2)}, u32[]{:S(2)}) %collective-permute-start.55) | collective-permute-done | bytes 524320 | tf_op jit(solution)/shard_map/ppermute | solution.py:41
  160.1 2.1 %shard_map.78 = bf16[4,512,512]{2,1,0:T(8,128)(2,1)} custom-call(s32[2]{0:T(128)S(1)} %pad_add_fusion.place_ref, bf16[512,512]{1,0:T(8,128)(2,1)S(1)} %get-tuple-element.14.current_ref.refs_0_, bf16[512,512]{1,0:T(8,128)(2,1)S(1)} %collective-permute-done.14.previous_ref.refs_1_, bf16[512,512]{1,0:T(8,128)(2,1)S(1)} %collective-permute-done.26.rest_8_.refs_2_.refs_7_, ...), custom_call_target="tpu_custom_call" | custom-call | tf_op jit(solution)/shard_map/pallas_call | solution.py:288
  (83 shorter events, 9.5 us)
Async XLA Ops:
  0.0 35.7 %copy-start = (bf16[4,1,20,128,128]{4,3,2,1,0:T(8,128)(2,1)S(1)}, bf16[4,1,20,128,128]{4,3,2,1,0:T(8,128)(2,1)}, u32[]{:S(2)}) copy-start(bf16[4,1,20,128,128]{4,3,2,1,0:T(8,128)(2,1)} %param.13) | copy-start | bytes 7864324
  4.5 9.9 %collective-permute-start.4 = (bf16[144,512]{1,0:T(8,128)(2,1)S(1)}, bf16[144,512]{1,0:T(8,128)(2,1)S(1)}, u32[]{:S(2)}, u32[]{:S(2)}) collective-permute-start(bf16[144,512]{1,0:T(8,128)(2,1)S(1)} %shard_map.73), channel_id=1, source_target_pairs={{0,2},{1,9},{2,4},{3,11},{4,6},{5,13},{6,0},{7,15},{8,10},{9,17},{... | collective-permute-start | bytes 442376 | tf_op jit(solution)/shard_map/ppermute | solution.py:32
  6.1 8.2 %collective-permute-start.5 = (bf16[144,512]{1,0:T(8,128)(2,1)S(1)}, bf16[144,512]{1,0:T(8,128)(2,1)}, u32[]{:S(2)}, u32[]{:S(2)}) collective-permute-start(bf16[144,512]{1,0:T(8,128)(2,1)S(1)} %shard_map.73), channel_id=1, source_target_pairs={{0,4},{1,17},{2,6},{3,19},{4,0},{5,21},{6,2},{7,23},{8,12},{9,25},... | collective-permute-start | bytes 442376 | tf_op jit(solution)/shard_map/ppermute | solution.py:32
  9.0 5.3 %collective-permute-start.6 = (bf16[144,512]{1,0:T(8,128)(2,1)S(1)}, bf16[144,512]{1,0:T(8,128)(2,1)}, u32[]{:S(2)}, u32[]{:S(2)}) collective-permute-start(bf16[144,512]{1,0:T(8,128)(2,1)S(1)} %shard_map.73), channel_id=1, source_target_pairs={{0,6},{1,25},{2,0},{3,27},{4,2},{5,29},{6,4},{7,31},{8,14},{9,1},{... | collective-permute-start | bytes 442376 | tf_op jit(solution)/shard_map/ppermute | solution.py:32
  11.3 26.6 %copy-start.1 = (bf16[512,512]{1,0:T(8,128)(2,1)S(1)}, bf16[512,512]{1,0:T(8,128)(2,1)}, u32[]{:S(2)}) copy-start(bf16[512,512]{1,0:T(8,128)(2,1)} %get-tuple-element.23.previous_ref) | copy-start | bytes 1572868
  11.4 26.6 %copy-start.2 = (s32[4,1,4]{2,1,0:T(1,128)S(1)}, s32[4,1,4]{2,1,0:T(1,128)}, u32[]{:S(2)}) copy-start(s32[4,1,4]{2,1,0:T(1,128)} %param.11) | copy-start | bytes 196
  11.4 26.6 %copy-start.3 = (s32[4,1,20]{2,1,0:T(1,128)S(1)}, s32[4,1,20]{2,1,0:T(1,128)}, u32[]{:S(2)}) copy-start(s32[4,1,20]{2,1,0:T(1,128)} %param.12) | copy-start | bytes 964
  11.4 9.6 %collective-permute-start = (bf16[256,512]{1,0:T(8,128)(2,1)S(1)}, bf16[256,512]{1,0:T(8,128)(2,1)S(1)}, u32[]{:S(2)}, u32[]{:S(2)}) collective-permute-start(bf16[256,512]{1,0:T(8,128)(2,1)S(1)} %dynamic-slice_bitcast_fusion.3), channel_id=1, source_target_pairs={{0,32},{32,64},{64,96},{96,0},{1,33},{33,65},{65,97},{97,1},{2,34}... | collective-permute-start | bytes 786440 | tf_op jit(solution)/shard_map/ppermute | solution.py:41
  12.0 10.8 %collective-permute-start.1 = (bf16[256,512]{1,0:T(8,128)(2,1)S(1)}, bf16[256,512]{1,0:T(8,128)(2,1)S(1)}, u32[]{:S(2)}, u32[]{:S(2)}) collective-permute-start(bf16[256,512]{1,0:T(8,128)(2,1)S(1)} %dynamic-slice_bitcast_fusion.3), channel_id=1, source_target_pairs={{0,64},{32,96},{64,0},{96,32},{1,65},{33,97},{65,1},{97,33},{2,66}... | collective-permute-start | bytes 786440 | tf_op jit(solution)/shard_map/ppermute | solution.py:41
  14.4 12.5 %collective-permute-start.2 = (bf16[256,512]{1,0:T(8,128)(2,1)S(1)}, bf16[256,512]{1,0:T(8,128)(2,1)S(1)}, u32[]{:S(2)}, u32[]{:S(2)}) collective-permute-start(bf16[256,512]{1,0:T(8,128)(2,1)S(1)} %dynamic-slice_bitcast_fusion.3), channel_id=1, source_target_pairs={{0,96},{32,0},{64,32},{96,64},{1,97},{33,1},{65,33},{97,65},{2,98}... | collective-permute-start | bytes 786440 | tf_op jit(solution)/shard_map/ppermute | solution.py:41
  15.4 12.1 %collective-permute-start.7 = (bf16[576,512]{1,0:T(8,128)(2,1)S(1)}, bf16[576,512]{1,0:T(8,128)(2,1)S(1)}, u32[]{:S(2)}, u32[]{:S(2)}) collective-permute-start(bf16[576,512]{1,0:T(8,128)(2,1)S(1)} %pad_maximum_fusion.1.rest_0_), channel_id=1, source_target_pairs={{0,8},{1,3},{2,10},{3,5},{4,12},{5,7},{6,14},{7,1},{8,16},{9,11},{... | collective-permute-start | bytes 1769480 | tf_op jit(solution)/shard_map/ppermute | solution.py:32
  17.4 17.8 %collective-permute-start.8 = (bf16[576,512]{1,0:T(8,128)(2,1)S(1)}, bf16[576,512]{1,0:T(8,128)(2,1)S(1)}, u32[]{:S(2)}, u32[]{:S(2)}) collective-permute-start(bf16[576,512]{1,0:T(8,128)(2,1)S(1)} %pad_maximum_fusion.1.rest_0_), channel_id=1, source_target_pairs={{0,16},{1,5},{2,18},{3,7},{4,20},{5,1},{6,22},{7,3},{8,24},{9,13},... | collective-permute-start | bytes 1769480 | tf_op jit(solution)/shard_map/ppermute | solution.py:32
  21.0 14.2 %collective-permute-start.9 = (bf16[576,512]{1,0:T(8,128)(2,1)S(1)}, bf16[576,512]{1,0:T(8,128)(2,1)S(1)}, u32[]{:S(2)}, u32[]{:S(2)}) collective-permute-start(bf16[576,512]{1,0:T(8,128)(2,1)S(1)} %pad_maximum_fusion.1.rest_0_), channel_id=1, source_target_pairs={{0,24},{1,7},{2,26},{3,1},{4,28},{5,3},{6,30},{7,5},{8,0},{9,15},{... | collective-permute-start | bytes 1769480 | tf_op jit(solution)/shard_map/ppermute | solution.py:32
  26.9 8.8 %collective-permute-start.3 = (bf16[1024,512]{1,0:T(8,128)(2,1)S(1)}, bf16[1024,512]{1,0:T(8,128)(2,1)S(1)}, u32[]{:S(2)}, u32[]{:S(2)}) collective-permute-start(bf16[1024,512]{1,0:T(8,128)(2,1)S(1)} %pad_maximum_fusion.halves_ref), channel_id=1, source_target_pairs={{0,1},{1,0},{2,3},{3,2},{4,5},{5,4},{6,7},{7,6},{8,9},{9,8},{10,11... | collective-permute-start | bytes 3145736 | tf_op jit(solution)/shard_map/ppermute | solution.py:37
  27.0 8.7 %collective-permute-start.10 = (bf16[576,512]{1,0:T(8,128)(2,1)S(1)}, bf16[576,512]{1,0:T(8,128)(2,1)S(1)}, u32[]{:S(2)}, u32[]{:S(2)}) collective-permute-start(bf16[576,512]{1,0:T(8,128)(2,1)S(1)} %pad_maximum_fusion.1.rest_0_), channel_id=1, source_target_pairs={{0,1},{1,0},{2,3},{3,2},{4,5},{5,4},{6,7},{7,6},{8,9},{9,8},{10,11... | collective-permute-start | bytes 1769480 | tf_op jit(solution)/shard_map/ppermute | solution.py:37
  27.5 8.2 %collective-permute-start.11 = (bf16[576,512]{1,0:T(8,128)(2,1)S(1)}, bf16[576,512]{1,0:T(8,128)(2,1)S(1)}, u32[]{:S(2)}, u32[]{:S(2)}) collective-permute-start(bf16[576,512]{1,0:T(8,128)(2,1)S(1)} %collective-permute-done.7.rest_1_), channel_id=1, source_target_pairs={{0,1},{1,0},{2,3},{3,2},{4,5},{5,4},{6,7},{7,6},{8,9},{9,8},{10,11... | collective-permute-start | bytes 1769480 | tf_op jit(solution)/shard_map/ppermute | solution.py:37
  35.1 2.0 %collective-permute-start.12 = (bf16[576,512]{1,0:T(8,128)(2,1)S(1)}, bf16[576,512]{1,0:T(8,128)(2,1)S(1)}, u32[]{:S(2)}, u32[]{:S(2)}) collective-permute-start(bf16[576,512]{1,0:T(8,128)(2,1)S(1)} %collective-permute-done.8.rest_2_), channel_id=1, source_target_pairs={{0,1},{1,0},{2,3},{3,2},{4,5},{5,4},{6,7},{7,6},{8,9},{9,8},{10,11... | collective-permute-start | bytes 1769480 | tf_op jit(solution)/shard_map/ppermute | solution.py:37
  35.1 2.8 %collective-permute-start.13 = (bf16[576,512]{1,0:T(8,128)(2,1)S(1)}, bf16[576,512]{1,0:T(8,128)(2,1)S(1)}, u32[]{:S(2)}, u32[]{:S(2)}) collective-permute-start(bf16[576,512]{1,0:T(8,128)(2,1)S(1)} %collective-permute-done.9.rest_3_), channel_id=1, source_target_pairs={{0,1},{1,0},{2,3},{3,2},{4,5},{5,4},{6,7},{7,6},{8,9},{9,8},{10,11... | collective-permute-start | bytes 1769480 | tf_op jit(solution)/shard_map/ppermute | solution.py:37
  43.2 6.8 %collective-permute-start.15 = (bf16[128,512]{1,0:T(8,128)(2,1)S(1)}, bf16[128,512]{1,0:T(8,128)(2,1)S(1)}, u32[]{:S(2)}, u32[]{:S(2)}) collective-permute-start(bf16[128,512]{1,0:T(8,128)(2,1)S(1)} %get-tuple-element.16), channel_id=1, source_target_pairs={{0,2},{1,9},{2,4},{3,11},{4,6},{5,13},{6,0},{7,15},{8,10},{9,17},{... | collective-permute-start | bytes 393224 | tf_op jit(solution)/shard_map/ppermute | solution.py:32
  44.4 7.2 %collective-permute-start.16 = (bf16[128,512]{1,0:T(8,128)(2,1)S(1)}, bf16[128,512]{1,0:T(8,128)(2,1)S(1)}, u32[]{:S(2)}, u32[]{:S(2)}) collective-permute-start(bf16[128,512]{1,0:T(8,128)(2,1)S(1)} %get-tuple-element.16), channel_id=1, source_target_pairs={{0,4},{1,17},{2,6},{3,19},{4,0},{5,21},{6,2},{7,23},{8,12},{9,25},... | collective-permute-start | bytes 393224 | tf_op jit(solution)/shard_map/ppermute | solution.py:32
  47.3 5.0 %collective-permute-start.17 = (bf16[128,512]{1,0:T(8,128)(2,1)S(1)}, bf16[128,512]{1,0:T(8,128)(2,1)S(1)}, u32[]{:S(2)}, u32[]{:S(2)}) collective-permute-start(bf16[128,512]{1,0:T(8,128)(2,1)S(1)} %get-tuple-element.16), channel_id=1, source_target_pairs={{0,6},{1,25},{2,0},{3,27},{4,2},{5,29},{6,4},{7,31},{8,14},{9,1},{... | collective-permute-start | bytes 393224 | tf_op jit(solution)/shard_map/ppermute | solution.py:32
  48.3 13.2 %collective-permute-start.14 = (bf16[512,512]{1,0:T(8,128)(2,1)S(1)}, bf16[512,512]{1,0:T(8,128)(2,1)S(1)}, u32[]{:S(2)}, u32[]{:S(2)}) collective-permute-start(bf16[512,512]{1,0:T(8,128)(2,1)S(1)} %get-tuple-element.14.current_ref.refs_0_), channel_id=1, source_target_pairs={{0,32},{32,64},{64,96},{96,0},{1,33},{33,65},{65,97},{97,1},{2,34}... | collective-permute-start | bytes 1572872 | tf_op jit(solution)/shard_map/ppermute | solution.py:41
  52.3 16.1 %collective-permute-start.18 = (bf16[512,512]{1,0:T(8,128)(2,1)S(1)}, bf16[512,512]{1,0:T(8,128)(2,1)S(1)}, u32[]{:S(2)}, u32[]{:S(2)}) collective-permute-start(bf16[512,512]{1,0:T(8,128)(2,1)S(1)} %constant_dynamic-update-slice_fusion.rest_0_), channel_id=1, source_target_pairs={{0,8},{1,3},{2,10},{3,5},{4,12},{5,7},{6,14},{7,1},{8,16},{9,11},{... | collective-permute-start | bytes 1572872 | tf_op jit(solution)/shard_map/ppermute | solution.py:32
  53.0 15.3 %collective-permute-start.19 = (bf16[512,512]{1,0:T(8,128)(2,1)S(1)}, bf16[512,512]{1,0:T(8,128)(2,1)S(1)}, u32[]{:S(2)}, u32[]{:S(2)}) collective-permute-start(bf16[512,512]{1,0:T(8,128)(2,1)S(1)} %constant_dynamic-update-slice_fusion.rest_0_), channel_id=1, source_target_pairs={{0,16},{1,5},{2,18},{3,7},{4,20},{5,1},{6,22},{7,3},{8,24},{9,13},... | collective-permute-start | bytes 1572872 | tf_op jit(solution)/shard_map/ppermute | solution.py:32
  55.2 14.1 %collective-permute-start.20 = (bf16[512,512]{1,0:T(8,128)(2,1)S(1)}, bf16[512,512]{1,0:T(8,128)(2,1)S(1)}, u32[]{:S(2)}, u32[]{:S(2)}) collective-permute-start(bf16[512,512]{1,0:T(8,128)(2,1)S(1)} %constant_dynamic-update-slice_fusion.rest_0_), channel_id=1, source_target_pairs={{0,24},{1,7},{2,26},{3,1},{4,28},{5,3},{6,30},{7,5},{8,0},{9,15},{... | collective-permute-start | bytes 1572872 | tf_op jit(solution)/shard_map/ppermute | solution.py:32
  56.7 12.6 %collective-permute-start.25 = (bf16[512,512]{1,0:T(8,128)(2,1)S(1)}, bf16[512,512]{1,0:T(8,128)(2,1)S(1)}, u32[]{:S(2)}, u32[]{:S(2)}) collective-permute-start(bf16[512,512]{1,0:T(8,128)(2,1)S(1)} %get-tuple-element.14.current_ref.refs_0_), channel_id=1, source_target_pairs={{32,0},{64,32},{33,1},{65,33},{34,2},{66,34},{35,3},{67,35},{36,4}... | collective-permute-start | bytes 1572872 | tf_op jit(solution)/shard_map/ppermute | solution.py:41
  61.6 7.7 %collective-permute-start.21 = (bf16[512,512]{1,0:T(8,128)(2,1)S(1)}, bf16[512,512]{1,0:T(8,128)(2,1)S(1)}, u32[]{:S(2)}, u32[]{:S(2)}) collective-permute-start(bf16[512,512]{1,0:T(8,128)(2,1)S(1)} %constant_dynamic-update-slice_fusion.rest_0_), channel_id=1, source_target_pairs={{0,1},{1,0},{2,3},{3,2},{4,5},{5,4},{6,7},{7,6},{8,9},{9,8},{10,11... | collective-permute-start | bytes 1572872 | tf_op jit(solution)/shard_map/ppermute | solution.py:37
  68.4 1.9 %collective-permute-start.22 = (bf16[512,512]{1,0:T(8,128)(2,1)S(1)}, bf16[512,512]{1,0:T(8,128)(2,1)S(1)}, u32[]{:S(2)}, u32[]{:S(2)}) collective-permute-start(bf16[512,512]{1,0:T(8,128)(2,1)S(1)} %collective-permute-done.18.rest_1_), channel_id=1, source_target_pairs={{0,1},{1,0},{2,3},{3,2},{4,5},{5,4},{6,7},{7,6},{8,9},{9,8},{10,11... | collective-permute-start | bytes 1572872 | tf_op jit(solution)/shard_map/ppermute | solution.py:37
  68.4 2.7 %collective-permute-start.23 = (bf16[512,512]{1,0:T(8,128)(2,1)S(1)}, bf16[512,512]{1,0:T(8,128)(2,1)S(1)}, u32[]{:S(2)}, u32[]{:S(2)}) collective-permute-start(bf16[512,512]{1,0:T(8,128)(2,1)S(1)} %collective-permute-done.19.rest_2_), channel_id=1, source_target_pairs={{0,1},{1,0},{2,3},{3,2},{4,5},{5,4},{6,7},{7,6},{8,9},{9,8},{10,11... | collective-permute-start | bytes 1572872 | tf_op jit(solution)/shard_map/ppermute | solution.py:37
  69.3 2.5 %collective-permute-start.24 = (bf16[512,512]{1,0:T(8,128)(2,1)S(1)}, bf16[512,512]{1,0:T(8,128)(2,1)S(1)}, u32[]{:S(2)}, u32[]{:S(2)}) collective-permute-start(bf16[512,512]{1,0:T(8,128)(2,1)S(1)} %collective-permute-done.20.rest_3_), channel_id=1, source_target_pairs={{0,1},{1,0},{2,3},{3,2},{4,5},{5,4},{6,7},{7,6},{8,9},{9,8},{10,11... | collective-permute-start | bytes 1572872 | tf_op jit(solution)/shard_map/ppermute | solution.py:37
  74.4 7.3 %collective-permute-start.28 = (bf16[128,512]{1,0:T(8,128)(2,1)S(1)}, bf16[128,512]{1,0:T(8,128)(2,1)S(1)}, u32[]{:S(2)}, u32[]{:S(2)}) collective-permute-start(bf16[128,512]{1,0:T(8,128)(2,1)S(1)} %get-tuple-element.19), channel_id=1, source_target_pairs={{0,2},{1,9},{2,4},{3,11},{4,6},{5,13},{6,0},{7,15},{8,10},{9,17},{... | collective-permute-start | bytes 393224 | tf_op jit(solution)/shard_map/ppermute | solution.py:32
  75.6 6.9 %collective-permute-start.29 = (bf16[128,512]{1,0:T(8,128)(2,1)S(1)}, bf16[128,512]{1,0:T(8,128)(2,1)S(1)}, u32[]{:S(2)}, u32[]{:S(2)}) collective-permute-start(bf16[128,512]{1,0:T(8,128)(2,1)S(1)} %get-tuple-element.19), channel_id=1, source_target_pairs={{0,4},{1,17},{2,6},{3,19},{4,0},{5,21},{6,2},{7,23},{8,12},{9,25},... | collective-permute-start | bytes 393224 | tf_op jit(solution)/shard_map/ppermute | solution.py:32
  78.2 5.0 %collective-permute-start.30 = (bf16[128,512]{1,0:T(8,128)(2,1)S(1)}, bf16[128,512]{1,0:T(8,128)(2,1)S(1)}, u32[]{:S(2)}, u32[]{:S(2)}) collective-permute-start(bf16[128,512]{1,0:T(8,128)(2,1)S(1)} %get-tuple-element.19), channel_id=1, source_target_pairs={{0,6},{1,25},{2,0},{3,27},{4,2},{5,29},{6,4},{7,31},{8,14},{9,1},{... | collective-permute-start | bytes 393224 | tf_op jit(solution)/shard_map/ppermute | solution.py:32
  79.0 12.7 %collective-permute-start.26 = (bf16[512,512]{1,0:T(8,128)(2,1)S(1)}, bf16[512,512]{1,0:T(8,128)(2,1)S(1)}, u32[]{:S(2)}, u32[]{:S(2)}) collective-permute-start(bf16[512,512]{1,0:T(8,128)(2,1)S(1)} %get-tuple-element.17), channel_id=1, source_target_pairs={{64,32},{96,64},{32,0},{65,33},{97,65},{33,1},{66,34},{98,66},{34,... | collective-permute-start | bytes 1572872 | tf_op jit(solution)/shard_map/ppermute | solution.py:41
  83.2 10.5 %collective-permute-start.31 = (bf16[512,512]{1,0:T(8,128)(2,1)S(1)}, bf16[512,512]{1,0:T(8,128)(2,1)S(1)}, u32[]{:S(2)}, u32[]{:S(2)}) collective-permute-start(bf16[512,512]{1,0:T(8,128)(2,1)S(1)} %constant_dynamic-update-slice_fusion.4.rest_0_), channel_id=1, source_target_pairs={{0,8},{1,3},{2,10},{3,5},{4,12},{5,7},{6,14},{7,1},{8,16},{9,11},{... | collective-permute-start | bytes 1572872 | tf_op jit(solution)/shard_map/ppermute | solution.py:32
  83.7 15.8 %collective-permute-start.32 = (bf16[512,512]{1,0:T(8,128)(2,1)S(1)}, bf16[512,512]{1,0:T(8,128)(2,1)S(1)}, u32[]{:S(2)}, u32[]{:S(2)}) collective-permute-start(bf16[512,512]{1,0:T(8,128)(2,1)S(1)} %constant_dynamic-update-slice_fusion.4.rest_0_), channel_id=1, source_target_pairs={{0,16},{1,5},{2,18},{3,7},{4,20},{5,1},{6,22},{7,3},{8,24},{9,13},... | collective-permute-start | bytes 1572872 | tf_op jit(solution)/shard_map/ppermute | solution.py:32
  86.8 13.4 %collective-permute-start.33 = (bf16[512,512]{1,0:T(8,128)(2,1)S(1)}, bf16[512,512]{1,0:T(8,128)(2,1)S(1)}, u32[]{:S(2)}, u32[]{:S(2)}) collective-permute-start(bf16[512,512]{1,0:T(8,128)(2,1)S(1)} %constant_dynamic-update-slice_fusion.4.rest_0_), channel_id=1, source_target_pairs={{0,24},{1,7},{2,26},{3,1},{4,28},{5,3},{6,30},{7,5},{8,0},{9,15},{... | collective-permute-start | bytes 1572872 | tf_op jit(solution)/shard_map/ppermute | solution.py:32
  87.0 13.2 %collective-permute-start.27 = (bf16[512,512]{1,0:T(8,128)(2,1)S(1)}, bf16[512,512]{1,0:T(8,128)(2,1)S(1)}, u32[]{:S(2)}, u32[]{:S(2)}) collective-permute-start(bf16[512,512]{1,0:T(8,128)(2,1)S(1)} %get-tuple-element.18.current_ref.refs_4_), channel_id=1, source_target_pairs={{0,32},{32,64},{64,96},{96,0},{1,33},{33,65},{65,97},{97,1},{2,34}... | collective-permute-start | bytes 1572872 | tf_op jit(solution)/shard_map/ppermute | solution.py:41
  91.7 8.5 %collective-permute-start.34 = (bf16[512,512]{1,0:T(8,128)(2,1)S(1)}, bf16[512,512]{1,0:T(8,128)(2,1)S(1)}, u32[]{:S(2)}, u32[]{:S(2)}) collective-permute-start(bf16[512,512]{1,0:T(8,128)(2,1)S(1)} %constant_dynamic-update-slice_fusion.4.rest_0_), channel_id=1, source_target_pairs={{0,1},{1,0},{2,3},{3,2},{4,5},{5,4},{6,7},{7,6},{8,9},{9,8},{10,11... | collective-permute-start | bytes 1572872 | tf_op jit(solution)/shard_map/ppermute | solution.py:37
  93.7 6.5 %collective-permute-start.35 = (bf16[512,512]{1,0:T(8,128)(2,1)S(1)}, bf16[512,512]{1,0:T(8,128)(2,1)S(1)}, u32[]{:S(2)}, u32[]{:S(2)}) collective-permute-start(bf16[512,512]{1,0:T(8,128)(2,1)S(1)} %collective-permute-done.31.rest_1_), channel_id=1, source_target_pairs={{0,1},{1,0},{2,3},{3,2},{4,5},{5,4},{6,7},{7,6},{8,9},{9,8},{10,11... | collective-permute-start | bytes 1572872 | tf_op jit(solution)/shard_map/ppermute | solution.py:37
  99.6 1.9 %collective-permute-start.36 = (bf16[512,512]{1,0:T(8,128)(2,1)S(1)}, bf16[512,512]{1,0:T(8,128)(2,1)S(1)}, u32[]{:S(2)}, u32[]{:S(2)}) collective-permute-start(bf16[512,512]{1,0:T(8,128)(2,1)S(1)} %collective-permute-done.32.rest_2_), channel_id=1, source_target_pairs={{0,1},{1,0},{2,3},{3,2},{4,5},{5,4},{6,7},{7,6},{8,9},{9,8},{10,11... | collective-permute-start | bytes 1572872 | tf_op jit(solution)/shard_map/ppermute | solution.py:37
  100.2 2.0 %collective-permute-start.37 = (bf16[512,512]{1,0:T(8,128)(2,1)S(1)}, bf16[512,512]{1,0:T(8,128)(2,1)S(1)}, u32[]{:S(2)}, u32[]{:S(2)}) collective-permute-start(bf16[512,512]{1,0:T(8,128)(2,1)S(1)} %collective-permute-done.33.rest_3_), channel_id=1, source_target_pairs={{0,1},{1,0},{2,3},{3,2},{4,5},{5,4},{6,7},{7,6},{8,9},{9,8},{10,11... | collective-permute-start | bytes 1572872 | tf_op jit(solution)/shard_map/ppermute | solution.py:37
  104.8 7.2 %collective-permute-start.41 = (bf16[128,512]{1,0:T(8,128)(2,1)S(1)}, bf16[128,512]{1,0:T(8,128)(2,1)S(1)}, u32[]{:S(2)}, u32[]{:S(2)}) collective-permute-start(bf16[128,512]{1,0:T(8,128)(2,1)S(1)} %get-tuple-element.22), channel_id=1, source_target_pairs={{0,2},{1,9},{2,4},{3,11},{4,6},{5,13},{6,0},{7,15},{8,10},{9,17},{... | collective-permute-start | bytes 393224 | tf_op jit(solution)/shard_map/ppermute | solution.py:32
  105.8 7.3 %collective-permute-start.42 = (bf16[128,512]{1,0:T(8,128)(2,1)S(1)}, bf16[128,512]{1,0:T(8,128)(2,1)S(1)}, u32[]{:S(2)}, u32[]{:S(2)}) collective-permute-start(bf16[128,512]{1,0:T(8,128)(2,1)S(1)} %get-tuple-element.22), channel_id=1, source_target_pairs={{0,4},{1,17},{2,6},{3,19},{4,0},{5,21},{6,2},{7,23},{8,12},{9,25},... | collective-permute-start | bytes 393224 | tf_op jit(solution)/shard_map/ppermute | solution.py:32
  108.7 5.0 %collective-permute-start.43 = (bf16[128,512]{1,0:T(8,128)(2,1)S(1)}, bf16[128,512]{1,0:T(8,128)(2,1)S(1)}, u32[]{:S(2)}, u32[]{:S(2)}) collective-permute-start(bf16[128,512]{1,0:T(8,128)(2,1)S(1)} %get-tuple-element.22), channel_id=1, source_target_pairs={{0,6},{1,25},{2,0},{3,27},{4,2},{5,29},{6,4},{7,31},{8,14},{9,1},{... | collective-permute-start | bytes 393224 | tf_op jit(solution)/shard_map/ppermute | solution.py:32
  109.1 16.4 %collective-permute-start.38 = (bf16[512,512]{1,0:T(8,128)(2,1)S(1)}, bf16[512,512]{1,0:T(8,128)(2,1)S(1)}, u32[]{:S(2)}, u32[]{:S(2)}) collective-permute-start(bf16[512,512]{1,0:T(8,128)(2,1)S(1)} %get-tuple-element.20), channel_id=1, source_target_pairs={{96,64},{0,96},{64,32},{97,65},{1,97},{65,33},{98,66},{2,98},{66,3... | collective-permute-start | bytes 1572872 | tf_op jit(solution)/shard_map/ppermute | solution.py:41
  113.8 11.7 %collective-permute-start.44 = (bf16[512,512]{1,0:T(8,128)(2,1)S(1)}, bf16[512,512]{1,0:T(8,128)(2,1)S(1)}, u32[]{:S(2)}, u32[]{:S(2)}) collective-permute-start(bf16[512,512]{1,0:T(8,128)(2,1)S(1)} %constant_dynamic-update-slice_fusion.8.rest_0_), channel_id=1, source_target_pairs={{0,8},{1,3},{2,10},{3,5},{4,12},{5,7},{6,14},{7,1},{8,16},{9,11},{... | collective-permute-start | bytes 1572872 | tf_op jit(solution)/shard_map/ppermute | solution.py:32
  114.2 16.4 %collective-permute-start.45 = (bf16[512,512]{1,0:T(8,128)(2,1)S(1)}, bf16[512,512]{1,0:T(8,128)(2,1)S(1)}, u32[]{:S(2)}, u32[]{:S(2)}) collective-permute-start(bf16[512,512]{1,0:T(8,128)(2,1)S(1)} %constant_dynamic-update-slice_fusion.8.rest_0_), channel_id=1, source_target_pairs={{0,16},{1,5},{2,18},{3,7},{4,20},{5,1},{6,22},{7,3},{8,24},{9,13},... | collective-permute-start | bytes 1572872 | tf_op jit(solution)/shard_map/ppermute | solution.py:32
  117.9 12.9 %collective-permute-start.46 = (bf16[512,512]{1,0:T(8,128)(2,1)S(1)}, bf16[512,512]{1,0:T(8,128)(2,1)S(1)}, u32[]{:S(2)}, u32[]{:S(2)}) collective-permute-start(bf16[512,512]{1,0:T(8,128)(2,1)S(1)} %constant_dynamic-update-slice_fusion.8.rest_0_), channel_id=1, source_target_pairs={{0,24},{1,7},{2,26},{3,1},{4,28},{5,3},{6,30},{7,5},{8,0},{9,15},{... | collective-permute-start | bytes 1572872 | tf_op jit(solution)/shard_map/ppermute | solution.py:32
  117.9 13.3 %collective-permute-start.39 = (bf16[512,512]{1,0:T(8,128)(2,1)S(1)}, bf16[512,512]{1,0:T(8,128)(2,1)S(1)}, u32[]{:S(2)}, u32[]{:S(2)}) collective-permute-start(bf16[512,512]{1,0:T(8,128)(2,1)S(1)} %get-tuple-element.21.current_ref.refs_8_), channel_id=1, source_target_pairs={{0,32},{32,64},{64,96},{96,0},{1,33},{33,65},{65,97},{97,1},{2,34}... | collective-permute-start | bytes 1572872 | tf_op jit(solution)/shard_map/ppermute | solution.py:41
  125.5 8.4 %collective-permute-start.47 = (bf16[512,512]{1,0:T(8,128)(2,1)S(1)}, bf16[512,512]{1,0:T(8,128)(2,1)S(1)}, u32[]{:S(2)}, u32[]{:S(2)}) collective-permute-start(bf16[512,512]{1,0:T(8,128)(2,1)S(1)} %constant_dynamic-update-slice_fusion.8.rest_0_), channel_id=1, source_target_pairs={{0,1},{1,0},{2,3},{3,2},{4,5},{5,4},{6,7},{7,6},{8,9},{9,8},{10,11... | collective-permute-start | bytes 1572872 | tf_op jit(solution)/shard_map/ppermute | solution.py:37
  125.5 8.4 %collective-permute-start.48 = (bf16[512,512]{1,0:T(8,128)(2,1)S(1)}, bf16[512,512]{1,0:T(8,128)(2,1)S(1)}, u32[]{:S(2)}, u32[]{:S(2)}) collective-permute-start(bf16[512,512]{1,0:T(8,128)(2,1)S(1)} %collective-permute-done.44.rest_1_), channel_id=1, source_target_pairs={{0,1},{1,0},{2,3},{3,2},{4,5},{5,4},{6,7},{7,6},{8,9},{9,8},{10,11... | collective-permute-start | bytes 1572872 | tf_op jit(solution)/shard_map/ppermute | solution.py:37
  130.6 3.3 %collective-permute-start.49 = (bf16[512,512]{1,0:T(8,128)(2,1)S(1)}, bf16[512,512]{1,0:T(8,128)(2,1)S(1)}, u32[]{:S(2)}, u32[]{:S(2)}) collective-permute-start(bf16[512,512]{1,0:T(8,128)(2,1)S(1)} %collective-permute-done.45.rest_2_), channel_id=1, source_target_pairs={{0,1},{1,0},{2,3},{3,2},{4,5},{5,4},{6,7},{7,6},{8,9},{9,8},{10,11... | collective-permute-start | bytes 1572872 | tf_op jit(solution)/shard_map/ppermute | solution.py:37
  130.8 3.2 %collective-permute-start.50 = (bf16[512,512]{1,0:T(8,128)(2,1)S(1)}, bf16[512,512]{1,0:T(8,128)(2,1)S(1)}, u32[]{:S(2)}, u32[]{:S(2)}) collective-permute-start(bf16[512,512]{1,0:T(8,128)(2,1)S(1)} %collective-permute-done.46.rest_3_), channel_id=1, source_target_pairs={{0,1},{1,0},{2,3},{3,2},{4,5},{5,4},{6,7},{7,6},{8,9},{9,8},{10,11... | collective-permute-start | bytes 1572872 | tf_op jit(solution)/shard_map/ppermute | solution.py:37
  131.1 14.2 %collective-permute-start.40 = (bf16[512,512]{1,0:T(8,128)(2,1)S(1)}, bf16[512,512]{1,0:T(8,128)(2,1)S(1)}, u32[]{:S(2)}, u32[]{:S(2)}) collective-permute-start(bf16[512,512]{1,0:T(8,128)(2,1)S(1)} %collective-permute-done.38.rest_8_.refs_6_.refs_11_), channel_id=1, source_target_pairs={{96,64},{97,65},{98,66},{99,67},{100,68},{101,69},{102,70},{103,71... | collective-permute-start | bytes 1572872 | tf_op jit(solution)/shard_map/ppermute | solution.py:41
  136.4 15.9 %collective-permute-start.51 = (bf16[512,512]{1,0:T(8,128)(2,1)S(1)}, bf16[512,512]{1,0:T(8,128)(2,1)S(1)}, u32[]{:S(2)}, u32[]{:S(2)}) collective-permute-start(bf16[512,512]{1,0:T(8,128)(2,1)S(1)} %shard_map.77.refs_12_), channel_id=1, source_target_pairs={{64,96},{65,97},{66,98},{67,99},{68,100},{69,101},{70,102},{71,103... | collective-permute-start | bytes 1572872 | tf_op jit(solution)/shard_map/ppermute | solution.py:41
  137.7 22.4 %collective-permute-start.55 = (bf16[512,512]{1,0:T(8,128)(2,1)S(1)}, bf16[512,512]{1,0:T(8,128)(2,1)S(1)}, u32[]{:S(2)}, u32[]{:S(2)}) collective-permute-start(bf16[512,512]{1,0:T(8,128)(2,1)S(1)} %shard_map.77.refs_12_), channel_id=1, source_target_pairs={{0,96},{1,97},{2,98},{3,99},{4,100},{5,101},{6,102},{7,103},{8,104... | collective-permute-start | bytes 1572872 | tf_op jit(solution)/shard_map/ppermute | solution.py:41
  139.0 2.0 %collective-permute-start.52 = (bf16[256,512]{1,0:T(8,128)(2,1)S(1)}, bf16[256,512]{1,0:T(8,128)(2,1)S(1)}, u32[]{:S(2)}, u32[]{:S(2)}) collective-permute-start(bf16[256,512]{1,0:T(8,128)(2,1)S(1)} %get-tuple-element.26), channel_id=1, source_target_pairs={{32,64},{33,65},{34,66},{35,67},{36,68},{37,69},{38,70},{39,71},{4... | collective-permute-start | bytes 786440 | tf_op jit(solution)/shard_map/ppermute | solution.py:41
  139.7 12.5 %collective-permute-start.54 = (bf16[256,512]{1,0:T(8,128)(2,1)S(1)}, bf16[256,512]{1,0:T(8,128)(2,1)S(1)}, u32[]{:S(2)}, u32[]{:S(2)}) collective-permute-start(bf16[256,512]{1,0:T(8,128)(2,1)S(1)} %get-tuple-element.25), channel_id=1, source_target_pairs={{32,96},{33,97},{34,98},{35,99},{36,100},{37,101},{38,102},{39,103... | collective-permute-start | bytes 786440 | tf_op jit(solution)/shard_map/ppermute | solution.py:41
  141.0 19.1 %collective-permute-start.53 = (bf16[256,512]{1,0:T(8,128)(2,1)S(1)}, bf16[256,512]{1,0:T(8,128)(2,1)S(1)}, u32[]{:S(2)}, u32[]{:S(2)}) collective-permute-start(bf16[256,512]{1,0:T(8,128)(2,1)S(1)} %collective-permute-done.52), channel_id=1, source_target_pairs={{64,96},{65,97},{66,98},{67,99},{68,100},{69,101},{70,102},{71,103... | collective-permute-start | bytes 786440 | tf_op jit(solution)/shard_map/ppermute | solution.py:41

commit v5 on v4

--- a/solution.py
+++ b/solution.py
@@ -13,6 +13,7 @@
 EXTRA = 16
 ANY = pl.BlockSpec(memory_space=pl.ANY)
 SMEM = pl.BlockSpec(memory_space=pltpu.SMEM)
+HBM = pl.BlockSpec(memory_space=pltpu.HBM)
 VMEM = pl.BlockSpec(memory_space=pltpu.VMEM)
 PLACES = [(z, y, core) for z in range(SIDE) for y in range(SIDE) for core in range(CORES)]
 
@@ -83,7 +84,6 @@
     each = mine_refs[0].shape[0] // SIDE
     if first:
         lists = rest[outs + 2]
-        lists[...] = jnp.zeros_like(lists)
         lane_block = pl.ds(pl.multiple_of((node // EXTRA) * TILE, TILE), TILE)
         wanted = lax.broadcasted_iota(jnp.int32, (EXTRA, TILE), 0) == node % EXTRA
     for refs, kind in ((mine_refs, core), (theirs_refs, 1 - core)):
@@ -97,7 +97,7 @@
                 if first:
                     raw = refs[j][pl.ds(k * each + offered, EXTRA), lane_block].astype(jnp.float32)
                     row = jnp.sum(jnp.where(wanted, raw, 0.0), axis=0, keepdims=True)
-                    lists[pl.ds(chip, 1), :] += row
+                    lists[pl.ds(chip + kind * SIDE * SIDE, 1), :] = row
     space[pl.ds(0, row_count), :] = current_ref[...]
 
     @pl.when(span == 0)
@@ -126,7 +126,9 @@
         col = cols_ref[span, f]
         if first:
             plain = lanes + TILE * (col % CORES)
-            listed = lists[pl.ds(jnp.maximum(col - own_tiles, 0), 1), :].astype(jnp.int32) + shift
+            chip = jnp.maximum(col - own_tiles, 0)
+            listed = lists[pl.ds(chip, 1), :] + lists[pl.ds(chip + SIDE * SIDE, 1), :]
+            listed = listed.astype(jnp.int32) + shift
             target = jnp.where(col < own_tiles, plain, listed)
             selector = (slot_rows == target).astype(jnp.bfloat16)
             wide = lax.dot_general(
@@ -163,35 +165,27 @@
             moved_ref[...] = fresh
 
 
-def place_kernel(place_ref, *refs):
-    out_ref, held, in_sems, out_sems = refs[-4:]
+def place_kernel(*refs):
+    out_ref, sems = refs[-2:]
     spans = out_ref.shape[0]
-    span = place_ref[0]
+    span = lax.axis_index("layer")
     first_ref = 0
     for layer_id in range(spans):
-        halved = 2 if layer_id == spans - 1 else 1
-        parts = []
-        for distance in range(spans):
-            pieces = halved if distance == 2 else 1
-            rows = held.shape[1] // pieces
-            parts += [(distance, rows * i, rows) for i in range(pieces)]
+        parts = [0, 1, 2, 2, 3] if layer_id == spans - 1 else list(range(spans))
         sources = refs[first_ref:first_ref + len(parts)]
         first_ref += len(parts)
 
         @pl.when(span == layer_id)
         def _():
-            ins, outs = [], []
-            for i, (distance, start, rows) in enumerate(parts):
-                staged = held.at[distance, pl.ds(start, rows)]
-                target = out_ref.at[(layer_id - distance) % spans, pl.ds(start, rows)]
-                ins.append(pltpu.make_async_copy(sources[i], staged, in_sems.at[i]))
-                outs.append(pltpu.make_async_copy(staged, target, out_sems.at[i]))
-            for copy in ins:
+            copies, start = [], 0
+            for i, (distance, source) in enumerate(zip(parts, sources)):
+                rows = source.shape[0]
+                target = out_ref.at[(layer_id - distance) % spans, pl.ds(start % out_ref.shape[1], rows)]
+                start += rows
+                copies.append(pltpu.make_async_copy(source, target, sems.at[i]))
+            for copy in copies:
                 copy.start()
-            for i in range(len(parts)):
-                ins[i].wait()
-                outs[i].start()
-            for copy in outs:
+            for copy in copies:
                 copy.wait()
 
 
@@ -243,7 +237,7 @@
             pltpu.VMEM((row_count, width), jnp.float32),
         ]
         if first:
-            scratch.append(pltpu.VMEM((SIDE * SIDE, TILE), jnp.float32))
+            scratch.append(pltpu.VMEM((CORES * SIDE * SIDE, TILE), jnp.float32))
         outs = [rows_shape] if last else [rows_shape, block_shape]
         if first:
             outs.append(wide_shape)
@@ -288,15 +282,11 @@
     return pl.pallas_call(
         place_kernel,
         out_shape=jax.ShapeDtypeStruct(features.shape, features.dtype),
-        in_specs=[SMEM] + [ANY] * len(placed),
-        out_specs=ANY,
-        scratch_shapes=[
-            pltpu.VMEM(features.shape, features.dtype),
-            pltpu.SemaphoreType.DMA((5,)),
-            pltpu.SemaphoreType.DMA((5,)),
-        ],
+        in_specs=[VMEM] * len(placed),
+        out_specs=HBM,
+        scratch_shapes=[pltpu.SemaphoreType.DMA((5,))],
         compiler_params=params,
-    )(place, *placed)
+    )(*placed)
 
 
 def solution(mesh):

time: 163 us -> 162 us (level)
  no operation moved by 1% of the time
where the time goes in v5:
time: 162 us
  waiting for transfers between devices  73 us (45%)
  starting transfers between devices  67.2 us (41%)
  Pallas kernels  14.9 us (9%)
  local copies, waits for them, and re-layouts  4.78 us (3%)
    ppermute x24, starting transfers between devices, along(): return lax.ppermute(block, 'node', route)  39.1 us
    ppermute x24, waiting for transfers between devices, along(): return lax.ppermute(block, 'node', route)  33.4 us
    ppermute x15, waiting for transfers between devices, to_plane(): return lax.ppermute(block, 'layer', pairs)  32.8 us
    ppermute x15, starting transfers between devices, to_plane(): return lax.ppermute(block, 'layer', pairs)  25.5 us
    pallas_call x4, Pallas kernels, on_device(): pl.pallas_call(functools.partial(layer_kernel, layer_id, first, last), ou...  12.7 us
    ppermute x17, waiting for transfers between devices, other_core(): return lax.ppermute(block, 'node', route)  6.75 us
  transfers between devices with their start and end apart: 56, of which 30 were waited for; matrix products, arithmetic and copies ran while one was open for 1% of the time, Pallas kernels for 1%

profile of v5, /device:TPU:6, one launch (start us, length us, event | category | flops | bytes accessed | tf_op | source)
XLA Modules:
  0.0 161.5 jit_solution(15433931017642164188)
XLA Ops:
  0.0 0.8 fusion.listed_ref
  0.8 0.7 dynamic-slice_bitcast_fusion.4.lists_ref
  1.5 2.1 %dynamic-slice_bitcast_fusion.1 = (bf16[512,512]{1,0:T(8,128)(2,1)}, bf16[512,512]{1,0:T(8,128)(2,1)S(1)}) fusion(bf16[4,512,512]{2,1,0:T(8,128)(2,1)} %param.7, s32[]{:T(128)S(6)} %max.3, s32[]{:T(128)S(6)} %select_n.21), kind=kLoop, calls=%fused_computation.3 | loop fusion | bytes 2097160 | tf_op jit(solution)/shard_map/jit(dynamic_index_in_dim)/squeeze | solution.py:216
  3.7 0.8 shard_map.73
  4.5 1.6 %collective-permute-start.4 = (bf16[144,512]{1,0:T(8,128)(2,1)S(1)}, bf16[144,512]{1,0:T(8,128)(2,1)S(1)}, u32[]{:S(2)}, u32[]{:S(2)}) collective-permute-start(bf16[144,512]{1,0:T(8,128)(2,1)S(1)} %shard_map.73), channel_id=1, source_target_pairs={{0,2},{1,9},{2,4},{3,11},{4,6},{5,13},{6,0},{7,15},{8,10},{9,17},{... | collective-permute-start | bytes 442376 | tf_op jit(solution)/shard_map/ppermute | solution.py:33
  6.1 2.9 %collective-permute-start.5 = (bf16[144,512]{1,0:T(8,128)(2,1)S(1)}, bf16[144,512]{1,0:T(8,128)(2,1)}, u32[]{:S(2)}, u32[]{:S(2)}) collective-permute-start(bf16[144,512]{1,0:T(8,128)(2,1)S(1)} %shard_map.73), channel_id=1, source_target_pairs={{0,4},{1,17},{2,6},{3,19},{4,0},{5,21},{6,2},{7,23},{8,12},{9,25},... | collective-permute-start | bytes 442376 | tf_op jit(solution)/shard_map/ppermute | solution.py:33
  9.0 1.3 collective-permute-start.6
  10.4 1.0 dynamic-slice_bitcast_fusion.3
  12.0 2.3 %collective-permute-start.1 = (bf16[256,512]{1,0:T(8,128)(2,1)S(1)}, bf16[256,512]{1,0:T(8,128)(2,1)S(1)}, u32[]{:S(2)}, u32[]{:S(2)}) collective-permute-start(bf16[256,512]{1,0:T(8,128)(2,1)S(1)} %dynamic-slice_bitcast_fusion.3), channel_id=1, source_target_pairs={{0,64},{32,96},{64,0},{96,32},{1,65},{33,97},{65,1},{97,33},{2,66}... | collective-permute-start | bytes 786440 | tf_op jit(solution)/shard_map/ppermute | solution.py:42
  14.4 1.0 pad_maximum_fusion.1.rest_0_
  15.4 2.0 %collective-permute-start.7 = (bf16[576,512]{1,0:T(8,128)(2,1)S(1)}, bf16[576,512]{1,0:T(8,128)(2,1)S(1)}, u32[]{:S(2)}, u32[]{:S(2)}) collective-permute-start(bf16[576,512]{1,0:T(8,128)(2,1)S(1)} %pad_maximum_fusion.1.rest_0_), channel_id=1, source_target_pairs={{0,8},{1,3},{2,10},{3,5},{4,12},{5,7},{6,14},{7,1},{8,16},{9,11},{... | collective-permute-start | bytes 1769480 | tf_op jit(solution)/shard_map/ppermute | solution.py:33
  17.4 3.6 %collective-permute-start.8 = (bf16[576,512]{1,0:T(8,128)(2,1)S(1)}, bf16[576,512]{1,0:T(8,128)(2,1)S(1)}, u32[]{:S(2)}, u32[]{:S(2)}) collective-permute-start(bf16[576,512]{1,0:T(8,128)(2,1)S(1)} %pad_maximum_fusion.1.rest_0_), channel_id=1, source_target_pairs={{0,16},{1,5},{2,18},{3,7},{4,20},{5,1},{6,22},{7,3},{8,24},{9,13},... | collective-permute-start | bytes 1769480 | tf_op jit(solution)/shard_map/ppermute | solution.py:33
  21.0 1.5 collective-permute-start.9
  22.8 4.0 %collective-permute-done.2 = bf16[256,512]{1,0:T(8,128)(2,1)S(1)} collective-permute-done((bf16[256,512]{1,0:T(8,128)(2,1)S(1)}, bf16[256,512]{1,0:T(8,128)(2,1)S(1)}, u32[]{:S(2)}, u32[]{:S(2)}) %collective-permute-start.2) | collective-permute-done | bytes 262176 | tf_op jit(solution)/shard_map/ppermute | solution.py:42
  27.6 7.5 %collective-permute-done.8.rest_2_ = bf16[576,512]{1,0:T(8,128)(2,1)S(1)} collective-permute-done((bf16[576,512]{1,0:T(8,128)(2,1)S(1)}, bf16[576,512]{1,0:T(8,128)(2,1)S(1)}, u32[]{:S(2)}, u32[]{:S(2)}) %collective-permute-start.8) | collective-permute-done | bytes 589856 | tf_op jit(solution)/shard_map/ppermute | solution.py:33
  35.7 1.4 collective-permute-done.12.rest_6_
  37.1 0.8 collective-permute-done.13.rest_7_
  38.0 5.2 %shard_map.74 = (bf16[512,512]{1,0:T(8,128)(2,1)S(1)}, bf16[128,512]{1,0:T(8,128)(2,1)S(1)}, bf16[20,128,256]{2,1,0:T(8,128)(2,1)S(1)}) custom-call(s32[2]{0:T(128)S(1)} %pad_add_fusion.place_ref, s32[4,4]{1,0:T(4,128)S(1)} %bitcast.16, s32[4,20]{1,0:T(4,128)S(1)} %bitcast.20, s32[1,128]{1,0:T(1,128)S(1)} %fusion.listed_ref, ...), custom_call_target="tpu_custom_call" | custom-call | tf_op jit(solution)/shard_map/pallas_call | solution.py:246
  43.2 1.2 collective-permute-start.15
  44.3 2.8 %collective-permute-start.16 = (bf16[128,512]{1,0:T(8,128)(2,1)S(1)}, bf16[128,512]{1,0:T(8,128)(2,1)S(1)}, u32[]{:S(2)}, u32[]{:S(2)}) collective-permute-start(bf16[128,512]{1,0:T(8,128)(2,1)S(1)} %get-tuple-element.16), channel_id=1, source_target_pairs={{0,4},{1,17},{2,6},{3,19},{4,0},{5,21},{6,2},{7,23},{8,12},{9,25},... | collective-permute-start | bytes 393224 | tf_op jit(solution)/shard_map/ppermute | solution.py:33
  47.2 1.1 collective-permute-start.17
  48.3 1.7 %collective-permute-start.14 = (bf16[512,512]{1,0:T(8,128)(2,1)S(1)}, bf16[512,512]{1,0:T(8,128)(2,1)S(1)}, u32[]{:S(2)}, u32[]{:S(2)}) collective-permute-start(bf16[512,512]{1,0:T(8,128)(2,1)S(1)} %get-tuple-element.14.current_ref.refs_0_), channel_id=1, source_target_pairs={{0,32},{32,64},{64,96},{96,0},{1,33},{33,65},{65,97},{97,1},{2,34}... | collective-permute-start | bytes 1572872 | tf_op jit(solution)/shard_map/ppermute | solution.py:42
  50.0 1.5 collective-permute-done.16
  51.5 0.7 collective-permute-done.17
  52.2 0.7 collective-permute-start.18
  53.0 2.1 %collective-permute-start.19 = (bf16[512,512]{1,0:T(8,128)(2,1)S(1)}, bf16[512,512]{1,0:T(8,128)(2,1)S(1)}, u32[]{:S(2)}, u32[]{:S(2)}) collective-permute-start(bf16[512,512]{1,0:T(8,128)(2,1)S(1)} %constant_dynamic-update-slice_fusion.rest_0_), channel_id=1, source_target_pairs={{0,16},{1,5},{2,18},{3,7},{4,20},{5,1},{6,22},{7,3},{8,24},{9,13},... | collective-permute-start | bytes 1572872 | tf_op jit(solution)/shard_map/ppermute | solution.py:33
  55.1 1.5 collective-permute-start.20
  57.3 4.2 %collective-permute-done.14.previous_ref.refs_1_ = bf16[512,512]{1,0:T(8,128)(2,1)S(1)} collective-permute-done((bf16[512,512]{1,0:T(8,128)(2,1)S(1)}, bf16[512,512]{1,0:T(8,128)(2,1)S(1)}, u32[]{:S(2)}, u32[]{:S(2)}) %collective-permute-start.14) | collective-permute-done | bytes 524320 | tf_op jit(solution)/shard_map/ppermute | solution.py:42
  61.5 6.8 %collective-permute-done.18.rest_1_ = bf16[512,512]{1,0:T(8,128)(2,1)S(1)} collective-permute-done((bf16[512,512]{1,0:T(8,128)(2,1)S(1)}, bf16[512,512]{1,0:T(8,128)(2,1)S(1)}, u32[]{:S(2)}, u32[]{:S(2)}) %collective-permute-start.18) | collective-permute-done | bytes 524320 | tf_op jit(solution)/shard_map/ppermute | solution.py:33
  69.2 1.0 collective-permute-done.22.rest_5_
  70.2 0.7 collective-permute-done.23.rest_6_
  71.0 0.7 collective-permute-done.24.rest_7_
  71.7 2.6 %shard_map.75 = (bf16[512,512]{1,0:T(8,128)(2,1)S(1)}, bf16[128,512]{1,0:T(8,128)(2,1)S(1)}, bf16[512,512]{1,0:T(8,128)(2,1)S(1)}) custom-call(s32[2]{0:T(128)S(1)} %pad_add_fusion.place_ref, s32[4,4]{1,0:T(4,128)S(1)} %bitcast.17, s32[4,20]{1,0:T(4,128)S(1)} %bitcast.21, s32[1,128]{1,0:T(1,128)S(1)} %fusion.listed_ref, ...), custom_call_target="tpu_custom_call" | custom-call | tf_op jit(solution)/shard_map/pallas_call | solution.py:246
  74.3 1.2 collective-permute-start.28
  75.6 2.5 %collective-permute-start.29 = (bf16[128,512]{1,0:T(8,128)(2,1)S(1)}, bf16[128,512]{1,0:T(8,128)(2,1)S(1)}, u32[]{:S(2)}, u32[]{:S(2)}) collective-permute-start(bf16[128,512]{1,0:T(8,128)(2,1)S(1)} %get-tuple-element.19), channel_id=1, source_target_pairs={{0,4},{1,17},{2,6},{3,19},{4,0},{5,21},{6,2},{7,23},{8,12},{9,25},... | collective-permute-start | bytes 393224 | tf_op jit(solution)/shard_map/ppermute | solution.py:33
  78.1 0.8 collective-permute-start.30
  78.9 2.8 %collective-permute-start.26 = (bf16[512,512]{1,0:T(8,128)(2,1)S(1)}, bf16[512,512]{1,0:T(8,128)(2,1)S(1)}, u32[]{:S(2)}, u32[]{:S(2)}) collective-permute-start(bf16[512,512]{1,0:T(8,128)(2,1)S(1)} %get-tuple-element.17), channel_id=1, source_target_pairs={{64,32},{96,64},{32,0},{65,33},{97,65},{33,1},{66,34},{98,66},{34,... | collective-permute-start | bytes 1572872 | tf_op jit(solution)/shard_map/ppermute | solution.py:42
  81.7 0.7 collective-permute-done.29
  83.6 3.1 %collective-permute-start.32 = (bf16[512,512]{1,0:T(8,128)(2,1)S(1)}, bf16[512,512]{1,0:T(8,128)(2,1)S(1)}, u32[]{:S(2)}, u32[]{:S(2)}) collective-permute-start(bf16[512,512]{1,0:T(8,128)(2,1)S(1)} %constant_dynamic-update-slice_fusion.4.rest_0_), channel_id=1, source_target_pairs={{0,16},{1,5},{2,18},{3,7},{4,20},{5,1},{6,22},{7,3},{8,24},{9,13},... | collective-permute-start | bytes 1572872 | tf_op jit(solution)/shard_map/ppermute | solution.py:33
  86.9 3.1 %collective-permute-start.27 = (bf16[512,512]{1,0:T(8,128)(2,1)S(1)}, bf16[512,512]{1,0:T(8,128)(2,1)S(1)}, u32[]{:S(2)}, u32[]{:S(2)}) collective-permute-start(bf16[512,512]{1,0:T(8,128)(2,1)S(1)} %get-tuple-element.18.current_ref.refs_4_), channel_id=1, source_target_pairs={{0,32},{32,64},{64,96},{96,0},{1,33},{33,65},{65,97},{97,1},{2,34}... | collective-permute-start | bytes 1572872 | tf_op jit(solution)/shard_map/ppermute | solution.py:42
  90.1 1.6 collective-permute-done.26.rest_8_.refs_2_.refs_7_
  91.6 2.0 %collective-permute-done.31.rest_1_ = bf16[512,512]{1,0:T(8,128)(2,1)S(1)} collective-permute-done((bf16[512,512]{1,0:T(8,128)(2,1)S(1)}, bf16[512,512]{1,0:T(8,128)(2,1)S(1)}, u32[]{:S(2)}, u32[]{:S(2)}) %collective-permute-start.31) | collective-permute-done | bytes 524320 | tf_op jit(solution)/shard_map/ppermute | solution.py:33
  93.6 5.9 %collective-permute-done.32.rest_2_ = bf16[512,512]{1,0:T(8,128)(2,1)S(1)} collective-permute-done((bf16[512,512]{1,0:T(8,128)(2,1)S(1)}, bf16[512,512]{1,0:T(8,128)(2,1)S(1)}, u32[]{:S(2)}, u32[]{:S(2)}) %collective-permute-start.32) | collective-permute-done | bytes 524320 | tf_op jit(solution)/shard_map/ppermute | solution.py:33
  100.2 1.2 collective-permute-done.36.rest_6_
  101.4 0.7 collective-permute-done.37.rest_7_
  102.1 2.6 %shard_map.76 = (bf16[512,512]{1,0:T(8,128)(2,1)S(1)}, bf16[128,512]{1,0:T(8,128)(2,1)S(1)}, bf16[512,512]{1,0:T(8,128)(2,1)S(1)}) custom-call(s32[2]{0:T(128)S(1)} %pad_add_fusion.place_ref, s32[4,4]{1,0:T(4,128)S(1)} %bitcast.18, s32[4,20]{1,0:T(4,128)S(1)} %bitcast.22, s32[1,128]{1,0:T(1,128)S(1)} %fusion.listed_ref, ...), custom_call_target="tpu_custom_call" | custom-call | tf_op jit(solution)/shard_map/pallas_call | solution.py:246
  104.7 0.9 collective-permute-start.41
  105.7 3.0 %collective-permute-start.42 = (bf16[128,512]{1,0:T(8,128)(2,1)S(1)}, bf16[128,512]{1,0:T(8,128)(2,1)S(1)}, u32[]{:S(2)}, u32[]{:S(2)}) collective-permute-start(bf16[128,512]{1,0:T(8,128)(2,1)S(1)} %get-tuple-element.22), channel_id=1, source_target_pairs={{0,4},{1,17},{2,6},{3,19},{4,0},{5,21},{6,2},{7,23},{8,12},{9,25},... | collective-permute-start | bytes 393224 | tf_op jit(solution)/shard_map/ppermute | solution.py:33
  109.0 3.0 %collective-permute-start.38 = (bf16[512,512]{1,0:T(8,128)(2,1)S(1)}, bf16[512,512]{1,0:T(8,128)(2,1)S(1)}, u32[]{:S(2)}, u32[]{:S(2)}) collective-permute-start(bf16[512,512]{1,0:T(8,128)(2,1)S(1)} %get-tuple-element.20), channel_id=1, source_target_pairs={{96,64},{0,96},{64,32},{97,65},{1,97},{65,33},{98,66},{2,98},{66,3... | collective-permute-start | bytes 1572872 | tf_op jit(solution)/shard_map/ppermute | solution.py:42
  112.0 1.0 collective-permute-done.42
  114.1 3.7 %collective-permute-start.45 = (bf16[512,512]{1,0:T(8,128)(2,1)S(1)}, bf16[512,512]{1,0:T(8,128)(2,1)S(1)}, u32[]{:S(2)}, u32[]{:S(2)}) collective-permute-start(bf16[512,512]{1,0:T(8,128)(2,1)S(1)} %constant_dynamic-update-slice_fusion.8.rest_0_), channel_id=1, source_target_pairs={{0,16},{1,5},{2,18},{3,7},{4,20},{5,1},{6,22},{7,3},{8,24},{9,13},... | collective-permute-start | bytes 1572872 | tf_op jit(solution)/shard_map/ppermute | solution.py:33
  117.8 2.7 %collective-permute-start.39 = (bf16[512,512]{1,0:T(8,128)(2,1)S(1)}, bf16[512,512]{1,0:T(8,128)(2,1)S(1)}, u32[]{:S(2)}, u32[]{:S(2)}) collective-permute-start(bf16[512,512]{1,0:T(8,128)(2,1)S(1)} %get-tuple-element.21.current_ref.refs_8_), channel_id=1, source_target_pairs={{0,32},{32,64},{64,96},{96,0},{1,33},{33,65},{65,97},{97,1},{2,34}... | collective-permute-start | bytes 1572872 | tf_op jit(solution)/shard_map/ppermute | solution.py:42
  120.5 4.9 %collective-permute-done.38.rest_8_.refs_6_.refs_11_ = bf16[512,512]{1,0:T(8,128)(2,1)S(1)} collective-permute-done((bf16[512,512]{1,0:T(8,128)(2,1)S(1)}, bf16[512,512]{1,0:T(8,128)(2,1)S(1)}, u32[]{:S(2)}, u32[]{:S(2)}) %collective-permute-start.38) | collective-permute-done | bytes 524320 | tf_op jit(solution)/shard_map/ppermute | solution.py:42
  125.9 4.6 %collective-permute-done.45.rest_2_ = bf16[512,512]{1,0:T(8,128)(2,1)S(1)} collective-permute-done((bf16[512,512]{1,0:T(8,128)(2,1)S(1)}, bf16[512,512]{1,0:T(8,128)(2,1)S(1)}, u32[]{:S(2)}, u32[]{:S(2)}) %collective-permute-start.45) | collective-permute-done | bytes 524320 | tf_op jit(solution)/shard_map/ppermute | solution.py:33
  131.1 2.7 %collective-permute-start.40 = (bf16[512,512]{1,0:T(8,128)(2,1)S(1)}, bf16[512,512]{1,0:T(8,128)(2,1)S(1)}, u32[]{:S(2)}, u32[]{:S(2)}) collective-permute-start(bf16[512,512]{1,0:T(8,128)(2,1)S(1)} %collective-permute-done.38.rest_8_.refs_6_.refs_11_), channel_id=1, source_target_pairs={{96,64},{97,65},{98,66},{99,67},{100,68},{101,69},{102,70},{103,71... | collective-permute-start | bytes 1572872 | tf_op jit(solution)/shard_map/ppermute | solution.py:42
  133.9 2.4 %shard_map.77.refs_12_ = bf16[512,512]{1,0:T(8,128)(2,1)S(1)} custom-call(s32[2]{0:T(128)S(1)} %pad_add_fusion.place_ref, s32[4,4]{1,0:T(4,128)S(1)} %bitcast.19, s32[4,20]{1,0:T(4,128)S(1)} %bitcast.23, s32[1,128]{1,0:T(1,128)S(1)} %fusion.listed_ref, bf16[512,512]{1,0:T(8,128)(2,1)S(1)} %get-tuple-element.21.current_ref.refs_8_, ...), custom_call_target="tpu_custom_call" | custom-call | tf_op jit(solution)/shard_map/pallas_call | solution.py:246
  136.3 1.3 collective-permute-start.51
  137.6 1.3 collective-permute-start.55
  139.6 1.3 collective-permute-start.54
  140.9 1.3 collective-permute-start.53
  142.2 3.1 %collective-permute-done.40.refs_10_ = bf16[512,512]{1,0:T(8,128)(2,1)S(1)} collective-permute-done((bf16[512,512]{1,0:T(8,128)(2,1)S(1)}, bf16[512,512]{1,0:T(8,128)(2,1)S(1)}, u32[]{:S(2)}, u32[]{:S(2)}) %collective-permute-start.40) | collective-permute-done | bytes 524320 | tf_op jit(solution)/shard_map/ppermute | solution.py:42
  145.3 6.9 %collective-permute-done.54.refs_15_ = bf16[256,512]{1,0:T(8,128)(2,1)S(1)} collective-permute-done((bf16[256,512]{1,0:T(8,128)(2,1)S(1)}, bf16[256,512]{1,0:T(8,128)(2,1)S(1)}, u32[]{:S(2)}, u32[]{:S(2)}) %collective-permute-start.54) | collective-permute-done | bytes 262176 | tf_op jit(solution)/shard_map/ppermute | solution.py:42
  152.2 7.8 %collective-permute-done.55.refs_16_ = bf16[512,512]{1,0:T(8,128)(2,1)S(1)} collective-permute-done((bf16[512,512]{1,0:T(8,128)(2,1)S(1)}, bf16[512,512]{1,0:T(8,128)(2,1)S(1)}, u32[]{:S(2)}, u32[]{:S(2)}) %collective-permute-start.55) | collective-permute-done | bytes 524320 | tf_op jit(solution)/shard_map/ppermute | solution.py:42
  160.0 1.4 shard_map.78
  (83 shorter events, 9.5 us)
Async XLA Ops:
  0.0 35.7 %copy-start = (bf16[4,1,20,128,128]{4,3,2,1,0:T(8,128)(2,1)S(1)}, bf16[4,1,20,128,128]{4,3,2,1,0:T(8,128)(2,1)}, u32[]{:S(2)}) copy-start(bf16[4,1,20,128,128]{4,3,2,1,0:T(8,128)(2,1)} %param.13) | copy-start | bytes 7864324
  4.5 9.9 %collective-permute-start.4 = (bf16[144,512]{1,0:T(8,128)(2,1)S(1)}, bf16[144,512]{1,0:T(8,128)(2,1)S(1)}, u32[]{:S(2)}, u32[]{:S(2)}) collective-permute-start(bf16[144,512]{1,0:T(8,128)(2,1)S(1)} %shard_map.73), channel_id=1, source_target_pairs={{0,2},{1,9},{2,4},{3,11},{4,6},{5,13},{6,0},{7,15},{8,10},{9,17},{... | collective-permute-start | bytes 442376 | tf_op jit(solution)/shard_map/ppermute | solution.py:33
  6.1 8.2 %collective-permute-start.5 = (bf16[144,512]{1,0:T(8,128)(2,1)S(1)}, bf16[144,512]{1,0:T(8,128)(2,1)}, u32[]{:S(2)}, u32[]{:S(2)}) collective-permute-start(bf16[144,512]{1,0:T(8,128)(2,1)S(1)} %shard_map.73), channel_id=1, source_target_pairs={{0,4},{1,17},{2,6},{3,19},{4,0},{5,21},{6,2},{7,23},{8,12},{9,25},... | collective-permute-start | bytes 442376 | tf_op jit(solution)/shard_map/ppermute | solution.py:33
  9.0 5.3 %collective-permute-start.6 = (bf16[144,512]{1,0:T(8,128)(2,1)S(1)}, bf16[144,512]{1,0:T(8,128)(2,1)}, u32[]{:S(2)}, u32[]{:S(2)}) collective-permute-start(bf16[144,512]{1,0:T(8,128)(2,1)S(1)} %shard_map.73), channel_id=1, source_target_pairs={{0,6},{1,25},{2,0},{3,27},{4,2},{5,29},{6,4},{7,31},{8,14},{9,1},{... | collective-permute-start | bytes 442376 | tf_op jit(solution)/shard_map/ppermute | solution.py:33
  11.3 26.6 %copy-start.1 = (bf16[512,512]{1,0:T(8,128)(2,1)S(1)}, bf16[512,512]{1,0:T(8,128)(2,1)}, u32[]{:S(2)}) copy-start(bf16[512,512]{1,0:T(8,128)(2,1)} %get-tuple-element.23.previous_ref) | copy-start | bytes 1572868
  11.4 26.6 %copy-start.2 = (s32[4,1,4]{2,1,0:T(1,128)S(1)}, s32[4,1,4]{2,1,0:T(1,128)}, u32[]{:S(2)}) copy-start(s32[4,1,4]{2,1,0:T(1,128)} %param.11) | copy-start | bytes 196
  11.4 26.6 %copy-start.3 = (s32[4,1,20]{2,1,0:T(1,128)S(1)}, s32[4,1,20]{2,1,0:T(1,128)}, u32[]{:S(2)}) copy-start(s32[4,1,20]{2,1,0:T(1,128)} %param.12) | copy-start | bytes 964
  11.4 9.6 %collective-permute-start = (bf16[256,512]{1,0:T(8,128)(2,1)S(1)}, bf16[256,512]{1,0:T(8,128)(2,1)S(1)}, u32[]{:S(2)}, u32[]{:S(2)}) collective-permute-start(bf16[256,512]{1,0:T(8,128)(2,1)S(1)} %dynamic-slice_bitcast_fusion.3), channel_id=1, source_target_pairs={{0,32},{32,64},{64,96},{96,0},{1,33},{33,65},{65,97},{97,1},{2,34}... | collective-permute-start | bytes 786440 | tf_op jit(solution)/shard_map/ppermute | solution.py:42
  12.0 10.8 %collective-permute-start.1 = (bf16[256,512]{1,0:T(8,128)(2,1)S(1)}, bf16[256,512]{1,0:T(8,128)(2,1)S(1)}, u32[]{:S(2)}, u32[]{:S(2)}) collective-permute-start(bf16[256,512]{1,0:T(8,128)(2,1)S(1)} %dynamic-slice_bitcast_fusion.3), channel_id=1, source_target_pairs={{0,64},{32,96},{64,0},{96,32},{1,65},{33,97},{65,1},{97,33},{2,66}... | collective-permute-start | bytes 786440 | tf_op jit(solution)/shard_map/ppermute | solution.py:42
  14.4 12.5 %collective-permute-start.2 = (bf16[256,512]{1,0:T(8,128)(2,1)S(1)}, bf16[256,512]{1,0:T(8,128)(2,1)S(1)}, u32[]{:S(2)}, u32[]{:S(2)}) collective-permute-start(bf16[256,512]{1,0:T(8,128)(2,1)S(1)} %dynamic-slice_bitcast_fusion.3), channel_id=1, source_target_pairs={{0,96},{32,0},{64,32},{96,64},{1,97},{33,1},{65,33},{97,65},{2,98}... | collective-permute-start | bytes 786440 | tf_op jit(solution)/shard_map/ppermute | solution.py:42
  15.4 12.1 %collective-permute-start.7 = (bf16[576,512]{1,0:T(8,128)(2,1)S(1)}, bf16[576,512]{1,0:T(8,128)(2,1)S(1)}, u32[]{:S(2)}, u32[]{:S(2)}) collective-permute-start(bf16[576,512]{1,0:T(8,128)(2,1)S(1)} %pad_maximum_fusion.1.rest_0_), channel_id=1, source_target_pairs={{0,8},{1,3},{2,10},{3,5},{4,12},{5,7},{6,14},{7,1},{8,16},{9,11},{... | collective-permute-start | bytes 1769480 | tf_op jit(solution)/shard_map/ppermute | solution.py:33
  17.4 17.8 %collective-permute-start.8 = (bf16[576,512]{1,0:T(8,128)(2,1)S(1)}, bf16[576,512]{1,0:T(8,128)(2,1)S(1)}, u32[]{:S(2)}, u32[]{:S(2)}) collective-permute-start(bf16[576,512]{1,0:T(8,128)(2,1)S(1)} %pad_maximum_fusion.1.rest_0_), channel_id=1, source_target_pairs={{0,16},{1,5},{2,18},{3,7},{4,20},{5,1},{6,22},{7,3},{8,24},{9,13},... | collective-permute-start | bytes 1769480 | tf_op jit(solution)/shard_map/ppermute | solution.py:33
  21.0 14.2 %collective-permute-start.9 = (bf16[576,512]{1,0:T(8,128)(2,1)S(1)}, bf16[576,512]{1,0:T(8,128)(2,1)S(1)}, u32[]{:S(2)}, u32[]{:S(2)}) collective-permute-start(bf16[576,512]{1,0:T(8,128)(2,1)S(1)} %pad_maximum_fusion.1.rest_0_), channel_id=1, source_target_pairs={{0,24},{1,7},{2,26},{3,1},{4,28},{5,3},{6,30},{7,5},{8,0},{9,15},{... | collective-permute-start | bytes 1769480 | tf_op jit(solution)/shard_map/ppermute | solution.py:33
  26.9 8.8 %collective-permute-start.3 = (bf16[1024,512]{1,0:T(8,128)(2,1)S(1)}, bf16[1024,512]{1,0:T(8,128)(2,1)S(1)}, u32[]{:S(2)}, u32[]{:S(2)}) collective-permute-start(bf16[1024,512]{1,0:T(8,128)(2,1)S(1)} %pad_maximum_fusion.halves_ref), channel_id=1, source_target_pairs={{0,1},{1,0},{2,3},{3,2},{4,5},{5,4},{6,7},{7,6},{8,9},{9,8},{10,11... | collective-permute-start | bytes 3145736 | tf_op jit(solution)/shard_map/ppermute | solution.py:38
  27.0 8.7 %collective-permute-start.10 = (bf16[576,512]{1,0:T(8,128)(2,1)S(1)}, bf16[576,512]{1,0:T(8,128)(2,1)S(1)}, u32[]{:S(2)}, u32[]{:S(2)}) collective-permute-start(bf16[576,512]{1,0:T(8,128)(2,1)S(1)} %pad_maximum_fusion.1.rest_0_), channel_id=1, source_target_pairs={{0,1},{1,0},{2,3},{3,2},{4,5},{5,4},{6,7},{7,6},{8,9},{9,8},{10,11... | collective-permute-start | bytes 1769480 | tf_op jit(solution)/shard_map/ppermute | solution.py:38
  27.5 8.2 %collective-permute-start.11 = (bf16[576,512]{1,0:T(8,128)(2,1)S(1)}, bf16[576,512]{1,0:T(8,128)(2,1)S(1)}, u32[]{:S(2)}, u32[]{:S(2)}) collective-permute-start(bf16[576,512]{1,0:T(8,128)(2,1)S(1)} %collective-permute-done.7.rest_1_), channel_id=1, source_target_pairs={{0,1},{1,0},{2,3},{3,2},{4,5},{5,4},{6,7},{7,6},{8,9},{9,8},{10,11... | collective-permute-start | bytes 1769480 | tf_op jit(solution)/shard_map/ppermute | solution.py:38
  35.1 2.0 %collective-permute-start.12 = (bf16[576,512]{1,0:T(8,128)(2,1)S(1)}, bf16[576,512]{1,0:T(8,128)(2,1)S(1)}, u32[]{:S(2)}, u32[]{:S(2)}) collective-permute-start(bf16[576,512]{1,0:T(8,128)(2,1)S(1)} %collective-permute-done.8.rest_2_), channel_id=1, source_target_pairs={{0,1},{1,0},{2,3},{3,2},{4,5},{5,4},{6,7},{7,6},{8,9},{9,8},{10,11... | collective-permute-start | bytes 1769480 | tf_op jit(solution)/shard_map/ppermute | solution.py:38
  35.1 2.8 %collective-permute-start.13 = (bf16[576,512]{1,0:T(8,128)(2,1)S(1)}, bf16[576,512]{1,0:T(8,128)(2,1)S(1)}, u32[]{:S(2)}, u32[]{:S(2)}) collective-permute-start(bf16[576,512]{1,0:T(8,128)(2,1)S(1)} %collective-permute-done.9.rest_3_), channel_id=1, source_target_pairs={{0,1},{1,0},{2,3},{3,2},{4,5},{5,4},{6,7},{7,6},{8,9},{9,8},{10,11... | collective-permute-start | bytes 1769480 | tf_op jit(solution)/shard_map/ppermute | solution.py:38
  43.2 6.8 %collective-permute-start.15 = (bf16[128,512]{1,0:T(8,128)(2,1)S(1)}, bf16[128,512]{1,0:T(8,128)(2,1)S(1)}, u32[]{:S(2)}, u32[]{:S(2)}) collective-permute-start(bf16[128,512]{1,0:T(8,128)(2,1)S(1)} %get-tuple-element.16), channel_id=1, source_target_pairs={{0,2},{1,9},{2,4},{3,11},{4,6},{5,13},{6,0},{7,15},{8,10},{9,17},{... | collective-permute-start | bytes 393224 | tf_op jit(solution)/shard_map/ppermute | solution.py:33
  44.3 7.2 %collective-permute-start.16 = (bf16[128,512]{1,0:T(8,128)(2,1)S(1)}, bf16[128,512]{1,0:T(8,128)(2,1)S(1)}, u32[]{:S(2)}, u32[]{:S(2)}) collective-permute-start(bf16[128,512]{1,0:T(8,128)(2,1)S(1)} %get-tuple-element.16), channel_id=1, source_target_pairs={{0,4},{1,17},{2,6},{3,19},{4,0},{5,21},{6,2},{7,23},{8,12},{9,25},... | collective-permute-start | bytes 393224 | tf_op jit(solution)/shard_map/ppermute | solution.py:33
  47.2 5.0 %collective-permute-start.17 = (bf16[128,512]{1,0:T(8,128)(2,1)S(1)}, bf16[128,512]{1,0:T(8,128)(2,1)S(1)}, u32[]{:S(2)}, u32[]{:S(2)}) collective-permute-start(bf16[128,512]{1,0:T(8,128)(2,1)S(1)} %get-tuple-element.16), channel_id=1, source_target_pairs={{0,6},{1,25},{2,0},{3,27},{4,2},{5,29},{6,4},{7,31},{8,14},{9,1},{... | collective-permute-start | bytes 393224 | tf_op jit(solution)/shard_map/ppermute | solution.py:33
  48.3 13.2 %collective-permute-start.14 = (bf16[512,512]{1,0:T(8,128)(2,1)S(1)}, bf16[512,512]{1,0:T(8,128)(2,1)S(1)}, u32[]{:S(2)}, u32[]{:S(2)}) collective-permute-start(bf16[512,512]{1,0:T(8,128)(2,1)S(1)} %get-tuple-element.14.current_ref.refs_0_), channel_id=1, source_target_pairs={{0,32},{32,64},{64,96},{96,0},{1,33},{33,65},{65,97},{97,1},{2,34}... | collective-permute-start | bytes 1572872 | tf_op jit(solution)/shard_map/ppermute | solution.py:42
  52.2 16.1 %collective-permute-start.18 = (bf16[512,512]{1,0:T(8,128)(2,1)S(1)}, bf16[512,512]{1,0:T(8,128)(2,1)S(1)}, u32[]{:S(2)}, u32[]{:S(2)}) collective-permute-start(bf16[512,512]{1,0:T(8,128)(2,1)S(1)} %constant_dynamic-update-slice_fusion.rest_0_), channel_id=1, source_target_pairs={{0,8},{1,3},{2,10},{3,5},{4,12},{5,7},{6,14},{7,1},{8,16},{9,11},{... | collective-permute-start | bytes 1572872 | tf_op jit(solution)/shard_map/ppermute | solution.py:33
  53.0 15.4 %collective-permute-start.19 = (bf16[512,512]{1,0:T(8,128)(2,1)S(1)}, bf16[512,512]{1,0:T(8,128)(2,1)S(1)}, u32[]{:S(2)}, u32[]{:S(2)}) collective-permute-start(bf16[512,512]{1,0:T(8,128)(2,1)S(1)} %constant_dynamic-update-slice_fusion.rest_0_), channel_id=1, source_target_pairs={{0,16},{1,5},{2,18},{3,7},{4,20},{5,1},{6,22},{7,3},{8,24},{9,13},... | collective-permute-start | bytes 1572872 | tf_op jit(solution)/shard_map/ppermute | solution.py:33
  55.1 14.1 %collective-permute-start.20 = (bf16[512,512]{1,0:T(8,128)(2,1)S(1)}, bf16[512,512]{1,0:T(8,128)(2,1)S(1)}, u32[]{:S(2)}, u32[]{:S(2)}) collective-permute-start(bf16[512,512]{1,0:T(8,128)(2,1)S(1)} %constant_dynamic-update-slice_fusion.rest_0_), channel_id=1, source_target_pairs={{0,24},{1,7},{2,26},{3,1},{4,28},{5,3},{6,30},{7,5},{8,0},{9,15},{... | collective-permute-start | bytes 1572872 | tf_op jit(solution)/shard_map/ppermute | solution.py:33
  56.6 12.6 %collective-permute-start.25 = (bf16[512,512]{1,0:T(8,128)(2,1)S(1)}, bf16[512,512]{1,0:T(8,128)(2,1)S(1)}, u32[]{:S(2)}, u32[]{:S(2)}) collective-permute-start(bf16[512,512]{1,0:T(8,128)(2,1)S(1)} %get-tuple-element.14.current_ref.refs_0_), channel_id=1, source_target_pairs={{32,0},{64,32},{33,1},{65,33},{34,2},{66,34},{35,3},{67,35},{36,4}... | collective-permute-start | bytes 1572872 | tf_op jit(solution)/shard_map/ppermute | solution.py:42
  61.5 7.7 %collective-permute-start.21 = (bf16[512,512]{1,0:T(8,128)(2,1)S(1)}, bf16[512,512]{1,0:T(8,128)(2,1)S(1)}, u32[]{:S(2)}, u32[]{:S(2)}) collective-permute-start(bf16[512,512]{1,0:T(8,128)(2,1)S(1)} %constant_dynamic-update-slice_fusion.rest_0_), channel_id=1, source_target_pairs={{0,1},{1,0},{2,3},{3,2},{4,5},{5,4},{6,7},{7,6},{8,9},{9,8},{10,11... | collective-permute-start | bytes 1572872 | tf_op jit(solution)/shard_map/ppermute | solution.py:38
  68.3 1.9 %collective-permute-start.22 = (bf16[512,512]{1,0:T(8,128)(2,1)S(1)}, bf16[512,512]{1,0:T(8,128)(2,1)S(1)}, u32[]{:S(2)}, u32[]{:S(2)}) collective-permute-start(bf16[512,512]{1,0:T(8,128)(2,1)S(1)} %collective-permute-done.18.rest_1_), channel_id=1, source_target_pairs={{0,1},{1,0},{2,3},{3,2},{4,5},{5,4},{6,7},{7,6},{8,9},{9,8},{10,11... | collective-permute-start | bytes 1572872 | tf_op jit(solution)/shard_map/ppermute | solution.py:38
  68.3 2.7 %collective-permute-start.23 = (bf16[512,512]{1,0:T(8,128)(2,1)S(1)}, bf16[512,512]{1,0:T(8,128)(2,1)S(1)}, u32[]{:S(2)}, u32[]{:S(2)}) collective-permute-start(bf16[512,512]{1,0:T(8,128)(2,1)S(1)} %collective-permute-done.19.rest_2_), channel_id=1, source_target_pairs={{0,1},{1,0},{2,3},{3,2},{4,5},{5,4},{6,7},{7,6},{8,9},{9,8},{10,11... | collective-permute-start | bytes 1572872 | tf_op jit(solution)/shard_map/ppermute | solution.py:38
  69.2 2.5 %collective-permute-start.24 = (bf16[512,512]{1,0:T(8,128)(2,1)S(1)}, bf16[512,512]{1,0:T(8,128)(2,1)S(1)}, u32[]{:S(2)}, u32[]{:S(2)}) collective-permute-start(bf16[512,512]{1,0:T(8,128)(2,1)S(1)} %collective-permute-done.20.rest_3_), channel_id=1, source_target_pairs={{0,1},{1,0},{2,3},{3,2},{4,5},{5,4},{6,7},{7,6},{8,9},{9,8},{10,11... | collective-permute-start | bytes 1572872 | tf_op jit(solution)/shard_map/ppermute | solution.py:38
  74.3 7.3 %collective-permute-start.28 = (bf16[128,512]{1,0:T(8,128)(2,1)S(1)}, bf16[128,512]{1,0:T(8,128)(2,1)S(1)}, u32[]{:S(2)}, u32[]{:S(2)}) collective-permute-start(bf16[128,512]{1,0:T(8,128)(2,1)S(1)} %get-tuple-element.19), channel_id=1, source_target_pairs={{0,2},{1,9},{2,4},{3,11},{4,6},{5,13},{6,0},{7,15},{8,10},{9,17},{... | collective-permute-start | bytes 393224 | tf_op jit(solution)/shard_map/ppermute | solution.py:33
  75.6 6.9 %collective-permute-start.29 = (bf16[128,512]{1,0:T(8,128)(2,1)S(1)}, bf16[128,512]{1,0:T(8,128)(2,1)S(1)}, u32[]{:S(2)}, u32[]{:S(2)}) collective-permute-start(bf16[128,512]{1,0:T(8,128)(2,1)S(1)} %get-tuple-element.19), channel_id=1, source_target_pairs={{0,4},{1,17},{2,6},{3,19},{4,0},{5,21},{6,2},{7,23},{8,12},{9,25},... | collective-permute-start | bytes 393224 | tf_op jit(solution)/shard_map/ppermute | solution.py:33
  78.1 5.0 %collective-permute-start.30 = (bf16[128,512]{1,0:T(8,128)(2,1)S(1)}, bf16[128,512]{1,0:T(8,128)(2,1)S(1)}, u32[]{:S(2)}, u32[]{:S(2)}) collective-permute-start(bf16[128,512]{1,0:T(8,128)(2,1)S(1)} %get-tuple-element.19), channel_id=1, source_target_pairs={{0,6},{1,25},{2,0},{3,27},{4,2},{5,29},{6,4},{7,31},{8,14},{9,1},{... | collective-permute-start | bytes 393224 | tf_op jit(solution)/shard_map/ppermute | solution.py:33
  78.9 12.8 %collective-permute-start.26 = (bf16[512,512]{1,0:T(8,128)(2,1)S(1)}, bf16[512,512]{1,0:T(8,128)(2,1)S(1)}, u32[]{:S(2)}, u32[]{:S(2)}) collective-permute-start(bf16[512,512]{1,0:T(8,128)(2,1)S(1)} %get-tuple-element.17), channel_id=1, source_target_pairs={{64,32},{96,64},{32,0},{65,33},{97,65},{33,1},{66,34},{98,66},{34,... | collective-permute-start | bytes 1572872 | tf_op jit(solution)/shard_map/ppermute | solution.py:42
  83.1 10.5 %collective-permute-start.31 = (bf16[512,512]{1,0:T(8,128)(2,1)S(1)}, bf16[512,512]{1,0:T(8,128)(2,1)S(1)}, u32[]{:S(2)}, u32[]{:S(2)}) collective-permute-start(bf16[512,512]{1,0:T(8,128)(2,1)S(1)} %constant_dynamic-update-slice_fusion.4.rest_0_), channel_id=1, source_target_pairs={{0,8},{1,3},{2,10},{3,5},{4,12},{5,7},{6,14},{7,1},{8,16},{9,11},{... | collective-permute-start | bytes 1572872 | tf_op jit(solution)/shard_map/ppermute | solution.py:33
  83.6 15.8 %collective-permute-start.32 = (bf16[512,512]{1,0:T(8,128)(2,1)S(1)}, bf16[512,512]{1,0:T(8,128)(2,1)S(1)}, u32[]{:S(2)}, u32[]{:S(2)}) collective-permute-start(bf16[512,512]{1,0:T(8,128)(2,1)S(1)} %constant_dynamic-update-slice_fusion.4.rest_0_), channel_id=1, source_target_pairs={{0,16},{1,5},{2,18},{3,7},{4,20},{5,1},{6,22},{7,3},{8,24},{9,13},... | collective-permute-start | bytes 1572872 | tf_op jit(solution)/shard_map/ppermute | solution.py:33
  86.7 13.4 %collective-permute-start.33 = (bf16[512,512]{1,0:T(8,128)(2,1)S(1)}, bf16[512,512]{1,0:T(8,128)(2,1)S(1)}, u32[]{:S(2)}, u32[]{:S(2)}) collective-permute-start(bf16[512,512]{1,0:T(8,128)(2,1)S(1)} %constant_dynamic-update-slice_fusion.4.rest_0_), channel_id=1, source_target_pairs={{0,24},{1,7},{2,26},{3,1},{4,28},{5,3},{6,30},{7,5},{8,0},{9,15},{... | collective-permute-start | bytes 1572872 | tf_op jit(solution)/shard_map/ppermute | solution.py:33
  86.9 13.2 %collective-permute-start.27 = (bf16[512,512]{1,0:T(8,128)(2,1)S(1)}, bf16[512,512]{1,0:T(8,128)(2,1)S(1)}, u32[]{:S(2)}, u32[]{:S(2)}) collective-permute-start(bf16[512,512]{1,0:T(8,128)(2,1)S(1)} %get-tuple-element.18.current_ref.refs_4_), channel_id=1, source_target_pairs={{0,32},{32,64},{64,96},{96,0},{1,33},{33,65},{65,97},{97,1},{2,34}... | collective-permute-start | bytes 1572872 | tf_op jit(solution)/shard_map/ppermute | solution.py:42
  91.6 8.5 %collective-permute-start.34 = (bf16[512,512]{1,0:T(8,128)(2,1)S(1)}, bf16[512,512]{1,0:T(8,128)(2,1)S(1)}, u32[]{:S(2)}, u32[]{:S(2)}) collective-permute-start(bf16[512,512]{1,0:T(8,128)(2,1)S(1)} %constant_dynamic-update-slice_fusion.4.rest_0_), channel_id=1, source_target_pairs={{0,1},{1,0},{2,3},{3,2},{4,5},{5,4},{6,7},{7,6},{8,9},{9,8},{10,11... | collective-permute-start | bytes 1572872 | tf_op jit(solution)/shard_map/ppermute | solution.py:38
  93.6 6.5 %collective-permute-start.35 = (bf16[512,512]{1,0:T(8,128)(2,1)S(1)}, bf16[512,512]{1,0:T(8,128)(2,1)S(1)}, u32[]{:S(2)}, u32[]{:S(2)}) collective-permute-start(bf16[512,512]{1,0:T(8,128)(2,1)S(1)} %collective-permute-done.31.rest_1_), channel_id=1, source_target_pairs={{0,1},{1,0},{2,3},{3,2},{4,5},{5,4},{6,7},{7,6},{8,9},{9,8},{10,11... | collective-permute-start | bytes 1572872 | tf_op jit(solution)/shard_map/ppermute | solution.py:38
  99.5 1.9 %collective-permute-start.36 = (bf16[512,512]{1,0:T(8,128)(2,1)S(1)}, bf16[512,512]{1,0:T(8,128)(2,1)S(1)}, u32[]{:S(2)}, u32[]{:S(2)}) collective-permute-start(bf16[512,512]{1,0:T(8,128)(2,1)S(1)} %collective-permute-done.32.rest_2_), channel_id=1, source_target_pairs={{0,1},{1,0},{2,3},{3,2},{4,5},{5,4},{6,7},{7,6},{8,9},{9,8},{10,11... | collective-permute-start | bytes 1572872 | tf_op jit(solution)/shard_map/ppermute | solution.py:38
  100.1 2.0 %collective-permute-start.37 = (bf16[512,512]{1,0:T(8,128)(2,1)S(1)}, bf16[512,512]{1,0:T(8,128)(2,1)S(1)}, u32[]{:S(2)}, u32[]{:S(2)}) collective-permute-start(bf16[512,512]{1,0:T(8,128)(2,1)S(1)} %collective-permute-done.33.rest_3_), channel_id=1, source_target_pairs={{0,1},{1,0},{2,3},{3,2},{4,5},{5,4},{6,7},{7,6},{8,9},{9,8},{10,11... | collective-permute-start | bytes 1572872 | tf_op jit(solution)/shard_map/ppermute | solution.py:38
  104.7 7.2 %collective-permute-start.41 = (bf16[128,512]{1,0:T(8,128)(2,1)S(1)}, bf16[128,512]{1,0:T(8,128)(2,1)S(1)}, u32[]{:S(2)}, u32[]{:S(2)}) collective-permute-start(bf16[128,512]{1,0:T(8,128)(2,1)S(1)} %get-tuple-element.22), channel_id=1, source_target_pairs={{0,2},{1,9},{2,4},{3,11},{4,6},{5,13},{6,0},{7,15},{8,10},{9,17},{... | collective-permute-start | bytes 393224 | tf_op jit(solution)/shard_map/ppermute | solution.py:33
  105.7 7.3 %collective-permute-start.42 = (bf16[128,512]{1,0:T(8,128)(2,1)S(1)}, bf16[128,512]{1,0:T(8,128)(2,1)S(1)}, u32[]{:S(2)}, u32[]{:S(2)}) collective-permute-start(bf16[128,512]{1,0:T(8,128)(2,1)S(1)} %get-tuple-element.22), channel_id=1, source_target_pairs={{0,4},{1,17},{2,6},{3,19},{4,0},{5,21},{6,2},{7,23},{8,12},{9,25},... | collective-permute-start | bytes 393224 | tf_op jit(solution)/shard_map/ppermute | solution.py:33
  108.7 5.0 %collective-permute-start.43 = (bf16[128,512]{1,0:T(8,128)(2,1)S(1)}, bf16[128,512]{1,0:T(8,128)(2,1)S(1)}, u32[]{:S(2)}, u32[]{:S(2)}) collective-permute-start(bf16[128,512]{1,0:T(8,128)(2,1)S(1)} %get-tuple-element.22), channel_id=1, source_target_pairs={{0,6},{1,25},{2,0},{3,27},{4,2},{5,29},{6,4},{7,31},{8,14},{9,1},{... | collective-permute-start | bytes 393224 | tf_op jit(solution)/shard_map/ppermute | solution.py:33
  109.0 16.4 %collective-permute-start.38 = (bf16[512,512]{1,0:T(8,128)(2,1)S(1)}, bf16[512,512]{1,0:T(8,128)(2,1)S(1)}, u32[]{:S(2)}, u32[]{:S(2)}) collective-permute-start(bf16[512,512]{1,0:T(8,128)(2,1)S(1)} %get-tuple-element.20), channel_id=1, source_target_pairs={{96,64},{0,96},{64,32},{97,65},{1,97},{65,33},{98,66},{2,98},{66,3... | collective-permute-start | bytes 1572872 | tf_op jit(solution)/shard_map/ppermute | solution.py:42
  113.7 11.7 %collective-permute-start.44 = (bf16[512,512]{1,0:T(8,128)(2,1)S(1)}, bf16[512,512]{1,0:T(8,128)(2,1)S(1)}, u32[]{:S(2)}, u32[]{:S(2)}) collective-permute-start(bf16[512,512]{1,0:T(8,128)(2,1)S(1)} %constant_dynamic-update-slice_fusion.8.rest_0_), channel_id=1, source_target_pairs={{0,8},{1,3},{2,10},{3,5},{4,12},{5,7},{6,14},{7,1},{8,16},{9,11},{... | collective-permute-start | bytes 1572872 | tf_op jit(solution)/shard_map/ppermute | solution.py:33
  114.1 16.4 %collective-permute-start.45 = (bf16[512,512]{1,0:T(8,128)(2,1)S(1)}, bf16[512,512]{1,0:T(8,128)(2,1)S(1)}, u32[]{:S(2)}, u32[]{:S(2)}) collective-permute-start(bf16[512,512]{1,0:T(8,128)(2,1)S(1)} %constant_dynamic-update-slice_fusion.8.rest_0_), channel_id=1, source_target_pairs={{0,16},{1,5},{2,18},{3,7},{4,20},{5,1},{6,22},{7,3},{8,24},{9,13},... | collective-permute-start | bytes 1572872 | tf_op jit(solution)/shard_map/ppermute | solution.py:33
  117.8 12.9 %collective-permute-start.46 = (bf16[512,512]{1,0:T(8,128)(2,1)S(1)}, bf16[512,512]{1,0:T(8,128)(2,1)S(1)}, u32[]{:S(2)}, u32[]{:S(2)}) collective-permute-start(bf16[512,512]{1,0:T(8,128)(2,1)S(1)} %constant_dynamic-update-slice_fusion.8.rest_0_), channel_id=1, source_target_pairs={{0,24},{1,7},{2,26},{3,1},{4,28},{5,3},{6,30},{7,5},{8,0},{9,15},{... | collective-permute-start | bytes 1572872 | tf_op jit(solution)/shard_map/ppermute | solution.py:33
  117.8 13.3 %collective-permute-start.39 = (bf16[512,512]{1,0:T(8,128)(2,1)S(1)}, bf16[512,512]{1,0:T(8,128)(2,1)S(1)}, u32[]{:S(2)}, u32[]{:S(2)}) collective-permute-start(bf16[512,512]{1,0:T(8,128)(2,1)S(1)} %get-tuple-element.21.current_ref.refs_8_), channel_id=1, source_target_pairs={{0,32},{32,64},{64,96},{96,0},{1,33},{33,65},{65,97},{97,1},{2,34}... | collective-permute-start | bytes 1572872 | tf_op jit(solution)/shard_map/ppermute | solution.py:42
  125.4 8.4 %collective-permute-start.47 = (bf16[512,512]{1,0:T(8,128)(2,1)S(1)}, bf16[512,512]{1,0:T(8,128)(2,1)S(1)}, u32[]{:S(2)}, u32[]{:S(2)}) collective-permute-start(bf16[512,512]{1,0:T(8,128)(2,1)S(1)} %constant_dynamic-update-slice_fusion.8.rest_0_), channel_id=1, source_target_pairs={{0,1},{1,0},{2,3},{3,2},{4,5},{5,4},{6,7},{7,6},{8,9},{9,8},{10,11... | collective-permute-start | bytes 1572872 | tf_op jit(solution)/shard_map/ppermute | solution.py:38
  125.4 8.4 %collective-permute-start.48 = (bf16[512,512]{1,0:T(8,128)(2,1)S(1)}, bf16[512,512]{1,0:T(8,128)(2,1)S(1)}, u32[]{:S(2)}, u32[]{:S(2)}) collective-permute-start(bf16[512,512]{1,0:T(8,128)(2,1)S(1)} %collective-permute-done.44.rest_1_), channel_id=1, source_target_pairs={{0,1},{1,0},{2,3},{3,2},{4,5},{5,4},{6,7},{7,6},{8,9},{9,8},{10,11... | collective-permute-start | bytes 1572872 | tf_op jit(solution)/shard_map/ppermute | solution.py:38
  130.6 3.3 %collective-permute-start.49 = (bf16[512,512]{1,0:T(8,128)(2,1)S(1)}, bf16[512,512]{1,0:T(8,128)(2,1)S(1)}, u32[]{:S(2)}, u32[]{:S(2)}) collective-permute-start(bf16[512,512]{1,0:T(8,128)(2,1)S(1)} %collective-permute-done.45.rest_2_), channel_id=1, source_target_pairs={{0,1},{1,0},{2,3},{3,2},{4,5},{5,4},{6,7},{7,6},{8,9},{9,8},{10,11... | collective-permute-start | bytes 1572872 | tf_op jit(solution)/shard_map/ppermute | solution.py:38
  130.7 3.2 %collective-permute-start.50 = (bf16[512,512]{1,0:T(8,128)(2,1)S(1)}, bf16[512,512]{1,0:T(8,128)(2,1)S(1)}, u32[]{:S(2)}, u32[]{:S(2)}) collective-permute-start(bf16[512,512]{1,0:T(8,128)(2,1)S(1)} %collective-permute-done.46.rest_3_), channel_id=1, source_target_pairs={{0,1},{1,0},{2,3},{3,2},{4,5},{5,4},{6,7},{7,6},{8,9},{9,8},{10,11... | collective-permute-start | bytes 1572872 | tf_op jit(solution)/shard_map/ppermute | solution.py:38
  131.1 14.2 %collective-permute-start.40 = (bf16[512,512]{1,0:T(8,128)(2,1)S(1)}, bf16[512,512]{1,0:T(8,128)(2,1)S(1)}, u32[]{:S(2)}, u32[]{:S(2)}) collective-permute-start(bf16[512,512]{1,0:T(8,128)(2,1)S(1)} %collective-permute-done.38.rest_8_.refs_6_.refs_11_), channel_id=1, source_target_pairs={{96,64},{97,65},{98,66},{99,67},{100,68},{101,69},{102,70},{103,71... | collective-permute-start | bytes 1572872 | tf_op jit(solution)/shard_map/ppermute | solution.py:42
  136.3 15.9 %collective-permute-start.51 = (bf16[512,512]{1,0:T(8,128)(2,1)S(1)}, bf16[512,512]{1,0:T(8,128)(2,1)S(1)}, u32[]{:S(2)}, u32[]{:S(2)}) collective-permute-start(bf16[512,512]{1,0:T(8,128)(2,1)S(1)} %shard_map.77.refs_12_), channel_id=1, source_target_pairs={{64,96},{65,97},{66,98},{67,99},{68,100},{69,101},{70,102},{71,103... | collective-permute-start | bytes 1572872 | tf_op jit(solution)/shard_map/ppermute | solution.py:42
  137.6 22.4 %collective-permute-start.55 = (bf16[512,512]{1,0:T(8,128)(2,1)S(1)}, bf16[512,512]{1,0:T(8,128)(2,1)S(1)}, u32[]{:S(2)}, u32[]{:S(2)}) collective-permute-start(bf16[512,512]{1,0:T(8,128)(2,1)S(1)} %shard_map.77.refs_12_), channel_id=1, source_target_pairs={{0,96},{1,97},{2,98},{3,99},{4,100},{5,101},{6,102},{7,103},{8,104... | collective-permute-start | bytes 1572872 | tf_op jit(solution)/shard_map/ppermute | solution.py:42
  138.9 2.0 %collective-permute-start.52 = (bf16[256,512]{1,0:T(8,128)(2,1)S(1)}, bf16[256,512]{1,0:T(8,128)(2,1)S(1)}, u32[]{:S(2)}, u32[]{:S(2)}) collective-permute-start(bf16[256,512]{1,0:T(8,128)(2,1)S(1)} %get-tuple-element.26), channel_id=1, source_target_pairs={{32,64},{33,65},{34,66},{35,67},{36,68},{37,69},{38,70},{39,71},{4... | collective-permute-start | bytes 786440 | tf_op jit(solution)/shard_map/ppermute | solution.py:42
  139.6 12.5 %collective-permute-start.54 = (bf16[256,512]{1,0:T(8,128)(2,1)S(1)}, bf16[256,512]{1,0:T(8,128)(2,1)S(1)}, u32[]{:S(2)}, u32[]{:S(2)}) collective-permute-start(bf16[256,512]{1,0:T(8,128)(2,1)S(1)} %get-tuple-element.25), channel_id=1, source_target_pairs={{32,96},{33,97},{34,98},{35,99},{36,100},{37,101},{38,102},{39,103... | collective-permute-start | bytes 786440 | tf_op jit(solution)/shard_map/ppermute | solution.py:42
  140.9 19.1 %collective-permute-start.53 = (bf16[256,512]{1,0:T(8,128)(2,1)S(1)}, bf16[256,512]{1,0:T(8,128)(2,1)S(1)}, u32[]{:S(2)}, u32[]{:S(2)}) collective-permute-start(bf16[256,512]{1,0:T(8,128)(2,1)S(1)} %collective-permute-done.52), channel_id=1, source_target_pairs={{64,96},{65,97},{66,98},{67,99},{68,100},{69,101},{70,102},{71,103... | collective-permute-start | bytes 786440 | tf_op jit(solution)/shard_map/ppermute | solution.py:42

commit v6 on v5

--- a/solution.py
+++ b/solution.py
@@ -52,18 +52,18 @@
 
 
 def first_kernel(place_ref, rows_ref, listed_ref, lists_ref, block_ref):
-    node = place_ref[1]
-    offered = listed_ref.shape[1]
-    nodes, picks = lists_ref.shape
+    span, node = place_ref[0], place_ref[1]
+    offered = listed_ref.shape[2]
+    nodes, picks = lists_ref.shape[2:]
     block_ref[pl.ds(offered, EXTRA), :] = jnp.zeros((EXTRA, block_ref.shape[1]), jnp.bfloat16)
-    lists = lists_ref[...].astype(jnp.float32).astype(jnp.bfloat16)
+    lists = lists_ref[span, 0].astype(jnp.float32).astype(jnp.bfloat16)
     for core in range(CORES):
         @pl.when(node % CORES == core)
         def _():
             for part in range(nodes // EXTRA):
                 lanes = pl.ds(part * CORES * picks + core * picks, picks)
                 block_ref[pl.ds(offered, EXTRA), lanes] = lists[part * EXTRA:(part + 1) * EXTRA]
-    block_ref[pl.ds(0, offered), :] = offered_rows(listed_ref[...], rows_ref[...])
+    block_ref[pl.ds(0, offered), :] = offered_rows(listed_ref[span], rows_ref[...])
 
 
 def layer_kernel(
@@ -79,7 +79,7 @@
     space, total = rest[outs:outs + 2]
     span, node = place_ref[0], place_ref[1]
     row_count = total.shape[0]
-    offered = listed_ref.shape[1]
+    offered = listed_ref.shape[2]
     z, y, core = node // (SIDE * CORES), (node // CORES) % SIDE, node % CORES
     each = mine_refs[0].shape[0] // SIDE
     if first:
@@ -152,7 +152,7 @@
     fresh = jnp.maximum(linear, 0.0).astype(jnp.bfloat16)
     out_ref[...] = fresh
     if not last:
-        rest[1][...] = offered_rows(listed_ref[...], fresh)
+        rest[1][...] = offered_rows(listed_ref[span], fresh)
     if not first and not last:
         moved_ref = rest[2]
 
@@ -199,8 +199,6 @@
     span = lax.axis_index("layer")
     place = jnp.stack([span, node]).astype(jnp.int32)
     current = lax.dynamic_index_in_dim(features, span, 0, keepdims=False)
-    listed = lax.dynamic_index_in_dim(boundary, span, 0, keepdims=False)
-    lists = lax.dynamic_index_in_dim(pick_index, span, 0, keepdims=False)[0]
     counts, tile_cols = counts[:, 0], tile_cols[:, 0]
     rows_shape = jax.ShapeDtypeStruct((row_count, width), jnp.bfloat16)
     wide_shape = jax.ShapeDtypeStruct((tile_total, TILE, CORES * offered), jnp.bfloat16)
@@ -212,7 +210,7 @@
         in_specs=[SMEM, VMEM, VMEM, VMEM],
         out_specs=VMEM,
         compiler_params=params,
-    )(place, current, listed, lists)
+    )(place, current, boundary, pick_index)
     previous = lax.dynamic_index_in_dim(features, jnp.maximum(span - 1, 0), 0, keepdims=False)
     tiles = lax.dynamic_index_in_dim(tile_vals, span, 0, keepdims=False)[0]
     known = forward = back = None
@@ -250,7 +248,7 @@
             out_specs=[VMEM] * len(outs),
             scratch_shapes=scratch,
             compiler_params=params,
-        )(place, counts, tile_cols, listed, current, previous, tiles, *known, *mine, *theirs, *([] if first else [back]))
+        )(place, counts, tile_cols, boundary, current, previous, tiles, *known, *mine, *theirs, *([] if first else [back]))
         current = results[0]
         if not last:
             block = results[1]

time: 162 us -> 160 us (0.988)
  no operation moved by 1% of the time
where the time goes in v6:
time: 160 us
  waiting for transfers between devices  73.1 us (46%)
  starting transfers between devices  67.1 us (42%)
  Pallas kernels  14.9 us (9%)
  local copies, waits for them, and re-layouts  3.41 us (2%)
    ppermute x24, starting transfers between devices, along(): return lax.ppermute(block, 'node', route)  39.1 us
    ppermute x24, waiting for transfers between devices, along(): return lax.ppermute(block, 'node', route)  33.6 us
    ppermute x15, waiting for transfers between devices, to_plane(): return lax.ppermute(block, 'layer', pairs)  32.8 us
    ppermute x15, starting transfers between devices, to_plane(): return lax.ppermute(block, 'layer', pairs)  25.4 us
    pallas_call x4, Pallas kernels, on_device(): pl.pallas_call(functools.partial(layer_kernel, layer_id, first, last), ou...  12.7 us
    ppermute x17, waiting for transfers between devices, other_core(): return lax.ppermute(block, 'node', route)  6.75 us
  transfers between devices with their start and end apart: 56, of which 30 were waited for; matrix products, arithmetic and copies ran while one was open for 1% of the time, Pallas kernels for 1%

profile of v6, /device:TPU:6, one launch (start us, length us, event | category | flops | bytes accessed | tf_op | source)
XLA Modules:
  0.0 160.2 jit_solution(12203016163641731295)
XLA Ops:
  0.1 2.2 %dynamic-slice_bitcast_fusion.1 = (bf16[512,512]{1,0:T(8,128)(2,1)}, bf16[512,512]{1,0:T(8,128)(2,1)S(1)}) fusion(bf16[4,512,512]{2,1,0:T(8,128)(2,1)} %param.7, s32[]{:T(128)S(6)} %max.3, s32[]{:T(128)S(6)} %select_n.17), kind=kLoop, calls=%fused_computation.3 | loop fusion | bytes 2097160 | tf_op jit(solution)/shard_map/jit(dynamic_index_in_dim)/squeeze | solution.py:214
  2.3 0.8 shard_map.73
  3.1 1.6 %collective-permute-start.4 = (bf16[144,512]{1,0:T(8,128)(2,1)S(1)}, bf16[144,512]{1,0:T(8,128)(2,1)S(1)}, u32[]{:S(2)}, u32[]{:S(2)}) collective-permute-start(bf16[144,512]{1,0:T(8,128)(2,1)S(1)} %shard_map.73), channel_id=1, source_target_pairs={{0,2},{1,9},{2,4},{3,11},{4,6},{5,13},{6,0},{7,15},{8,10},{9,17},{... | collective-permute-start | bytes 442376 | tf_op jit(solution)/shard_map/ppermute | solution.py:33
  4.8 2.9 %collective-permute-start.5 = (bf16[144,512]{1,0:T(8,128)(2,1)S(1)}, bf16[144,512]{1,0:T(8,128)(2,1)}, u32[]{:S(2)}, u32[]{:S(2)}) collective-permute-start(bf16[144,512]{1,0:T(8,128)(2,1)S(1)} %shard_map.73), channel_id=1, source_target_pairs={{0,4},{1,17},{2,6},{3,19},{4,0},{5,21},{6,2},{7,23},{8,12},{9,25},... | collective-permute-start | bytes 442376 | tf_op jit(solution)/shard_map/ppermute | solution.py:33
  7.7 1.3 collective-permute-start.6
  9.0 1.0 dynamic-slice_bitcast_fusion.3
  10.6 2.4 %collective-permute-start.1 = (bf16[256,512]{1,0:T(8,128)(2,1)S(1)}, bf16[256,512]{1,0:T(8,128)(2,1)S(1)}, u32[]{:S(2)}, u32[]{:S(2)}) collective-permute-start(bf16[256,512]{1,0:T(8,128)(2,1)S(1)} %dynamic-slice_bitcast_fusion.3), channel_id=1, source_target_pairs={{0,64},{32,96},{64,0},{96,32},{1,65},{33,97},{65,1},{97,33},{2,66}... | collective-permute-start | bytes 786440 | tf_op jit(solution)/shard_map/ppermute | solution.py:42
  13.0 1.0 pad_maximum_fusion.1.rest_0_
  14.0 2.0 %collective-permute-start.7 = (bf16[576,512]{1,0:T(8,128)(2,1)S(1)}, bf16[576,512]{1,0:T(8,128)(2,1)S(1)}, u32[]{:S(2)}, u32[]{:S(2)}) collective-permute-start(bf16[576,512]{1,0:T(8,128)(2,1)S(1)} %pad_maximum_fusion.1.rest_0_), channel_id=1, source_target_pairs={{0,8},{1,3},{2,10},{3,5},{4,12},{5,7},{6,14},{7,1},{8,16},{9,11},{... | collective-permute-start | bytes 1769480 | tf_op jit(solution)/shard_map/ppermute | solution.py:33
  16.0 3.6 %collective-permute-start.8 = (bf16[576,512]{1,0:T(8,128)(2,1)S(1)}, bf16[576,512]{1,0:T(8,128)(2,1)S(1)}, u32[]{:S(2)}, u32[]{:S(2)}) collective-permute-start(bf16[576,512]{1,0:T(8,128)(2,1)S(1)} %pad_maximum_fusion.1.rest_0_), channel_id=1, source_target_pairs={{0,16},{1,5},{2,18},{3,7},{4,20},{5,1},{6,22},{7,3},{8,24},{9,13},... | collective-permute-start | bytes 1769480 | tf_op jit(solution)/shard_map/ppermute | solution.py:33
  19.6 1.5 collective-permute-start.9
  21.4 4.0 %collective-permute-done.2 = bf16[256,512]{1,0:T(8,128)(2,1)S(1)} collective-permute-done((bf16[256,512]{1,0:T(8,128)(2,1)S(1)}, bf16[256,512]{1,0:T(8,128)(2,1)S(1)}, u32[]{:S(2)}, u32[]{:S(2)}) %collective-permute-start.2) | collective-permute-done | bytes 262176 | tf_op jit(solution)/shard_map/ppermute | solution.py:42
  26.1 7.7 %collective-permute-done.8.rest_2_ = bf16[576,512]{1,0:T(8,128)(2,1)S(1)} collective-permute-done((bf16[576,512]{1,0:T(8,128)(2,1)S(1)}, bf16[576,512]{1,0:T(8,128)(2,1)S(1)}, u32[]{:S(2)}, u32[]{:S(2)}) %collective-permute-start.8) | collective-permute-done | bytes 589856 | tf_op jit(solution)/shard_map/ppermute | solution.py:33
  34.4 1.4 collective-permute-done.12.rest_6_
  35.8 0.8 collective-permute-done.13.rest_7_
  36.7 5.2 %shard_map.74 = (bf16[512,512]{1,0:T(8,128)(2,1)S(1)}, bf16[128,512]{1,0:T(8,128)(2,1)S(1)}, bf16[20,128,256]{2,1,0:T(8,128)(2,1)S(1)}) custom-call(s32[2]{0:T(128)S(1)} %pad_add_fusion.place_ref, s32[4,4]{1,0:T(4,128)S(1)} %bitcast.12, s32[4,20]{1,0:T(4,128)S(1)} %bitcast.16, s32[4,1,128]{2,1,0:T(1,128)S(1)} %copy-done.3, ...), custom_call_target="tpu_custom_call" | custom-call | tf_op jit(solution)/shard_map/pallas_call | solution.py:244
  41.8 1.2 collective-permute-start.15
  43.0 2.8 %collective-permute-start.16 = (bf16[128,512]{1,0:T(8,128)(2,1)S(1)}, bf16[128,512]{1,0:T(8,128)(2,1)S(1)}, u32[]{:S(2)}, u32[]{:S(2)}) collective-permute-start(bf16[128,512]{1,0:T(8,128)(2,1)S(1)} %get-tuple-element.16), channel_id=1, source_target_pairs={{0,4},{1,17},{2,6},{3,19},{4,0},{5,21},{6,2},{7,23},{8,12},{9,25},... | collective-permute-start | bytes 393224 | tf_op jit(solution)/shard_map/ppermute | solution.py:33
  45.8 1.1 collective-permute-start.17
  46.9 1.7 %collective-permute-start.14 = (bf16[512,512]{1,0:T(8,128)(2,1)S(1)}, bf16[512,512]{1,0:T(8,128)(2,1)S(1)}, u32[]{:S(2)}, u32[]{:S(2)}) collective-permute-start(bf16[512,512]{1,0:T(8,128)(2,1)S(1)} %get-tuple-element.14.current_ref.refs_0_), channel_id=1, source_target_pairs={{0,32},{32,64},{64,96},{96,0},{1,33},{33,65},{65,97},{97,1},{2,34}... | collective-permute-start | bytes 1572872 | tf_op jit(solution)/shard_map/ppermute | solution.py:42
  48.7 1.5 collective-permute-done.16
  50.2 0.7 collective-permute-done.17
  50.9 0.7 collective-permute-start.18
  51.6 2.1 %collective-permute-start.19 = (bf16[512,512]{1,0:T(8,128)(2,1)S(1)}, bf16[512,512]{1,0:T(8,128)(2,1)S(1)}, u32[]{:S(2)}, u32[]{:S(2)}) collective-permute-start(bf16[512,512]{1,0:T(8,128)(2,1)S(1)} %constant_dynamic-update-slice_fusion.rest_0_), channel_id=1, source_target_pairs={{0,16},{1,5},{2,18},{3,7},{4,20},{5,1},{6,22},{7,3},{8,24},{9,13},... | collective-permute-start | bytes 1572872 | tf_op jit(solution)/shard_map/ppermute | solution.py:33
  53.7 1.5 collective-permute-start.20
  55.9 4.2 %collective-permute-done.14.previous_ref.refs_1_ = bf16[512,512]{1,0:T(8,128)(2,1)S(1)} collective-permute-done((bf16[512,512]{1,0:T(8,128)(2,1)S(1)}, bf16[512,512]{1,0:T(8,128)(2,1)S(1)}, u32[]{:S(2)}, u32[]{:S(2)}) %collective-permute-start.14) | collective-permute-done | bytes 524320 | tf_op jit(solution)/shard_map/ppermute | solution.py:42
  60.1 6.8 %collective-permute-done.18.rest_1_ = bf16[512,512]{1,0:T(8,128)(2,1)S(1)} collective-permute-done((bf16[512,512]{1,0:T(8,128)(2,1)S(1)}, bf16[512,512]{1,0:T(8,128)(2,1)S(1)}, u32[]{:S(2)}, u32[]{:S(2)}) %collective-permute-start.18) | collective-permute-done | bytes 524320 | tf_op jit(solution)/shard_map/ppermute | solution.py:33
  67.9 1.0 collective-permute-done.22.rest_5_
  68.9 0.7 collective-permute-done.23.rest_6_
  69.6 0.7 collective-permute-done.24.rest_7_
  70.4 2.6 %shard_map.75 = (bf16[512,512]{1,0:T(8,128)(2,1)S(1)}, bf16[128,512]{1,0:T(8,128)(2,1)S(1)}, bf16[512,512]{1,0:T(8,128)(2,1)S(1)}) custom-call(s32[2]{0:T(128)S(1)} %pad_add_fusion.place_ref, s32[4,4]{1,0:T(4,128)S(1)} %bitcast.13, s32[4,20]{1,0:T(4,128)S(1)} %bitcast.17, s32[4,1,128]{2,1,0:T(1,128)S(1)} %copy-done.3, ...), custom_call_target="tpu_custom_call" | custom-call | tf_op jit(solution)/shard_map/pallas_call | solution.py:244
  73.0 1.2 collective-permute-start.28
  74.2 2.5 %collective-permute-start.29 = (bf16[128,512]{1,0:T(8,128)(2,1)S(1)}, bf16[128,512]{1,0:T(8,128)(2,1)S(1)}, u32[]{:S(2)}, u32[]{:S(2)}) collective-permute-start(bf16[128,512]{1,0:T(8,128)(2,1)S(1)} %get-tuple-element.19), channel_id=1, source_target_pairs={{0,4},{1,17},{2,6},{3,19},{4,0},{5,21},{6,2},{7,23},{8,12},{9,25},... | collective-permute-start | bytes 393224 | tf_op jit(solution)/shard_map/ppermute | solution.py:33
  76.8 0.8 collective-permute-start.30
  77.5 2.8 %collective-permute-start.26 = (bf16[512,512]{1,0:T(8,128)(2,1)S(1)}, bf16[512,512]{1,0:T(8,128)(2,1)S(1)}, u32[]{:S(2)}, u32[]{:S(2)}) collective-permute-start(bf16[512,512]{1,0:T(8,128)(2,1)S(1)} %get-tuple-element.17), channel_id=1, source_target_pairs={{64,32},{96,64},{32,0},{65,33},{97,65},{33,1},{66,34},{98,66},{34,... | collective-permute-start | bytes 1572872 | tf_op jit(solution)/shard_map/ppermute | solution.py:42
  80.3 0.8 collective-permute-done.29
  81.1 0.7 collective-permute-done.30
  82.3 3.1 %collective-permute-start.32 = (bf16[512,512]{1,0:T(8,128)(2,1)S(1)}, bf16[512,512]{1,0:T(8,128)(2,1)S(1)}, u32[]{:S(2)}, u32[]{:S(2)}) collective-permute-start(bf16[512,512]{1,0:T(8,128)(2,1)S(1)} %constant_dynamic-update-slice_fusion.4.rest_0_), channel_id=1, source_target_pairs={{0,16},{1,5},{2,18},{3,7},{4,20},{5,1},{6,22},{7,3},{8,24},{9,13},... | collective-permute-start | bytes 1572872 | tf_op jit(solution)/shard_map/ppermute | solution.py:33
  85.6 3.1 %collective-permute-start.27 = (bf16[512,512]{1,0:T(8,128)(2,1)S(1)}, bf16[512,512]{1,0:T(8,128)(2,1)S(1)}, u32[]{:S(2)}, u32[]{:S(2)}) collective-permute-start(bf16[512,512]{1,0:T(8,128)(2,1)S(1)} %get-tuple-element.18.current_ref.refs_4_), channel_id=1, source_target_pairs={{0,32},{32,64},{64,96},{96,0},{1,33},{33,65},{65,97},{97,1},{2,34}... | collective-permute-start | bytes 1572872 | tf_op jit(solution)/shard_map/ppermute | solution.py:42
  88.7 1.6 collective-permute-done.26.rest_8_.refs_2_.refs_7_
  90.3 2.0 %collective-permute-done.31.rest_1_ = bf16[512,512]{1,0:T(8,128)(2,1)S(1)} collective-permute-done((bf16[512,512]{1,0:T(8,128)(2,1)S(1)}, bf16[512,512]{1,0:T(8,128)(2,1)S(1)}, u32[]{:S(2)}, u32[]{:S(2)}) %collective-permute-start.31) | collective-permute-done | bytes 524320 | tf_op jit(solution)/shard_map/ppermute | solution.py:33
  92.3 5.9 %collective-permute-done.32.rest_2_ = bf16[512,512]{1,0:T(8,128)(2,1)S(1)} collective-permute-done((bf16[512,512]{1,0:T(8,128)(2,1)S(1)}, bf16[512,512]{1,0:T(8,128)(2,1)S(1)}, u32[]{:S(2)}, u32[]{:S(2)}) %collective-permute-start.32) | collective-permute-done | bytes 524320 | tf_op jit(solution)/shard_map/ppermute | solution.py:33
  98.8 1.2 collective-permute-done.36.rest_6_
  100.1 0.7 collective-permute-done.37.rest_7_
  100.8 2.6 %shard_map.76 = (bf16[512,512]{1,0:T(8,128)(2,1)S(1)}, bf16[128,512]{1,0:T(8,128)(2,1)S(1)}, bf16[512,512]{1,0:T(8,128)(2,1)S(1)}) custom-call(s32[2]{0:T(128)S(1)} %pad_add_fusion.place_ref, s32[4,4]{1,0:T(4,128)S(1)} %bitcast.14, s32[4,20]{1,0:T(4,128)S(1)} %bitcast.18, s32[4,1,128]{2,1,0:T(1,128)S(1)} %copy-done.3, ...), custom_call_target="tpu_custom_call" | custom-call | tf_op jit(solution)/shard_map/pallas_call | solution.py:244
  103.4 0.9 collective-permute-start.41
  104.3 3.0 %collective-permute-start.42 = (bf16[128,512]{1,0:T(8,128)(2,1)S(1)}, bf16[128,512]{1,0:T(8,128)(2,1)S(1)}, u32[]{:S(2)}, u32[]{:S(2)}) collective-permute-start(bf16[128,512]{1,0:T(8,128)(2,1)S(1)} %get-tuple-element.22), channel_id=1, source_target_pairs={{0,4},{1,17},{2,6},{3,19},{4,0},{5,21},{6,2},{7,23},{8,12},{9,25},... | collective-permute-start | bytes 393224 | tf_op jit(solution)/shard_map/ppermute | solution.py:33
  107.7 2.8 %collective-permute-start.38 = (bf16[512,512]{1,0:T(8,128)(2,1)S(1)}, bf16[512,512]{1,0:T(8,128)(2,1)S(1)}, u32[]{:S(2)}, u32[]{:S(2)}) collective-permute-start(bf16[512,512]{1,0:T(8,128)(2,1)S(1)} %get-tuple-element.20), channel_id=1, source_target_pairs={{96,64},{0,96},{64,32},{97,65},{1,97},{65,33},{98,66},{2,98},{66,3... | collective-permute-start | bytes 1572872 | tf_op jit(solution)/shard_map/ppermute | solution.py:42
  110.5 1.1 collective-permute-done.42
  111.7 0.7 collective-permute-done.43
  112.8 3.7 %collective-permute-start.45 = (bf16[512,512]{1,0:T(8,128)(2,1)S(1)}, bf16[512,512]{1,0:T(8,128)(2,1)S(1)}, u32[]{:S(2)}, u32[]{:S(2)}) collective-permute-start(bf16[512,512]{1,0:T(8,128)(2,1)S(1)} %constant_dynamic-update-slice_fusion.8.rest_0_), channel_id=1, source_target_pairs={{0,16},{1,5},{2,18},{3,7},{4,20},{5,1},{6,22},{7,3},{8,24},{9,13},... | collective-permute-start | bytes 1572872 | tf_op jit(solution)/shard_map/ppermute | solution.py:33
  116.4 2.7 %collective-permute-start.39 = (bf16[512,512]{1,0:T(8,128)(2,1)S(1)}, bf16[512,512]{1,0:T(8,128)(2,1)S(1)}, u32[]{:S(2)}, u32[]{:S(2)}) collective-permute-start(bf16[512,512]{1,0:T(8,128)(2,1)S(1)} %get-tuple-element.21.current_ref.refs_8_), channel_id=1, source_target_pairs={{0,32},{32,64},{64,96},{96,0},{1,33},{33,65},{65,97},{97,1},{2,34}... | collective-permute-start | bytes 1572872 | tf_op jit(solution)/shard_map/ppermute | solution.py:42
  119.2 4.9 %collective-permute-done.38.rest_8_.refs_6_.refs_11_ = bf16[512,512]{1,0:T(8,128)(2,1)S(1)} collective-permute-done((bf16[512,512]{1,0:T(8,128)(2,1)S(1)}, bf16[512,512]{1,0:T(8,128)(2,1)S(1)}, u32[]{:S(2)}, u32[]{:S(2)}) %collective-permute-start.38) | collective-permute-done | bytes 524320 | tf_op jit(solution)/shard_map/ppermute | solution.py:42
  124.6 4.6 %collective-permute-done.45.rest_2_ = bf16[512,512]{1,0:T(8,128)(2,1)S(1)} collective-permute-done((bf16[512,512]{1,0:T(8,128)(2,1)S(1)}, bf16[512,512]{1,0:T(8,128)(2,1)S(1)}, u32[]{:S(2)}, u32[]{:S(2)}) %collective-permute-start.45) | collective-permute-done | bytes 524320 | tf_op jit(solution)/shard_map/ppermute | solution.py:33
  129.7 2.8 %collective-permute-start.40 = (bf16[512,512]{1,0:T(8,128)(2,1)S(1)}, bf16[512,512]{1,0:T(8,128)(2,1)S(1)}, u32[]{:S(2)}, u32[]{:S(2)}) collective-permute-start(bf16[512,512]{1,0:T(8,128)(2,1)S(1)} %collective-permute-done.38.rest_8_.refs_6_.refs_11_), channel_id=1, source_target_pairs={{96,64},{97,65},{98,66},{99,67},{100,68},{101,69},{102,70},{103,71... | collective-permute-start | bytes 1572872 | tf_op jit(solution)/shard_map/ppermute | solution.py:42
  132.5 2.4 %shard_map.77.refs_12_ = bf16[512,512]{1,0:T(8,128)(2,1)S(1)} custom-call(s32[2]{0:T(128)S(1)} %pad_add_fusion.place_ref, s32[4,4]{1,0:T(4,128)S(1)} %bitcast.15, s32[4,20]{1,0:T(4,128)S(1)} %bitcast.19, s32[4,1,128]{2,1,0:T(1,128)S(1)} %copy-done.3, bf16[512,512]{1,0:T(8,128)(2,1)S(1)} %get-tuple-element.21.current_ref.refs_8_, ...), custom_call_target="tpu_custom_call" | custom-call | tf_op jit(solution)/shard_map/pallas_call | solution.py:244
  135.0 1.3 collective-permute-start.51
  136.3 1.3 collective-permute-start.55
  138.2 1.3 collective-permute-start.54
  139.5 1.3 collective-permute-start.53
  140.8 3.1 %collective-permute-done.40.refs_10_ = bf16[512,512]{1,0:T(8,128)(2,1)S(1)} collective-permute-done((bf16[512,512]{1,0:T(8,128)(2,1)S(1)}, bf16[512,512]{1,0:T(8,128)(2,1)S(1)}, u32[]{:S(2)}, u32[]{:S(2)}) %collective-permute-start.40) | collective-permute-done | bytes 524320 | tf_op jit(solution)/shard_map/ppermute | solution.py:42
  143.9 6.9 %collective-permute-done.54.refs_15_ = bf16[256,512]{1,0:T(8,128)(2,1)S(1)} collective-permute-done((bf16[256,512]{1,0:T(8,128)(2,1)S(1)}, bf16[256,512]{1,0:T(8,128)(2,1)S(1)}, u32[]{:S(2)}, u32[]{:S(2)}) %collective-permute-start.54) | collective-permute-done | bytes 262176 | tf_op jit(solution)/shard_map/ppermute | solution.py:42
  150.9 7.8 %collective-permute-done.55.refs_16_ = bf16[512,512]{1,0:T(8,128)(2,1)S(1)} collective-permute-done((bf16[512,512]{1,0:T(8,128)(2,1)S(1)}, bf16[512,512]{1,0:T(8,128)(2,1)S(1)}, u32[]{:S(2)}, u32[]{:S(2)}) %collective-permute-start.55) | collective-permute-done | bytes 524320 | tf_op jit(solution)/shard_map/ppermute | solution.py:42
  158.7 1.4 shard_map.78
  (85 shorter events, 7.9 us)
Async XLA Ops:
  0.0 34.3 %copy-start = (bf16[4,1,20,128,128]{4,3,2,1,0:T(8,128)(2,1)S(1)}, bf16[4,1,20,128,128]{4,3,2,1,0:T(8,128)(2,1)}, u32[]{:S(2)}) copy-start(bf16[4,1,20,128,128]{4,3,2,1,0:T(8,128)(2,1)} %param.13) | copy-start | bytes 7864324
  0.0 2.3 %copy-start.2 = (s32[4,1,32,64]{3,2,1,0:T(8,128)S(1)}, s32[4,1,32,64]{3,2,1,0:T(8,128)}, u32[]{:S(2)}) copy-start(s32[4,1,32,64]{3,2,1,0:T(8,128)} %lists_ref.1) | copy-start | bytes 98308
  0.0 2.3 %copy-start.3 = (s32[4,1,128]{2,1,0:T(1,128)S(1)}, s32[4,1,128]{2,1,0:T(1,128)}, u32[]{:S(2)}) copy-start(s32[4,1,128]{2,1,0:T(1,128)} %listed_ref.9) | copy-start | bytes 6148
  3.1 9.9 %collective-permute-start.4 = (bf16[144,512]{1,0:T(8,128)(2,1)S(1)}, bf16[144,512]{1,0:T(8,128)(2,1)S(1)}, u32[]{:S(2)}, u32[]{:S(2)}) collective-permute-start(bf16[144,512]{1,0:T(8,128)(2,1)S(1)} %shard_map.73), channel_id=1, source_target_pairs={{0,2},{1,9},{2,4},{3,11},{4,6},{5,13},{6,0},{7,15},{8,10},{9,17},{... | collective-permute-start | bytes 442376 | tf_op jit(solution)/shard_map/ppermute | solution.py:33
  4.8 8.2 %collective-permute-start.5 = (bf16[144,512]{1,0:T(8,128)(2,1)S(1)}, bf16[144,512]{1,0:T(8,128)(2,1)}, u32[]{:S(2)}, u32[]{:S(2)}) collective-permute-start(bf16[144,512]{1,0:T(8,128)(2,1)S(1)} %shard_map.73), channel_id=1, source_target_pairs={{0,4},{1,17},{2,6},{3,19},{4,0},{5,21},{6,2},{7,23},{8,12},{9,25},... | collective-permute-start | bytes 442376 | tf_op jit(solution)/shard_map/ppermute | solution.py:33
  7.7 5.3 %collective-permute-start.6 = (bf16[144,512]{1,0:T(8,128)(2,1)S(1)}, bf16[144,512]{1,0:T(8,128)(2,1)}, u32[]{:S(2)}, u32[]{:S(2)}) collective-permute-start(bf16[144,512]{1,0:T(8,128)(2,1)S(1)} %shard_map.73), channel_id=1, source_target_pairs={{0,6},{1,25},{2,0},{3,27},{4,2},{5,29},{6,4},{7,31},{8,14},{9,1},{... | collective-permute-start | bytes 442376 | tf_op jit(solution)/shard_map/ppermute | solution.py:33
  10.0 26.6 %copy-start.1 = (bf16[512,512]{1,0:T(8,128)(2,1)S(1)}, bf16[512,512]{1,0:T(8,128)(2,1)}, u32[]{:S(2)}) copy-start(bf16[512,512]{1,0:T(8,128)(2,1)} %get-tuple-element.23.previous_ref) | copy-start | bytes 1572868
  10.0 26.6 %copy-start.4 = (s32[4,1,4]{2,1,0:T(1,128)S(1)}, s32[4,1,4]{2,1,0:T(1,128)}, u32[]{:S(2)}) copy-start(s32[4,1,4]{2,1,0:T(1,128)} %param.11) | copy-start | bytes 196
  10.0 26.6 %copy-start.5 = (s32[4,1,20]{2,1,0:T(1,128)S(1)}, s32[4,1,20]{2,1,0:T(1,128)}, u32[]{:S(2)}) copy-start(s32[4,1,20]{2,1,0:T(1,128)} %param.12) | copy-start | bytes 964
  10.0 9.6 %collective-permute-start = (bf16[256,512]{1,0:T(8,128)(2,1)S(1)}, bf16[256,512]{1,0:T(8,128)(2,1)S(1)}, u32[]{:S(2)}, u32[]{:S(2)}) collective-permute-start(bf16[256,512]{1,0:T(8,128)(2,1)S(1)} %dynamic-slice_bitcast_fusion.3), channel_id=1, source_target_pairs={{0,32},{32,64},{64,96},{96,0},{1,33},{33,65},{65,97},{97,1},{2,34}... | collective-permute-start | bytes 786440 | tf_op jit(solution)/shard_map/ppermute | solution.py:42
  10.6 10.8 %collective-permute-start.1 = (bf16[256,512]{1,0:T(8,128)(2,1)S(1)}, bf16[256,512]{1,0:T(8,128)(2,1)S(1)}, u32[]{:S(2)}, u32[]{:S(2)}) collective-permute-start(bf16[256,512]{1,0:T(8,128)(2,1)S(1)} %dynamic-slice_bitcast_fusion.3), channel_id=1, source_target_pairs={{0,64},{32,96},{64,0},{96,32},{1,65},{33,97},{65,1},{97,33},{2,66}... | collective-permute-start | bytes 786440 | tf_op jit(solution)/shard_map/ppermute | solution.py:42
  13.0 12.4 %collective-permute-start.2 = (bf16[256,512]{1,0:T(8,128)(2,1)S(1)}, bf16[256,512]{1,0:T(8,128)(2,1)S(1)}, u32[]{:S(2)}, u32[]{:S(2)}) collective-permute-start(bf16[256,512]{1,0:T(8,128)(2,1)S(1)} %dynamic-slice_bitcast_fusion.3), channel_id=1, source_target_pairs={{0,96},{32,0},{64,32},{96,64},{1,97},{33,1},{65,33},{97,65},{2,98}... | collective-permute-start | bytes 786440 | tf_op jit(solution)/shard_map/ppermute | solution.py:42
  14.0 12.0 %collective-permute-start.7 = (bf16[576,512]{1,0:T(8,128)(2,1)S(1)}, bf16[576,512]{1,0:T(8,128)(2,1)S(1)}, u32[]{:S(2)}, u32[]{:S(2)}) collective-permute-start(bf16[576,512]{1,0:T(8,128)(2,1)S(1)} %pad_maximum_fusion.1.rest_0_), channel_id=1, source_target_pairs={{0,8},{1,3},{2,10},{3,5},{4,12},{5,7},{6,14},{7,1},{8,16},{9,11},{... | collective-permute-start | bytes 1769480 | tf_op jit(solution)/shard_map/ppermute | solution.py:33
  16.0 17.8 %collective-permute-start.8 = (bf16[576,512]{1,0:T(8,128)(2,1)S(1)}, bf16[576,512]{1,0:T(8,128)(2,1)S(1)}, u32[]{:S(2)}, u32[]{:S(2)}) collective-permute-start(bf16[576,512]{1,0:T(8,128)(2,1)S(1)} %pad_maximum_fusion.1.rest_0_), channel_id=1, source_target_pairs={{0,16},{1,5},{2,18},{3,7},{4,20},{5,1},{6,22},{7,3},{8,24},{9,13},... | collective-permute-start | bytes 1769480 | tf_op jit(solution)/shard_map/ppermute | solution.py:33
  19.6 14.2 %collective-permute-start.9 = (bf16[576,512]{1,0:T(8,128)(2,1)S(1)}, bf16[576,512]{1,0:T(8,128)(2,1)S(1)}, u32[]{:S(2)}, u32[]{:S(2)}) collective-permute-start(bf16[576,512]{1,0:T(8,128)(2,1)S(1)} %pad_maximum_fusion.1.rest_0_), channel_id=1, source_target_pairs={{0,24},{1,7},{2,26},{3,1},{4,28},{5,3},{6,30},{7,5},{8,0},{9,15},{... | collective-permute-start | bytes 1769480 | tf_op jit(solution)/shard_map/ppermute | solution.py:33
  25.4 8.9 %collective-permute-start.3 = (bf16[1024,512]{1,0:T(8,128)(2,1)S(1)}, bf16[1024,512]{1,0:T(8,128)(2,1)S(1)}, u32[]{:S(2)}, u32[]{:S(2)}) collective-permute-start(bf16[1024,512]{1,0:T(8,128)(2,1)S(1)} %pad_maximum_fusion.halves_ref), channel_id=1, source_target_pairs={{0,1},{1,0},{2,3},{3,2},{4,5},{5,4},{6,7},{7,6},{8,9},{9,8},{10,11... | collective-permute-start | bytes 3145736 | tf_op jit(solution)/shard_map/ppermute | solution.py:38
  25.5 8.8 %collective-permute-start.10 = (bf16[576,512]{1,0:T(8,128)(2,1)S(1)}, bf16[576,512]{1,0:T(8,128)(2,1)S(1)}, u32[]{:S(2)}, u32[]{:S(2)}) collective-permute-start(bf16[576,512]{1,0:T(8,128)(2,1)S(1)} %pad_maximum_fusion.1.rest_0_), channel_id=1, source_target_pairs={{0,1},{1,0},{2,3},{3,2},{4,5},{5,4},{6,7},{7,6},{8,9},{9,8},{10,11... | collective-permute-start | bytes 1769480 | tf_op jit(solution)/shard_map/ppermute | solution.py:38
  26.0 8.4 %collective-permute-start.11 = (bf16[576,512]{1,0:T(8,128)(2,1)S(1)}, bf16[576,512]{1,0:T(8,128)(2,1)S(1)}, u32[]{:S(2)}, u32[]{:S(2)}) collective-permute-start(bf16[576,512]{1,0:T(8,128)(2,1)S(1)} %collective-permute-done.7.rest_1_), channel_id=1, source_target_pairs={{0,1},{1,0},{2,3},{3,2},{4,5},{5,4},{6,7},{7,6},{8,9},{9,8},{10,11... | collective-permute-start | bytes 1769480 | tf_op jit(solution)/shard_map/ppermute | solution.py:38
  33.8 2.0 %collective-permute-start.12 = (bf16[576,512]{1,0:T(8,128)(2,1)S(1)}, bf16[576,512]{1,0:T(8,128)(2,1)S(1)}, u32[]{:S(2)}, u32[]{:S(2)}) collective-permute-start(bf16[576,512]{1,0:T(8,128)(2,1)S(1)} %collective-permute-done.8.rest_2_), channel_id=1, source_target_pairs={{0,1},{1,0},{2,3},{3,2},{4,5},{5,4},{6,7},{7,6},{8,9},{9,8},{10,11... | collective-permute-start | bytes 1769480 | tf_op jit(solution)/shard_map/ppermute | solution.py:38
  33.8 2.8 %collective-permute-start.13 = (bf16[576,512]{1,0:T(8,128)(2,1)S(1)}, bf16[576,512]{1,0:T(8,128)(2,1)S(1)}, u32[]{:S(2)}, u32[]{:S(2)}) collective-permute-start(bf16[576,512]{1,0:T(8,128)(2,1)S(1)} %collective-permute-done.9.rest_3_), channel_id=1, source_target_pairs={{0,1},{1,0},{2,3},{3,2},{4,5},{5,4},{6,7},{7,6},{8,9},{9,8},{10,11... | collective-permute-start | bytes 1769480 | tf_op jit(solution)/shard_map/ppermute | solution.py:38
  41.8 6.8 %collective-permute-start.15 = (bf16[128,512]{1,0:T(8,128)(2,1)S(1)}, bf16[128,512]{1,0:T(8,128)(2,1)S(1)}, u32[]{:S(2)}, u32[]{:S(2)}) collective-permute-start(bf16[128,512]{1,0:T(8,128)(2,1)S(1)} %get-tuple-element.16), channel_id=1, source_target_pairs={{0,2},{1,9},{2,4},{3,11},{4,6},{5,13},{6,0},{7,15},{8,10},{9,17},{... | collective-permute-start | bytes 393224 | tf_op jit(solution)/shard_map/ppermute | solution.py:33
  43.0 7.2 %collective-permute-start.16 = (bf16[128,512]{1,0:T(8,128)(2,1)S(1)}, bf16[128,512]{1,0:T(8,128)(2,1)S(1)}, u32[]{:S(2)}, u32[]{:S(2)}) collective-permute-start(bf16[128,512]{1,0:T(8,128)(2,1)S(1)} %get-tuple-element.16), channel_id=1, source_target_pairs={{0,4},{1,17},{2,6},{3,19},{4,0},{5,21},{6,2},{7,23},{8,12},{9,25},... | collective-permute-start | bytes 393224 | tf_op jit(solution)/shard_map/ppermute | solution.py:33
  45.8 5.0 %collective-permute-start.17 = (bf16[128,512]{1,0:T(8,128)(2,1)S(1)}, bf16[128,512]{1,0:T(8,128)(2,1)S(1)}, u32[]{:S(2)}, u32[]{:S(2)}) collective-permute-start(bf16[128,512]{1,0:T(8,128)(2,1)S(1)} %get-tuple-element.16), channel_id=1, source_target_pairs={{0,6},{1,25},{2,0},{3,27},{4,2},{5,29},{6,4},{7,31},{8,14},{9,1},{... | collective-permute-start | bytes 393224 | tf_op jit(solution)/shard_map/ppermute | solution.py:33
  46.9 13.2 %collective-permute-start.14 = (bf16[512,512]{1,0:T(8,128)(2,1)S(1)}, bf16[512,512]{1,0:T(8,128)(2,1)S(1)}, u32[]{:S(2)}, u32[]{:S(2)}) collective-permute-start(bf16[512,512]{1,0:T(8,128)(2,1)S(1)} %get-tuple-element.14.current_ref.refs_0_), channel_id=1, source_target_pairs={{0,32},{32,64},{64,96},{96,0},{1,33},{33,65},{65,97},{97,1},{2,34}... | collective-permute-start | bytes 1572872 | tf_op jit(solution)/shard_map/ppermute | solution.py:42
  50.9 16.1 %collective-permute-start.18 = (bf16[512,512]{1,0:T(8,128)(2,1)S(1)}, bf16[512,512]{1,0:T(8,128)(2,1)S(1)}, u32[]{:S(2)}, u32[]{:S(2)}) collective-permute-start(bf16[512,512]{1,0:T(8,128)(2,1)S(1)} %constant_dynamic-update-slice_fusion.rest_0_), channel_id=1, source_target_pairs={{0,8},{1,3},{2,10},{3,5},{4,12},{5,7},{6,14},{7,1},{8,16},{9,11},{... | collective-permute-start | bytes 1572872 | tf_op jit(solution)/shard_map/ppermute | solution.py:33
  51.6 15.3 %collective-permute-start.19 = (bf16[512,512]{1,0:T(8,128)(2,1)S(1)}, bf16[512,512]{1,0:T(8,128)(2,1)S(1)}, u32[]{:S(2)}, u32[]{:S(2)}) collective-permute-start(bf16[512,512]{1,0:T(8,128)(2,1)S(1)} %constant_dynamic-update-slice_fusion.rest_0_), channel_id=1, source_target_pairs={{0,16},{1,5},{2,18},{3,7},{4,20},{5,1},{6,22},{7,3},{8,24},{9,13},... | collective-permute-start | bytes 1572872 | tf_op jit(solution)/shard_map/ppermute | solution.py:33
  53.7 14.1 %collective-permute-start.20 = (bf16[512,512]{1,0:T(8,128)(2,1)S(1)}, bf16[512,512]{1,0:T(8,128)(2,1)S(1)}, u32[]{:S(2)}, u32[]{:S(2)}) collective-permute-start(bf16[512,512]{1,0:T(8,128)(2,1)S(1)} %constant_dynamic-update-slice_fusion.rest_0_), channel_id=1, source_target_pairs={{0,24},{1,7},{2,26},{3,1},{4,28},{5,3},{6,30},{7,5},{8,0},{9,15},{... | collective-permute-start | bytes 1572872 | tf_op jit(solution)/shard_map/ppermute | solution.py:33
  55.3 12.6 %collective-permute-start.25 = (bf16[512,512]{1,0:T(8,128)(2,1)S(1)}, bf16[512,512]{1,0:T(8,128)(2,1)S(1)}, u32[]{:S(2)}, u32[]{:S(2)}) collective-permute-start(bf16[512,512]{1,0:T(8,128)(2,1)S(1)} %get-tuple-element.14.current_ref.refs_0_), channel_id=1, source_target_pairs={{32,0},{64,32},{33,1},{65,33},{34,2},{66,34},{35,3},{67,35},{36,4}... | collective-permute-start | bytes 1572872 | tf_op jit(solution)/shard_map/ppermute | solution.py:42
  60.1 7.7 %collective-permute-start.21 = (bf16[512,512]{1,0:T(8,128)(2,1)S(1)}, bf16[512,512]{1,0:T(8,128)(2,1)S(1)}, u32[]{:S(2)}, u32[]{:S(2)}) collective-permute-start(bf16[512,512]{1,0:T(8,128)(2,1)S(1)} %constant_dynamic-update-slice_fusion.rest_0_), channel_id=1, source_target_pairs={{0,1},{1,0},{2,3},{3,2},{4,5},{5,4},{6,7},{7,6},{8,9},{9,8},{10,11... | collective-permute-start | bytes 1572872 | tf_op jit(solution)/shard_map/ppermute | solution.py:38
  67.0 1.9 %collective-permute-start.22 = (bf16[512,512]{1,0:T(8,128)(2,1)S(1)}, bf16[512,512]{1,0:T(8,128)(2,1)S(1)}, u32[]{:S(2)}, u32[]{:S(2)}) collective-permute-start(bf16[512,512]{1,0:T(8,128)(2,1)S(1)} %collective-permute-done.18.rest_1_), channel_id=1, source_target_pairs={{0,1},{1,0},{2,3},{3,2},{4,5},{5,4},{6,7},{7,6},{8,9},{9,8},{10,11... | collective-permute-start | bytes 1572872 | tf_op jit(solution)/shard_map/ppermute | solution.py:38
  67.0 2.7 %collective-permute-start.23 = (bf16[512,512]{1,0:T(8,128)(2,1)S(1)}, bf16[512,512]{1,0:T(8,128)(2,1)S(1)}, u32[]{:S(2)}, u32[]{:S(2)}) collective-permute-start(bf16[512,512]{1,0:T(8,128)(2,1)S(1)} %collective-permute-done.19.rest_2_), channel_id=1, source_target_pairs={{0,1},{1,0},{2,3},{3,2},{4,5},{5,4},{6,7},{7,6},{8,9},{9,8},{10,11... | collective-permute-start | bytes 1572872 | tf_op jit(solution)/shard_map/ppermute | solution.py:38
  67.9 2.5 %collective-permute-start.24 = (bf16[512,512]{1,0:T(8,128)(2,1)S(1)}, bf16[512,512]{1,0:T(8,128)(2,1)S(1)}, u32[]{:S(2)}, u32[]{:S(2)}) collective-permute-start(bf16[512,512]{1,0:T(8,128)(2,1)S(1)} %collective-permute-done.20.rest_3_), channel_id=1, source_target_pairs={{0,1},{1,0},{2,3},{3,2},{4,5},{5,4},{6,7},{7,6},{8,9},{9,8},{10,11... | collective-permute-start | bytes 1572872 | tf_op jit(solution)/shard_map/ppermute | solution.py:38
  73.0 7.3 %collective-permute-start.28 = (bf16[128,512]{1,0:T(8,128)(2,1)S(1)}, bf16[128,512]{1,0:T(8,128)(2,1)S(1)}, u32[]{:S(2)}, u32[]{:S(2)}) collective-permute-start(bf16[128,512]{1,0:T(8,128)(2,1)S(1)} %get-tuple-element.19), channel_id=1, source_target_pairs={{0,2},{1,9},{2,4},{3,11},{4,6},{5,13},{6,0},{7,15},{8,10},{9,17},{... | collective-permute-start | bytes 393224 | tf_op jit(solution)/shard_map/ppermute | solution.py:33
  74.2 6.9 %collective-permute-start.29 = (bf16[128,512]{1,0:T(8,128)(2,1)S(1)}, bf16[128,512]{1,0:T(8,128)(2,1)S(1)}, u32[]{:S(2)}, u32[]{:S(2)}) collective-permute-start(bf16[128,512]{1,0:T(8,128)(2,1)S(1)} %get-tuple-element.19), channel_id=1, source_target_pairs={{0,4},{1,17},{2,6},{3,19},{4,0},{5,21},{6,2},{7,23},{8,12},{9,25},... | collective-permute-start | bytes 393224 | tf_op jit(solution)/shard_map/ppermute | solution.py:33
  76.8 5.0 %collective-permute-start.30 = (bf16[128,512]{1,0:T(8,128)(2,1)S(1)}, bf16[128,512]{1,0:T(8,128)(2,1)S(1)}, u32[]{:S(2)}, u32[]{:S(2)}) collective-permute-start(bf16[128,512]{1,0:T(8,128)(2,1)S(1)} %get-tuple-element.19), channel_id=1, source_target_pairs={{0,6},{1,25},{2,0},{3,27},{4,2},{5,29},{6,4},{7,31},{8,14},{9,1},{... | collective-permute-start | bytes 393224 | tf_op jit(solution)/shard_map/ppermute | solution.py:33
  77.5 12.7 %collective-permute-start.26 = (bf16[512,512]{1,0:T(8,128)(2,1)S(1)}, bf16[512,512]{1,0:T(8,128)(2,1)S(1)}, u32[]{:S(2)}, u32[]{:S(2)}) collective-permute-start(bf16[512,512]{1,0:T(8,128)(2,1)S(1)} %get-tuple-element.17), channel_id=1, source_target_pairs={{64,32},{96,64},{32,0},{65,33},{97,65},{33,1},{66,34},{98,66},{34,... | collective-permute-start | bytes 1572872 | tf_op jit(solution)/shard_map/ppermute | solution.py:42
  81.8 10.5 %collective-permute-start.31 = (bf16[512,512]{1,0:T(8,128)(2,1)S(1)}, bf16[512,512]{1,0:T(8,128)(2,1)S(1)}, u32[]{:S(2)}, u32[]{:S(2)}) collective-permute-start(bf16[512,512]{1,0:T(8,128)(2,1)S(1)} %constant_dynamic-update-slice_fusion.4.rest_0_), channel_id=1, source_target_pairs={{0,8},{1,3},{2,10},{3,5},{4,12},{5,7},{6,14},{7,1},{8,16},{9,11},{... | collective-permute-start | bytes 1572872 | tf_op jit(solution)/shard_map/ppermute | solution.py:33
  82.3 15.9 %collective-permute-start.32 = (bf16[512,512]{1,0:T(8,128)(2,1)S(1)}, bf16[512,512]{1,0:T(8,128)(2,1)S(1)}, u32[]{:S(2)}, u32[]{:S(2)}) collective-permute-start(bf16[512,512]{1,0:T(8,128)(2,1)S(1)} %constant_dynamic-update-slice_fusion.4.rest_0_), channel_id=1, source_target_pairs={{0,16},{1,5},{2,18},{3,7},{4,20},{5,1},{6,22},{7,3},{8,24},{9,13},... | collective-permute-start | bytes 1572872 | tf_op jit(solution)/shard_map/ppermute | solution.py:33
  85.4 13.4 %collective-permute-start.33 = (bf16[512,512]{1,0:T(8,128)(2,1)S(1)}, bf16[512,512]{1,0:T(8,128)(2,1)S(1)}, u32[]{:S(2)}, u32[]{:S(2)}) collective-permute-start(bf16[512,512]{1,0:T(8,128)(2,1)S(1)} %constant_dynamic-update-slice_fusion.4.rest_0_), channel_id=1, source_target_pairs={{0,24},{1,7},{2,26},{3,1},{4,28},{5,3},{6,30},{7,5},{8,0},{9,15},{... | collective-permute-start | bytes 1572872 | tf_op jit(solution)/shard_map/ppermute | solution.py:33
  85.6 13.2 %collective-permute-start.27 = (bf16[512,512]{1,0:T(8,128)(2,1)S(1)}, bf16[512,512]{1,0:T(8,128)(2,1)S(1)}, u32[]{:S(2)}, u32[]{:S(2)}) collective-permute-start(bf16[512,512]{1,0:T(8,128)(2,1)S(1)} %get-tuple-element.18.current_ref.refs_4_), channel_id=1, source_target_pairs={{0,32},{32,64},{64,96},{96,0},{1,33},{33,65},{65,97},{97,1},{2,34}... | collective-permute-start | bytes 1572872 | tf_op jit(solution)/shard_map/ppermute | solution.py:42
  90.3 8.5 %collective-permute-start.34 = (bf16[512,512]{1,0:T(8,128)(2,1)S(1)}, bf16[512,512]{1,0:T(8,128)(2,1)S(1)}, u32[]{:S(2)}, u32[]{:S(2)}) collective-permute-start(bf16[512,512]{1,0:T(8,128)(2,1)S(1)} %constant_dynamic-update-slice_fusion.4.rest_0_), channel_id=1, source_target_pairs={{0,1},{1,0},{2,3},{3,2},{4,5},{5,4},{6,7},{7,6},{8,9},{9,8},{10,11... | collective-permute-start | bytes 1572872 | tf_op jit(solution)/shard_map/ppermute | solution.py:38
  92.3 6.5 %collective-permute-start.35 = (bf16[512,512]{1,0:T(8,128)(2,1)S(1)}, bf16[512,512]{1,0:T(8,128)(2,1)S(1)}, u32[]{:S(2)}, u32[]{:S(2)}) collective-permute-start(bf16[512,512]{1,0:T(8,128)(2,1)S(1)} %collective-permute-done.31.rest_1_), channel_id=1, source_target_pairs={{0,1},{1,0},{2,3},{3,2},{4,5},{5,4},{6,7},{7,6},{8,9},{9,8},{10,11... | collective-permute-start | bytes 1572872 | tf_op jit(solution)/shard_map/ppermute | solution.py:38
  98.1 1.9 %collective-permute-start.36 = (bf16[512,512]{1,0:T(8,128)(2,1)S(1)}, bf16[512,512]{1,0:T(8,128)(2,1)S(1)}, u32[]{:S(2)}, u32[]{:S(2)}) collective-permute-start(bf16[512,512]{1,0:T(8,128)(2,1)S(1)} %collective-permute-done.32.rest_2_), channel_id=1, source_target_pairs={{0,1},{1,0},{2,3},{3,2},{4,5},{5,4},{6,7},{7,6},{8,9},{9,8},{10,11... | collective-permute-start | bytes 1572872 | tf_op jit(solution)/shard_map/ppermute | solution.py:38
  98.8 2.0 %collective-permute-start.37 = (bf16[512,512]{1,0:T(8,128)(2,1)S(1)}, bf16[512,512]{1,0:T(8,128)(2,1)S(1)}, u32[]{:S(2)}, u32[]{:S(2)}) collective-permute-start(bf16[512,512]{1,0:T(8,128)(2,1)S(1)} %collective-permute-done.33.rest_3_), channel_id=1, source_target_pairs={{0,1},{1,0},{2,3},{3,2},{4,5},{5,4},{6,7},{7,6},{8,9},{9,8},{10,11... | collective-permute-start | bytes 1572872 | tf_op jit(solution)/shard_map/ppermute | solution.py:38
  103.4 7.1 %collective-permute-start.41 = (bf16[128,512]{1,0:T(8,128)(2,1)S(1)}, bf16[128,512]{1,0:T(8,128)(2,1)S(1)}, u32[]{:S(2)}, u32[]{:S(2)}) collective-permute-start(bf16[128,512]{1,0:T(8,128)(2,1)S(1)} %get-tuple-element.22), channel_id=1, source_target_pairs={{0,2},{1,9},{2,4},{3,11},{4,6},{5,13},{6,0},{7,15},{8,10},{9,17},{... | collective-permute-start | bytes 393224 | tf_op jit(solution)/shard_map/ppermute | solution.py:33
  104.3 7.3 %collective-permute-start.42 = (bf16[128,512]{1,0:T(8,128)(2,1)S(1)}, bf16[128,512]{1,0:T(8,128)(2,1)S(1)}, u32[]{:S(2)}, u32[]{:S(2)}) collective-permute-start(bf16[128,512]{1,0:T(8,128)(2,1)S(1)} %get-tuple-element.22), channel_id=1, source_target_pairs={{0,4},{1,17},{2,6},{3,19},{4,0},{5,21},{6,2},{7,23},{8,12},{9,25},... | collective-permute-start | bytes 393224 | tf_op jit(solution)/shard_map/ppermute | solution.py:33
  107.3 5.0 %collective-permute-start.43 = (bf16[128,512]{1,0:T(8,128)(2,1)S(1)}, bf16[128,512]{1,0:T(8,128)(2,1)S(1)}, u32[]{:S(2)}, u32[]{:S(2)}) collective-permute-start(bf16[128,512]{1,0:T(8,128)(2,1)S(1)} %get-tuple-element.22), channel_id=1, source_target_pairs={{0,6},{1,25},{2,0},{3,27},{4,2},{5,29},{6,4},{7,31},{8,14},{9,1},{... | collective-permute-start | bytes 393224 | tf_op jit(solution)/shard_map/ppermute | solution.py:33
  107.7 16.4 %collective-permute-start.38 = (bf16[512,512]{1,0:T(8,128)(2,1)S(1)}, bf16[512,512]{1,0:T(8,128)(2,1)S(1)}, u32[]{:S(2)}, u32[]{:S(2)}) collective-permute-start(bf16[512,512]{1,0:T(8,128)(2,1)S(1)} %get-tuple-element.20), channel_id=1, source_target_pairs={{96,64},{0,96},{64,32},{97,65},{1,97},{65,33},{98,66},{2,98},{66,3... | collective-permute-start | bytes 1572872 | tf_op jit(solution)/shard_map/ppermute | solution.py:42
  112.4 11.7 %collective-permute-start.44 = (bf16[512,512]{1,0:T(8,128)(2,1)S(1)}, bf16[512,512]{1,0:T(8,128)(2,1)S(1)}, u32[]{:S(2)}, u32[]{:S(2)}) collective-permute-start(bf16[512,512]{1,0:T(8,128)(2,1)S(1)} %constant_dynamic-update-slice_fusion.8.rest_0_), channel_id=1, source_target_pairs={{0,8},{1,3},{2,10},{3,5},{4,12},{5,7},{6,14},{7,1},{8,16},{9,11},{... | collective-permute-start | bytes 1572872 | tf_op jit(solution)/shard_map/ppermute | solution.py:33
  112.8 16.4 %collective-permute-start.45 = (bf16[512,512]{1,0:T(8,128)(2,1)S(1)}, bf16[512,512]{1,0:T(8,128)(2,1)S(1)}, u32[]{:S(2)}, u32[]{:S(2)}) collective-permute-start(bf16[512,512]{1,0:T(8,128)(2,1)S(1)} %constant_dynamic-update-slice_fusion.8.rest_0_), channel_id=1, source_target_pairs={{0,16},{1,5},{2,18},{3,7},{4,20},{5,1},{6,22},{7,3},{8,24},{9,13},... | collective-permute-start | bytes 1572872 | tf_op jit(solution)/shard_map/ppermute | solution.py:33
  116.4 12.9 %collective-permute-start.46 = (bf16[512,512]{1,0:T(8,128)(2,1)S(1)}, bf16[512,512]{1,0:T(8,128)(2,1)S(1)}, u32[]{:S(2)}, u32[]{:S(2)}) collective-permute-start(bf16[512,512]{1,0:T(8,128)(2,1)S(1)} %constant_dynamic-update-slice_fusion.8.rest_0_), channel_id=1, source_target_pairs={{0,24},{1,7},{2,26},{3,1},{4,28},{5,3},{6,30},{7,5},{8,0},{9,15},{... | collective-permute-start | bytes 1572872 | tf_op jit(solution)/shard_map/ppermute | solution.py:33
  116.4 13.3 %collective-permute-start.39 = (bf16[512,512]{1,0:T(8,128)(2,1)S(1)}, bf16[512,512]{1,0:T(8,128)(2,1)S(1)}, u32[]{:S(2)}, u32[]{:S(2)}) collective-permute-start(bf16[512,512]{1,0:T(8,128)(2,1)S(1)} %get-tuple-element.21.current_ref.refs_8_), channel_id=1, source_target_pairs={{0,32},{32,64},{64,96},{96,0},{1,33},{33,65},{65,97},{97,1},{2,34}... | collective-permute-start | bytes 1572872 | tf_op jit(solution)/shard_map/ppermute | solution.py:42
  124.1 8.4 %collective-permute-start.47 = (bf16[512,512]{1,0:T(8,128)(2,1)S(1)}, bf16[512,512]{1,0:T(8,128)(2,1)S(1)}, u32[]{:S(2)}, u32[]{:S(2)}) collective-permute-start(bf16[512,512]{1,0:T(8,128)(2,1)S(1)} %constant_dynamic-update-slice_fusion.8.rest_0_), channel_id=1, source_target_pairs={{0,1},{1,0},{2,3},{3,2},{4,5},{5,4},{6,7},{7,6},{8,9},{9,8},{10,11... | collective-permute-start | bytes 1572872 | tf_op jit(solution)/shard_map/ppermute | solution.py:38
  124.1 8.4 %collective-permute-start.48 = (bf16[512,512]{1,0:T(8,128)(2,1)S(1)}, bf16[512,512]{1,0:T(8,128)(2,1)S(1)}, u32[]{:S(2)}, u32[]{:S(2)}) collective-permute-start(bf16[512,512]{1,0:T(8,128)(2,1)S(1)} %collective-permute-done.44.rest_1_), channel_id=1, source_target_pairs={{0,1},{1,0},{2,3},{3,2},{4,5},{5,4},{6,7},{7,6},{8,9},{9,8},{10,11... | collective-permute-start | bytes 1572872 | tf_op jit(solution)/shard_map/ppermute | solution.py:38
  129.2 3.3 %collective-permute-start.49 = (bf16[512,512]{1,0:T(8,128)(2,1)S(1)}, bf16[512,512]{1,0:T(8,128)(2,1)S(1)}, u32[]{:S(2)}, u32[]{:S(2)}) collective-permute-start(bf16[512,512]{1,0:T(8,128)(2,1)S(1)} %collective-permute-done.45.rest_2_), channel_id=1, source_target_pairs={{0,1},{1,0},{2,3},{3,2},{4,5},{5,4},{6,7},{7,6},{8,9},{9,8},{10,11... | collective-permute-start | bytes 1572872 | tf_op jit(solution)/shard_map/ppermute | solution.py:38
  129.3 3.2 %collective-permute-start.50 = (bf16[512,512]{1,0:T(8,128)(2,1)S(1)}, bf16[512,512]{1,0:T(8,128)(2,1)S(1)}, u32[]{:S(2)}, u32[]{:S(2)}) collective-permute-start(bf16[512,512]{1,0:T(8,128)(2,1)S(1)} %collective-permute-done.46.rest_3_), channel_id=1, source_target_pairs={{0,1},{1,0},{2,3},{3,2},{4,5},{5,4},{6,7},{7,6},{8,9},{9,8},{10,11... | collective-permute-start | bytes 1572872 | tf_op jit(solution)/shard_map/ppermute | solution.py:38
  129.7 14.2 %collective-permute-start.40 = (bf16[512,512]{1,0:T(8,128)(2,1)S(1)}, bf16[512,512]{1,0:T(8,128)(2,1)S(1)}, u32[]{:S(2)}, u32[]{:S(2)}) collective-permute-start(bf16[512,512]{1,0:T(8,128)(2,1)S(1)} %collective-permute-done.38.rest_8_.refs_6_.refs_11_), channel_id=1, source_target_pairs={{96,64},{97,65},{98,66},{99,67},{100,68},{101,69},{102,70},{103,71... | collective-permute-start | bytes 1572872 | tf_op jit(solution)/shard_map/ppermute | solution.py:42
  135.0 15.9 %collective-permute-start.51 = (bf16[512,512]{1,0:T(8,128)(2,1)S(1)}, bf16[512,512]{1,0:T(8,128)(2,1)S(1)}, u32[]{:S(2)}, u32[]{:S(2)}) collective-permute-start(bf16[512,512]{1,0:T(8,128)(2,1)S(1)} %shard_map.77.refs_12_), channel_id=1, source_target_pairs={{64,96},{65,97},{66,98},{67,99},{68,100},{69,101},{70,102},{71,103... | collective-permute-start | bytes 1572872 | tf_op jit(solution)/shard_map/ppermute | solution.py:42
  136.3 22.4 %collective-permute-start.55 = (bf16[512,512]{1,0:T(8,128)(2,1)S(1)}, bf16[512,512]{1,0:T(8,128)(2,1)S(1)}, u32[]{:S(2)}, u32[]{:S(2)}) collective-permute-start(bf16[512,512]{1,0:T(8,128)(2,1)S(1)} %shard_map.77.refs_12_), channel_id=1, source_target_pairs={{0,96},{1,97},{2,98},{3,99},{4,100},{5,101},{6,102},{7,103},{8,104... | collective-permute-start | bytes 1572872 | tf_op jit(solution)/shard_map/ppermute | solution.py:42
  137.6 2.0 %collective-permute-start.52 = (bf16[256,512]{1,0:T(8,128)(2,1)S(1)}, bf16[256,512]{1,0:T(8,128)(2,1)S(1)}, u32[]{:S(2)}, u32[]{:S(2)}) collective-permute-start(bf16[256,512]{1,0:T(8,128)(2,1)S(1)} %get-tuple-element.26), channel_id=1, source_target_pairs={{32,64},{33,65},{34,66},{35,67},{36,68},{37,69},{38,70},{39,71},{4... | collective-permute-start | bytes 786440 | tf_op jit(solution)/shard_map/ppermute | solution.py:42
  138.2 12.5 %collective-permute-start.54 = (bf16[256,512]{1,0:T(8,128)(2,1)S(1)}, bf16[256,512]{1,0:T(8,128)(2,1)S(1)}, u32[]{:S(2)}, u32[]{:S(2)}) collective-permute-start(bf16[256,512]{1,0:T(8,128)(2,1)S(1)} %get-tuple-element.25), channel_id=1, source_target_pairs={{32,96},{33,97},{34,98},{35,99},{36,100},{37,101},{38,102},{39,103... | collective-permute-start | bytes 786440 | tf_op jit(solution)/shard_map/ppermute | solution.py:42
  139.5 19.1 %collective-permute-start.53 = (bf16[256,512]{1,0:T(8,128)(2,1)S(1)}, bf16[256,512]{1,0:T(8,128)(2,1)S(1)}, u32[]{:S(2)}, u32[]{:S(2)}) collective-permute-start(bf16[256,512]{1,0:T(8,128)(2,1)S(1)} %collective-permute-done.52), channel_id=1, source_target_pairs={{64,96},{65,97},{66,98},{67,99},{68,100},{69,101},{70,102},{71,103... | collective-permute-start | bytes 786440 | tf_op jit(solution)/shard_map/ppermute | solution.py:42

commit v7 on v6

--- a/solution.py
+++ b/solution.py
@@ -66,6 +66,13 @@
     block_ref[pl.ds(0, offered), :] = offered_rows(listed_ref[span], rows_ref[...])
 
 
+def selector_kernel(place_ref, listed_ref, selector_ref):
+    listed = listed_ref[place_ref[0]]
+    row_ids = lax.broadcasted_iota(jnp.int32, (selector_ref.shape[1], listed.shape[1]), 0)
+    selector = (row_ids == listed).astype(jnp.float32)
+    selector_ref[...] = jnp.transpose(selector).astype(jnp.bfloat16)
+
+
 def layer_kernel(
     layer_id, first, last,
     place_ref, counts_ref, cols_ref, listed_ref, current_ref, previous_ref, tiles_ref, halves_ref, others_ref,
@@ -79,7 +86,7 @@
     space, total = rest[outs:outs + 2]
     span, node = place_ref[0], place_ref[1]
     row_count = total.shape[0]
-    offered = listed_ref.shape[2]
+    offered = listed_ref.shape[0]
     z, y, core = node // (SIDE * CORES), (node // CORES) % SIDE, node % CORES
     each = mine_refs[0].shape[0] // SIDE
     if first:
@@ -108,7 +115,6 @@
     def _():
         space[pl.ds(row_count, row_count), :] = previous_ref[...]
 
-    total[...] = jnp.zeros_like(total)
     if first:
         wide_ref = rest[2]
         lanes = lax.broadcasted_iota(jnp.int32, (1, TILE), 1)
@@ -121,6 +127,7 @@
         reached = reached + counts_ref[span, r]
         ends.append(reached)
     own_tiles = 2 * row_count // TILE
+    begins = [0] + ends
     for f in range(cols_ref.shape[1]):
         owner = sum((f >= end).astype(jnp.int32) for end in ends)
         col = cols_ref[span, f]
@@ -140,7 +147,9 @@
         slot = jnp.where(col < own_tiles, col // CORES, col - own_tiles // CORES)
         row_at = pl.ds(pl.multiple_of(owner * TILE, TILE), TILE)
         slot_at = pl.ds(pl.multiple_of(slot * CORES * offered, CORES * offered), CORES * offered)
-        total[row_at, :] += jnp.dot(wide, space[slot_at, :], preferred_element_type=jnp.float32)
+        product = jnp.dot(wide, space[slot_at, :], preferred_element_type=jnp.float32)
+        opens = functools.reduce(jnp.logical_or, [f == begin for begin in begins])
+        total[row_at, :] = jnp.where(opens, product, total[row_at, :] + product)
     half = halves_ref.shape[0] // SIDE
     distance = (span + SIDE - layer_id) % SIDE
     held = pl.ds(pl.multiple_of(distance * half, half), half)
@@ -152,7 +161,8 @@
     fresh = jnp.maximum(linear, 0.0).astype(jnp.bfloat16)
     out_ref[...] = fresh
     if not last:
-        rest[1][...] = offered_rows(listed_ref[span], fresh)
+        picked = jnp.dot(listed_ref[...], fresh, preferred_element_type=jnp.float32)
+        rest[1][...] = picked.astype(jnp.bfloat16)
     if not first and not last:
         moved_ref = rest[2]
 
@@ -199,6 +209,13 @@
     span = lax.axis_index("layer")
     place = jnp.stack([span, node]).astype(jnp.int32)
     current = lax.dynamic_index_in_dim(features, span, 0, keepdims=False)
+    selector = pl.pallas_call(
+        selector_kernel,
+        out_shape=jax.ShapeDtypeStruct((offered, row_count), jnp.bfloat16),
+        in_specs=[SMEM, VMEM],
+        out_specs=VMEM,
+        compiler_params=pltpu.CompilerParams(vmem_limit_bytes=16 << 20),
+    )(place, boundary)
     counts, tile_cols = counts[:, 0], tile_cols[:, 0]
     rows_shape = jax.ShapeDtypeStruct((row_count, width), jnp.bfloat16)
     wide_shape = jax.ShapeDtypeStruct((tile_total, TILE, CORES * offered), jnp.bfloat16)
@@ -248,7 +265,7 @@
             out_specs=[VMEM] * len(outs),
             scratch_shapes=scratch,
             compiler_params=params,
-        )(place, counts, tile_cols, boundary, current, previous, tiles, *known, *mine, *theirs, *([] if first else [back]))
+        )(place, counts, tile_cols, selector, current, previous, tiles, *known, *mine, *theirs, *([] if first else [back]))
         current = results[0]
         if not last:
             block = results[1]

time: 160 us -> 160 us (level)
  transfers between devices with their start and end apart: 56 -> 56, of which waited for: 30 -> 30; matrix products, arithmetic and copies ran while one was open for 1% -> 1% of each run, Pallas kernels for 1% -> 2%
where the time goes in v7:
time: 160 us
  waiting for transfers between devices  72.4 us (45%)
  starting transfers between devices  67.2 us (42%)
  Pallas kernels  15.6 us (10%)
  local copies, waits for them, and re-layouts  3.41 us (2%)
    ppermute x24, starting transfers between devices, along(): return lax.ppermute(block, 'node', route)  39.1 us
    ppermute x24, waiting for transfers between devices, along(): return lax.ppermute(block, 'node', route)  33.6 us
    ppermute x15, waiting for transfers between devices, to_plane(): return lax.ppermute(block, 'layer', pairs)  32.7 us
    ppermute x15, starting transfers between devices, to_plane(): return lax.ppermute(block, 'layer', pairs)  25.5 us
    pallas_call x4, Pallas kernels, on_device(): pl.pallas_call(functools.partial(layer_kernel, layer_id, first, last), ou...  12.8 us
    ppermute x17, waiting for transfers between devices, other_core(): return lax.ppermute(block, 'node', route)  6.1 us
  transfers between devices with their start and end apart: 56, of which 30 were waited for; matrix products, arithmetic and copies ran while one was open for 1% of the time, Pallas kernels for 2%

profile of v7, /device:TPU:6, one launch (start us, length us, event | category | flops | bytes accessed | tf_op | source)
XLA Modules:
  0.0 160.2 jit_solution(4612026761276672032)
XLA Ops:
  0.1 2.2 %dynamic-slice_bitcast_fusion.1 = (bf16[512,512]{1,0:T(8,128)(2,1)}, bf16[512,512]{1,0:T(8,128)(2,1)S(1)}) fusion(bf16[4,512,512]{2,1,0:T(8,128)(2,1)} %param.7, s32[]{:T(128)S(6)} %max.3, s32[]{:T(128)S(6)} %select_n.17), kind=kLoop, calls=%fused_computation.3 | loop fusion | bytes 2097160 | tf_op jit(solution)/shard_map/jit(dynamic_index_in_dim)/squeeze | solution.py:231
  2.3 0.8 shard_map.74
  3.1 1.6 %collective-permute-start.4 = (bf16[144,512]{1,0:T(8,128)(2,1)S(1)}, bf16[144,512]{1,0:T(8,128)(2,1)S(1)}, u32[]{:S(2)}, u32[]{:S(2)}) collective-permute-start(bf16[144,512]{1,0:T(8,128)(2,1)S(1)} %shard_map.74), channel_id=1, source_target_pairs={{0,2},{1,9},{2,4},{3,11},{4,6},{5,13},{6,0},{7,15},{8,10},{9,17},{... | collective-permute-start | bytes 442376 | tf_op jit(solution)/shard_map/ppermute | solution.py:33
  4.8 2.9 %collective-permute-start.5 = (bf16[144,512]{1,0:T(8,128)(2,1)S(1)}, bf16[144,512]{1,0:T(8,128)(2,1)}, u32[]{:S(2)}, u32[]{:S(2)}) collective-permute-start(bf16[144,512]{1,0:T(8,128)(2,1)S(1)} %shard_map.74), channel_id=1, source_target_pairs={{0,4},{1,17},{2,6},{3,19},{4,0},{5,21},{6,2},{7,23},{8,12},{9,25},... | collective-permute-start | bytes 442376 | tf_op jit(solution)/shard_map/ppermute | solution.py:33
  7.7 1.3 collective-permute-start.6
  9.0 1.0 dynamic-slice_bitcast_fusion.3
  10.6 2.4 %collective-permute-start.1 = (bf16[256,512]{1,0:T(8,128)(2,1)S(1)}, bf16[256,512]{1,0:T(8,128)(2,1)S(1)}, u32[]{:S(2)}, u32[]{:S(2)}) collective-permute-start(bf16[256,512]{1,0:T(8,128)(2,1)S(1)} %dynamic-slice_bitcast_fusion.3), channel_id=1, source_target_pairs={{0,64},{32,96},{64,0},{96,32},{1,65},{33,97},{65,1},{97,33},{2,66}... | collective-permute-start | bytes 786440 | tf_op jit(solution)/shard_map/ppermute | solution.py:42
  13.0 1.0 pad_maximum_fusion.1.rest_0_
  14.0 2.0 %collective-permute-start.7 = (bf16[576,512]{1,0:T(8,128)(2,1)S(1)}, bf16[576,512]{1,0:T(8,128)(2,1)S(1)}, u32[]{:S(2)}, u32[]{:S(2)}) collective-permute-start(bf16[576,512]{1,0:T(8,128)(2,1)S(1)} %pad_maximum_fusion.1.rest_0_), channel_id=1, source_target_pairs={{0,8},{1,3},{2,10},{3,5},{4,12},{5,7},{6,14},{7,1},{8,16},{9,11},{... | collective-permute-start | bytes 1769480 | tf_op jit(solution)/shard_map/ppermute | solution.py:33
  16.0 3.6 %collective-permute-start.8 = (bf16[576,512]{1,0:T(8,128)(2,1)S(1)}, bf16[576,512]{1,0:T(8,128)(2,1)S(1)}, u32[]{:S(2)}, u32[]{:S(2)}) collective-permute-start(bf16[576,512]{1,0:T(8,128)(2,1)S(1)} %pad_maximum_fusion.1.rest_0_), channel_id=1, source_target_pairs={{0,16},{1,5},{2,18},{3,7},{4,20},{5,1},{6,22},{7,3},{8,24},{9,13},... | collective-permute-start | bytes 1769480 | tf_op jit(solution)/shard_map/ppermute | solution.py:33
  19.6 1.5 collective-permute-start.9
  21.4 4.0 %collective-permute-done.2 = bf16[256,512]{1,0:T(8,128)(2,1)S(1)} collective-permute-done((bf16[256,512]{1,0:T(8,128)(2,1)S(1)}, bf16[256,512]{1,0:T(8,128)(2,1)S(1)}, u32[]{:S(2)}, u32[]{:S(2)}) %collective-permute-start.2) | collective-permute-done | bytes 262176 | tf_op jit(solution)/shard_map/ppermute | solution.py:42
  26.1 7.7 %collective-permute-done.8.rest_2_ = bf16[576,512]{1,0:T(8,128)(2,1)S(1)} collective-permute-done((bf16[576,512]{1,0:T(8,128)(2,1)S(1)}, bf16[576,512]{1,0:T(8,128)(2,1)S(1)}, u32[]{:S(2)}, u32[]{:S(2)}) %collective-permute-start.8) | collective-permute-done | bytes 589856 | tf_op jit(solution)/shard_map/ppermute | solution.py:33
  35.1 0.7 collective-permute-done.12.rest_6_
  35.8 0.8 collective-permute-done.13.rest_7_
  36.7 5.2 %shard_map.75 = (bf16[512,512]{1,0:T(8,128)(2,1)S(1)}, bf16[128,512]{1,0:T(8,128)(2,1)S(1)}, bf16[20,128,256]{2,1,0:T(8,128)(2,1)S(1)}) custom-call(s32[2]{0:T(128)S(1)} %pad_add_fusion.place_ref, s32[4,4]{1,0:T(4,128)S(1)} %bitcast.12, s32[4,20]{1,0:T(4,128)S(1)} %bitcast.16, bf16[128,512]{1,0:T(8,128)(2,1)S(1)} %shard_map.73.listed_ref, ...), custom_call_target="tpu_custom_call" | custom-call | tf_op jit(solution)/shard_map/pallas_call | solution.py:261
  41.8 1.2 collective-permute-start.15
  43.0 2.8 %collective-permute-start.16 = (bf16[128,512]{1,0:T(8,128)(2,1)S(1)}, bf16[128,512]{1,0:T(8,128)(2,1)S(1)}, u32[]{:S(2)}, u32[]{:S(2)}) collective-permute-start(bf16[128,512]{1,0:T(8,128)(2,1)S(1)} %get-tuple-element.16), channel_id=1, source_target_pairs={{0,4},{1,17},{2,6},{3,19},{4,0},{5,21},{6,2},{7,23},{8,12},{9,25},... | collective-permute-start | bytes 393224 | tf_op jit(solution)/shard_map/ppermute | solution.py:33
  45.8 1.1 collective-permute-start.17
  46.9 1.7 %collective-permute-start.14 = (bf16[512,512]{1,0:T(8,128)(2,1)S(1)}, bf16[512,512]{1,0:T(8,128)(2,1)S(1)}, u32[]{:S(2)}, u32[]{:S(2)}) collective-permute-start(bf16[512,512]{1,0:T(8,128)(2,1)S(1)} %get-tuple-element.14.current_ref.refs_0_), channel_id=1, source_target_pairs={{0,32},{32,64},{64,96},{96,0},{1,33},{33,65},{65,97},{97,1},{2,34}... | collective-permute-start | bytes 1572872 | tf_op jit(solution)/shard_map/ppermute | solution.py:42
  48.7 1.5 collective-permute-done.16
  50.2 0.7 collective-permute-done.17
  50.9 0.7 collective-permute-start.18
  51.6 2.1 %collective-permute-start.19 = (bf16[512,512]{1,0:T(8,128)(2,1)S(1)}, bf16[512,512]{1,0:T(8,128)(2,1)S(1)}, u32[]{:S(2)}, u32[]{:S(2)}) collective-permute-start(bf16[512,512]{1,0:T(8,128)(2,1)S(1)} %constant_dynamic-update-slice_fusion.rest_0_), channel_id=1, source_target_pairs={{0,16},{1,5},{2,18},{3,7},{4,20},{5,1},{6,22},{7,3},{8,24},{9,13},... | collective-permute-start | bytes 1572872 | tf_op jit(solution)/shard_map/ppermute | solution.py:33
  53.7 1.5 collective-permute-start.20
  56.0 4.2 %collective-permute-done.14.previous_ref.refs_1_ = bf16[512,512]{1,0:T(8,128)(2,1)S(1)} collective-permute-done((bf16[512,512]{1,0:T(8,128)(2,1)S(1)}, bf16[512,512]{1,0:T(8,128)(2,1)S(1)}, u32[]{:S(2)}, u32[]{:S(2)}) %collective-permute-start.14) | collective-permute-done | bytes 524320 | tf_op jit(solution)/shard_map/ppermute | solution.py:42
  60.2 6.8 %collective-permute-done.18.rest_1_ = bf16[512,512]{1,0:T(8,128)(2,1)S(1)} collective-permute-done((bf16[512,512]{1,0:T(8,128)(2,1)S(1)}, bf16[512,512]{1,0:T(8,128)(2,1)S(1)}, u32[]{:S(2)}, u32[]{:S(2)}) %collective-permute-start.18) | collective-permute-done | bytes 524320 | tf_op jit(solution)/shard_map/ppermute | solution.py:33
  67.9 1.0 collective-permute-done.22.rest_5_
  68.9 0.7 collective-permute-done.23.rest_6_
  69.6 0.7 collective-permute-done.24.rest_7_
  70.4 2.6 %shard_map.76 = (bf16[512,512]{1,0:T(8,128)(2,1)S(1)}, bf16[128,512]{1,0:T(8,128)(2,1)S(1)}, bf16[512,512]{1,0:T(8,128)(2,1)S(1)}) custom-call(s32[2]{0:T(128)S(1)} %pad_add_fusion.place_ref, s32[4,4]{1,0:T(4,128)S(1)} %bitcast.13, s32[4,20]{1,0:T(4,128)S(1)} %bitcast.17, bf16[128,512]{1,0:T(8,128)(2,1)S(1)} %shard_map.73.listed_ref, ...), custom_call_target="tpu_custom_call" | custom-call | tf_op jit(solution)/shard_map/pallas_call | solution.py:261
  73.0 1.3 collective-permute-start.28
  74.2 2.5 %collective-permute-start.29 = (bf16[128,512]{1,0:T(8,128)(2,1)S(1)}, bf16[128,512]{1,0:T(8,128)(2,1)S(1)}, u32[]{:S(2)}, u32[]{:S(2)}) collective-permute-start(bf16[128,512]{1,0:T(8,128)(2,1)S(1)} %get-tuple-element.19), channel_id=1, source_target_pairs={{0,4},{1,17},{2,6},{3,19},{4,0},{5,21},{6,2},{7,23},{8,12},{9,25},... | collective-permute-start | bytes 393224 | tf_op jit(solution)/shard_map/ppermute | solution.py:33
  76.8 0.8 collective-permute-start.30
  77.5 2.8 %collective-permute-start.26 = (bf16[512,512]{1,0:T(8,128)(2,1)S(1)}, bf16[512,512]{1,0:T(8,128)(2,1)S(1)}, u32[]{:S(2)}, u32[]{:S(2)}) collective-permute-start(bf16[512,512]{1,0:T(8,128)(2,1)S(1)} %get-tuple-element.17), channel_id=1, source_target_pairs={{64,32},{96,64},{32,0},{65,33},{97,65},{33,1},{66,34},{98,66},{34,... | collective-permute-start | bytes 1572872 | tf_op jit(solution)/shard_map/ppermute | solution.py:42
  80.3 0.8 collective-permute-done.29
  81.1 0.7 collective-permute-done.30
  82.3 3.1 %collective-permute-start.32 = (bf16[512,512]{1,0:T(8,128)(2,1)S(1)}, bf16[512,512]{1,0:T(8,128)(2,1)S(1)}, u32[]{:S(2)}, u32[]{:S(2)}) collective-permute-start(bf16[512,512]{1,0:T(8,128)(2,1)S(1)} %constant_dynamic-update-slice_fusion.4.rest_0_), channel_id=1, source_target_pairs={{0,16},{1,5},{2,18},{3,7},{4,20},{5,1},{6,22},{7,3},{8,24},{9,13},... | collective-permute-start | bytes 1572872 | tf_op jit(solution)/shard_map/ppermute | solution.py:33
  85.6 3.1 %collective-permute-start.27 = (bf16[512,512]{1,0:T(8,128)(2,1)S(1)}, bf16[512,512]{1,0:T(8,128)(2,1)S(1)}, u32[]{:S(2)}, u32[]{:S(2)}) collective-permute-start(bf16[512,512]{1,0:T(8,128)(2,1)S(1)} %get-tuple-element.18.current_ref.refs_4_), channel_id=1, source_target_pairs={{0,32},{32,64},{64,96},{96,0},{1,33},{33,65},{65,97},{97,1},{2,34}... | collective-permute-start | bytes 1572872 | tf_op jit(solution)/shard_map/ppermute | solution.py:42
  88.7 1.6 collective-permute-done.26.rest_8_.refs_2_.refs_7_
  90.3 2.0 %collective-permute-done.31.rest_1_ = bf16[512,512]{1,0:T(8,128)(2,1)S(1)} collective-permute-done((bf16[512,512]{1,0:T(8,128)(2,1)S(1)}, bf16[512,512]{1,0:T(8,128)(2,1)S(1)}, u32[]{:S(2)}, u32[]{:S(2)}) %collective-permute-start.31) | collective-permute-done | bytes 524320 | tf_op jit(solution)/shard_map/ppermute | solution.py:33
  92.3 5.9 %collective-permute-done.32.rest_2_ = bf16[512,512]{1,0:T(8,128)(2,1)S(1)} collective-permute-done((bf16[512,512]{1,0:T(8,128)(2,1)S(1)}, bf16[512,512]{1,0:T(8,128)(2,1)S(1)}, u32[]{:S(2)}, u32[]{:S(2)}) %collective-permute-start.32) | collective-permute-done | bytes 524320 | tf_op jit(solution)/shard_map/ppermute | solution.py:33
  98.8 1.2 collective-permute-done.36.rest_6_
  100.1 0.7 collective-permute-done.37.rest_7_
  100.8 2.6 %shard_map.77 = (bf16[512,512]{1,0:T(8,128)(2,1)S(1)}, bf16[128,512]{1,0:T(8,128)(2,1)S(1)}, bf16[512,512]{1,0:T(8,128)(2,1)S(1)}) custom-call(s32[2]{0:T(128)S(1)} %pad_add_fusion.place_ref, s32[4,4]{1,0:T(4,128)S(1)} %bitcast.14, s32[4,20]{1,0:T(4,128)S(1)} %bitcast.18, bf16[128,512]{1,0:T(8,128)(2,1)S(1)} %shard_map.73.listed_ref, ...), custom_call_target="tpu_custom_call" | custom-call | tf_op jit(solution)/shard_map/pallas_call | solution.py:261
  103.4 0.9 collective-permute-start.41
  104.3 3.0 %collective-permute-start.42 = (bf16[128,512]{1,0:T(8,128)(2,1)S(1)}, bf16[128,512]{1,0:T(8,128)(2,1)S(1)}, u32[]{:S(2)}, u32[]{:S(2)}) collective-permute-start(bf16[128,512]{1,0:T(8,128)(2,1)S(1)} %get-tuple-element.22), channel_id=1, source_target_pairs={{0,4},{1,17},{2,6},{3,19},{4,0},{5,21},{6,2},{7,23},{8,12},{9,25},... | collective-permute-start | bytes 393224 | tf_op jit(solution)/shard_map/ppermute | solution.py:33
  107.7 2.8 %collective-permute-start.38 = (bf16[512,512]{1,0:T(8,128)(2,1)S(1)}, bf16[512,512]{1,0:T(8,128)(2,1)S(1)}, u32[]{:S(2)}, u32[]{:S(2)}) collective-permute-start(bf16[512,512]{1,0:T(8,128)(2,1)S(1)} %get-tuple-element.20), channel_id=1, source_target_pairs={{96,64},{0,96},{64,32},{97,65},{1,97},{65,33},{98,66},{2,98},{66,3... | collective-permute-start | bytes 1572872 | tf_op jit(solution)/shard_map/ppermute | solution.py:42
  110.5 1.1 collective-permute-done.42
  111.7 0.7 collective-permute-done.43
  112.8 3.7 %collective-permute-start.45 = (bf16[512,512]{1,0:T(8,128)(2,1)S(1)}, bf16[512,512]{1,0:T(8,128)(2,1)S(1)}, u32[]{:S(2)}, u32[]{:S(2)}) collective-permute-start(bf16[512,512]{1,0:T(8,128)(2,1)S(1)} %constant_dynamic-update-slice_fusion.8.rest_0_), channel_id=1, source_target_pairs={{0,16},{1,5},{2,18},{3,7},{4,20},{5,1},{6,22},{7,3},{8,24},{9,13},... | collective-permute-start | bytes 1572872 | tf_op jit(solution)/shard_map/ppermute | solution.py:33
  116.4 2.8 %collective-permute-start.39 = (bf16[512,512]{1,0:T(8,128)(2,1)S(1)}, bf16[512,512]{1,0:T(8,128)(2,1)S(1)}, u32[]{:S(2)}, u32[]{:S(2)}) collective-permute-start(bf16[512,512]{1,0:T(8,128)(2,1)S(1)} %get-tuple-element.21.current_ref.refs_8_), channel_id=1, source_target_pairs={{0,32},{32,64},{64,96},{96,0},{1,33},{33,65},{65,97},{97,1},{2,34}... | collective-permute-start | bytes 1572872 | tf_op jit(solution)/shard_map/ppermute | solution.py:42
  119.2 4.9 %collective-permute-done.38.rest_8_.refs_6_.refs_11_ = bf16[512,512]{1,0:T(8,128)(2,1)S(1)} collective-permute-done((bf16[512,512]{1,0:T(8,128)(2,1)S(1)}, bf16[512,512]{1,0:T(8,128)(2,1)S(1)}, u32[]{:S(2)}, u32[]{:S(2)}) %collective-permute-start.38) | collective-permute-done | bytes 524320 | tf_op jit(solution)/shard_map/ppermute | solution.py:42
  124.6 4.6 %collective-permute-done.45.rest_2_ = bf16[512,512]{1,0:T(8,128)(2,1)S(1)} collective-permute-done((bf16[512,512]{1,0:T(8,128)(2,1)S(1)}, bf16[512,512]{1,0:T(8,128)(2,1)S(1)}, u32[]{:S(2)}, u32[]{:S(2)}) %collective-permute-start.45) | collective-permute-done | bytes 524320 | tf_op jit(solution)/shard_map/ppermute | solution.py:33
  129.7 2.8 %collective-permute-start.40 = (bf16[512,512]{1,0:T(8,128)(2,1)S(1)}, bf16[512,512]{1,0:T(8,128)(2,1)S(1)}, u32[]{:S(2)}, u32[]{:S(2)}) collective-permute-start(bf16[512,512]{1,0:T(8,128)(2,1)S(1)} %collective-permute-done.38.rest_8_.refs_6_.refs_11_), channel_id=1, source_target_pairs={{96,64},{97,65},{98,66},{99,67},{100,68},{101,69},{102,70},{103,71... | collective-permute-start | bytes 1572872 | tf_op jit(solution)/shard_map/ppermute | solution.py:42
  132.5 2.4 %shard_map.78.refs_12_ = bf16[512,512]{1,0:T(8,128)(2,1)S(1)} custom-call(s32[2]{0:T(128)S(1)} %pad_add_fusion.place_ref, s32[4,4]{1,0:T(4,128)S(1)} %bitcast.15, s32[4,20]{1,0:T(4,128)S(1)} %bitcast.19, bf16[128,512]{1,0:T(8,128)(2,1)S(1)} %shard_map.73.listed_ref, bf16[512,512]{1,0:T(8,128)(2,1)S(1)} %get-tuple-element.21.current_ref.refs_8_, ...), custom_call_target="tpu_custom_call" | custom-call | tf_op jit(solution)/shard_map/pallas_call | solution.py:261
  135.0 1.3 collective-permute-start.51
  136.3 1.3 collective-permute-start.55
  138.3 1.3 collective-permute-start.54
  139.6 1.3 collective-permute-start.53
  140.9 3.1 %collective-permute-done.40.refs_10_ = bf16[512,512]{1,0:T(8,128)(2,1)S(1)} collective-permute-done((bf16[512,512]{1,0:T(8,128)(2,1)S(1)}, bf16[512,512]{1,0:T(8,128)(2,1)S(1)}, u32[]{:S(2)}, u32[]{:S(2)}) %collective-permute-start.40) | collective-permute-done | bytes 524320 | tf_op jit(solution)/shard_map/ppermute | solution.py:42
  143.9 6.9 %collective-permute-done.54.refs_15_ = bf16[256,512]{1,0:T(8,128)(2,1)S(1)} collective-permute-done((bf16[256,512]{1,0:T(8,128)(2,1)S(1)}, bf16[256,512]{1,0:T(8,128)(2,1)S(1)}, u32[]{:S(2)}, u32[]{:S(2)}) %collective-permute-start.54) | collective-permute-done | bytes 262176 | tf_op jit(solution)/shard_map/ppermute | solution.py:42
  150.9 7.8 %collective-permute-done.55.refs_16_ = bf16[512,512]{1,0:T(8,128)(2,1)S(1)} collective-permute-done((bf16[512,512]{1,0:T(8,128)(2,1)S(1)}, bf16[512,512]{1,0:T(8,128)(2,1)S(1)}, u32[]{:S(2)}, u32[]{:S(2)}) %collective-permute-start.55) | collective-permute-done | bytes 524320 | tf_op jit(solution)/shard_map/ppermute | solution.py:42
  158.7 1.4 shard_map.79
  (86 shorter events, 8.6 us)
Async XLA Ops:
  0.0 35.0 %copy-start = (bf16[4,1,20,128,128]{4,3,2,1,0:T(8,128)(2,1)S(1)}, bf16[4,1,20,128,128]{4,3,2,1,0:T(8,128)(2,1)}, u32[]{:S(2)}) copy-start(bf16[4,1,20,128,128]{4,3,2,1,0:T(8,128)(2,1)} %param.13) | copy-start | bytes 7864324
  0.0 2.3 %copy-start.2 = (s32[4,1,32,64]{3,2,1,0:T(8,128)S(1)}, s32[4,1,32,64]{3,2,1,0:T(8,128)}, u32[]{:S(2)}) copy-start(s32[4,1,32,64]{3,2,1,0:T(8,128)} %lists_ref.1) | copy-start | bytes 98308
  0.0 2.3 %copy-start.5 = (s32[4,1,128]{2,1,0:T(1,128)S(1)}, s32[4,1,128]{2,1,0:T(1,128)}, u32[]{:S(2)}) copy-start(s32[4,1,128]{2,1,0:T(1,128)} %listed_ref.3) | copy-start | bytes 6148
  3.1 9.9 %collective-permute-start.4 = (bf16[144,512]{1,0:T(8,128)(2,1)S(1)}, bf16[144,512]{1,0:T(8,128)(2,1)S(1)}, u32[]{:S(2)}, u32[]{:S(2)}) collective-permute-start(bf16[144,512]{1,0:T(8,128)(2,1)S(1)} %shard_map.74), channel_id=1, source_target_pairs={{0,2},{1,9},{2,4},{3,11},{4,6},{5,13},{6,0},{7,15},{8,10},{9,17},{... | collective-permute-start | bytes 442376 | tf_op jit(solution)/shard_map/ppermute | solution.py:33
  4.8 8.2 %collective-permute-start.5 = (bf16[144,512]{1,0:T(8,128)(2,1)S(1)}, bf16[144,512]{1,0:T(8,128)(2,1)}, u32[]{:S(2)}, u32[]{:S(2)}) collective-permute-start(bf16[144,512]{1,0:T(8,128)(2,1)S(1)} %shard_map.74), channel_id=1, source_target_pairs={{0,4},{1,17},{2,6},{3,19},{4,0},{5,21},{6,2},{7,23},{8,12},{9,25},... | collective-permute-start | bytes 442376 | tf_op jit(solution)/shard_map/ppermute | solution.py:33
  7.7 5.3 %collective-permute-start.6 = (bf16[144,512]{1,0:T(8,128)(2,1)S(1)}, bf16[144,512]{1,0:T(8,128)(2,1)}, u32[]{:S(2)}, u32[]{:S(2)}) collective-permute-start(bf16[144,512]{1,0:T(8,128)(2,1)S(1)} %shard_map.74), channel_id=1, source_target_pairs={{0,6},{1,25},{2,0},{3,27},{4,2},{5,29},{6,4},{7,31},{8,14},{9,1},{... | collective-permute-start | bytes 442376 | tf_op jit(solution)/shard_map/ppermute | solution.py:33
  10.0 26.6 %copy-start.1 = (bf16[512,512]{1,0:T(8,128)(2,1)S(1)}, bf16[512,512]{1,0:T(8,128)(2,1)}, u32[]{:S(2)}) copy-start(bf16[512,512]{1,0:T(8,128)(2,1)} %get-tuple-element.23.previous_ref) | copy-start | bytes 1572868
  10.0 26.6 %copy-start.3 = (s32[4,1,4]{2,1,0:T(1,128)S(1)}, s32[4,1,4]{2,1,0:T(1,128)}, u32[]{:S(2)}) copy-start(s32[4,1,4]{2,1,0:T(1,128)} %param.11) | copy-start | bytes 196
  10.0 26.6 %copy-start.4 = (s32[4,1,20]{2,1,0:T(1,128)S(1)}, s32[4,1,20]{2,1,0:T(1,128)}, u32[]{:S(2)}) copy-start(s32[4,1,20]{2,1,0:T(1,128)} %param.12) | copy-start | bytes 964
  10.0 9.6 %collective-permute-start = (bf16[256,512]{1,0:T(8,128)(2,1)S(1)}, bf16[256,512]{1,0:T(8,128)(2,1)S(1)}, u32[]{:S(2)}, u32[]{:S(2)}) collective-permute-start(bf16[256,512]{1,0:T(8,128)(2,1)S(1)} %dynamic-slice_bitcast_fusion.3), channel_id=1, source_target_pairs={{0,32},{32,64},{64,96},{96,0},{1,33},{33,65},{65,97},{97,1},{2,34}... | collective-permute-start | bytes 786440 | tf_op jit(solution)/shard_map/ppermute | solution.py:42
  10.6 10.8 %collective-permute-start.1 = (bf16[256,512]{1,0:T(8,128)(2,1)S(1)}, bf16[256,512]{1,0:T(8,128)(2,1)S(1)}, u32[]{:S(2)}, u32[]{:S(2)}) collective-permute-start(bf16[256,512]{1,0:T(8,128)(2,1)S(1)} %dynamic-slice_bitcast_fusion.3), channel_id=1, source_target_pairs={{0,64},{32,96},{64,0},{96,32},{1,65},{33,97},{65,1},{97,33},{2,66}... | collective-permute-start | bytes 786440 | tf_op jit(solution)/shard_map/ppermute | solution.py:42
  13.0 12.4 %collective-permute-start.2 = (bf16[256,512]{1,0:T(8,128)(2,1)S(1)}, bf16[256,512]{1,0:T(8,128)(2,1)S(1)}, u32[]{:S(2)}, u32[]{:S(2)}) collective-permute-start(bf16[256,512]{1,0:T(8,128)(2,1)S(1)} %dynamic-slice_bitcast_fusion.3), channel_id=1, source_target_pairs={{0,96},{32,0},{64,32},{96,64},{1,97},{33,1},{65,33},{97,65},{2,98}... | collective-permute-start | bytes 786440 | tf_op jit(solution)/shard_map/ppermute | solution.py:42
  14.0 12.0 %collective-permute-start.7 = (bf16[576,512]{1,0:T(8,128)(2,1)S(1)}, bf16[576,512]{1,0:T(8,128)(2,1)S(1)}, u32[]{:S(2)}, u32[]{:S(2)}) collective-permute-start(bf16[576,512]{1,0:T(8,128)(2,1)S(1)} %pad_maximum_fusion.1.rest_0_), channel_id=1, source_target_pairs={{0,8},{1,3},{2,10},{3,5},{4,12},{5,7},{6,14},{7,1},{8,16},{9,11},{... | collective-permute-start | bytes 1769480 | tf_op jit(solution)/shard_map/ppermute | solution.py:33
  16.0 17.8 %collective-permute-start.8 = (bf16[576,512]{1,0:T(8,128)(2,1)S(1)}, bf16[576,512]{1,0:T(8,128)(2,1)S(1)}, u32[]{:S(2)}, u32[]{:S(2)}) collective-permute-start(bf16[576,512]{1,0:T(8,128)(2,1)S(1)} %pad_maximum_fusion.1.rest_0_), channel_id=1, source_target_pairs={{0,16},{1,5},{2,18},{3,7},{4,20},{5,1},{6,22},{7,3},{8,24},{9,13},... | collective-permute-start | bytes 1769480 | tf_op jit(solution)/shard_map/ppermute | solution.py:33
  19.6 14.2 %collective-permute-start.9 = (bf16[576,512]{1,0:T(8,128)(2,1)S(1)}, bf16[576,512]{1,0:T(8,128)(2,1)S(1)}, u32[]{:S(2)}, u32[]{:S(2)}) collective-permute-start(bf16[576,512]{1,0:T(8,128)(2,1)S(1)} %pad_maximum_fusion.1.rest_0_), channel_id=1, source_target_pairs={{0,24},{1,7},{2,26},{3,1},{4,28},{5,3},{6,30},{7,5},{8,0},{9,15},{... | collective-permute-start | bytes 1769480 | tf_op jit(solution)/shard_map/ppermute | solution.py:33
  25.4 9.6 %collective-permute-start.3 = (bf16[1024,512]{1,0:T(8,128)(2,1)S(1)}, bf16[1024,512]{1,0:T(8,128)(2,1)S(1)}, u32[]{:S(2)}, u32[]{:S(2)}) collective-permute-start(bf16[1024,512]{1,0:T(8,128)(2,1)S(1)} %pad_maximum_fusion.halves_ref), channel_id=1, source_target_pairs={{0,1},{1,0},{2,3},{3,2},{4,5},{5,4},{6,7},{7,6},{8,9},{9,8},{10,11... | collective-permute-start | bytes 3145736 | tf_op jit(solution)/shard_map/ppermute | solution.py:38
  25.5 9.5 %collective-permute-start.10 = (bf16[576,512]{1,0:T(8,128)(2,1)S(1)}, bf16[576,512]{1,0:T(8,128)(2,1)S(1)}, u32[]{:S(2)}, u32[]{:S(2)}) collective-permute-start(bf16[576,512]{1,0:T(8,128)(2,1)S(1)} %pad_maximum_fusion.1.rest_0_), channel_id=1, source_target_pairs={{0,1},{1,0},{2,3},{3,2},{4,5},{5,4},{6,7},{7,6},{8,9},{9,8},{10,11... | collective-permute-start | bytes 1769480 | tf_op jit(solution)/shard_map/ppermute | solution.py:38
  26.0 9.0 %collective-permute-start.11 = (bf16[576,512]{1,0:T(8,128)(2,1)S(1)}, bf16[576,512]{1,0:T(8,128)(2,1)S(1)}, u32[]{:S(2)}, u32[]{:S(2)}) collective-permute-start(bf16[576,512]{1,0:T(8,128)(2,1)S(1)} %collective-permute-done.7.rest_1_), channel_id=1, source_target_pairs={{0,1},{1,0},{2,3},{3,2},{4,5},{5,4},{6,7},{7,6},{8,9},{9,8},{10,11... | collective-permute-start | bytes 1769480 | tf_op jit(solution)/shard_map/ppermute | solution.py:38
  33.8 2.0 %collective-permute-start.12 = (bf16[576,512]{1,0:T(8,128)(2,1)S(1)}, bf16[576,512]{1,0:T(8,128)(2,1)S(1)}, u32[]{:S(2)}, u32[]{:S(2)}) collective-permute-start(bf16[576,512]{1,0:T(8,128)(2,1)S(1)} %collective-permute-done.8.rest_2_), channel_id=1, source_target_pairs={{0,1},{1,0},{2,3},{3,2},{4,5},{5,4},{6,7},{7,6},{8,9},{9,8},{10,11... | collective-permute-start | bytes 1769480 | tf_op jit(solution)/shard_map/ppermute | solution.py:38
  33.8 2.8 %collective-permute-start.13 = (bf16[576,512]{1,0:T(8,128)(2,1)S(1)}, bf16[576,512]{1,0:T(8,128)(2,1)S(1)}, u32[]{:S(2)}, u32[]{:S(2)}) collective-permute-start(bf16[576,512]{1,0:T(8,128)(2,1)S(1)} %collective-permute-done.9.rest_3_), channel_id=1, source_target_pairs={{0,1},{1,0},{2,3},{3,2},{4,5},{5,4},{6,7},{7,6},{8,9},{9,8},{10,11... | collective-permute-start | bytes 1769480 | tf_op jit(solution)/shard_map/ppermute | solution.py:38
  41.8 6.8 %collective-permute-start.15 = (bf16[128,512]{1,0:T(8,128)(2,1)S(1)}, bf16[128,512]{1,0:T(8,128)(2,1)S(1)}, u32[]{:S(2)}, u32[]{:S(2)}) collective-permute-start(bf16[128,512]{1,0:T(8,128)(2,1)S(1)} %get-tuple-element.16), channel_id=1, source_target_pairs={{0,2},{1,9},{2,4},{3,11},{4,6},{5,13},{6,0},{7,15},{8,10},{9,17},{... | collective-permute-start | bytes 393224 | tf_op jit(solution)/shard_map/ppermute | solution.py:33
  43.0 7.2 %collective-permute-start.16 = (bf16[128,512]{1,0:T(8,128)(2,1)S(1)}, bf16[128,512]{1,0:T(8,128)(2,1)S(1)}, u32[]{:S(2)}, u32[]{:S(2)}) collective-permute-start(bf16[128,512]{1,0:T(8,128)(2,1)S(1)} %get-tuple-element.16), channel_id=1, source_target_pairs={{0,4},{1,17},{2,6},{3,19},{4,0},{5,21},{6,2},{7,23},{8,12},{9,25},... | collective-permute-start | bytes 393224 | tf_op jit(solution)/shard_map/ppermute | solution.py:33
  45.8 5.0 %collective-permute-start.17 = (bf16[128,512]{1,0:T(8,128)(2,1)S(1)}, bf16[128,512]{1,0:T(8,128)(2,1)S(1)}, u32[]{:S(2)}, u32[]{:S(2)}) collective-permute-start(bf16[128,512]{1,0:T(8,128)(2,1)S(1)} %get-tuple-element.16), channel_id=1, source_target_pairs={{0,6},{1,25},{2,0},{3,27},{4,2},{5,29},{6,4},{7,31},{8,14},{9,1},{... | collective-permute-start | bytes 393224 | tf_op jit(solution)/shard_map/ppermute | solution.py:33
  46.9 13.2 %collective-permute-start.14 = (bf16[512,512]{1,0:T(8,128)(2,1)S(1)}, bf16[512,512]{1,0:T(8,128)(2,1)S(1)}, u32[]{:S(2)}, u32[]{:S(2)}) collective-permute-start(bf16[512,512]{1,0:T(8,128)(2,1)S(1)} %get-tuple-element.14.current_ref.refs_0_), channel_id=1, source_target_pairs={{0,32},{32,64},{64,96},{96,0},{1,33},{33,65},{65,97},{97,1},{2,34}... | collective-permute-start | bytes 1572872 | tf_op jit(solution)/shard_map/ppermute | solution.py:42
  50.9 16.1 %collective-permute-start.18 = (bf16[512,512]{1,0:T(8,128)(2,1)S(1)}, bf16[512,512]{1,0:T(8,128)(2,1)S(1)}, u32[]{:S(2)}, u32[]{:S(2)}) collective-permute-start(bf16[512,512]{1,0:T(8,128)(2,1)S(1)} %constant_dynamic-update-slice_fusion.rest_0_), channel_id=1, source_target_pairs={{0,8},{1,3},{2,10},{3,5},{4,12},{5,7},{6,14},{7,1},{8,16},{9,11},{... | collective-permute-start | bytes 1572872 | tf_op jit(solution)/shard_map/ppermute | solution.py:33
  51.6 15.3 %collective-permute-start.19 = (bf16[512,512]{1,0:T(8,128)(2,1)S(1)}, bf16[512,512]{1,0:T(8,128)(2,1)S(1)}, u32[]{:S(2)}, u32[]{:S(2)}) collective-permute-start(bf16[512,512]{1,0:T(8,128)(2,1)S(1)} %constant_dynamic-update-slice_fusion.rest_0_), channel_id=1, source_target_pairs={{0,16},{1,5},{2,18},{3,7},{4,20},{5,1},{6,22},{7,3},{8,24},{9,13},... | collective-permute-start | bytes 1572872 | tf_op jit(solution)/shard_map/ppermute | solution.py:33
  53.7 14.1 %collective-permute-start.20 = (bf16[512,512]{1,0:T(8,128)(2,1)S(1)}, bf16[512,512]{1,0:T(8,128)(2,1)S(1)}, u32[]{:S(2)}, u32[]{:S(2)}) collective-permute-start(bf16[512,512]{1,0:T(8,128)(2,1)S(1)} %constant_dynamic-update-slice_fusion.rest_0_), channel_id=1, source_target_pairs={{0,24},{1,7},{2,26},{3,1},{4,28},{5,3},{6,30},{7,5},{8,0},{9,15},{... | collective-permute-start | bytes 1572872 | tf_op jit(solution)/shard_map/ppermute | solution.py:33
  55.3 12.6 %collective-permute-start.25 = (bf16[512,512]{1,0:T(8,128)(2,1)S(1)}, bf16[512,512]{1,0:T(8,128)(2,1)S(1)}, u32[]{:S(2)}, u32[]{:S(2)}) collective-permute-start(bf16[512,512]{1,0:T(8,128)(2,1)S(1)} %get-tuple-element.14.current_ref.refs_0_), channel_id=1, source_target_pairs={{32,0},{64,32},{33,1},{65,33},{34,2},{66,34},{35,3},{67,35},{36,4}... | collective-permute-start | bytes 1572872 | tf_op jit(solution)/shard_map/ppermute | solution.py:42
  60.1 7.7 %collective-permute-start.21 = (bf16[512,512]{1,0:T(8,128)(2,1)S(1)}, bf16[512,512]{1,0:T(8,128)(2,1)S(1)}, u32[]{:S(2)}, u32[]{:S(2)}) collective-permute-start(bf16[512,512]{1,0:T(8,128)(2,1)S(1)} %constant_dynamic-update-slice_fusion.rest_0_), channel_id=1, source_target_pairs={{0,1},{1,0},{2,3},{3,2},{4,5},{5,4},{6,7},{7,6},{8,9},{9,8},{10,11... | collective-permute-start | bytes 1572872 | tf_op jit(solution)/shard_map/ppermute | solution.py:38
  67.0 1.9 %collective-permute-start.22 = (bf16[512,512]{1,0:T(8,128)(2,1)S(1)}, bf16[512,512]{1,0:T(8,128)(2,1)S(1)}, u32[]{:S(2)}, u32[]{:S(2)}) collective-permute-start(bf16[512,512]{1,0:T(8,128)(2,1)S(1)} %collective-permute-done.18.rest_1_), channel_id=1, source_target_pairs={{0,1},{1,0},{2,3},{3,2},{4,5},{5,4},{6,7},{7,6},{8,9},{9,8},{10,11... | collective-permute-start | bytes 1572872 | tf_op jit(solution)/shard_map/ppermute | solution.py:38
  67.0 2.7 %collective-permute-start.23 = (bf16[512,512]{1,0:T(8,128)(2,1)S(1)}, bf16[512,512]{1,0:T(8,128)(2,1)S(1)}, u32[]{:S(2)}, u32[]{:S(2)}) collective-permute-start(bf16[512,512]{1,0:T(8,128)(2,1)S(1)} %collective-permute-done.19.rest_2_), channel_id=1, source_target_pairs={{0,1},{1,0},{2,3},{3,2},{4,5},{5,4},{6,7},{7,6},{8,9},{9,8},{10,11... | collective-permute-start | bytes 1572872 | tf_op jit(solution)/shard_map/ppermute | solution.py:38
  67.9 2.5 %collective-permute-start.24 = (bf16[512,512]{1,0:T(8,128)(2,1)S(1)}, bf16[512,512]{1,0:T(8,128)(2,1)S(1)}, u32[]{:S(2)}, u32[]{:S(2)}) collective-permute-start(bf16[512,512]{1,0:T(8,128)(2,1)S(1)} %collective-permute-done.20.rest_3_), channel_id=1, source_target_pairs={{0,1},{1,0},{2,3},{3,2},{4,5},{5,4},{6,7},{7,6},{8,9},{9,8},{10,11... | collective-permute-start | bytes 1572872 | tf_op jit(solution)/shard_map/ppermute | solution.py:38
  73.0 7.3 %collective-permute-start.28 = (bf16[128,512]{1,0:T(8,128)(2,1)S(1)}, bf16[128,512]{1,0:T(8,128)(2,1)S(1)}, u32[]{:S(2)}, u32[]{:S(2)}) collective-permute-start(bf16[128,512]{1,0:T(8,128)(2,1)S(1)} %get-tuple-element.19), channel_id=1, source_target_pairs={{0,2},{1,9},{2,4},{3,11},{4,6},{5,13},{6,0},{7,15},{8,10},{9,17},{... | collective-permute-start | bytes 393224 | tf_op jit(solution)/shard_map/ppermute | solution.py:33
  74.2 6.9 %collective-permute-start.29 = (bf16[128,512]{1,0:T(8,128)(2,1)S(1)}, bf16[128,512]{1,0:T(8,128)(2,1)S(1)}, u32[]{:S(2)}, u32[]{:S(2)}) collective-permute-start(bf16[128,512]{1,0:T(8,128)(2,1)S(1)} %get-tuple-element.19), channel_id=1, source_target_pairs={{0,4},{1,17},{2,6},{3,19},{4,0},{5,21},{6,2},{7,23},{8,12},{9,25},... | collective-permute-start | bytes 393224 | tf_op jit(solution)/shard_map/ppermute | solution.py:33
  76.8 5.0 %collective-permute-start.30 = (bf16[128,512]{1,0:T(8,128)(2,1)S(1)}, bf16[128,512]{1,0:T(8,128)(2,1)S(1)}, u32[]{:S(2)}, u32[]{:S(2)}) collective-permute-start(bf16[128,512]{1,0:T(8,128)(2,1)S(1)} %get-tuple-element.19), channel_id=1, source_target_pairs={{0,6},{1,25},{2,0},{3,27},{4,2},{5,29},{6,4},{7,31},{8,14},{9,1},{... | collective-permute-start | bytes 393224 | tf_op jit(solution)/shard_map/ppermute | solution.py:33
  77.5 12.7 %collective-permute-start.26 = (bf16[512,512]{1,0:T(8,128)(2,1)S(1)}, bf16[512,512]{1,0:T(8,128)(2,1)S(1)}, u32[]{:S(2)}, u32[]{:S(2)}) collective-permute-start(bf16[512,512]{1,0:T(8,128)(2,1)S(1)} %get-tuple-element.17), channel_id=1, source_target_pairs={{64,32},{96,64},{32,0},{65,33},{97,65},{33,1},{66,34},{98,66},{34,... | collective-permute-start | bytes 1572872 | tf_op jit(solution)/shard_map/ppermute | solution.py:42
  81.8 10.5 %collective-permute-start.31 = (bf16[512,512]{1,0:T(8,128)(2,1)S(1)}, bf16[512,512]{1,0:T(8,128)(2,1)S(1)}, u32[]{:S(2)}, u32[]{:S(2)}) collective-permute-start(bf16[512,512]{1,0:T(8,128)(2,1)S(1)} %constant_dynamic-update-slice_fusion.4.rest_0_), channel_id=1, source_target_pairs={{0,8},{1,3},{2,10},{3,5},{4,12},{5,7},{6,14},{7,1},{8,16},{9,11},{... | collective-permute-start | bytes 1572872 | tf_op jit(solution)/shard_map/ppermute | solution.py:33
  82.3 15.8 %collective-permute-start.32 = (bf16[512,512]{1,0:T(8,128)(2,1)S(1)}, bf16[512,512]{1,0:T(8,128)(2,1)S(1)}, u32[]{:S(2)}, u32[]{:S(2)}) collective-permute-start(bf16[512,512]{1,0:T(8,128)(2,1)S(1)} %constant_dynamic-update-slice_fusion.4.rest_0_), channel_id=1, source_target_pairs={{0,16},{1,5},{2,18},{3,7},{4,20},{5,1},{6,22},{7,3},{8,24},{9,13},... | collective-permute-start | bytes 1572872 | tf_op jit(solution)/shard_map/ppermute | solution.py:33
  85.4 13.4 %collective-permute-start.33 = (bf16[512,512]{1,0:T(8,128)(2,1)S(1)}, bf16[512,512]{1,0:T(8,128)(2,1)S(1)}, u32[]{:S(2)}, u32[]{:S(2)}) collective-permute-start(bf16[512,512]{1,0:T(8,128)(2,1)S(1)} %constant_dynamic-update-slice_fusion.4.rest_0_), channel_id=1, source_target_pairs={{0,24},{1,7},{2,26},{3,1},{4,28},{5,3},{6,30},{7,5},{8,0},{9,15},{... | collective-permute-start | bytes 1572872 | tf_op jit(solution)/shard_map/ppermute | solution.py:33
  85.6 13.2 %collective-permute-start.27 = (bf16[512,512]{1,0:T(8,128)(2,1)S(1)}, bf16[512,512]{1,0:T(8,128)(2,1)S(1)}, u32[]{:S(2)}, u32[]{:S(2)}) collective-permute-start(bf16[512,512]{1,0:T(8,128)(2,1)S(1)} %get-tuple-element.18.current_ref.refs_4_), channel_id=1, source_target_pairs={{0,32},{32,64},{64,96},{96,0},{1,33},{33,65},{65,97},{97,1},{2,34}... | collective-permute-start | bytes 1572872 | tf_op jit(solution)/shard_map/ppermute | solution.py:42
  90.3 8.5 %collective-permute-start.34 = (bf16[512,512]{1,0:T(8,128)(2,1)S(1)}, bf16[512,512]{1,0:T(8,128)(2,1)S(1)}, u32[]{:S(2)}, u32[]{:S(2)}) collective-permute-start(bf16[512,512]{1,0:T(8,128)(2,1)S(1)} %constant_dynamic-update-slice_fusion.4.rest_0_), channel_id=1, source_target_pairs={{0,1},{1,0},{2,3},{3,2},{4,5},{5,4},{6,7},{7,6},{8,9},{9,8},{10,11... | collective-permute-start | bytes 1572872 | tf_op jit(solution)/shard_map/ppermute | solution.py:38
  92.3 6.5 %collective-permute-start.35 = (bf16[512,512]{1,0:T(8,128)(2,1)S(1)}, bf16[512,512]{1,0:T(8,128)(2,1)S(1)}, u32[]{:S(2)}, u32[]{:S(2)}) collective-permute-start(bf16[512,512]{1,0:T(8,128)(2,1)S(1)} %collective-permute-done.31.rest_1_), channel_id=1, source_target_pairs={{0,1},{1,0},{2,3},{3,2},{4,5},{5,4},{6,7},{7,6},{8,9},{9,8},{10,11... | collective-permute-start | bytes 1572872 | tf_op jit(solution)/shard_map/ppermute | solution.py:38
  98.1 1.9 %collective-permute-start.36 = (bf16[512,512]{1,0:T(8,128)(2,1)S(1)}, bf16[512,512]{1,0:T(8,128)(2,1)S(1)}, u32[]{:S(2)}, u32[]{:S(2)}) collective-permute-start(bf16[512,512]{1,0:T(8,128)(2,1)S(1)} %collective-permute-done.32.rest_2_), channel_id=1, source_target_pairs={{0,1},{1,0},{2,3},{3,2},{4,5},{5,4},{6,7},{7,6},{8,9},{9,8},{10,11... | collective-permute-start | bytes 1572872 | tf_op jit(solution)/shard_map/ppermute | solution.py:38
  98.8 2.0 %collective-permute-start.37 = (bf16[512,512]{1,0:T(8,128)(2,1)S(1)}, bf16[512,512]{1,0:T(8,128)(2,1)S(1)}, u32[]{:S(2)}, u32[]{:S(2)}) collective-permute-start(bf16[512,512]{1,0:T(8,128)(2,1)S(1)} %collective-permute-done.33.rest_3_), channel_id=1, source_target_pairs={{0,1},{1,0},{2,3},{3,2},{4,5},{5,4},{6,7},{7,6},{8,9},{9,8},{10,11... | collective-permute-start | bytes 1572872 | tf_op jit(solution)/shard_map/ppermute | solution.py:38
  103.4 7.1 %collective-permute-start.41 = (bf16[128,512]{1,0:T(8,128)(2,1)S(1)}, bf16[128,512]{1,0:T(8,128)(2,1)S(1)}, u32[]{:S(2)}, u32[]{:S(2)}) collective-permute-start(bf16[128,512]{1,0:T(8,128)(2,1)S(1)} %get-tuple-element.22), channel_id=1, source_target_pairs={{0,2},{1,9},{2,4},{3,11},{4,6},{5,13},{6,0},{7,15},{8,10},{9,17},{... | collective-permute-start | bytes 393224 | tf_op jit(solution)/shard_map/ppermute | solution.py:33
  104.3 7.3 %collective-permute-start.42 = (bf16[128,512]{1,0:T(8,128)(2,1)S(1)}, bf16[128,512]{1,0:T(8,128)(2,1)S(1)}, u32[]{:S(2)}, u32[]{:S(2)}) collective-permute-start(bf16[128,512]{1,0:T(8,128)(2,1)S(1)} %get-tuple-element.22), channel_id=1, source_target_pairs={{0,4},{1,17},{2,6},{3,19},{4,0},{5,21},{6,2},{7,23},{8,12},{9,25},... | collective-permute-start | bytes 393224 | tf_op jit(solution)/shard_map/ppermute | solution.py:33
  107.3 5.0 %collective-permute-start.43 = (bf16[128,512]{1,0:T(8,128)(2,1)S(1)}, bf16[128,512]{1,0:T(8,128)(2,1)S(1)}, u32[]{:S(2)}, u32[]{:S(2)}) collective-permute-start(bf16[128,512]{1,0:T(8,128)(2,1)S(1)} %get-tuple-element.22), channel_id=1, source_target_pairs={{0,6},{1,25},{2,0},{3,27},{4,2},{5,29},{6,4},{7,31},{8,14},{9,1},{... | collective-permute-start | bytes 393224 | tf_op jit(solution)/shard_map/ppermute | solution.py:33
  107.7 16.4 %collective-permute-start.38 = (bf16[512,512]{1,0:T(8,128)(2,1)S(1)}, bf16[512,512]{1,0:T(8,128)(2,1)S(1)}, u32[]{:S(2)}, u32[]{:S(2)}) collective-permute-start(bf16[512,512]{1,0:T(8,128)(2,1)S(1)} %get-tuple-element.20), channel_id=1, source_target_pairs={{96,64},{0,96},{64,32},{97,65},{1,97},{65,33},{98,66},{2,98},{66,3... | collective-permute-start | bytes 1572872 | tf_op jit(solution)/shard_map/ppermute | solution.py:42
  112.4 11.7 %collective-permute-start.44 = (bf16[512,512]{1,0:T(8,128)(2,1)S(1)}, bf16[512,512]{1,0:T(8,128)(2,1)S(1)}, u32[]{:S(2)}, u32[]{:S(2)}) collective-permute-start(bf16[512,512]{1,0:T(8,128)(2,1)S(1)} %constant_dynamic-update-slice_fusion.8.rest_0_), channel_id=1, source_target_pairs={{0,8},{1,3},{2,10},{3,5},{4,12},{5,7},{6,14},{7,1},{8,16},{9,11},{... | collective-permute-start | bytes 1572872 | tf_op jit(solution)/shard_map/ppermute | solution.py:33
  112.8 16.4 %collective-permute-start.45 = (bf16[512,512]{1,0:T(8,128)(2,1)S(1)}, bf16[512,512]{1,0:T(8,128)(2,1)S(1)}, u32[]{:S(2)}, u32[]{:S(2)}) collective-permute-start(bf16[512,512]{1,0:T(8,128)(2,1)S(1)} %constant_dynamic-update-slice_fusion.8.rest_0_), channel_id=1, source_target_pairs={{0,16},{1,5},{2,18},{3,7},{4,20},{5,1},{6,22},{7,3},{8,24},{9,13},... | collective-permute-start | bytes 1572872 | tf_op jit(solution)/shard_map/ppermute | solution.py:33
  116.4 12.9 %collective-permute-start.46 = (bf16[512,512]{1,0:T(8,128)(2,1)S(1)}, bf16[512,512]{1,0:T(8,128)(2,1)S(1)}, u32[]{:S(2)}, u32[]{:S(2)}) collective-permute-start(bf16[512,512]{1,0:T(8,128)(2,1)S(1)} %constant_dynamic-update-slice_fusion.8.rest_0_), channel_id=1, source_target_pairs={{0,24},{1,7},{2,26},{3,1},{4,28},{5,3},{6,30},{7,5},{8,0},{9,15},{... | collective-permute-start | bytes 1572872 | tf_op jit(solution)/shard_map/ppermute | solution.py:33
  116.4 13.3 %collective-permute-start.39 = (bf16[512,512]{1,0:T(8,128)(2,1)S(1)}, bf16[512,512]{1,0:T(8,128)(2,1)S(1)}, u32[]{:S(2)}, u32[]{:S(2)}) collective-permute-start(bf16[512,512]{1,0:T(8,128)(2,1)S(1)} %get-tuple-element.21.current_ref.refs_8_), channel_id=1, source_target_pairs={{0,32},{32,64},{64,96},{96,0},{1,33},{33,65},{65,97},{97,1},{2,34}... | collective-permute-start | bytes 1572872 | tf_op jit(solution)/shard_map/ppermute | solution.py:42
  124.1 8.4 %collective-permute-start.47 = (bf16[512,512]{1,0:T(8,128)(2,1)S(1)}, bf16[512,512]{1,0:T(8,128)(2,1)S(1)}, u32[]{:S(2)}, u32[]{:S(2)}) collective-permute-start(bf16[512,512]{1,0:T(8,128)(2,1)S(1)} %constant_dynamic-update-slice_fusion.8.rest_0_), channel_id=1, source_target_pairs={{0,1},{1,0},{2,3},{3,2},{4,5},{5,4},{6,7},{7,6},{8,9},{9,8},{10,11... | collective-permute-start | bytes 1572872 | tf_op jit(solution)/shard_map/ppermute | solution.py:38
  124.1 8.4 %collective-permute-start.48 = (bf16[512,512]{1,0:T(8,128)(2,1)S(1)}, bf16[512,512]{1,0:T(8,128)(2,1)S(1)}, u32[]{:S(2)}, u32[]{:S(2)}) collective-permute-start(bf16[512,512]{1,0:T(8,128)(2,1)S(1)} %collective-permute-done.44.rest_1_), channel_id=1, source_target_pairs={{0,1},{1,0},{2,3},{3,2},{4,5},{5,4},{6,7},{7,6},{8,9},{9,8},{10,11... | collective-permute-start | bytes 1572872 | tf_op jit(solution)/shard_map/ppermute | solution.py:38
  129.2 3.3 %collective-permute-start.49 = (bf16[512,512]{1,0:T(8,128)(2,1)S(1)}, bf16[512,512]{1,0:T(8,128)(2,1)S(1)}, u32[]{:S(2)}, u32[]{:S(2)}) collective-permute-start(bf16[512,512]{1,0:T(8,128)(2,1)S(1)} %collective-permute-done.45.rest_2_), channel_id=1, source_target_pairs={{0,1},{1,0},{2,3},{3,2},{4,5},{5,4},{6,7},{7,6},{8,9},{9,8},{10,11... | collective-permute-start | bytes 1572872 | tf_op jit(solution)/shard_map/ppermute | solution.py:38
  129.3 3.2 %collective-permute-start.50 = (bf16[512,512]{1,0:T(8,128)(2,1)S(1)}, bf16[512,512]{1,0:T(8,128)(2,1)S(1)}, u32[]{:S(2)}, u32[]{:S(2)}) collective-permute-start(bf16[512,512]{1,0:T(8,128)(2,1)S(1)} %collective-permute-done.46.rest_3_), channel_id=1, source_target_pairs={{0,1},{1,0},{2,3},{3,2},{4,5},{5,4},{6,7},{7,6},{8,9},{9,8},{10,11... | collective-permute-start | bytes 1572872 | tf_op jit(solution)/shard_map/ppermute | solution.py:38
  129.7 14.2 %collective-permute-start.40 = (bf16[512,512]{1,0:T(8,128)(2,1)S(1)}, bf16[512,512]{1,0:T(8,128)(2,1)S(1)}, u32[]{:S(2)}, u32[]{:S(2)}) collective-permute-start(bf16[512,512]{1,0:T(8,128)(2,1)S(1)} %collective-permute-done.38.rest_8_.refs_6_.refs_11_), channel_id=1, source_target_pairs={{96,64},{97,65},{98,66},{99,67},{100,68},{101,69},{102,70},{103,71... | collective-permute-start | bytes 1572872 | tf_op jit(solution)/shard_map/ppermute | solution.py:42
  135.0 16.0 %collective-permute-start.51 = (bf16[512,512]{1,0:T(8,128)(2,1)S(1)}, bf16[512,512]{1,0:T(8,128)(2,1)S(1)}, u32[]{:S(2)}, u32[]{:S(2)}) collective-permute-start(bf16[512,512]{1,0:T(8,128)(2,1)S(1)} %shard_map.78.refs_12_), channel_id=1, source_target_pairs={{64,96},{65,97},{66,98},{67,99},{68,100},{69,101},{70,102},{71,103... | collective-permute-start | bytes 1572872 | tf_op jit(solution)/shard_map/ppermute | solution.py:42
  136.3 22.4 %collective-permute-start.55 = (bf16[512,512]{1,0:T(8,128)(2,1)S(1)}, bf16[512,512]{1,0:T(8,128)(2,1)S(1)}, u32[]{:S(2)}, u32[]{:S(2)}) collective-permute-start(bf16[512,512]{1,0:T(8,128)(2,1)S(1)} %shard_map.78.refs_12_), channel_id=1, source_target_pairs={{0,96},{1,97},{2,98},{3,99},{4,100},{5,101},{6,102},{7,103},{8,104... | collective-permute-start | bytes 1572872 | tf_op jit(solution)/shard_map/ppermute | solution.py:42
  137.6 2.0 %collective-permute-start.52 = (bf16[256,512]{1,0:T(8,128)(2,1)S(1)}, bf16[256,512]{1,0:T(8,128)(2,1)S(1)}, u32[]{:S(2)}, u32[]{:S(2)}) collective-permute-start(bf16[256,512]{1,0:T(8,128)(2,1)S(1)} %get-tuple-element.26), channel_id=1, source_target_pairs={{32,64},{33,65},{34,66},{35,67},{36,68},{37,69},{38,70},{39,71},{4... | collective-permute-start | bytes 786440 | tf_op jit(solution)/shard_map/ppermute | solution.py:42
  138.3 12.5 %collective-permute-start.54 = (bf16[256,512]{1,0:T(8,128)(2,1)S(1)}, bf16[256,512]{1,0:T(8,128)(2,1)S(1)}, u32[]{:S(2)}, u32[]{:S(2)}) collective-permute-start(bf16[256,512]{1,0:T(8,128)(2,1)S(1)} %get-tuple-element.25), channel_id=1, source_target_pairs={{32,96},{33,97},{34,98},{35,99},{36,100},{37,101},{38,102},{39,103... | collective-permute-start | bytes 786440 | tf_op jit(solution)/shard_map/ppermute | solution.py:42
  139.6 19.1 %collective-permute-start.53 = (bf16[256,512]{1,0:T(8,128)(2,1)S(1)}, bf16[256,512]{1,0:T(8,128)(2,1)S(1)}, u32[]{:S(2)}, u32[]{:S(2)}) collective-permute-start(bf16[256,512]{1,0:T(8,128)(2,1)S(1)} %collective-permute-done.52), channel_id=1, source_target_pairs={{64,96},{65,97},{66,98},{67,99},{68,100},{69,101},{70,102},{71,103... | collective-permute-start | bytes 786440 | tf_op jit(solution)/shard_map/ppermute | solution.py:42

commit v8 on v7

--- a/solution.py
+++ b/solution.py
@@ -11,6 +11,7 @@
 SIDE = 4
 CORES = 2
 EXTRA = 16
+PIECES = 4
 ANY = pl.BlockSpec(memory_space=pl.ANY)
 SMEM = pl.BlockSpec(memory_space=pltpu.SMEM)
 HBM = pl.BlockSpec(memory_space=pltpu.HBM)
@@ -192,7 +193,11 @@
                 rows = source.shape[0]
                 target = out_ref.at[(layer_id - distance) % spans, pl.ds(start % out_ref.shape[1], rows)]
                 start += rows
-                copies.append(pltpu.make_async_copy(source, target, sems.at[i]))
+                piece = rows // PIECES
+                for at in range(PIECES):
+                    within = pl.ds(at * piece, piece)
+                    sem = sems.at[i * PIECES + at]
+                    copies.append(pltpu.make_async_copy(source.at[within], target.at[within], sem))
             for copy in copies:
                 copy.start()
             for copy in copies:
@@ -299,7 +304,7 @@
         out_shape=jax.ShapeDtypeStruct(features.shape, features.dtype),
         in_specs=[VMEM] * len(placed),
         out_specs=HBM,
-        scratch_shapes=[pltpu.SemaphoreType.DMA((5,))],
+        scratch_shapes=[pltpu.SemaphoreType.DMA((5 * PIECES,))],
         compiler_params=params,
     )(*placed)
 

time: 160 us -> 161 us (level)
  no operation moved by 1% of the time
where the time goes in v8:
time: 161 us; the launch traced here: 160 us
  waiting for transfers between devices  72.4 us (45%)
  starting transfers between devices  67.2 us (42%)
  Pallas kernels  15.7 us (10%)
  local copies, waits for them, and re-layouts  3.41 us (2%)
    ppermute x24, starting transfers between devices, along(): return lax.ppermute(block, 'node', route)  39.1 us
    ppermute x24, waiting for transfers between devices, along(): return lax.ppermute(block, 'node', route)  33.6 us
    ppermute x15, waiting for transfers between devices, to_plane(): return lax.ppermute(block, 'layer', pairs)  32.7 us
    ppermute x15, starting transfers between devices, to_plane(): return lax.ppermute(block, 'layer', pairs)  25.5 us
    pallas_call x4, Pallas kernels, on_device(): pl.pallas_call(functools.partial(layer_kernel, layer_id, first, last), ou...  12.8 us
    ppermute x17, waiting for transfers between devices, other_core(): return lax.ppermute(block, 'node', route)  6.1 us
  transfers between devices with their start and end apart: 56, of which 30 were waited for; matrix products, arithmetic and copies ran while one was open for 1% of the time, Pallas kernels for 2%

profile of v8, /device:TPU:6, one launch (start us, length us, event | category | flops | bytes accessed | tf_op | source)
XLA Modules:
  0.0 160.3 jit_solution(6988756861939303343)
XLA Ops:
  0.1 2.2 %dynamic-slice_bitcast_fusion.1 = (bf16[512,512]{1,0:T(8,128)(2,1)}, bf16[512,512]{1,0:T(8,128)(2,1)S(1)}) fusion(bf16[4,512,512]{2,1,0:T(8,128)(2,1)} %param.7, s32[]{:T(128)S(6)} %max.3, s32[]{:T(128)S(6)} %select_n.17), kind=kLoop, calls=%fused_computation.3 | loop fusion | bytes 2097160 | tf_op jit(solution)/shard_map/jit(dynamic_index_in_dim)/squeeze | solution.py:236
  2.3 0.8 shard_map.74
  3.1 1.6 %collective-permute-start.4 = (bf16[144,512]{1,0:T(8,128)(2,1)S(1)}, bf16[144,512]{1,0:T(8,128)(2,1)S(1)}, u32[]{:S(2)}, u32[]{:S(2)}) collective-permute-start(bf16[144,512]{1,0:T(8,128)(2,1)S(1)} %shard_map.74), channel_id=1, source_target_pairs={{0,2},{1,9},{2,4},{3,11},{4,6},{5,13},{6,0},{7,15},{8,10},{9,17},{... | collective-permute-start | bytes 442376 | tf_op jit(solution)/shard_map/ppermute | solution.py:34
  4.8 2.9 %collective-permute-start.5 = (bf16[144,512]{1,0:T(8,128)(2,1)S(1)}, bf16[144,512]{1,0:T(8,128)(2,1)}, u32[]{:S(2)}, u32[]{:S(2)}) collective-permute-start(bf16[144,512]{1,0:T(8,128)(2,1)S(1)} %shard_map.74), channel_id=1, source_target_pairs={{0,4},{1,17},{2,6},{3,19},{4,0},{5,21},{6,2},{7,23},{8,12},{9,25},... | collective-permute-start | bytes 442376 | tf_op jit(solution)/shard_map/ppermute | solution.py:34
  7.7 1.3 collective-permute-start.6
  9.0 1.0 dynamic-slice_bitcast_fusion.3
  10.6 2.4 %collective-permute-start.1 = (bf16[256,512]{1,0:T(8,128)(2,1)S(1)}, bf16[256,512]{1,0:T(8,128)(2,1)S(1)}, u32[]{:S(2)}, u32[]{:S(2)}) collective-permute-start(bf16[256,512]{1,0:T(8,128)(2,1)S(1)} %dynamic-slice_bitcast_fusion.3), channel_id=1, source_target_pairs={{0,64},{32,96},{64,0},{96,32},{1,65},{33,97},{65,1},{97,33},{2,66}... | collective-permute-start | bytes 786440 | tf_op jit(solution)/shard_map/ppermute | solution.py:43
  13.0 1.0 pad_maximum_fusion.1.rest_0_
  14.0 2.0 %collective-permute-start.7 = (bf16[576,512]{1,0:T(8,128)(2,1)S(1)}, bf16[576,512]{1,0:T(8,128)(2,1)S(1)}, u32[]{:S(2)}, u32[]{:S(2)}) collective-permute-start(bf16[576,512]{1,0:T(8,128)(2,1)S(1)} %pad_maximum_fusion.1.rest_0_), channel_id=1, source_target_pairs={{0,8},{1,3},{2,10},{3,5},{4,12},{5,7},{6,14},{7,1},{8,16},{9,11},{... | collective-permute-start | bytes 1769480 | tf_op jit(solution)/shard_map/ppermute | solution.py:34
  16.0 3.6 %collective-permute-start.8 = (bf16[576,512]{1,0:T(8,128)(2,1)S(1)}, bf16[576,512]{1,0:T(8,128)(2,1)S(1)}, u32[]{:S(2)}, u32[]{:S(2)}) collective-permute-start(bf16[576,512]{1,0:T(8,128)(2,1)S(1)} %pad_maximum_fusion.1.rest_0_), channel_id=1, source_target_pairs={{0,16},{1,5},{2,18},{3,7},{4,20},{5,1},{6,22},{7,3},{8,24},{9,13},... | collective-permute-start | bytes 1769480 | tf_op jit(solution)/shard_map/ppermute | solution.py:34
  19.6 1.5 collective-permute-start.9
  21.4 4.0 %collective-permute-done.2 = bf16[256,512]{1,0:T(8,128)(2,1)S(1)} collective-permute-done((bf16[256,512]{1,0:T(8,128)(2,1)S(1)}, bf16[256,512]{1,0:T(8,128)(2,1)S(1)}, u32[]{:S(2)}, u32[]{:S(2)}) %collective-permute-start.2) | collective-permute-done | bytes 262176 | tf_op jit(solution)/shard_map/ppermute | solution.py:43
  26.1 7.7 %collective-permute-done.8.rest_2_ = bf16[576,512]{1,0:T(8,128)(2,1)S(1)} collective-permute-done((bf16[576,512]{1,0:T(8,128)(2,1)S(1)}, bf16[576,512]{1,0:T(8,128)(2,1)S(1)}, u32[]{:S(2)}, u32[]{:S(2)}) %collective-permute-start.8) | collective-permute-done | bytes 589856 | tf_op jit(solution)/shard_map/ppermute | solution.py:34
  35.1 0.7 collective-permute-done.12.rest_6_
  35.8 0.8 collective-permute-done.13.rest_7_
  36.7 5.2 %shard_map.75 = (bf16[512,512]{1,0:T(8,128)(2,1)S(1)}, bf16[128,512]{1,0:T(8,128)(2,1)S(1)}, bf16[20,128,256]{2,1,0:T(8,128)(2,1)S(1)}) custom-call(s32[2]{0:T(128)S(1)} %pad_add_fusion.place_ref, s32[4,4]{1,0:T(4,128)S(1)} %bitcast.12, s32[4,20]{1,0:T(4,128)S(1)} %bitcast.16, bf16[128,512]{1,0:T(8,128)(2,1)S(1)} %shard_map.73.listed_ref, ...), custom_call_target="tpu_custom_call" | custom-call | tf_op jit(solution)/shard_map/pallas_call | solution.py:266
  41.8 1.2 collective-permute-start.15
  43.0 2.8 %collective-permute-start.16 = (bf16[128,512]{1,0:T(8,128)(2,1)S(1)}, bf16[128,512]{1,0:T(8,128)(2,1)S(1)}, u32[]{:S(2)}, u32[]{:S(2)}) collective-permute-start(bf16[128,512]{1,0:T(8,128)(2,1)S(1)} %get-tuple-element.16), channel_id=1, source_target_pairs={{0,4},{1,17},{2,6},{3,19},{4,0},{5,21},{6,2},{7,23},{8,12},{9,25},... | collective-permute-start | bytes 393224 | tf_op jit(solution)/shard_map/ppermute | solution.py:34
  45.8 1.1 collective-permute-start.17
  46.9 1.7 %collective-permute-start.14 = (bf16[512,512]{1,0:T(8,128)(2,1)S(1)}, bf16[512,512]{1,0:T(8,128)(2,1)S(1)}, u32[]{:S(2)}, u32[]{:S(2)}) collective-permute-start(bf16[512,512]{1,0:T(8,128)(2,1)S(1)} %get-tuple-element.14.current_ref.refs_0_), channel_id=1, source_target_pairs={{0,32},{32,64},{64,96},{96,0},{1,33},{33,65},{65,97},{97,1},{2,34}... | collective-permute-start | bytes 1572872 | tf_op jit(solution)/shard_map/ppermute | solution.py:43
  48.7 1.5 collective-permute-done.16
  50.2 0.7 collective-permute-done.17
  50.9 0.7 collective-permute-start.18
  51.6 2.1 %collective-permute-start.19 = (bf16[512,512]{1,0:T(8,128)(2,1)S(1)}, bf16[512,512]{1,0:T(8,128)(2,1)S(1)}, u32[]{:S(2)}, u32[]{:S(2)}) collective-permute-start(bf16[512,512]{1,0:T(8,128)(2,1)S(1)} %constant_dynamic-update-slice_fusion.rest_0_), channel_id=1, source_target_pairs={{0,16},{1,5},{2,18},{3,7},{4,20},{5,1},{6,22},{7,3},{8,24},{9,13},... | collective-permute-start | bytes 1572872 | tf_op jit(solution)/shard_map/ppermute | solution.py:34
  53.7 1.5 collective-permute-start.20
  56.0 4.2 %collective-permute-done.14.previous_ref.refs_1_ = bf16[512,512]{1,0:T(8,128)(2,1)S(1)} collective-permute-done((bf16[512,512]{1,0:T(8,128)(2,1)S(1)}, bf16[512,512]{1,0:T(8,128)(2,1)S(1)}, u32[]{:S(2)}, u32[]{:S(2)}) %collective-permute-start.14) | collective-permute-done | bytes 524320 | tf_op jit(solution)/shard_map/ppermute | solution.py:43
  60.2 6.8 %collective-permute-done.18.rest_1_ = bf16[512,512]{1,0:T(8,128)(2,1)S(1)} collective-permute-done((bf16[512,512]{1,0:T(8,128)(2,1)S(1)}, bf16[512,512]{1,0:T(8,128)(2,1)S(1)}, u32[]{:S(2)}, u32[]{:S(2)}) %collective-permute-start.18) | collective-permute-done | bytes 524320 | tf_op jit(solution)/shard_map/ppermute | solution.py:34
  67.9 1.0 collective-permute-done.22.rest_5_
  68.9 0.7 collective-permute-done.23.rest_6_
  69.6 0.7 collective-permute-done.24.rest_7_
  70.4 2.6 %shard_map.76 = (bf16[512,512]{1,0:T(8,128)(2,1)S(1)}, bf16[128,512]{1,0:T(8,128)(2,1)S(1)}, bf16[512,512]{1,0:T(8,128)(2,1)S(1)}) custom-call(s32[2]{0:T(128)S(1)} %pad_add_fusion.place_ref, s32[4,4]{1,0:T(4,128)S(1)} %bitcast.13, s32[4,20]{1,0:T(4,128)S(1)} %bitcast.17, bf16[128,512]{1,0:T(8,128)(2,1)S(1)} %shard_map.73.listed_ref, ...), custom_call_target="tpu_custom_call" | custom-call | tf_op jit(solution)/shard_map/pallas_call | solution.py:266
  73.0 1.3 collective-permute-start.28
  74.2 2.5 %collective-permute-start.29 = (bf16[128,512]{1,0:T(8,128)(2,1)S(1)}, bf16[128,512]{1,0:T(8,128)(2,1)S(1)}, u32[]{:S(2)}, u32[]{:S(2)}) collective-permute-start(bf16[128,512]{1,0:T(8,128)(2,1)S(1)} %get-tuple-element.19), channel_id=1, source_target_pairs={{0,4},{1,17},{2,6},{3,19},{4,0},{5,21},{6,2},{7,23},{8,12},{9,25},... | collective-permute-start | bytes 393224 | tf_op jit(solution)/shard_map/ppermute | solution.py:34
  76.8 0.8 collective-permute-start.30
  77.5 2.8 %collective-permute-start.26 = (bf16[512,512]{1,0:T(8,128)(2,1)S(1)}, bf16[512,512]{1,0:T(8,128)(2,1)S(1)}, u32[]{:S(2)}, u32[]{:S(2)}) collective-permute-start(bf16[512,512]{1,0:T(8,128)(2,1)S(1)} %get-tuple-element.17), channel_id=1, source_target_pairs={{64,32},{96,64},{32,0},{65,33},{97,65},{33,1},{66,34},{98,66},{34,... | collective-permute-start | bytes 1572872 | tf_op jit(solution)/shard_map/ppermute | solution.py:43
  80.3 0.8 collective-permute-done.29
  81.1 0.7 collective-permute-done.30
  82.3 3.1 %collective-permute-start.32 = (bf16[512,512]{1,0:T(8,128)(2,1)S(1)}, bf16[512,512]{1,0:T(8,128)(2,1)S(1)}, u32[]{:S(2)}, u32[]{:S(2)}) collective-permute-start(bf16[512,512]{1,0:T(8,128)(2,1)S(1)} %constant_dynamic-update-slice_fusion.4.rest_0_), channel_id=1, source_target_pairs={{0,16},{1,5},{2,18},{3,7},{4,20},{5,1},{6,22},{7,3},{8,24},{9,13},... | collective-permute-start | bytes 1572872 | tf_op jit(solution)/shard_map/ppermute | solution.py:34
  85.6 3.1 %collective-permute-start.27 = (bf16[512,512]{1,0:T(8,128)(2,1)S(1)}, bf16[512,512]{1,0:T(8,128)(2,1)S(1)}, u32[]{:S(2)}, u32[]{:S(2)}) collective-permute-start(bf16[512,512]{1,0:T(8,128)(2,1)S(1)} %get-tuple-element.18.current_ref.refs_4_), channel_id=1, source_target_pairs={{0,32},{32,64},{64,96},{96,0},{1,33},{33,65},{65,97},{97,1},{2,34}... | collective-permute-start | bytes 1572872 | tf_op jit(solution)/shard_map/ppermute | solution.py:43
  88.7 1.6 collective-permute-done.26.rest_8_.refs_2_.refs_7_
  90.3 2.0 %collective-permute-done.31.rest_1_ = bf16[512,512]{1,0:T(8,128)(2,1)S(1)} collective-permute-done((bf16[512,512]{1,0:T(8,128)(2,1)S(1)}, bf16[512,512]{1,0:T(8,128)(2,1)S(1)}, u32[]{:S(2)}, u32[]{:S(2)}) %collective-permute-start.31) | collective-permute-done | bytes 524320 | tf_op jit(solution)/shard_map/ppermute | solution.py:34
  92.3 5.9 %collective-permute-done.32.rest_2_ = bf16[512,512]{1,0:T(8,128)(2,1)S(1)} collective-permute-done((bf16[512,512]{1,0:T(8,128)(2,1)S(1)}, bf16[512,512]{1,0:T(8,128)(2,1)S(1)}, u32[]{:S(2)}, u32[]{:S(2)}) %collective-permute-start.32) | collective-permute-done | bytes 524320 | tf_op jit(solution)/shard_map/ppermute | solution.py:34
  98.8 1.2 collective-permute-done.36.rest_6_
  100.1 0.7 collective-permute-done.37.rest_7_
  100.8 2.6 %shard_map.77 = (bf16[512,512]{1,0:T(8,128)(2,1)S(1)}, bf16[128,512]{1,0:T(8,128)(2,1)S(1)}, bf16[512,512]{1,0:T(8,128)(2,1)S(1)}) custom-call(s32[2]{0:T(128)S(1)} %pad_add_fusion.place_ref, s32[4,4]{1,0:T(4,128)S(1)} %bitcast.14, s32[4,20]{1,0:T(4,128)S(1)} %bitcast.18, bf16[128,512]{1,0:T(8,128)(2,1)S(1)} %shard_map.73.listed_ref, ...), custom_call_target="tpu_custom_call" | custom-call | tf_op jit(solution)/shard_map/pallas_call | solution.py:266
  103.4 0.9 collective-permute-start.41
  104.3 3.0 %collective-permute-start.42 = (bf16[128,512]{1,0:T(8,128)(2,1)S(1)}, bf16[128,512]{1,0:T(8,128)(2,1)S(1)}, u32[]{:S(2)}, u32[]{:S(2)}) collective-permute-start(bf16[128,512]{1,0:T(8,128)(2,1)S(1)} %get-tuple-element.22), channel_id=1, source_target_pairs={{0,4},{1,17},{2,6},{3,19},{4,0},{5,21},{6,2},{7,23},{8,12},{9,25},... | collective-permute-start | bytes 393224 | tf_op jit(solution)/shard_map/ppermute | solution.py:34
  107.7 2.8 %collective-permute-start.38 = (bf16[512,512]{1,0:T(8,128)(2,1)S(1)}, bf16[512,512]{1,0:T(8,128)(2,1)S(1)}, u32[]{:S(2)}, u32[]{:S(2)}) collective-permute-start(bf16[512,512]{1,0:T(8,128)(2,1)S(1)} %get-tuple-element.20), channel_id=1, source_target_pairs={{96,64},{0,96},{64,32},{97,65},{1,97},{65,33},{98,66},{2,98},{66,3... | collective-permute-start | bytes 1572872 | tf_op jit(solution)/shard_map/ppermute | solution.py:43
  110.5 1.1 collective-permute-done.42
  111.7 0.7 collective-permute-done.43
  112.8 3.7 %collective-permute-start.45 = (bf16[512,512]{1,0:T(8,128)(2,1)S(1)}, bf16[512,512]{1,0:T(8,128)(2,1)S(1)}, u32[]{:S(2)}, u32[]{:S(2)}) collective-permute-start(bf16[512,512]{1,0:T(8,128)(2,1)S(1)} %constant_dynamic-update-slice_fusion.8.rest_0_), channel_id=1, source_target_pairs={{0,16},{1,5},{2,18},{3,7},{4,20},{5,1},{6,22},{7,3},{8,24},{9,13},... | collective-permute-start | bytes 1572872 | tf_op jit(solution)/shard_map/ppermute | solution.py:34
  116.4 2.8 %collective-permute-start.39 = (bf16[512,512]{1,0:T(8,128)(2,1)S(1)}, bf16[512,512]{1,0:T(8,128)(2,1)S(1)}, u32[]{:S(2)}, u32[]{:S(2)}) collective-permute-start(bf16[512,512]{1,0:T(8,128)(2,1)S(1)} %get-tuple-element.21.current_ref.refs_8_), channel_id=1, source_target_pairs={{0,32},{32,64},{64,96},{96,0},{1,33},{33,65},{65,97},{97,1},{2,34}... | collective-permute-start | bytes 1572872 | tf_op jit(solution)/shard_map/ppermute | solution.py:43
  119.2 4.9 %collective-permute-done.38.rest_8_.refs_6_.refs_11_ = bf16[512,512]{1,0:T(8,128)(2,1)S(1)} collective-permute-done((bf16[512,512]{1,0:T(8,128)(2,1)S(1)}, bf16[512,512]{1,0:T(8,128)(2,1)S(1)}, u32[]{:S(2)}, u32[]{:S(2)}) %collective-permute-start.38) | collective-permute-done | bytes 524320 | tf_op jit(solution)/shard_map/ppermute | solution.py:43
  124.6 4.6 %collective-permute-done.45.rest_2_ = bf16[512,512]{1,0:T(8,128)(2,1)S(1)} collective-permute-done((bf16[512,512]{1,0:T(8,128)(2,1)S(1)}, bf16[512,512]{1,0:T(8,128)(2,1)S(1)}, u32[]{:S(2)}, u32[]{:S(2)}) %collective-permute-start.45) | collective-permute-done | bytes 524320 | tf_op jit(solution)/shard_map/ppermute | solution.py:34
  129.7 2.8 %collective-permute-start.40 = (bf16[512,512]{1,0:T(8,128)(2,1)S(1)}, bf16[512,512]{1,0:T(8,128)(2,1)S(1)}, u32[]{:S(2)}, u32[]{:S(2)}) collective-permute-start(bf16[512,512]{1,0:T(8,128)(2,1)S(1)} %collective-permute-done.38.rest_8_.refs_6_.refs_11_), channel_id=1, source_target_pairs={{96,64},{97,65},{98,66},{99,67},{100,68},{101,69},{102,70},{103,71... | collective-permute-start | bytes 1572872 | tf_op jit(solution)/shard_map/ppermute | solution.py:43
  132.5 2.4 %shard_map.78.refs_12_ = bf16[512,512]{1,0:T(8,128)(2,1)S(1)} custom-call(s32[2]{0:T(128)S(1)} %pad_add_fusion.place_ref, s32[4,4]{1,0:T(4,128)S(1)} %bitcast.15, s32[4,20]{1,0:T(4,128)S(1)} %bitcast.19, bf16[128,512]{1,0:T(8,128)(2,1)S(1)} %shard_map.73.listed_ref, bf16[512,512]{1,0:T(8,128)(2,1)S(1)} %get-tuple-element.21.current_ref.refs_8_, ...), custom_call_target="tpu_custom_call" | custom-call | tf_op jit(solution)/shard_map/pallas_call | solution.py:266
  135.0 1.3 collective-permute-start.51
  136.3 1.3 collective-permute-start.55
  138.3 1.3 collective-permute-start.54
  139.6 1.3 collective-permute-start.53
  140.9 3.1 %collective-permute-done.40.refs_10_ = bf16[512,512]{1,0:T(8,128)(2,1)S(1)} collective-permute-done((bf16[512,512]{1,0:T(8,128)(2,1)S(1)}, bf16[512,512]{1,0:T(8,128)(2,1)S(1)}, u32[]{:S(2)}, u32[]{:S(2)}) %collective-permute-start.40) | collective-permute-done | bytes 524320 | tf_op jit(solution)/shard_map/ppermute | solution.py:43
  143.9 6.9 %collective-permute-done.54.refs_15_ = bf16[256,512]{1,0:T(8,128)(2,1)S(1)} collective-permute-done((bf16[256,512]{1,0:T(8,128)(2,1)S(1)}, bf16[256,512]{1,0:T(8,128)(2,1)S(1)}, u32[]{:S(2)}, u32[]{:S(2)}) %collective-permute-start.54) | collective-permute-done | bytes 262176 | tf_op jit(solution)/shard_map/ppermute | solution.py:43
  150.9 7.8 %collective-permute-done.55.refs_16_ = bf16[512,512]{1,0:T(8,128)(2,1)S(1)} collective-permute-done((bf16[512,512]{1,0:T(8,128)(2,1)S(1)}, bf16[512,512]{1,0:T(8,128)(2,1)S(1)}, u32[]{:S(2)}, u32[]{:S(2)}) %collective-permute-start.55) | collective-permute-done | bytes 524320 | tf_op jit(solution)/shard_map/ppermute | solution.py:43
  158.7 1.5 shard_map.79
  (86 shorter events, 8.6 us)
Async XLA Ops:
  0.0 35.0 %copy-start = (bf16[4,1,20,128,128]{4,3,2,1,0:T(8,128)(2,1)S(1)}, bf16[4,1,20,128,128]{4,3,2,1,0:T(8,128)(2,1)}, u32[]{:S(2)}) copy-start(bf16[4,1,20,128,128]{4,3,2,1,0:T(8,128)(2,1)} %param.13) | copy-start | bytes 7864324
  0.0 2.3 %copy-start.2 = (s32[4,1,32,64]{3,2,1,0:T(8,128)S(1)}, s32[4,1,32,64]{3,2,1,0:T(8,128)}, u32[]{:S(2)}) copy-start(s32[4,1,32,64]{3,2,1,0:T(8,128)} %lists_ref.1) | copy-start | bytes 98308
  0.0 2.3 %copy-start.5 = (s32[4,1,128]{2,1,0:T(1,128)S(1)}, s32[4,1,128]{2,1,0:T(1,128)}, u32[]{:S(2)}) copy-start(s32[4,1,128]{2,1,0:T(1,128)} %listed_ref.3) | copy-start | bytes 6148
  3.1 9.9 %collective-permute-start.4 = (bf16[144,512]{1,0:T(8,128)(2,1)S(1)}, bf16[144,512]{1,0:T(8,128)(2,1)S(1)}, u32[]{:S(2)}, u32[]{:S(2)}) collective-permute-start(bf16[144,512]{1,0:T(8,128)(2,1)S(1)} %shard_map.74), channel_id=1, source_target_pairs={{0,2},{1,9},{2,4},{3,11},{4,6},{5,13},{6,0},{7,15},{8,10},{9,17},{... | collective-permute-start | bytes 442376 | tf_op jit(solution)/shard_map/ppermute | solution.py:34
  4.8 8.2 %collective-permute-start.5 = (bf16[144,512]{1,0:T(8,128)(2,1)S(1)}, bf16[144,512]{1,0:T(8,128)(2,1)}, u32[]{:S(2)}, u32[]{:S(2)}) collective-permute-start(bf16[144,512]{1,0:T(8,128)(2,1)S(1)} %shard_map.74), channel_id=1, source_target_pairs={{0,4},{1,17},{2,6},{3,19},{4,0},{5,21},{6,2},{7,23},{8,12},{9,25},... | collective-permute-start | bytes 442376 | tf_op jit(solution)/shard_map/ppermute | solution.py:34
  7.7 5.3 %collective-permute-start.6 = (bf16[144,512]{1,0:T(8,128)(2,1)S(1)}, bf16[144,512]{1,0:T(8,128)(2,1)}, u32[]{:S(2)}, u32[]{:S(2)}) collective-permute-start(bf16[144,512]{1,0:T(8,128)(2,1)S(1)} %shard_map.74), channel_id=1, source_target_pairs={{0,6},{1,25},{2,0},{3,27},{4,2},{5,29},{6,4},{7,31},{8,14},{9,1},{... | collective-permute-start | bytes 442376 | tf_op jit(solution)/shard_map/ppermute | solution.py:34
  10.0 26.6 %copy-start.1 = (bf16[512,512]{1,0:T(8,128)(2,1)S(1)}, bf16[512,512]{1,0:T(8,128)(2,1)}, u32[]{:S(2)}) copy-start(bf16[512,512]{1,0:T(8,128)(2,1)} %get-tuple-element.23.previous_ref) | copy-start | bytes 1572868
  10.0 26.6 %copy-start.3 = (s32[4,1,4]{2,1,0:T(1,128)S(1)}, s32[4,1,4]{2,1,0:T(1,128)}, u32[]{:S(2)}) copy-start(s32[4,1,4]{2,1,0:T(1,128)} %param.11) | copy-start | bytes 196
  10.0 26.6 %copy-start.4 = (s32[4,1,20]{2,1,0:T(1,128)S(1)}, s32[4,1,20]{2,1,0:T(1,128)}, u32[]{:S(2)}) copy-start(s32[4,1,20]{2,1,0:T(1,128)} %param.12) | copy-start | bytes 964
  10.0 9.6 %collective-permute-start = (bf16[256,512]{1,0:T(8,128)(2,1)S(1)}, bf16[256,512]{1,0:T(8,128)(2,1)S(1)}, u32[]{:S(2)}, u32[]{:S(2)}) collective-permute-start(bf16[256,512]{1,0:T(8,128)(2,1)S(1)} %dynamic-slice_bitcast_fusion.3), channel_id=1, source_target_pairs={{0,32},{32,64},{64,96},{96,0},{1,33},{33,65},{65,97},{97,1},{2,34}... | collective-permute-start | bytes 786440 | tf_op jit(solution)/shard_map/ppermute | solution.py:43
  10.6 10.8 %collective-permute-start.1 = (bf16[256,512]{1,0:T(8,128)(2,1)S(1)}, bf16[256,512]{1,0:T(8,128)(2,1)S(1)}, u32[]{:S(2)}, u32[]{:S(2)}) collective-permute-start(bf16[256,512]{1,0:T(8,128)(2,1)S(1)} %dynamic-slice_bitcast_fusion.3), channel_id=1, source_target_pairs={{0,64},{32,96},{64,0},{96,32},{1,65},{33,97},{65,1},{97,33},{2,66}... | collective-permute-start | bytes 786440 | tf_op jit(solution)/shard_map/ppermute | solution.py:43
  13.0 12.4 %collective-permute-start.2 = (bf16[256,512]{1,0:T(8,128)(2,1)S(1)}, bf16[256,512]{1,0:T(8,128)(2,1)S(1)}, u32[]{:S(2)}, u32[]{:S(2)}) collective-permute-start(bf16[256,512]{1,0:T(8,128)(2,1)S(1)} %dynamic-slice_bitcast_fusion.3), channel_id=1, source_target_pairs={{0,96},{32,0},{64,32},{96,64},{1,97},{33,1},{65,33},{97,65},{2,98}... | collective-permute-start | bytes 786440 | tf_op jit(solution)/shard_map/ppermute | solution.py:43
  14.0 12.0 %collective-permute-start.7 = (bf16[576,512]{1,0:T(8,128)(2,1)S(1)}, bf16[576,512]{1,0:T(8,128)(2,1)S(1)}, u32[]{:S(2)}, u32[]{:S(2)}) collective-permute-start(bf16[576,512]{1,0:T(8,128)(2,1)S(1)} %pad_maximum_fusion.1.rest_0_), channel_id=1, source_target_pairs={{0,8},{1,3},{2,10},{3,5},{4,12},{5,7},{6,14},{7,1},{8,16},{9,11},{... | collective-permute-start | bytes 1769480 | tf_op jit(solution)/shard_map/ppermute | solution.py:34
  16.0 17.8 %collective-permute-start.8 = (bf16[576,512]{1,0:T(8,128)(2,1)S(1)}, bf16[576,512]{1,0:T(8,128)(2,1)S(1)}, u32[]{:S(2)}, u32[]{:S(2)}) collective-permute-start(bf16[576,512]{1,0:T(8,128)(2,1)S(1)} %pad_maximum_fusion.1.rest_0_), channel_id=1, source_target_pairs={{0,16},{1,5},{2,18},{3,7},{4,20},{5,1},{6,22},{7,3},{8,24},{9,13},... | collective-permute-start | bytes 1769480 | tf_op jit(solution)/shard_map/ppermute | solution.py:34
  19.6 14.2 %collective-permute-start.9 = (bf16[576,512]{1,0:T(8,128)(2,1)S(1)}, bf16[576,512]{1,0:T(8,128)(2,1)S(1)}, u32[]{:S(2)}, u32[]{:S(2)}) collective-permute-start(bf16[576,512]{1,0:T(8,128)(2,1)S(1)} %pad_maximum_fusion.1.rest_0_), channel_id=1, source_target_pairs={{0,24},{1,7},{2,26},{3,1},{4,28},{5,3},{6,30},{7,5},{8,0},{9,15},{... | collective-permute-start | bytes 1769480 | tf_op jit(solution)/shard_map/ppermute | solution.py:34
  25.4 9.6 %collective-permute-start.3 = (bf16[1024,512]{1,0:T(8,128)(2,1)S(1)}, bf16[1024,512]{1,0:T(8,128)(2,1)S(1)}, u32[]{:S(2)}, u32[]{:S(2)}) collective-permute-start(bf16[1024,512]{1,0:T(8,128)(2,1)S(1)} %pad_maximum_fusion.halves_ref), channel_id=1, source_target_pairs={{0,1},{1,0},{2,3},{3,2},{4,5},{5,4},{6,7},{7,6},{8,9},{9,8},{10,11... | collective-permute-start | bytes 3145736 | tf_op jit(solution)/shard_map/ppermute | solution.py:39
  25.5 9.5 %collective-permute-start.10 = (bf16[576,512]{1,0:T(8,128)(2,1)S(1)}, bf16[576,512]{1,0:T(8,128)(2,1)S(1)}, u32[]{:S(2)}, u32[]{:S(2)}) collective-permute-start(bf16[576,512]{1,0:T(8,128)(2,1)S(1)} %pad_maximum_fusion.1.rest_0_), channel_id=1, source_target_pairs={{0,1},{1,0},{2,3},{3,2},{4,5},{5,4},{6,7},{7,6},{8,9},{9,8},{10,11... | collective-permute-start | bytes 1769480 | tf_op jit(solution)/shard_map/ppermute | solution.py:39
  26.0 9.0 %collective-permute-start.11 = (bf16[576,512]{1,0:T(8,128)(2,1)S(1)}, bf16[576,512]{1,0:T(8,128)(2,1)S(1)}, u32[]{:S(2)}, u32[]{:S(2)}) collective-permute-start(bf16[576,512]{1,0:T(8,128)(2,1)S(1)} %collective-permute-done.7.rest_1_), channel_id=1, source_target_pairs={{0,1},{1,0},{2,3},{3,2},{4,5},{5,4},{6,7},{7,6},{8,9},{9,8},{10,11... | collective-permute-start | bytes 1769480 | tf_op jit(solution)/shard_map/ppermute | solution.py:39
  33.8 2.0 %collective-permute-start.12 = (bf16[576,512]{1,0:T(8,128)(2,1)S(1)}, bf16[576,512]{1,0:T(8,128)(2,1)S(1)}, u32[]{:S(2)}, u32[]{:S(2)}) collective-permute-start(bf16[576,512]{1,0:T(8,128)(2,1)S(1)} %collective-permute-done.8.rest_2_), channel_id=1, source_target_pairs={{0,1},{1,0},{2,3},{3,2},{4,5},{5,4},{6,7},{7,6},{8,9},{9,8},{10,11... | collective-permute-start | bytes 1769480 | tf_op jit(solution)/shard_map/ppermute | solution.py:39
  33.8 2.8 %collective-permute-start.13 = (bf16[576,512]{1,0:T(8,128)(2,1)S(1)}, bf16[576,512]{1,0:T(8,128)(2,1)S(1)}, u32[]{:S(2)}, u32[]{:S(2)}) collective-permute-start(bf16[576,512]{1,0:T(8,128)(2,1)S(1)} %collective-permute-done.9.rest_3_), channel_id=1, source_target_pairs={{0,1},{1,0},{2,3},{3,2},{4,5},{5,4},{6,7},{7,6},{8,9},{9,8},{10,11... | collective-permute-start | bytes 1769480 | tf_op jit(solution)/shard_map/ppermute | solution.py:39
  41.8 6.8 %collective-permute-start.15 = (bf16[128,512]{1,0:T(8,128)(2,1)S(1)}, bf16[128,512]{1,0:T(8,128)(2,1)S(1)}, u32[]{:S(2)}, u32[]{:S(2)}) collective-permute-start(bf16[128,512]{1,0:T(8,128)(2,1)S(1)} %get-tuple-element.16), channel_id=1, source_target_pairs={{0,2},{1,9},{2,4},{3,11},{4,6},{5,13},{6,0},{7,15},{8,10},{9,17},{... | collective-permute-start | bytes 393224 | tf_op jit(solution)/shard_map/ppermute | solution.py:34
  43.0 7.2 %collective-permute-start.16 = (bf16[128,512]{1,0:T(8,128)(2,1)S(1)}, bf16[128,512]{1,0:T(8,128)(2,1)S(1)}, u32[]{:S(2)}, u32[]{:S(2)}) collective-permute-start(bf16[128,512]{1,0:T(8,128)(2,1)S(1)} %get-tuple-element.16), channel_id=1, source_target_pairs={{0,4},{1,17},{2,6},{3,19},{4,0},{5,21},{6,2},{7,23},{8,12},{9,25},... | collective-permute-start | bytes 393224 | tf_op jit(solution)/shard_map/ppermute | solution.py:34
  45.8 5.0 %collective-permute-start.17 = (bf16[128,512]{1,0:T(8,128)(2,1)S(1)}, bf16[128,512]{1,0:T(8,128)(2,1)S(1)}, u32[]{:S(2)}, u32[]{:S(2)}) collective-permute-start(bf16[128,512]{1,0:T(8,128)(2,1)S(1)} %get-tuple-element.16), channel_id=1, source_target_pairs={{0,6},{1,25},{2,0},{3,27},{4,2},{5,29},{6,4},{7,31},{8,14},{9,1},{... | collective-permute-start | bytes 393224 | tf_op jit(solution)/shard_map/ppermute | solution.py:34
  46.9 13.2 %collective-permute-start.14 = (bf16[512,512]{1,0:T(8,128)(2,1)S(1)}, bf16[512,512]{1,0:T(8,128)(2,1)S(1)}, u32[]{:S(2)}, u32[]{:S(2)}) collective-permute-start(bf16[512,512]{1,0:T(8,128)(2,1)S(1)} %get-tuple-element.14.current_ref.refs_0_), channel_id=1, source_target_pairs={{0,32},{32,64},{64,96},{96,0},{1,33},{33,65},{65,97},{97,1},{2,34}... | collective-permute-start | bytes 1572872 | tf_op jit(solution)/shard_map/ppermute | solution.py:43
  50.9 16.1 %collective-permute-start.18 = (bf16[512,512]{1,0:T(8,128)(2,1)S(1)}, bf16[512,512]{1,0:T(8,128)(2,1)S(1)}, u32[]{:S(2)}, u32[]{:S(2)}) collective-permute-start(bf16[512,512]{1,0:T(8,128)(2,1)S(1)} %constant_dynamic-update-slice_fusion.rest_0_), channel_id=1, source_target_pairs={{0,8},{1,3},{2,10},{3,5},{4,12},{5,7},{6,14},{7,1},{8,16},{9,11},{... | collective-permute-start | bytes 1572872 | tf_op jit(solution)/shard_map/ppermute | solution.py:34
  51.6 15.3 %collective-permute-start.19 = (bf16[512,512]{1,0:T(8,128)(2,1)S(1)}, bf16[512,512]{1,0:T(8,128)(2,1)S(1)}, u32[]{:S(2)}, u32[]{:S(2)}) collective-permute-start(bf16[512,512]{1,0:T(8,128)(2,1)S(1)} %constant_dynamic-update-slice_fusion.rest_0_), channel_id=1, source_target_pairs={{0,16},{1,5},{2,18},{3,7},{4,20},{5,1},{6,22},{7,3},{8,24},{9,13},... | collective-permute-start | bytes 1572872 | tf_op jit(solution)/shard_map/ppermute | solution.py:34
  53.7 14.1 %collective-permute-start.20 = (bf16[512,512]{1,0:T(8,128)(2,1)S(1)}, bf16[512,512]{1,0:T(8,128)(2,1)S(1)}, u32[]{:S(2)}, u32[]{:S(2)}) collective-permute-start(bf16[512,512]{1,0:T(8,128)(2,1)S(1)} %constant_dynamic-update-slice_fusion.rest_0_), channel_id=1, source_target_pairs={{0,24},{1,7},{2,26},{3,1},{4,28},{5,3},{6,30},{7,5},{8,0},{9,15},{... | collective-permute-start | bytes 1572872 | tf_op jit(solution)/shard_map/ppermute | solution.py:34
  55.3 12.6 %collective-permute-start.25 = (bf16[512,512]{1,0:T(8,128)(2,1)S(1)}, bf16[512,512]{1,0:T(8,128)(2,1)S(1)}, u32[]{:S(2)}, u32[]{:S(2)}) collective-permute-start(bf16[512,512]{1,0:T(8,128)(2,1)S(1)} %get-tuple-element.14.current_ref.refs_0_), channel_id=1, source_target_pairs={{32,0},{64,32},{33,1},{65,33},{34,2},{66,34},{35,3},{67,35},{36,4}... | collective-permute-start | bytes 1572872 | tf_op jit(solution)/shard_map/ppermute | solution.py:43
  60.1 7.7 %collective-permute-start.21 = (bf16[512,512]{1,0:T(8,128)(2,1)S(1)}, bf16[512,512]{1,0:T(8,128)(2,1)S(1)}, u32[]{:S(2)}, u32[]{:S(2)}) collective-permute-start(bf16[512,512]{1,0:T(8,128)(2,1)S(1)} %constant_dynamic-update-slice_fusion.rest_0_), channel_id=1, source_target_pairs={{0,1},{1,0},{2,3},{3,2},{4,5},{5,4},{6,7},{7,6},{8,9},{9,8},{10,11... | collective-permute-start | bytes 1572872 | tf_op jit(solution)/shard_map/ppermute | solution.py:39
  67.0 1.9 %collective-permute-start.22 = (bf16[512,512]{1,0:T(8,128)(2,1)S(1)}, bf16[512,512]{1,0:T(8,128)(2,1)S(1)}, u32[]{:S(2)}, u32[]{:S(2)}) collective-permute-start(bf16[512,512]{1,0:T(8,128)(2,1)S(1)} %collective-permute-done.18.rest_1_), channel_id=1, source_target_pairs={{0,1},{1,0},{2,3},{3,2},{4,5},{5,4},{6,7},{7,6},{8,9},{9,8},{10,11... | collective-permute-start | bytes 1572872 | tf_op jit(solution)/shard_map/ppermute | solution.py:39
  67.0 2.7 %collective-permute-start.23 = (bf16[512,512]{1,0:T(8,128)(2,1)S(1)}, bf16[512,512]{1,0:T(8,128)(2,1)S(1)}, u32[]{:S(2)}, u32[]{:S(2)}) collective-permute-start(bf16[512,512]{1,0:T(8,128)(2,1)S(1)} %collective-permute-done.19.rest_2_), channel_id=1, source_target_pairs={{0,1},{1,0},{2,3},{3,2},{4,5},{5,4},{6,7},{7,6},{8,9},{9,8},{10,11... | collective-permute-start | bytes 1572872 | tf_op jit(solution)/shard_map/ppermute | solution.py:39
  67.9 2.5 %collective-permute-start.24 = (bf16[512,512]{1,0:T(8,128)(2,1)S(1)}, bf16[512,512]{1,0:T(8,128)(2,1)S(1)}, u32[]{:S(2)}, u32[]{:S(2)}) collective-permute-start(bf16[512,512]{1,0:T(8,128)(2,1)S(1)} %collective-permute-done.20.rest_3_), channel_id=1, source_target_pairs={{0,1},{1,0},{2,3},{3,2},{4,5},{5,4},{6,7},{7,6},{8,9},{9,8},{10,11... | collective-permute-start | bytes 1572872 | tf_op jit(solution)/shard_map/ppermute | solution.py:39
  73.0 7.3 %collective-permute-start.28 = (bf16[128,512]{1,0:T(8,128)(2,1)S(1)}, bf16[128,512]{1,0:T(8,128)(2,1)S(1)}, u32[]{:S(2)}, u32[]{:S(2)}) collective-permute-start(bf16[128,512]{1,0:T(8,128)(2,1)S(1)} %get-tuple-element.19), channel_id=1, source_target_pairs={{0,2},{1,9},{2,4},{3,11},{4,6},{5,13},{6,0},{7,15},{8,10},{9,17},{... | collective-permute-start | bytes 393224 | tf_op jit(solution)/shard_map/ppermute | solution.py:34
  74.2 6.9 %collective-permute-start.29 = (bf16[128,512]{1,0:T(8,128)(2,1)S(1)}, bf16[128,512]{1,0:T(8,128)(2,1)S(1)}, u32[]{:S(2)}, u32[]{:S(2)}) collective-permute-start(bf16[128,512]{1,0:T(8,128)(2,1)S(1)} %get-tuple-element.19), channel_id=1, source_target_pairs={{0,4},{1,17},{2,6},{3,19},{4,0},{5,21},{6,2},{7,23},{8,12},{9,25},... | collective-permute-start | bytes 393224 | tf_op jit(solution)/shard_map/ppermute | solution.py:34
  76.8 5.0 %collective-permute-start.30 = (bf16[128,512]{1,0:T(8,128)(2,1)S(1)}, bf16[128,512]{1,0:T(8,128)(2,1)S(1)}, u32[]{:S(2)}, u32[]{:S(2)}) collective-permute-start(bf16[128,512]{1,0:T(8,128)(2,1)S(1)} %get-tuple-element.19), channel_id=1, source_target_pairs={{0,6},{1,25},{2,0},{3,27},{4,2},{5,29},{6,4},{7,31},{8,14},{9,1},{... | collective-permute-start | bytes 393224 | tf_op jit(solution)/shard_map/ppermute | solution.py:34
  77.5 12.7 %collective-permute-start.26 = (bf16[512,512]{1,0:T(8,128)(2,1)S(1)}, bf16[512,512]{1,0:T(8,128)(2,1)S(1)}, u32[]{:S(2)}, u32[]{:S(2)}) collective-permute-start(bf16[512,512]{1,0:T(8,128)(2,1)S(1)} %get-tuple-element.17), channel_id=1, source_target_pairs={{64,32},{96,64},{32,0},{65,33},{97,65},{33,1},{66,34},{98,66},{34,... | collective-permute-start | bytes 1572872 | tf_op jit(solution)/shard_map/ppermute | solution.py:43
  81.8 10.5 %collective-permute-start.31 = (bf16[512,512]{1,0:T(8,128)(2,1)S(1)}, bf16[512,512]{1,0:T(8,128)(2,1)S(1)}, u32[]{:S(2)}, u32[]{:S(2)}) collective-permute-start(bf16[512,512]{1,0:T(8,128)(2,1)S(1)} %constant_dynamic-update-slice_fusion.4.rest_0_), channel_id=1, source_target_pairs={{0,8},{1,3},{2,10},{3,5},{4,12},{5,7},{6,14},{7,1},{8,16},{9,11},{... | collective-permute-start | bytes 1572872 | tf_op jit(solution)/shard_map/ppermute | solution.py:34
  82.3 15.8 %collective-permute-start.32 = (bf16[512,512]{1,0:T(8,128)(2,1)S(1)}, bf16[512,512]{1,0:T(8,128)(2,1)S(1)}, u32[]{:S(2)}, u32[]{:S(2)}) collective-permute-start(bf16[512,512]{1,0:T(8,128)(2,1)S(1)} %constant_dynamic-update-slice_fusion.4.rest_0_), channel_id=1, source_target_pairs={{0,16},{1,5},{2,18},{3,7},{4,20},{5,1},{6,22},{7,3},{8,24},{9,13},... | collective-permute-start | bytes 1572872 | tf_op jit(solution)/shard_map/ppermute | solution.py:34
  85.4 13.4 %collective-permute-start.33 = (bf16[512,512]{1,0:T(8,128)(2,1)S(1)}, bf16[512,512]{1,0:T(8,128)(2,1)S(1)}, u32[]{:S(2)}, u32[]{:S(2)}) collective-permute-start(bf16[512,512]{1,0:T(8,128)(2,1)S(1)} %constant_dynamic-update-slice_fusion.4.rest_0_), channel_id=1, source_target_pairs={{0,24},{1,7},{2,26},{3,1},{4,28},{5,3},{6,30},{7,5},{8,0},{9,15},{... | collective-permute-start | bytes 1572872 | tf_op jit(solution)/shard_map/ppermute | solution.py:34
  85.6 13.2 %collective-permute-start.27 = (bf16[512,512]{1,0:T(8,128)(2,1)S(1)}, bf16[512,512]{1,0:T(8,128)(2,1)S(1)}, u32[]{:S(2)}, u32[]{:S(2)}) collective-permute-start(bf16[512,512]{1,0:T(8,128)(2,1)S(1)} %get-tuple-element.18.current_ref.refs_4_), channel_id=1, source_target_pairs={{0,32},{32,64},{64,96},{96,0},{1,33},{33,65},{65,97},{97,1},{2,34}... | collective-permute-start | bytes 1572872 | tf_op jit(solution)/shard_map/ppermute | solution.py:43
  90.3 8.5 %collective-permute-start.34 = (bf16[512,512]{1,0:T(8,128)(2,1)S(1)}, bf16[512,512]{1,0:T(8,128)(2,1)S(1)}, u32[]{:S(2)}, u32[]{:S(2)}) collective-permute-start(bf16[512,512]{1,0:T(8,128)(2,1)S(1)} %constant_dynamic-update-slice_fusion.4.rest_0_), channel_id=1, source_target_pairs={{0,1},{1,0},{2,3},{3,2},{4,5},{5,4},{6,7},{7,6},{8,9},{9,8},{10,11... | collective-permute-start | bytes 1572872 | tf_op jit(solution)/shard_map/ppermute | solution.py:39
  92.3 6.5 %collective-permute-start.35 = (bf16[512,512]{1,0:T(8,128)(2,1)S(1)}, bf16[512,512]{1,0:T(8,128)(2,1)S(1)}, u32[]{:S(2)}, u32[]{:S(2)}) collective-permute-start(bf16[512,512]{1,0:T(8,128)(2,1)S(1)} %collective-permute-done.31.rest_1_), channel_id=1, source_target_pairs={{0,1},{1,0},{2,3},{3,2},{4,5},{5,4},{6,7},{7,6},{8,9},{9,8},{10,11... | collective-permute-start | bytes 1572872 | tf_op jit(solution)/shard_map/ppermute | solution.py:39
  98.1 1.9 %collective-permute-start.36 = (bf16[512,512]{1,0:T(8,128)(2,1)S(1)}, bf16[512,512]{1,0:T(8,128)(2,1)S(1)}, u32[]{:S(2)}, u32[]{:S(2)}) collective-permute-start(bf16[512,512]{1,0:T(8,128)(2,1)S(1)} %collective-permute-done.32.rest_2_), channel_id=1, source_target_pairs={{0,1},{1,0},{2,3},{3,2},{4,5},{5,4},{6,7},{7,6},{8,9},{9,8},{10,11... | collective-permute-start | bytes 1572872 | tf_op jit(solution)/shard_map/ppermute | solution.py:39
  98.8 2.0 %collective-permute-start.37 = (bf16[512,512]{1,0:T(8,128)(2,1)S(1)}, bf16[512,512]{1,0:T(8,128)(2,1)S(1)}, u32[]{:S(2)}, u32[]{:S(2)}) collective-permute-start(bf16[512,512]{1,0:T(8,128)(2,1)S(1)} %collective-permute-done.33.rest_3_), channel_id=1, source_target_pairs={{0,1},{1,0},{2,3},{3,2},{4,5},{5,4},{6,7},{7,6},{8,9},{9,8},{10,11... | collective-permute-start | bytes 1572872 | tf_op jit(solution)/shard_map/ppermute | solution.py:39
  103.4 7.1 %collective-permute-start.41 = (bf16[128,512]{1,0:T(8,128)(2,1)S(1)}, bf16[128,512]{1,0:T(8,128)(2,1)S(1)}, u32[]{:S(2)}, u32[]{:S(2)}) collective-permute-start(bf16[128,512]{1,0:T(8,128)(2,1)S(1)} %get-tuple-element.22), channel_id=1, source_target_pairs={{0,2},{1,9},{2,4},{3,11},{4,6},{5,13},{6,0},{7,15},{8,10},{9,17},{... | collective-permute-start | bytes 393224 | tf_op jit(solution)/shard_map/ppermute | solution.py:34
  104.3 7.3 %collective-permute-start.42 = (bf16[128,512]{1,0:T(8,128)(2,1)S(1)}, bf16[128,512]{1,0:T(8,128)(2,1)S(1)}, u32[]{:S(2)}, u32[]{:S(2)}) collective-permute-start(bf16[128,512]{1,0:T(8,128)(2,1)S(1)} %get-tuple-element.22), channel_id=1, source_target_pairs={{0,4},{1,17},{2,6},{3,19},{4,0},{5,21},{6,2},{7,23},{8,12},{9,25},... | collective-permute-start | bytes 393224 | tf_op jit(solution)/shard_map/ppermute | solution.py:34
  107.3 5.0 %collective-permute-start.43 = (bf16[128,512]{1,0:T(8,128)(2,1)S(1)}, bf16[128,512]{1,0:T(8,128)(2,1)S(1)}, u32[]{:S(2)}, u32[]{:S(2)}) collective-permute-start(bf16[128,512]{1,0:T(8,128)(2,1)S(1)} %get-tuple-element.22), channel_id=1, source_target_pairs={{0,6},{1,25},{2,0},{3,27},{4,2},{5,29},{6,4},{7,31},{8,14},{9,1},{... | collective-permute-start | bytes 393224 | tf_op jit(solution)/shard_map/ppermute | solution.py:34
  107.7 16.4 %collective-permute-start.38 = (bf16[512,512]{1,0:T(8,128)(2,1)S(1)}, bf16[512,512]{1,0:T(8,128)(2,1)S(1)}, u32[]{:S(2)}, u32[]{:S(2)}) collective-permute-start(bf16[512,512]{1,0:T(8,128)(2,1)S(1)} %get-tuple-element.20), channel_id=1, source_target_pairs={{96,64},{0,96},{64,32},{97,65},{1,97},{65,33},{98,66},{2,98},{66,3... | collective-permute-start | bytes 1572872 | tf_op jit(solution)/shard_map/ppermute | solution.py:43
  112.4 11.7 %collective-permute-start.44 = (bf16[512,512]{1,0:T(8,128)(2,1)S(1)}, bf16[512,512]{1,0:T(8,128)(2,1)S(1)}, u32[]{:S(2)}, u32[]{:S(2)}) collective-permute-start(bf16[512,512]{1,0:T(8,128)(2,1)S(1)} %constant_dynamic-update-slice_fusion.8.rest_0_), channel_id=1, source_target_pairs={{0,8},{1,3},{2,10},{3,5},{4,12},{5,7},{6,14},{7,1},{8,16},{9,11},{... | collective-permute-start | bytes 1572872 | tf_op jit(solution)/shard_map/ppermute | solution.py:34
  112.8 16.4 %collective-permute-start.45 = (bf16[512,512]{1,0:T(8,128)(2,1)S(1)}, bf16[512,512]{1,0:T(8,128)(2,1)S(1)}, u32[]{:S(2)}, u32[]{:S(2)}) collective-permute-start(bf16[512,512]{1,0:T(8,128)(2,1)S(1)} %constant_dynamic-update-slice_fusion.8.rest_0_), channel_id=1, source_target_pairs={{0,16},{1,5},{2,18},{3,7},{4,20},{5,1},{6,22},{7,3},{8,24},{9,13},... | collective-permute-start | bytes 1572872 | tf_op jit(solution)/shard_map/ppermute | solution.py:34
  116.4 12.9 %collective-permute-start.46 = (bf16[512,512]{1,0:T(8,128)(2,1)S(1)}, bf16[512,512]{1,0:T(8,128)(2,1)S(1)}, u32[]{:S(2)}, u32[]{:S(2)}) collective-permute-start(bf16[512,512]{1,0:T(8,128)(2,1)S(1)} %constant_dynamic-update-slice_fusion.8.rest_0_), channel_id=1, source_target_pairs={{0,24},{1,7},{2,26},{3,1},{4,28},{5,3},{6,30},{7,5},{8,0},{9,15},{... | collective-permute-start | bytes 1572872 | tf_op jit(solution)/shard_map/ppermute | solution.py:34
  116.4 13.3 %collective-permute-start.39 = (bf16[512,512]{1,0:T(8,128)(2,1)S(1)}, bf16[512,512]{1,0:T(8,128)(2,1)S(1)}, u32[]{:S(2)}, u32[]{:S(2)}) collective-permute-start(bf16[512,512]{1,0:T(8,128)(2,1)S(1)} %get-tuple-element.21.current_ref.refs_8_), channel_id=1, source_target_pairs={{0,32},{32,64},{64,96},{96,0},{1,33},{33,65},{65,97},{97,1},{2,34}... | collective-permute-start | bytes 1572872 | tf_op jit(solution)/shard_map/ppermute | solution.py:43
  124.1 8.4 %collective-permute-start.47 = (bf16[512,512]{1,0:T(8,128)(2,1)S(1)}, bf16[512,512]{1,0:T(8,128)(2,1)S(1)}, u32[]{:S(2)}, u32[]{:S(2)}) collective-permute-start(bf16[512,512]{1,0:T(8,128)(2,1)S(1)} %constant_dynamic-update-slice_fusion.8.rest_0_), channel_id=1, source_target_pairs={{0,1},{1,0},{2,3},{3,2},{4,5},{5,4},{6,7},{7,6},{8,9},{9,8},{10,11... | collective-permute-start | bytes 1572872 | tf_op jit(solution)/shard_map/ppermute | solution.py:39
  124.1 8.4 %collective-permute-start.48 = (bf16[512,512]{1,0:T(8,128)(2,1)S(1)}, bf16[512,512]{1,0:T(8,128)(2,1)S(1)}, u32[]{:S(2)}, u32[]{:S(2)}) collective-permute-start(bf16[512,512]{1,0:T(8,128)(2,1)S(1)} %collective-permute-done.44.rest_1_), channel_id=1, source_target_pairs={{0,1},{1,0},{2,3},{3,2},{4,5},{5,4},{6,7},{7,6},{8,9},{9,8},{10,11... | collective-permute-start | bytes 1572872 | tf_op jit(solution)/shard_map/ppermute | solution.py:39
  129.2 3.3 %collective-permute-start.49 = (bf16[512,512]{1,0:T(8,128)(2,1)S(1)}, bf16[512,512]{1,0:T(8,128)(2,1)S(1)}, u32[]{:S(2)}, u32[]{:S(2)}) collective-permute-start(bf16[512,512]{1,0:T(8,128)(2,1)S(1)} %collective-permute-done.45.rest_2_), channel_id=1, source_target_pairs={{0,1},{1,0},{2,3},{3,2},{4,5},{5,4},{6,7},{7,6},{8,9},{9,8},{10,11... | collective-permute-start | bytes 1572872 | tf_op jit(solution)/shard_map/ppermute | solution.py:39
  129.3 3.2 %collective-permute-start.50 = (bf16[512,512]{1,0:T(8,128)(2,1)S(1)}, bf16[512,512]{1,0:T(8,128)(2,1)S(1)}, u32[]{:S(2)}, u32[]{:S(2)}) collective-permute-start(bf16[512,512]{1,0:T(8,128)(2,1)S(1)} %collective-permute-done.46.rest_3_), channel_id=1, source_target_pairs={{0,1},{1,0},{2,3},{3,2},{4,5},{5,4},{6,7},{7,6},{8,9},{9,8},{10,11... | collective-permute-start | bytes 1572872 | tf_op jit(solution)/shard_map/ppermute | solution.py:39
  129.7 14.2 %collective-permute-start.40 = (bf16[512,512]{1,0:T(8,128)(2,1)S(1)}, bf16[512,512]{1,0:T(8,128)(2,1)S(1)}, u32[]{:S(2)}, u32[]{:S(2)}) collective-permute-start(bf16[512,512]{1,0:T(8,128)(2,1)S(1)} %collective-permute-done.38.rest_8_.refs_6_.refs_11_), channel_id=1, source_target_pairs={{96,64},{97,65},{98,66},{99,67},{100,68},{101,69},{102,70},{103,71... | collective-permute-start | bytes 1572872 | tf_op jit(solution)/shard_map/ppermute | solution.py:43
  135.0 16.0 %collective-permute-start.51 = (bf16[512,512]{1,0:T(8,128)(2,1)S(1)}, bf16[512,512]{1,0:T(8,128)(2,1)S(1)}, u32[]{:S(2)}, u32[]{:S(2)}) collective-permute-start(bf16[512,512]{1,0:T(8,128)(2,1)S(1)} %shard_map.78.refs_12_), channel_id=1, source_target_pairs={{64,96},{65,97},{66,98},{67,99},{68,100},{69,101},{70,102},{71,103... | collective-permute-start | bytes 1572872 | tf_op jit(solution)/shard_map/ppermute | solution.py:43
  136.3 22.4 %collective-permute-start.55 = (bf16[512,512]{1,0:T(8,128)(2,1)S(1)}, bf16[512,512]{1,0:T(8,128)(2,1)S(1)}, u32[]{:S(2)}, u32[]{:S(2)}) collective-permute-start(bf16[512,512]{1,0:T(8,128)(2,1)S(1)} %shard_map.78.refs_12_), channel_id=1, source_target_pairs={{0,96},{1,97},{2,98},{3,99},{4,100},{5,101},{6,102},{7,103},{8,104... | collective-permute-start | bytes 1572872 | tf_op jit(solution)/shard_map/ppermute | solution.py:43
  137.6 2.0 %collective-permute-start.52 = (bf16[256,512]{1,0:T(8,128)(2,1)S(1)}, bf16[256,512]{1,0:T(8,128)(2,1)S(1)}, u32[]{:S(2)}, u32[]{:S(2)}) collective-permute-start(bf16[256,512]{1,0:T(8,128)(2,1)S(1)} %get-tuple-element.26), channel_id=1, source_target_pairs={{32,64},{33,65},{34,66},{35,67},{36,68},{37,69},{38,70},{39,71},{4... | collective-permute-start | bytes 786440 | tf_op jit(solution)/shard_map/ppermute | solution.py:43
  138.3 12.5 %collective-permute-start.54 = (bf16[256,512]{1,0:T(8,128)(2,1)S(1)}, bf16[256,512]{1,0:T(8,128)(2,1)S(1)}, u32[]{:S(2)}, u32[]{:S(2)}) collective-permute-start(bf16[256,512]{1,0:T(8,128)(2,1)S(1)} %get-tuple-element.25), channel_id=1, source_target_pairs={{32,96},{33,97},{34,98},{35,99},{36,100},{37,101},{38,102},{39,103... | collective-permute-start | bytes 786440 | tf_op jit(solution)/shard_map/ppermute | solution.py:43
  139.6 19.1 %collective-permute-start.53 = (bf16[256,512]{1,0:T(8,128)(2,1)S(1)}, bf16[256,512]{1,0:T(8,128)(2,1)S(1)}, u32[]{:S(2)}, u32[]{:S(2)}) collective-permute-start(bf16[256,512]{1,0:T(8,128)(2,1)S(1)} %collective-permute-done.52), channel_id=1, source_target_pairs={{64,96},{65,97},{66,98},{67,99},{68,100},{69,101},{70,102},{71,103... | collective-permute-start | bytes 786440 | tf_op jit(solution)/shard_map/ppermute | solution.py:43
